TPU v7x, 32 devices: a whole 2x2x4 slice. The times are simulated.
32 devices in a mesh: dp: 2 (over x), blk: 4 (over y, core), head: 4 (over z).
Axes of the slice: x: 2, y: 2, z: 4, core: 2. Of those that a mesh axis runs over, the one named last changes fastest.
Arguments:
- hidden: bfloat16 [2, 4096, 2048], P('dp', ('blk', 'head')), may hold values from -6 to 6
- teacher: bfloat16 [2, 4096, 2048], P('dp', ('blk', 'head')), may hold values from -6 to 6
- lengths: int32 [2], P('dp'), may hold values from 3073 to 4096, as said below
- attn_gain: bfloat16 [2048], P(('dp', 'blk', 'head')), may hold values from 0.5 to 1.5
- w_query: bfloat16 [2048, 2048], P(('dp', 'blk', 'head')), may hold values from -0.4375 to 0.4375
- key_projection: bfloat16 [2048, 512], P(('dp', 'blk', 'head')), may hold values from -0.4375 to 0.4375
- value_projection: bfloat16 [2048, 512], P(('dp', 'blk', 'head')), may hold values from -0.125 to 0.125
- w_out: bfloat16 [2048, 2048], P(('dp', 'blk', 'head')), may hold values from -4 to 4
- mlp_gain: bfloat16 [2048], P(('dp', 'blk', 'head')), may hold values from 0.5 to 1.5
- w_gate: bfloat16 [2048, 8192], P(('dp', 'blk', 'head')), may hold values from -0.125 to 0.125
- w_up: bfloat16 [2048, 8192], P(('dp', 'blk', 'head')), may hold values from -0.125 to 0.125
- w_down: bfloat16 [8192, 2048], P(('dp', 'blk', 'head')), may hold values from -0.25 to 0.25
Outputs:
- output: bfloat16 [2, 4096, 2048], P('dp', ('blk', 'head'))
- mse_loss: float32 [], replicated
- grad_hidden: float32 [2, 4096, 2048], P('dp', ('blk', 'head'))
- grad_attn_gain: float32 [2048], P(('dp', 'blk', 'head'))
- grad_query: float32 [2048, 2048], P(('dp', 'blk', 'head'))
- grad_key: float32 [2048, 512], P(('dp', 'blk', 'head'))
- grad_value: float32 [2048, 512], P(('dp', 'blk', 'head'))
- grad_out: float32 [2048, 2048], P(('dp', 'blk', 'head'))
- grad_mlp_gain: float32 [2048], P(('dp', 'blk', 'head'))
- grad_gate: float32 [2048, 8192], P(('dp', 'blk', 'head'))
- grad_up: float32 [2048, 8192], P(('dp', 'blk', 'head'))
- grad_down: float32 [8192, 2048], P(('dp', 'blk', 'head'))
Inputs may be any that keep to these rules, and one draw needn't show every extreme that they name: `lengths`: in every draw some sequence has all 4096 slots valid; unused slots of a sequence lie within its last 1024 slots.
All inputs are finite; a program needn't handle non-finite values.
Results may differ from a plain program's by a relative error of at most 0.014.
Values may be sent and summed in bfloat16 or wider, within the bound.
A program may use at most 448 MiB of HBM per device.

v0:
```python
import jax
import jax.numpy as jnp
from jax import lax
from jax.sharding import PartitionSpec as P

MODEL_WIDTH = 2048
HEAD_SIZE = 64


ROPE_BASE = 10000000.0
NORM_EPS = 1e-05
ATTN_SCALE = 0.015625
RESIDUAL_SCALE = 0.22
MASKED = -1e30


def rope_tables(places):
    half_size = HEAD_SIZE // 2
    frequency = ROPE_BASE ** (-(jnp.arange(half_size).astype(jnp.float32) * 2.0) / HEAD_SIZE)
    angles = places.astype(jnp.float32)[:, None] * frequency[None, :]
    cosine = jnp.concatenate([jnp.cos(angles), jnp.cos(angles)], axis=1)
    sine_table = jnp.concatenate([jnp.sin(angles), jnp.sin(angles)], axis=1)
    return (cosine, sine_table)


def rotate_rows(values, cosine, sine_table):
    shape_in = values.shape
    half_size = HEAD_SIZE // 2
    pieces = values.reshape(shape_in[0], shape_in[1], shape_in[2] // HEAD_SIZE, HEAD_SIZE)
    turned = jnp.concatenate([-pieces[..., half_size:], pieces[..., :half_size]], axis=-1)
    result = pieces * cosine[None, :, None, :] + turned * sine_table[None, :, None, :]
    return result.reshape(shape_in)


def rotate_back(grads_in, cosine, sine_table):
    shape_in = grads_in.shape
    half_size = HEAD_SIZE // 2
    pieces = grads_in.reshape(shape_in[0], shape_in[1], shape_in[2] // HEAD_SIZE, HEAD_SIZE)
    scaled = pieces * sine_table[None, :, None, :]
    turned = jnp.concatenate([scaled[..., half_size:], -scaled[..., :half_size]], axis=-1)
    return (pieces * cosine[None, :, None, :] + turned).reshape(shape_in)


def norm_forward(values, gain_vec):
    inverse_rms = lax.rsqrt(jnp.mean(values * values, axis=-1, keepdims=True) + NORM_EPS)
    normal = values * inverse_rms
    return (normal, inverse_rms, normal * gain_vec)


def norm_back(grad_scaled, normal, inverse_rms, gain_vec):
    gain_grad = jnp.sum(grad_scaled * normal, axis=(0, 1))
    grad_normal = grad_scaled * gain_vec
    grad_in = inverse_rms * (
        grad_normal - normal * jnp.mean(grad_normal * normal, axis=-1, keepdims=True)
    )
    return (grad_in, gain_grad)


def split_heads(values):
    return values.reshape(
        values.shape[0], values.shape[1], values.shape[2] // HEAD_SIZE, HEAD_SIZE
    ).transpose(0, 2, 1, 3)


def join_heads(values):
    return values.transpose(0, 2, 1, 3).reshape(
        values.shape[0], values.shape[2], values.shape[1] * HEAD_SIZE
    )


def add_rows(buffer, extra, first_row):
    current = lax.dynamic_slice_in_dim(buffer, first_row, extra.shape[0], 0)
    return lax.dynamic_update_slice_in_dim(buffer, current + extra, first_row, 0)


def shards(
    hidden,
    teacher,
    lengths,
    attn_gain,
    w_query,
    key_projection,
    value_projection,
    w_out,
    mlp_gain,
    w_gate,
    w_up,
    w_down,
):
    seq_count = hidden.shape[0]
    tok_rows = hidden.shape[1]
    head_count = lax.axis_size("head")
    all_count = lax.axis_size(("dp", "blk", "head"))
    block_rows = tok_rows * head_count
    blk_index = lax.axis_index("blk")
    span_index = blk_index * head_count + lax.axis_index("head")
    places = span_index * tok_rows + jnp.arange(tok_rows)
    cosine, sine_table = rope_tables(places)
    forward_set = (
        lax.all_gather(attn_gain, ("dp", "blk", "head"), axis=0, tiled=True),
        lax.all_gather(w_query, ("dp", "blk", "head"), axis=0, tiled=True),
        lax.all_gather(key_projection, ("dp", "blk", "head"), axis=0, tiled=True),
        lax.all_gather(value_projection, ("dp", "blk", "head"), axis=0, tiled=True),
        lax.all_gather(w_out, ("dp", "blk", "head"), axis=0, tiled=True),
        lax.all_gather(mlp_gain, ("dp", "blk", "head"), axis=0, tiled=True),
        lax.all_gather(w_gate, ("dp", "blk", "head"), axis=0, tiled=True),
        lax.all_gather(w_up, ("dp", "blk", "head"), axis=0, tiled=True),
        lax.all_gather(w_down, ("dp", "blk", "head"), axis=0, tiled=True),
    )
    (
        gain_one,
        query_weight,
        key_weight,
        value_weight,
        out_weight,
        gain_two,
        gate_weight,
        up_weight,
        down_weight,
    ) = forward_set
    inputs = hidden.astype(jnp.float32)
    normal_one, inverse_one, scaled_one = norm_forward(inputs, gain_one.astype(jnp.float32))
    normed_one = scaled_one.astype(jnp.bfloat16)
    query_rows = rotate_rows(
        jnp.dot(normed_one, query_weight, preferred_element_type=jnp.float32), cosine, sine_table
    ).astype(jnp.bfloat16)
    key_row_block = rotate_rows(
        jnp.dot(normed_one, key_weight, preferred_element_type=jnp.float32), cosine, sine_table
    ).astype(jnp.bfloat16)
    value_row_block = jnp.dot(normed_one, value_weight, preferred_element_type=jnp.float32).astype(
        jnp.bfloat16
    )
    query_local, key_local, value_local = (
        lax.all_to_all(query_rows, "head", split_axis=2, concat_axis=1, tiled=True),
        lax.all_to_all(key_row_block, "head", split_axis=2, concat_axis=1, tiled=True),
        lax.all_to_all(value_row_block, "head", split_axis=2, concat_axis=1, tiled=True),
    )
    key_whole, value_whole = (
        lax.all_gather(key_local, "blk", axis=1, tiled=True),
        lax.all_gather(value_local, "blk", axis=1, tiled=True),
    )
    local_q = query_local.shape[2] // HEAD_SIZE
    local_kv = key_local.shape[2] // HEAD_SIZE
    heads_per_group = local_q // local_kv
    seq_full = key_whole.shape[1]
    query_heads = split_heads(query_local)
    key_head_split = split_heads(key_whole)
    value_head_split = split_heads(value_whole)
    query_places = blk_index * block_rows + jnp.arange(block_rows)
    block_count = blk_index + 1

    def block_scores(query_one, key_one, block_start, length):
        key_block = lax.dynamic_slice_in_dim(key_one, block_start, block_rows, 0)
        scores = (
            jnp.einsum("qd,kd->qk", query_one, key_block, preferred_element_type=jnp.float32)
            * ATTN_SCALE
        )
        key_places = block_start + jnp.arange(block_rows)
        allowed = (key_places[None, :] <= query_places[:, None]) & (key_places[None, :] < length)
        return (jnp.where(allowed, scores, MASKED), allowed)

    def forward_item(item_index):
        sequence = item_index // local_q
        head_pos = item_index % local_q
        kv_pos = head_pos // heads_per_group
        query_one = query_heads[sequence, head_pos]
        key_one = key_head_split[sequence, kv_pos]
        value_one = value_head_split[sequence, kv_pos]
        length = lengths[sequence]

        def max_step(block_id, state_in):
            running, totals = state_in
            scores, allowed = block_scores(query_one, key_one, block_id * block_rows, length)
            newest = jnp.maximum(running, jnp.max(scores, axis=-1))
            fresh = jnp.where(allowed, jnp.exp(scores - newest[:, None]), 0.0)
            return (newest, totals * jnp.exp(running - newest) + jnp.sum(fresh, axis=-1))

        running, totals = lax.fori_loop(
            0,
            block_count,
            max_step,
            (jnp.full((block_rows,), MASKED, jnp.float32), jnp.zeros((block_rows,), jnp.float32)),
        )
        log_total = running + jnp.log(totals)

        def value_step(block_id, state_in):
            rounded_sum, exact_sum = state_in
            block_start = block_id * block_rows
            scores, allowed = block_scores(query_one, key_one, block_start, length)
            weights = jnp.where(allowed, jnp.exp(scores - log_total[:, None]), 0.0)
            value_block = lax.dynamic_slice_in_dim(value_one, block_start, block_rows, 0)
            rounded_sum = rounded_sum + jnp.dot(
                weights.astype(jnp.bfloat16), value_block, preferred_element_type=jnp.float32
            )
            exact_sum = exact_sum + jnp.dot(
                weights, value_block.astype(jnp.float32), preferred_element_type=jnp.float32
            )
            return (rounded_sum, exact_sum)

        empty = jnp.zeros((block_rows, HEAD_SIZE), jnp.float32)
        attended, exact = lax.fori_loop(0, block_count, value_step, (empty, empty))
        return (attended, exact, log_total)

    attended_items, exact_items, log_items = lax.map(forward_item, jnp.arange(seq_count * local_q))
    attended_heads = attended_items.reshape(seq_count, local_q, block_rows, HEAD_SIZE)
    exact_heads = exact_items.reshape(seq_count, local_q, block_rows, HEAD_SIZE)
    log_heads = log_items.reshape(seq_count, local_q, block_rows)
    mixed_local = join_heads(attended_heads).astype(jnp.bfloat16)
    mixed = lax.all_to_all(mixed_local, "head", split_axis=1, concat_axis=2, tiled=True)
    middle = inputs + RESIDUAL_SCALE * jnp.dot(
        mixed, out_weight, preferred_element_type=jnp.float32
    )
    normal_two, inverse_two, scaled_two = norm_forward(middle, gain_two.astype(jnp.float32))
    normed_two = scaled_two.astype(jnp.bfloat16)
    gate_proj = jnp.dot(normed_two, gate_weight, preferred_element_type=jnp.float32)
    upward = jnp.dot(normed_two, up_weight, preferred_element_type=jnp.float32)
    sigma_gate = jax.nn.sigmoid(gate_proj)
    silu_gate = gate_proj * sigma_gate
    hidden_units = (silu_gate * upward).astype(jnp.bfloat16)
    result = middle + RESIDUAL_SCALE * jnp.dot(
        hidden_units, down_weight, preferred_element_type=jnp.float32
    )
    output = result.astype(jnp.bfloat16)
    valid_rows = places[None, :] < lengths[:, None]
    misfit = jnp.where(valid_rows[:, :, None], result - teacher.astype(jnp.float32), 0.0)
    squares, valid_count = lax.psum(
        (jnp.sum(misfit * misfit), jnp.sum(valid_rows.astype(jnp.float32))), ("dp", "blk", "head")
    )
    mse_loss = squares / (MODEL_WIDTH * valid_count)
    grad_result = misfit * (seq_count * tok_rows * all_count / valid_count)
    grad_branch = (RESIDUAL_SCALE * grad_result).astype(jnp.bfloat16)
    grad_units = jnp.einsum(
        "std,fd->stf", grad_branch, down_weight, preferred_element_type=jnp.float32
    )
    grad_gate_rows = (
        grad_units * upward * sigma_gate * (1.0 + gate_proj * (1.0 - sigma_gate))
    ).astype(jnp.bfloat16)
    grad_up_rows = (grad_units * silu_gate).astype(jnp.bfloat16)
    grad_normed_two = jnp.einsum(
        "stf,cf->stc", grad_gate_rows, gate_weight, preferred_element_type=jnp.float32
    ) + jnp.einsum("stf,cf->stc", grad_up_rows, up_weight, preferred_element_type=jnp.float32)
    grad_middle, grad_gain_two = norm_back(
        grad_normed_two, normal_two, inverse_two, gain_two.astype(jnp.float32)
    )
    grad_middle = grad_result + grad_middle
    grad_gate_full = jnp.einsum(
        "stc,stf->cf", normed_two, grad_gate_rows, preferred_element_type=jnp.float32
    )
    grad_up_full = jnp.einsum(
        "stc,stf->cf", normed_two, grad_up_rows, preferred_element_type=jnp.float32
    )
    grad_down_full = jnp.einsum(
        "stf,std->fd", hidden_units, grad_branch, preferred_element_type=jnp.float32
    )
    grad_gate, grad_up, grad_down = (
        lax.psum_scatter(grad_gate_full, ("dp", "blk", "head"), scatter_dimension=0, tiled=True),
        lax.psum_scatter(grad_up_full, ("dp", "blk", "head"), scatter_dimension=0, tiled=True),
        lax.psum_scatter(grad_down_full, ("dp", "blk", "head"), scatter_dimension=0, tiled=True),
    )
    grad_attn_rows = (RESIDUAL_SCALE * grad_middle).astype(jnp.bfloat16)
    grad_out = jnp.einsum("stc,std->cd", mixed, grad_attn_rows, preferred_element_type=jnp.float32)
    grad_mixed = jnp.einsum(
        "std,cd->stc", grad_attn_rows, out_weight, preferred_element_type=jnp.float32
    ).astype(jnp.bfloat16)
    dout_local = lax.all_to_all(grad_mixed, "head", split_axis=2, concat_axis=1, tiled=True)
    dout_heads = split_heads(dout_local)
    delta_heads = jnp.sum(dout_heads.astype(jnp.float32) * exact_heads, axis=-1)

    def backward_item(item_index):
        sequence = item_index // local_kv
        kv_pos = item_index % local_kv
        key_one = key_head_split[sequence, kv_pos]
        value_one = value_head_split[sequence, kv_pos]
        length = lengths[sequence]
        key_grad = jnp.zeros((seq_full, HEAD_SIZE), jnp.float32)
        value_grad = jnp.zeros((seq_full, HEAD_SIZE), jnp.float32)
        query_grads = []
        for member in range(heads_per_group):
            head_pos = kv_pos * heads_per_group + member
            query_one = query_heads[sequence, head_pos]
            dout_one = dout_heads[sequence, head_pos]
            log_one = log_heads[sequence, head_pos]
            delta_one = delta_heads[sequence, head_pos]

            def grad_step(block_id, state_in):
                query_grad, key_acc, value_acc = state_in
                block_start = block_id * block_rows
                scores, allowed = block_scores(query_one, key_one, block_start, length)
                weights = jnp.where(allowed, jnp.exp(scores - log_one[:, None]), 0.0)
                key_block = lax.dynamic_slice_in_dim(key_one, block_start, block_rows, 0)
                value_block = lax.dynamic_slice_in_dim(value_one, block_start, block_rows, 0)
                value_part = jnp.einsum(
                    "qk,qd->kd",
                    weights.astype(jnp.bfloat16),
                    dout_one,
                    preferred_element_type=jnp.float32,
                )
                grad_weights = jnp.einsum(
                    "qd,kd->qk", dout_one, value_block, preferred_element_type=jnp.float32
                )
                score_grad = (weights * (grad_weights - delta_one[:, None])).astype(jnp.bfloat16)
                query_grad = (
                    query_grad
                    + jnp.dot(score_grad, key_block, preferred_element_type=jnp.float32)
                    * ATTN_SCALE
                )
                key_part = (
                    jnp.einsum(
                        "qk,qd->kd", score_grad, query_one, preferred_element_type=jnp.float32
                    )
                    * ATTN_SCALE
                )
                return (
                    query_grad,
                    add_rows(key_acc, key_part, block_start),
                    add_rows(value_acc, value_part, block_start),
                )

            query_grad, key_grad, value_grad = lax.fori_loop(
                0,
                block_count,
                grad_step,
                (jnp.zeros((block_rows, HEAD_SIZE), jnp.float32), key_grad, value_grad),
            )
            query_grads.append(query_grad)
        return (jnp.stack(query_grads), key_grad, value_grad)

    query_grad_items, key_grad_items, value_grad_items = lax.map(
        backward_item, jnp.arange(seq_count * local_kv)
    )
    query_grad_local = join_heads(
        query_grad_items.reshape(seq_count, local_q, block_rows, HEAD_SIZE)
    ).astype(jnp.bfloat16)
    key_grad_whole = join_heads(key_grad_items.reshape(seq_count, local_kv, seq_full, HEAD_SIZE))
    value_grad_whole = join_heads(
        value_grad_items.reshape(seq_count, local_kv, seq_full, HEAD_SIZE)
    )
    key_grad_local, value_grad_local = (
        lax.psum_scatter(
            key_grad_whole.astype(jnp.bfloat16), "blk", scatter_dimension=1, tiled=True
        ).astype(jnp.float32),
        lax.psum_scatter(
            value_grad_whole.astype(jnp.bfloat16), "blk", scatter_dimension=1, tiled=True
        ).astype(jnp.float32),
    )
    query_grad_rows, key_grad_rows, value_grad_rows = (
        lax.all_to_all(query_grad_local, "head", split_axis=1, concat_axis=2, tiled=True),
        lax.all_to_all(
            key_grad_local.astype(jnp.bfloat16), "head", split_axis=1, concat_axis=2, tiled=True
        ),
        lax.all_to_all(
            value_grad_local.astype(jnp.bfloat16), "head", split_axis=1, concat_axis=2, tiled=True
        ),
    )
    query_grad_rows = rotate_back(query_grad_rows.astype(jnp.float32), cosine, sine_table).astype(
        jnp.bfloat16
    )
    key_grad_rows = rotate_back(key_grad_rows.astype(jnp.float32), cosine, sine_table).astype(
        jnp.bfloat16
    )
    grad_query = jnp.einsum(
        "stc,stk->ck", normed_one, query_grad_rows, preferred_element_type=jnp.float32
    )
    grad_key = jnp.einsum(
        "stc,stk->ck", normed_one, key_grad_rows, preferred_element_type=jnp.float32
    )
    grad_value = jnp.einsum(
        "stc,stk->ck", normed_one, value_grad_rows, preferred_element_type=jnp.float32
    )
    grad_normed_one = (
        jnp.einsum("stk,ck->stc", query_grad_rows, query_weight, preferred_element_type=jnp.float32)
        + jnp.einsum("stk,ck->stc", key_grad_rows, key_weight, preferred_element_type=jnp.float32)
        + jnp.einsum(
            "stk,ck->stc", value_grad_rows, value_weight, preferred_element_type=jnp.float32
        )
    )
    grad_inputs, grad_gain_one = norm_back(
        grad_normed_one, normal_one, inverse_one, gain_one.astype(jnp.float32)
    )
    grad_hidden = grad_middle + grad_inputs
    attn_sums = (
        lax.psum_scatter(grad_gain_one, ("dp", "blk", "head"), scatter_dimension=0, tiled=True),
        lax.psum_scatter(grad_query, ("dp", "blk", "head"), scatter_dimension=0, tiled=True),
        lax.psum_scatter(grad_key, ("dp", "blk", "head"), scatter_dimension=0, tiled=True),
        lax.psum_scatter(grad_value, ("dp", "blk", "head"), scatter_dimension=0, tiled=True),
        lax.psum_scatter(grad_out, ("dp", "blk", "head"), scatter_dimension=0, tiled=True),
        lax.psum_scatter(grad_gain_two, ("dp", "blk", "head"), scatter_dimension=0, tiled=True),
    )
    return (
        output,
        mse_loss,
        grad_hidden,
        attn_sums[0],
        attn_sums[1],
        attn_sums[2],
        attn_sums[3],
        attn_sums[4],
        attn_sums[5],
        grad_gate,
        grad_up,
        grad_down,
    )


def solution(mesh):
    in_specs = (
        P("dp", ("blk", "head"), None),
        P("dp", ("blk", "head"), None),
        P("dp"),
        P(("dp", "blk", "head")),
        P(("dp", "blk", "head"), None),
        P(("dp", "blk", "head"), None),
        P(("dp", "blk", "head"), None),
        P(("dp", "blk", "head"), None),
        P(("dp", "blk", "head")),
        P(("dp", "blk", "head"), None),
        P(("dp", "blk", "head"), None),
        P(("dp", "blk", "head"), None),
    )
    out_specs = (
        P("dp", ("blk", "head"), None),
        P(),
        P("dp", ("blk", "head"), None),
        P(("dp", "blk", "head")),
        P(("dp", "blk", "head"), None),
        P(("dp", "blk", "head"), None),
        P(("dp", "blk", "head"), None),
        P(("dp", "blk", "head"), None),
        P(("dp", "blk", "head")),
        P(("dp", "blk", "head"), None),
        P(("dp", "blk", "head"), None),
        P(("dp", "blk", "head"), None),
    )
    return jax.shard_map(shards, mesh=mesh, in_specs=in_specs, out_specs=out_specs, check_vma=False)
```

profile of v0, /device:TPU:0, one launch (start us, length us, event | category | flops | bytes accessed | tf_op | source)
XLA Modules:
  0.0 6753.8 jit_solution(13088111725232629270)
XLA Ops:
  11.2 42.1 all-reduce.5
  54.4 15.8 all-gather.10.cloned.1.call-done
  78.3 13.5 all_to_all.114
  93.1 35.8 all-gather.16.cloned.1.call-done
  134.0 16.3 all_to_all.115
  157.7 52.2 all-gather.14.cloned.1.call-done
  251.3 23.3 all-to-all-done.1
  284.0 170.6 %while.206 = (s32[]{:T(128)}, bf16[8,1024,64]{1,2,0:T(8,128)(2,1)}, f32[8,1024,64]{1,2,0:T(8,128)}, f32[8,1024]{1,0:T(8,128)}, s32[8]{0:T(128)S(1)}, /*index=5*/...) while((s32[]{:T(128)}, bf16[8,1024,64]{1,2,0:T(8,128)(2,1)}, ...), condition=%wide.region_8.9_spmd.clone, body=%wide.region_1.8_spmd.clone.sunk | while | flops 563226624 | bytes 33959272 | solution.py:204
  476.7 277.1 %psum.15 = f32[]{:T(128)} all-reduce(f32[]{:T(128)} %get-tuple-element.1113), channel_id=1, replica_groups=mesh['dp'=2,'blk'=4,'head'=4] {'dp','blk','head'}, use_global_device_ids=true, to_apply=%region_13.14 | all-reduce | flops 1 | bytes 8 | tf_op jit(solution)/shard_map/psum | solution.py:226
  767.4 17.6 fusion.204
  785.0 20.7 multiply_convert_fusion.2
  805.7 146.9 %all-gather.26.cloned.1.call-done = bf16[8192,2048]{1,0:T(8,128)(2,1)} async-done(((bf16[256,2048]{1,0:T(8,128)(2,1)}), bf16[8192,2048]{1,0:T(8,128)(2,1)}) %all-gather.26.cloned.1.call-update) | async-done | bytes 33554448 | tf_op jit(solution)/shard_map/all_gather | solution.py:108
  952.6 17.5 fusion.154
  970.1 22.9 multiply_convert_fusion
  993.0 16.9 fusion.205
  1009.9 19.2 fusion.163
  1059.4 26.3 all-to-all-done.4
  1090.8 103.4 %while.211 = (s32[]{:T(128)}, bf16[2,4,1024,64]{2,3,1,0:T(8,128)(2,1)}, bf16[2,4096,64]{1,2,0:T(8,128)(2,1)}, bf16[2,4096,64]{1,2,0:T(8,128)(2,1)}, s32[2]{0:T(1...) while((s32[]{:T(128)}, ...), condition=%wide.region_25.26_spmd.clone, body=%wide.region_16.0_spmd.clone.sunk | while | flops 2754884608 | bytes 107956848 | solution.py:328
  1195.1 245.1 %reduce-scatter.10.cloned.1.call-done = bf16[1,1024,128]{1,2,0:T(8,128)(2,1)} async-done(((bf16[1,4096,128]{1,2,0:T(8,128)(2,1)}), bf16[1,1024,128]{1,2,0:T(8,128)(2,1)}) %reduce-scatter.10.cloned.1.call-update) | async-done | bytes 262160 | tf_op jit(solution)/shard_map/reduce_scatter | solution.py:339
  1443.8 13.4 all_to_all.116
  1471.4 19.7 all_to_all.117
  1521.6 49.4 all_to_all.118
  1587.9 26.7 fusion.207
  1614.7 26.4 fusion.208
  1641.8 27.4 fusion.179
  1682.0 38.6 all-reduce.4
  1725.9 51.1 reduce-scatter.18.cloned.1.call-done
  1777.0 365.2 %reduce-scatter.20.cloned.1.call-done = f32[64,2048]{1,0:T(8,128)} async-done(((f32[2048,2048]{1,0:T(8,128)}), f32[64,2048]{1,0:T(8,128)}) %reduce-scatter.20.cloned.1.call-update) | async-done | bytes 524304 | tf_op jit(solution)/shard_map/reduce_scatter | solution.py:386
  2142.2 364.9 %reduce-scatter.14.cloned.1.call-done = f32[64,2048]{1,0:T(8,128)} async-done(((f32[2048,2048]{1,0:T(8,128)}), f32[64,2048]{1,0:T(8,128)}) %reduce-scatter.14.cloned.1.call-update) | async-done | bytes 524304 | tf_op jit(solution)/shard_map/reduce_scatter | solution.py:383
  2507.2 1411.4 %reduce-scatter.22.cloned.1.call-done = f32[64,8192]{1,0:T(8,128)} async-done(((f32[2048,8192]{1,0:T(8,128)}), f32[64,8192]{1,0:T(8,128)}) %reduce-scatter.22.cloned.1.call-update) | async-done | bytes 2097168 | tf_op jit(solution)/shard_map/reduce_scatter | solution.py:256
  3918.5 1413.4 %reduce-scatter.24.cloned.1.call-done = f32[64,8192]{1,0:T(8,128)} async-done(((f32[2048,8192]{1,0:T(8,128)}), f32[64,8192]{1,0:T(8,128)}) %reduce-scatter.24.cloned.1.call-update) | async-done | bytes 2097168 | tf_op jit(solution)/shard_map/reduce_scatter | solution.py:257
  5331.9 1413.4 %reduce-scatter.26.cloned.1.call-done = f32[256,2048]{1,0:T(8,128)} async-done(((f32[8192,2048]{1,0:T(8,128)}), f32[256,2048]{1,0:T(8,128)}) %reduce-scatter.26.cloned.1.call-update) | async-done | bytes 2097168 | tf_op jit(solution)/shard_map/reduce_scatter | solution.py:258
  (653 shorter events, 629.6 us)
Async XLA Ops:
  7.2 46.9 copy-start
  7.2 63.0 all-gather.10.cloned.1.call-start
  7.9 121.0 %all-gather.16.cloned.1.call-start = ((), (), s32[]{:S(2)}) async-start(), calls=%async_computation.20 | async-start | bytes 2162688 | tf_op jit(solution)/shard_map/all_gather | solution.py:103
  8.7 201.2 %all-gather.14.cloned.1.call-start = ((), (), s32[]{:S(2)}) async-start(), calls=%async_computation.19 | async-start | bytes 8650752 | tf_op jit(solution)/shard_map/all_gather | solution.py:101
  9.4 234.4 %all-gather.12.cloned.1.call-start = ((), (), s32[]{:S(2)}) async-start(), calls=%async_computation.18 | async-start | bytes 1310720 | tf_op jit(solution)/shard_map/all_gather | solution.py:139
  53.3 156.6 %copy-start.31 = (f32[2048]{0:T(1024)}, f32[2048]{0:T(1024)S(1)}, u32[]{:S(2)}) copy-start(f32[2048]{0:T(1024)S(1)} %convert_element_type.339) | copy-start | bytes 24580
  53.5 100.0 %copy-start.29 = (f32[256,64]{0,1:T(8,128)}, f32[256,64]{0,1:T(8,128)S(1)}, u32[]{:S(2)}) copy-start(f32[256,64]{0,1:T(8,128)S(1)} %pad_maximum_fusion.5) | copy-start | bytes 196612
  53.8 101.8 %copy-start.21 = (f32[256,64]{0,1:T(8,128)}, f32[256,64]{0,1:T(8,128)S(1)}, u32[]{:S(2)}) copy-start(f32[256,64]{0,1:T(8,128)S(1)} %pad_maximum_fusion.4) | copy-start | bytes 196612
  54.4 155.5 %copy-start.35 = (f32[256]{0:T(256)}, f32[256]{0:T(256)S(1)}, u32[]{:S(2)}) copy-start(f32[256]{0:T(256)S(1)} %add_rsqrt_fusion.1) | copy-start | bytes 3076
  93.0 154.0 %all-gather.18.cloned.1.call-start = ((), (), s32[]{:S(2)}) async-start(), calls=%async_computation.21 | async-start | bytes 1310720 | tf_op jit(solution)/shard_map/all_gather | solution.py:140
  151.5 609.4 %all-gather.20.cloned.1.call-start = ((), (), s32[]{:S(2)}) async-start(), calls=%async_computation.22 | async-start | bytes 8650752 | tf_op jit(solution)/shard_map/all_gather | solution.py:104
  152.0 615.4 %all-gather.22.cloned.1.call-start = ((), (), s32[]{:S(2)}) async-start(), calls=%async_computation.23 | async-start | bytes 34603008 | tf_op jit(solution)/shard_map/all_gather | solution.py:106
  152.8 632.2 %all-gather.24.cloned.1.call-start = ((), (), s32[]{:S(2)}) async-start(), calls=%async_computation.24 | async-start | bytes 34603008 | tf_op jit(solution)/shard_map/all_gather | solution.py:107
  239.4 35.2 all-to-all-start.1
  243.0 709.6 %all-gather.26.cloned.1.call-start = ((), (), s32[]{:S(2)}) async-start(), calls=%async_computation.25 | async-start | bytes 34603008 | tf_op jit(solution)/shard_map/all_gather | solution.py:108
  461.2 292.7 %copy-start.40 = (bf16[2048]{0:T(1024)(128)(2,1)S(1)}, bf16[2048]{0:T(1024)(128)(2,1)}, u32[]{:S(2)}) copy-start(bf16[2048]{0:T(1024)(128)(2,1)} %get-tuple-element.1112) | copy-start | bytes 12292
  471.2 283.4 %all-to-all-start.3 = ((bf16[4,2,65536]{2,1,0:T(2,128)(2,1)}), bf16[4,2,65536]{2,1,0:T(2,128)(2,1)}, u32[]{:S(2)}, u32[]{:S(2)}) async-start(bf16[4,2,65536]{2,1,0:T(2,128)(2,1)} %reshape.635), calls=%async_computation.3 | async-start | bytes 2097152 | tf_op jit(solution)/shard_map/all_to_all | solution.py:209
  476.7 552.3 %copy-start.38 = (pred[256]{0:T(512)(128)(4,1)}, pred[256]{0:T(512)(128)(4,1)S(1)}, u32[]{:S(2)}) copy-start(pred[256]{0:T(512)(128)(4,1)S(1)} %get-tuple-element.1114) | copy-start | bytes 772
  767.4 17.6 copy-start.13
  1055.8 29.9 all-to-all-start.4
  1059.3 380.9 %reduce-scatter.10.cloned.1.call-start = ((), (), s32[]{:S(2)}) async-start(), calls=%async_computation.26 | async-start | bytes 1310720 | tf_op jit(solution)/shard_map/reduce_scatter | solution.py:339
  1194.2 263.5 %copy-start.30 = (f32[256,64]{0,1:T(8,128)S(1)}, f32[256,64]{0,1:T(8,128)}, u32[]{:S(2)}) copy-start(f32[256,64]{0,1:T(8,128)} %copy-done.29) | copy-start | bytes 196612
  1194.3 273.5 %reduce-scatter.12.cloned.1.call-start = ((), (), s32[]{:S(2)}) async-start(), calls=%async_computation.27 | async-start | bytes 1310720 | tf_op jit(solution)/shard_map/reduce_scatter | solution.py:342
  1195.0 262.9 %copy-start.22 = (f32[256,64]{0,1:T(8,128)S(1)}, f32[256,64]{0,1:T(8,128)}, u32[]{:S(2)}) copy-start(f32[256,64]{0,1:T(8,128)} %copy-done.21) | copy-start | bytes 196612
  1195.0 530.9 %reduce-scatter.16.cloned.1.call-start = ((), (), s32[]{:S(2)}) async-start(), calls=%async_computation.29 | async-start | bytes 4325376 | tf_op jit(solution)/shard_map/reduce_scatter | solution.py:384
  1461.7 315.3 %reduce-scatter.18.cloned.1.call-start = ((), (), s32[]{:S(2)}) async-start(), calls=%async_computation.30 | async-start | bytes 4325376 | tf_op jit(solution)/shard_map/reduce_scatter | solution.py:385
  1495.1 647.1 %reduce-scatter.20.cloned.1.call-start = ((), (), s32[]{:S(2)}) async-start(), calls=%async_computation.31 | async-start | bytes 17301504 | tf_op jit(solution)/shard_map/reduce_scatter | solution.py:386
  1506.1 1001.0 %reduce-scatter.14.cloned.1.call-start = ((), (), s32[]{:S(2)}) async-start(), calls=%async_computation.28 | async-start | bytes 17301504 | tf_op jit(solution)/shard_map/reduce_scatter | solution.py:383
  1587.9 2330.7 %reduce-scatter.22.cloned.1.call-start = ((), (), s32[]{:S(2)}) async-start(), calls=%async_computation.32 | async-start | bytes 69206016 | tf_op jit(solution)/shard_map/reduce_scatter | solution.py:256
  1614.7 3717.3 %reduce-scatter.24.cloned.1.call-start = ((), (), s32[]{:S(2)}) async-start(), calls=%async_computation.33 | async-start | bytes 69206016 | tf_op jit(solution)/shard_map/reduce_scatter | solution.py:257
  1641.2 5104.2 %reduce-scatter.26.cloned.1.call-start = ((), (), s32[]{:S(2)}) async-start(), calls=%async_computation.34 | async-start | bytes 69206016 | tf_op jit(solution)/shard_map/reduce_scatter | solution.py:258
  1679.4 43.0 copy-start.12
  (76 other events, 237.0 us)
Sparse Core Ops, SparseCore 0:
  11.0 59.1 all-gather.9
  73.2 55.6 all-gather.15
  131.9 77.9 all-gather.13
  211.8 15.3 all-gather.11
  229.2 16.7 all-gather.17
  248.8 81.2 all-gather.19
  333.0 202.1 all-gather.21
  538.2 209.2 all-gather.23
  750.4 202.1 all-gather.25
  1194.4 245.7 reduce-scatter.9
  1442.9 24.8 reduce-scatter.11
  1470.5 155.9 reduce-scatter.15
  1629.4 147.5 reduce-scatter.17
  1779.7 362.4 reduce-scatter.19
  2144.9 362.1 reduce-scatter.13
  2509.9 1408.5 reduce-scatter.21
  3921.3 1410.6 reduce-scatter.23
  5334.7 1410.5 reduce-scatter.25
where the time goes:
time: 6770 us; the launch traced here: 6750 us
  waiting for transfers between devices  5580 us (82%)
  blocking collectives  470 us (7%)
  matrix products  362 us (5%)
  local copies, waits for them, and re-layouts  189 us (3%)
  other arithmetic  102 us (2%)
    reduce_scatter x1, waiting for transfers between devices, shards(): lax.psum_scatter(grad_up_full, ('dp', 'blk', 'head'), scatter_dimension=0...  1410 us
    reduce_scatter x1, waiting for transfers between devices, shards(): lax.psum_scatter(grad_down_full, ('dp', 'blk', 'head'), scatter_dimension...  1410 us
    reduce_scatter x1, waiting for transfers between devices, shards(): lax.psum_scatter(grad_gate_full, ('dp', 'blk', 'head'), scatter_dimension...  1410 us
    reduce_scatter x1, waiting for transfers between devices, shards(): lax.psum_scatter(grad_out, ('dp', 'blk', 'head'), scatter_dimension=0, ti...  365 us
    reduce_scatter x1, waiting for transfers between devices, shards(): lax.psum_scatter(grad_query, ('dp', 'blk', 'head'), scatter_dimension=0,...  365 us
    psum x2, blocking collectives, shards(): lax.psum((jnp.sum(misfit * misfit), jnp.sum(valid_rows.astype(jnp.float32...  316 us
    reduce_scatter x1, waiting for transfers between devices, shards(): lax.psum_scatter(key_grad_whole.astype(jnp.bfloat16), 'blk', scatter_dime...  245 us
    all_gather x1, waiting for transfers between devices, shards(): lax.all_gather(w_down, ('dp', 'blk', 'head'), axis=0, tiled=True)  147 us
  transfers between devices with their start and end apart: 21, of which 14 were waited for; matrix products, arithmetic and copies ran while one was open for 6% of the time, Pallas kernels for 0%

commit v1 on v0

v1 whole, which is shorter than its diff:
```python
import functools

import jax
import jax.numpy as jnp
from jax import lax
from jax.experimental import pallas as pl
from jax.experimental.pallas import tpu as pltpu
from jax.sharding import Mesh, PartitionSpec as P

MODEL_WIDTH = 2048
HEAD_SIZE = 64
ROPE_BASE = 10000000.0
NORM_EPS = 1e-05
ATTN_SCALE = 0.015625
RESIDUAL_SCALE = 0.22
MASKED = -1e30

ALL = ("dp", "blk", "hi", "lo")
SQUARE = ("blk", "lo")
COPIES = ("dp", "hi")
SEQ = ("blk", "hi", "lo")
F32 = jnp.float32
BF16 = jnp.bfloat16
VMEM_LIMIT = 56 * 1024 * 1024


def dot32(a, b, dims=((1,), (0,))):
    return lax.dot_general(a, b, (dims, ((), ())), preferred_element_type=F32)


def proj_kernel(rows_ref, weight_ref, cos_ref, sina_ref, sinb_ref, out_ref):
    made = dot32(rows_ref[...], weight_ref[...])
    cosine, sina, sinb = cos_ref[...], sina_ref[...], sinb_ref[...]
    low = lanes_low(cosine.shape)
    half = HEAD_SIZE // 2
    for part in range(3):
        u = made[:, 128 * part : 128 * part + 128]
        up, down = pltpu.roll(u, 128 - half, 1), pltpu.roll(u, half, 1)
        turned = u * cosine + up * sina + down * sinb
        if part < 2:
            out_ref[:, 128 * part : 128 * part + 128] = (
                turned.astype(BF16).astype(F32) * ATTN_SCALE
            ).astype(BF16)
        else:
            out_ref[:, 256:384] = jnp.where(low, turned, u).astype(BF16)


def project(rows, weight, tables, tile):
    count, depth = rows.shape
    wide = weight.shape[1]
    table_spec = pl.BlockSpec((tile, 128), lambda i: (i, 0))
    return pl.pallas_call(
        proj_kernel,
        grid=(count // tile,),
        in_specs=[
            pl.BlockSpec((tile, depth), lambda i: (i, 0)),
            pl.BlockSpec((depth, wide), lambda i: (0, 0)),
            table_spec,
            table_spec,
            table_spec,
        ],
        out_specs=pl.BlockSpec((tile, wide), lambda i: (i, 0)),
        out_shape=jax.ShapeDtypeStruct((count, wide), BF16),
        compiler_params=pltpu.CompilerParams(vmem_limit_bytes=VMEM_LIMIT),
        cost_estimate=pl.CostEstimate(
            flops=2 * count * depth * wide, bytes_accessed=4 * count * depth, transcendentals=0
        ),
        name="project",
    )(rows, weight, *tables)


def back_rope_kernel(dq_ref, own_ref, other_ref, cos_ref, sina_ref, sinb_ref, out_ref):
    cosine, sina, sinb = cos_ref[...], sina_ref[...], sinb_ref[...]
    low = lanes_low(cosine.shape)
    half = HEAD_SIZE // 2
    shared = (own_ref[...].astype(F32) + other_ref[...].astype(F32)).astype(BF16)
    for part in range(3):
        w = (dq_ref[:, 128 * part : 128 * part + 128] if part < 2 else shared).astype(F32)
        turned = w * cosine + pltpu.roll(w * sinb, 128 - half, 1) + pltpu.roll(w * sina, half, 1)
        if part == 2:
            turned = jnp.where(low, turned, w)
        out_ref[:, 128 * part : 128 * part + 128] = turned.astype(BF16)


def back_rope(dq, own, other, tables, tile):
    count = dq.shape[0]
    rows = lambda wide: pl.BlockSpec((tile, wide), lambda i: (i, 0))
    return pl.pallas_call(
        back_rope_kernel,
        grid=(count // tile,),
        in_specs=[rows(256)] + [rows(128)] * 5,
        out_specs=rows(384),
        out_shape=jax.ShapeDtypeStruct((count, 384), BF16),
        compiler_params=pltpu.CompilerParams(vmem_limit_bytes=VMEM_LIMIT),
        name="back_rope",
    )(dq, own, other, *tables)


def lanes_low(shape):
    return lax.broadcasted_iota(jnp.int32, shape, 1) < HEAD_SIZE


def both_keys(kv):
    low = lanes_low(kv.shape)
    keys = kv.astype(F32)
    return (
        jnp.where(low, keys, 0.0).astype(BF16),
        jnp.where(low, 0.0, pltpu.roll(keys, HEAD_SIZE, 1)).astype(BF16),
    )


def both_values(kv):
    low = lanes_low(kv.shape)
    values = kv.astype(F32)
    return (
        jnp.where(low, pltpu.roll(values, HEAD_SIZE, 1), 0.0).astype(BF16),
        jnp.where(low, 0.0, values).astype(BF16),
    )


def attend_kernel(scalar_ref, qkv_ref, other_ref, out_ref, log_ref, keys, values, peak, sums):
    b = pl.program_id(0)
    blocks, unit, _ = qkv_ref.shape
    units = 2 * blocks
    length, hi = scalar_ref[0], scalar_ref[1]
    n = 2 * b + hi

    @pl.when(b == 0)
    def _():
        def spread(c, carry):
            for j, kv in (
                (2 * c + hi, qkv_ref[c, :, 256:384]),
                (2 * c + 1 - hi, other_ref[c]),
            ):
                keys[0, j], keys[1, j] = both_keys(kv)
                across = jnp.transpose(kv.astype(F32))[HEAD_SIZE:, :]
                values[j] = jnp.concatenate(
                    [across, jnp.ones((16, unit), F32)], axis=0
                ).astype(BF16)
            return carry

        lax.fori_loop(0, blocks, spread, 0)

    peak[...] = jnp.full_like(peak, MASKED)
    sums[...] = jnp.zeros_like(sums)

    def step(j, masked):
        for h in range(4):
            query = qkv_ref[b, :, 128 * (h // 2) : 128 * (h // 2) + 128]
            scores = dot32(keys[h % 2, j], query, ((1,), (1,)))
            if masked:
                row = j * unit + lax.broadcasted_iota(jnp.int32, scores.shape, 0)
                col = n * unit + lax.broadcasted_iota(jnp.int32, scores.shape, 1)
                scores = jnp.where((row <= col) & (row < length), scores, MASKED)
            old = peak[h, 0:1, :]
            new = jnp.maximum(old, jnp.max(scores, axis=0, keepdims=True))
            weights = jnp.exp(scores - new).astype(BF16)
            sums[h] = sums[h] * jnp.exp(old - new) + dot32(values[j], weights)
            peak[h, 0:1, :] = new

    first_ragged = units - units // 4

    def plain(j, carry):
        step(j, False)
        return carry

    def checked(j, carry):
        step(j, True)
        return carry

    lax.fori_loop(0, jnp.minimum(n, first_ragged), plain, 0)
    lax.fori_loop(jnp.minimum(n, first_ragged), n + 1, checked, 0)

    for pair in range(2):
        parts = []
        for h in (2 * pair, 2 * pair + 1):
            total = sums[h, HEAD_SIZE : HEAD_SIZE + 1, :]
            parts.append(sums[h, 0:HEAD_SIZE, :] / total)
            log_ref[0, h : h + 1, :] = peak[h, 0:1, :] + jnp.log(total)
        out_ref[0, :, 128 * pair : 128 * pair + 128] = jnp.transpose(
            jnp.concatenate(parts, axis=0)
        ).astype(BF16)


def attend(scalars, qkv, other):
    blocks, unit, _ = qkv.shape
    units = 2 * blocks
    whole = lambda a: pl.BlockSpec(a.shape, lambda i: (0,) * a.ndim)
    return pl.pallas_call(
        attend_kernel,
        grid=(blocks,),
        in_specs=[pl.BlockSpec(memory_space=pltpu.SMEM), whole(qkv), whole(other)],
        out_specs=[
            pl.BlockSpec((1, unit, 256), lambda i: (i, 0, 0)),
            pl.BlockSpec((1, 8, unit), lambda i: (i, 0, 0)),
        ],
        out_shape=[
            jax.ShapeDtypeStruct((blocks, unit, 256), BF16),
            jax.ShapeDtypeStruct((blocks, 8, unit), F32),
        ],
        scratch_shapes=[
            pltpu.VMEM((2, units, unit, 128), BF16),
            pltpu.VMEM((units, HEAD_SIZE + 16, unit), BF16),
            pltpu.VMEM((4, 8, unit), F32),
            pltpu.VMEM((4, HEAD_SIZE + 16, unit), F32),
        ],
        compiler_params=pltpu.CompilerParams(vmem_limit_bytes=VMEM_LIMIT),
        cost_estimate=pl.CostEstimate(
            flops=40_000_000_000, bytes_accessed=8_000_000, transcendentals=20_000_000
        ),
        name="attend",
    )(scalars, qkv, other)


def attend_back_kernel(
    scalar_ref, qkv_ref, other_ref, dout_ref, out_ref, log_ref, dq_ref, dkv_ref, delta, dq, dk, dv
):
    j = pl.program_id(0)
    blocks, unit, _ = qkv_ref.shape
    units = 2 * blocks
    length, hi = scalar_ref[0], scalar_ref[1]

    @pl.when(j == 0)
    def _():
        dq[...] = jnp.zeros_like(dq)
        pick = jnp.where(
            lax.broadcasted_iota(jnp.int32, (8, 256), 0)
            == lax.broadcasted_iota(jnp.int32, (8, 256), 1) // HEAD_SIZE,
            1.0,
            0.0,
        )

        def dots(b, carry):
            product = dout_ref[b].astype(F32) * out_ref[b].astype(F32)
            delta[b] = lax.dot_general(
                pick,
                product,
                (((1,), (1,)), ((), ())),
                precision=lax.Precision.HIGHEST,
                preferred_element_type=F32,
            )
            return carry

        lax.fori_loop(0, blocks, dots, 0)

    foreign = jnp.where(j % 2 == hi, 0, 1)
    kv = jnp.where(foreign == 0, qkv_ref[j // 2, :, 256:384], other_ref[j // 2])
    keys, values = both_keys(kv), both_values(kv)
    dk[...] = jnp.zeros_like(dk)
    dv[...] = jnp.zeros_like(dv)

    def step(b, masked):
        n = 2 * b + hi
        for pair in range(2):
            lanes = slice(128 * pair, 128 * pair + 128)
            query = qkv_ref[b, :, lanes]
            dout = dout_ref[b, :, lanes]
            dq_part = None
            for side in range(2):
                h = 2 * pair + side
                scores = dot32(keys[side], query, ((1,), (1,)))
                weights = jnp.exp(scores - log_ref[b, h : h + 1, :])
                if masked:
                    row = j * unit + lax.broadcasted_iota(jnp.int32, scores.shape, 0)
                    col = n * unit + lax.broadcasted_iota(jnp.int32, scores.shape, 1)
                    weights = jnp.where((row <= col) & (row < length), weights, 0.0)
                dweights = dot32(values[side], dout, ((1,), (1,)))
                dscores = (weights * (dweights - delta[b, h : h + 1, :])).astype(BF16)
                dv[side] += dot32(weights.astype(BF16), dout)
                dk[side] += dot32(dscores, query)
                part = dot32(dscores, keys[side], ((0,), (0,)))
                dq_part = part if dq_part is None else dq_part + part
            dq[b, :, lanes] += dq_part

    first_ragged = units - units // 4

    def plain(b, carry):
        step(b, False)
        return carry

    def checked(b, carry):
        step(b, True)
        return carry

    first = (j + 1 - hi) // 2
    masked_until = jnp.where(j >= first_ragged, blocks, jnp.where(foreign == 0, first + 1, first))
    lax.fori_loop(first, masked_until, checked, 0)
    lax.fori_loop(masked_until, blocks, plain, 0)

    low = lanes_low((unit, 128))
    dkey = dk[0] + pltpu.roll(dk[1], HEAD_SIZE, 1)
    dvalue = pltpu.roll(dv[0], HEAD_SIZE, 1) + dv[1]
    dkv_ref[foreign, j // 2] = jnp.where(low, dkey, dvalue).astype(BF16)

    @pl.when(j == units - 1)
    def _():
        def store(b, carry):
            dq_ref[b] = (dq[b] * ATTN_SCALE).astype(BF16)
            return carry

        lax.fori_loop(0, blocks, store, 0)


def attend_back(scalars, qkv, other, dout, out, log):
    blocks, unit, _ = qkv.shape
    units = 2 * blocks
    whole = lambda a: pl.BlockSpec(a.shape, lambda i: (0,) * a.ndim)
    dq_shape = jax.ShapeDtypeStruct((blocks, unit, 256), BF16)
    dkv_shape = jax.ShapeDtypeStruct((2, blocks, unit, 128), BF16)
    return pl.pallas_call(
        attend_back_kernel,
        grid=(units,),
        in_specs=[
            pl.BlockSpec(memory_space=pltpu.SMEM),
            whole(qkv),
            whole(other),
            whole(dout),
            whole(out),
            whole(log),
        ],
        out_specs=[whole(dq_shape), whole(dkv_shape)],
        out_shape=[dq_shape, dkv_shape],
        scratch_shapes=[
            pltpu.VMEM((blocks, 8, unit), F32),
            pltpu.VMEM((blocks, unit, 256), F32),
            pltpu.VMEM((2, unit, 128), F32),
            pltpu.VMEM((2, unit, 128), F32),
        ],
        compiler_params=pltpu.CompilerParams(vmem_limit_bytes=VMEM_LIMIT),
        cost_estimate=pl.CostEstimate(
            flops=60_000_000_000, bytes_accessed=10_000_000, transcendentals=20_000_000
        ),
        name="attend_back",
    )(scalars, qkv, other, dout, out, log)


PIECES = 4
MESH_ID = pl.DeviceIdType.MESH


def square_places():
    blk, lo = lax.axis_index("blk"), lax.axis_index("lo")
    mate, side = blk + 1 - 2 * (blk % 2), (blk + 2) % 4
    return blk, lo, mate, side


def greet(ids):
    barrier = pltpu.get_barrier_semaphore()
    for one in ids:
        pl.semaphore_signal(barrier, inc=1, device_id=one, device_id_type=MESH_ID)
    pl.semaphore_wait(barrier, len(ids))


def gather_kernel(rows_ref, out_ref, send, recv, local):
    blk, lo, mate, side = square_places()
    slot = lambda b, l: b * 2 + l
    mine = slot(blk, lo)
    to_mate, to_side, to_next = {"blk": mate}, {"blk": side}, {"lo": 1 - lo}
    greet([to_mate, to_side, to_next])
    step = rows_ref.shape[0] // PIECES

    def push(source, place, piece, kind, to):
        rows = pl.ds(piece * step, step)
        copy = pltpu.make_async_remote_copy(
            src_ref=source,
            dst_ref=out_ref.at[place, rows],
            send_sem=send.at[kind, piece],
            recv_sem=recv.at[kind, piece],
            device_id=to,
            device_id_type=MESH_ID,
        )
        copy.start()
        return copy

    own = pltpu.make_async_copy(rows_ref, out_ref.at[mine], local)
    own.start()
    piece_of = lambda p: rows_ref.at[pl.ds(p * step, step)]
    held = lambda place, p: out_ref.at[place, pl.ds(p * step, step)]
    side_order, next_order = (2, 3, 0, 1), (0, 1, 2, 3)
    by_side, by_next, by_mate, across = {}, {}, [], {}
    for k in range(PIECES):
        p, q = side_order[k], next_order[k]
        by_side[p] = push(piece_of(p), mine, p, 0, to_side)
        by_next[q] = push(piece_of(q), mine, q, 1, to_next)
    for p in range(PIECES):
        by_mate.append(push(piece_of(p), mine, p, 3, to_mate))
    from_side, from_next, from_across = slot(side, lo), slot(blk, 1 - lo), slot(side, 1 - lo)
    for k in range(PIECES):
        p, q = side_order[k], next_order[k]
        by_side[p].wait_recv()
        if p >= 2:
            across[p] = push(held(from_side, p), from_side, p, 2, to_next)
        by_mate.append(push(held(from_side, p), from_side, p, 4, to_mate))
        by_next[q].wait_recv()
        if q < 2:
            across[q] = push(held(from_next, q), from_next, q, 2, to_side)
        by_mate.append(push(held(from_next, q), from_next, q, 5, to_mate))
    for p in (0, 2, 1, 3):
        across[p].wait_recv()
        by_mate.append(push(held(from_across, p), from_across, p, 6, to_mate))
    for copy in by_mate:
        copy.wait()
    for copies in (by_side, by_next, across):
        for copy in copies.values():
            copy.wait_send()
    own.wait()


def gather_square(rows, number):
    tok, width = rows.shape
    return pl.pallas_call(
        gather_kernel,
        in_specs=[pl.BlockSpec(memory_space=pl.ANY)],
        out_specs=pl.BlockSpec(memory_space=pl.ANY),
        out_shape=jax.ShapeDtypeStruct((8, tok, width), rows.dtype),
        scratch_shapes=[
            pltpu.SemaphoreType.DMA((7, PIECES)),
            pltpu.SemaphoreType.DMA((7, PIECES)),
            pltpu.SemaphoreType.DMA,
        ],
        compiler_params=pltpu.CompilerParams(collective_id=number, has_side_effects=True),
        cost_estimate=pl.CostEstimate(flops=0, bytes_accessed=120_000_000, transcendentals=0),
        name="gather_square",
    )(rows).reshape(8 * tok, width)


def scatter_kernel(
    parts_ref, out_ref, mine, mates, made, got_across, got_side, got_next, send, recv, local
):
    blk, lo, mate, side = square_places()
    slot = lambda b, l: b * 2 + l
    to_mate, to_side, to_next = {"blk": mate}, {"blk": side}, {"lo": 1 - lo}
    mate_side = (mate + 2) % 4
    own_slots = (slot(side, 1 - lo), slot(side, lo), slot(blk, 1 - lo), slot(blk, lo))
    mate_slots = (slot(mate_side, 1 - lo), slot(mate_side, lo), slot(mate, 1 - lo), slot(mate, lo))
    step = parts_ref.shape[1] // PIECES
    loads = []
    for k in range(4):
        copy = pltpu.make_async_copy(parts_ref.at[own_slots[k]], mine.at[k], local.at[k])
        copy.start()
        loads.append(copy)
    greet([to_mate, to_side, to_next])

    def push(source, target, kind, piece, to):
        copy = pltpu.make_async_remote_copy(
            src_ref=source,
            dst_ref=target,
            send_sem=send.at[kind, piece],
            recv_sem=recv.at[kind, piece],
            device_id=to,
            device_id_type=MESH_ID,
        )
        copy.start()
        return copy

    rows = lambda p: pl.ds(p * step, step)
    orders = ((0, 2, 1, 3), (0, 1, 2, 3), (2, 3, 0, 1), (0, 1, 2, 3))
    from_mate = {}
    for k in range(4):
        for p in orders[k]:
            from_mate[k, p] = push(
                parts_ref.at[mate_slots[k], rows(p)], mates.at[k, rows(p)], k, p, to_mate
            )

    def summed(k, p):
        from_mate[k, p].wait_recv()
        return mine[k, rows(p), :].astype(F32) + mates[k, rows(p), :].astype(F32)

    sent = {}
    loads[0].wait()
    for p in orders[0]:
        made[0, rows(p), :] = summed(0, p).astype(BF16)
        sent[0, p] = push(
            made.at[0, rows(p)],
            got_across.at[rows(p)],
            4,
            p,
            to_side if p < 2 else to_next,
        )
    loads[1].wait()
    loads[2].wait()
    for k, p in ((1, 0), (2, 2), (1, 1), (2, 3), (1, 2), (2, 0), (1, 3), (2, 1)):
        total = summed(k, p)
        if (k == 1) == (p >= 2):
            sent[0, p].wait_recv()
            total = total + got_across[rows(p), :].astype(F32)
        made[k, rows(p), :] = total.astype(BF16)
        sent[k, p] = push(
            made.at[k, rows(p)],
            (got_side if k == 1 else got_next).at[rows(p)],
            4 + k,
            p,
            to_side if k == 1 else to_next,
        )
    loads[3].wait()
    for p in range(PIECES):
        total = summed(3, p)
        sent[1, p].wait_recv()
        sent[2, p].wait_recv()
        out_ref[rows(p), :] = (
            total + got_side[rows(p), :].astype(F32) + got_next[rows(p), :].astype(F32)
        )
    for copy in from_mate.values():
        copy.wait_send()
    for copy in sent.values():
        copy.wait_send()


def scatter_square(parts, number):
    count, width = parts.shape
    tok = count // 8
    return pl.pallas_call(
        scatter_kernel,
        in_specs=[pl.BlockSpec(memory_space=pl.ANY)],
        out_specs=pl.BlockSpec(memory_space=pltpu.VMEM),
        out_shape=jax.ShapeDtypeStruct((tok, width), F32),
        scratch_shapes=[
            pltpu.VMEM((4, tok, width), BF16),
            pltpu.VMEM((4, tok, width), BF16),
            pltpu.VMEM((3, tok, width), BF16),
            pltpu.VMEM((tok, width), BF16),
            pltpu.VMEM((tok, width), BF16),
            pltpu.VMEM((tok, width), BF16),
            pltpu.SemaphoreType.DMA((7, PIECES)),
            pltpu.SemaphoreType.DMA((7, PIECES)),
            pltpu.SemaphoreType.DMA((4,)),
        ],
        compiler_params=pltpu.CompilerParams(
            collective_id=number, has_side_effects=True, vmem_limit_bytes=VMEM_LIMIT
        ),
        cost_estimate=pl.CostEstimate(flops=0, bytes_accessed=120_000_000, transcendentals=0),
        name="scatter_square",
    )(parts.astype(BF16).reshape(8, tok, width))


def swap_square(blocks):
    return lax.all_to_all(blocks, SQUARE, split_axis=0, concat_axis=0, tiled=True)


def swap_pair(block, axis):
    return lax.ppermute(block, axis, [(0, 1), (1, 0)])


def gather_axis(rows, axis):
    if lax.axis_size(axis) != 2:
        return lax.all_gather(rows, axis, axis=0, tiled=False)
    other = swap_pair(rows, axis)
    first = lax.axis_index(axis) == 0
    return jnp.stack([jnp.where(first, rows, other), jnp.where(first, other, rows)])


def gather_copies(rows):
    both = gather_axis(gather_axis(rows, "hi"), "dp")
    return both.reshape((-1,) + rows.shape[1:])


def scatter_axis(parts, axis):
    if lax.axis_size(axis) != 2:
        return lax.psum_scatter(parts.astype(BF16), axis, scatter_dimension=0, tiled=False).astype(F32)
    place = lax.axis_index(axis)
    away = lax.dynamic_index_in_dim(parts, 1 - place, 0, False).astype(BF16)
    own = lax.dynamic_index_in_dim(parts, place, 0, False)
    return own + swap_pair(away, axis).astype(F32)


def scatter_copies(rows):
    dp_n, hi_n = lax.axis_size("dp"), lax.axis_size("hi")
    parts = rows.reshape((dp_n, hi_n, rows.shape[0] // (dp_n * hi_n)) + rows.shape[1:])
    return scatter_axis(scatter_axis(parts, "dp"), "hi")


def total_of(value, axes, count):
    spread = jnp.broadcast_to(value.reshape(1, 1), (count, 1))
    return jnp.sum(lax.all_to_all(spread, axes, split_axis=0, concat_axis=0, tiled=True))


def norm_parts(rows):
    inverse = lax.rsqrt(jnp.mean(rows * rows, axis=-1, keepdims=True) + NORM_EPS)
    return rows * inverse, inverse


def reorder(pairs, block, source, target, cast):
    for at, to in pairs:
        target[:, to * block : to * block + block] = cast(source[:, at * block : at * block + block])


def out_kernel(order, pairs, block, mixed_ref, weight_ref, rows_ref, gain_ref, middle_ref, normed_ref, total):
    f = pl.program_id(0)

    @pl.when(f == 0)
    def _():
        total[...] = jnp.zeros_like(total)

    total[...] += dot32(mixed_ref[0], weight_ref[...])

    @pl.when(f == pl.num_programs(0) - 1)
    def _():
        middle = rows_ref[...].astype(F32) + RESIDUAL_SCALE * total[...]
        middle_ref[...] = middle
        total[...] = norm_parts(middle)[0] * gain_ref[...]
        reorder(pairs, block, total, normed_ref, lambda v: v.astype(BF16))


def out_project(mixed, weight, rows, gain, order, pairs, block):
    group, tok, cols = mixed.shape
    width = weight.shape[1]
    whole = pl.BlockSpec((tok, width), lambda f: (0, 0))
    return pl.pallas_call(
        functools.partial(out_kernel, order, pairs, block),
        grid=(group,),
        in_specs=[
            pl.BlockSpec((1, tok, cols), lambda f: (f, 0, 0)),
            pl.BlockSpec((cols, width), lambda f: (order(f), 0)),
            whole,
            pl.BlockSpec((1, width), lambda f: (0, 0)),
        ],
        out_specs=[whole, whole],
        out_shape=[
            jax.ShapeDtypeStruct((tok, width), F32),
            jax.ShapeDtypeStruct((tok, width), BF16),
        ],
        scratch_shapes=[pltpu.VMEM((tok, width), F32)],
        compiler_params=pltpu.CompilerParams(vmem_limit_bytes=VMEM_LIMIT),
        cost_estimate=pl.CostEstimate(
            flops=2 * tok * width * width, bytes_accessed=16_000_000, transcendentals=0
        ),
        name="out_project",
    )(mixed, weight, rows, gain)


def out_back_kernel(
    pairs, block, grad_ref, middle_ref, result_ref, gain_ref, weight_ref, sum_ref, rows_ref, mixed_ref, work
):
    f = pl.program_id(0)

    @pl.when(f == 0)
    def _():
        reorder(pairs, block, grad_ref, work, lambda v: v)
        normal, inverse = norm_parts(middle_ref[...])
        grad = work[...] * gain_ref[...]
        total = result_ref[...] + inverse * (
            grad - normal * jnp.mean(grad * normal, axis=-1, keepdims=True)
        )
        sum_ref[...] = total
        rows_ref[...] = (RESIDUAL_SCALE * total).astype(BF16)

    mixed_ref[0] = dot32(rows_ref[...], weight_ref[...], ((1,), (1,))).astype(BF16)


def out_back(grad, middle, result, gain, weight, cols, order, pairs, block):
    tok, width = middle.shape
    group = width // cols
    whole = pl.BlockSpec((tok, width), lambda f: (0, 0))
    return pl.pallas_call(
        functools.partial(out_back_kernel, pairs, block),
        grid=(group,),
        in_specs=[
            whole,
            whole,
            whole,
            pl.BlockSpec((1, width), lambda f: (0, 0)),
            pl.BlockSpec((cols, width), lambda f: (order(f), 0)),
        ],
        out_specs=[whole, whole, pl.BlockSpec((1, tok, cols), lambda f: (f, 0, 0))],
        out_shape=[
            jax.ShapeDtypeStruct((tok, width), F32),
            jax.ShapeDtypeStruct((tok, width), BF16),
            jax.ShapeDtypeStruct((group, tok, cols), BF16),
        ],
        scratch_shapes=[pltpu.VMEM((tok, width), F32)],
        compiler_params=pltpu.CompilerParams(vmem_limit_bytes=VMEM_LIMIT),
        cost_estimate=pl.CostEstimate(
            flops=2 * tok * width * width, bytes_accessed=20_000_000, transcendentals=0
        ),
        name="out_back",
    )(grad, middle, result, gain, weight)


def deal_kernel(places, wide, gate_ref, up_ref, gates_ref, ups_ref):
    for at, (f, to) in enumerate(places):
        here, there = slice(at * wide, at * wide + wide), slice(to * wide, to * wide + wide)
        gates_ref[f, :, there] = gate_ref[:, here]
        ups_ref[f, :, there] = up_ref[:, here]


def collect_kernel(
    places, wide, gates_ref, ups_ref, gate_ref, up_ref, gain_ref, dgate_ref, dup_ref, dgain_ref
):
    total = jnp.zeros((gate_ref.shape[0], wide), F32)
    for at, (f, to) in enumerate(places):
        here, there = slice(at * wide, at * wide + wide), slice(to * wide, to * wide + wide)
        dgate, dup = gates_ref[f, :, there].astype(F32), ups_ref[f, :, there].astype(F32)
        dgate_ref[:, here] = dgate
        dup_ref[:, here] = dup
        total += gate_ref[:, here].astype(F32) * dgate + up_ref[:, here].astype(F32) * dup
    dgain_ref[...] = jnp.sum(total, axis=1, keepdims=True) / gain_ref[...]


def shards(
    hidden,
    teacher,
    lengths,
    attn_gain,
    w_query,
    key_projection,
    value_projection,
    w_out,
    mlp_gain,
    w_gate,
    w_up,
    w_down,
):
    dp_n, blk_n, hi_n, lo_n = (lax.axis_size(a) for a in ALL)
    group = blk_n * lo_n
    every = dp_n * blk_n * hi_n * lo_n
    hi, lo = lax.axis_index("hi"), lax.axis_index("lo")
    blk = lax.axis_index("blk")
    tok = hidden.shape[1]
    seq_len = tok * blk_n * hi_n * lo_n
    width = hidden.shape[2]
    rows_w = w_query.shape[0]
    units_w = w_down.shape[0]
    ff_part = w_gate.shape[1] // group

    block = lo_n * rows_w
    if block % 128 == 0:
        to_inner = [
            ((d * blk_n + b) * hi_n + h, (d * hi_n + h) * blk_n + b)
            for d in range(dp_n)
            for b in range(blk_n)
            for h in range(hi_n)
        ]
        reblock = block
    else:
        to_inner, reblock = [(0, 0)], width
    to_outer = [(to, at) for at, to in to_inner]

    def inner(a):
        if reblock == block:
            return a
        return a.reshape(-1, dp_n, blk_n, hi_n, block).transpose(0, 1, 3, 2, 4).reshape(-1, width)

    def outer(a):
        if reblock == block:
            return a
        return a.reshape(-1, dp_n, hi_n, blk_n, block).transpose(0, 1, 3, 2, 4).reshape(-1, width)

    key_head = lambda f: (f % lo_n) * blk_n + f // lo_n

    def head_columns(w):
        cols = w.shape[1] // group
        return w.reshape(rows_w, lo_n, blk_n, cols).transpose(2, 1, 0, 3).reshape(group, rows_w, cols)

    def head_columns_back(g):
        cols = g.shape[2]
        return (
            g.reshape(blk_n, lo_n, rows_w, cols).transpose(2, 1, 0, 3).reshape(rows_w, group * cols)
        )

    def unit_columns(w):
        return (
            w.reshape(rows_w, dp_n, blk_n, hi_n, lo_n, units_w)
            .transpose(2, 4, 0, 1, 3, 5)
            .reshape(group, rows_w, ff_part)
        )

    def unit_columns_back(g):
        return (
            g.reshape(blk_n, lo_n, rows_w, dp_n, hi_n, units_w)
            .transpose(2, 3, 0, 4, 1, 5)
            .reshape(rows_w, group * ff_part)
        )

    gains = jnp.stack([attn_gain, mlp_gain]).reshape(1, 2 * rows_w)
    gains = lax.all_to_all(
        jnp.broadcast_to(gains, (every, 2 * rows_w)), ALL, split_axis=0, concat_axis=0, tiled=True
    )
    gains = gains.astype(F32).reshape(every, 2, rows_w)
    gain_one, gain_two = gains[:, 0].reshape(1, width), gains[:, 1].reshape(1, width)

    q_cols = w_query.shape[1] // group
    k_cols = key_projection.shape[1] // group
    head_parts = jnp.concatenate(
        [head_columns(w) for w in (w_query, key_projection, value_projection)], axis=2
    )
    head_wide = head_parts.shape[2]
    head_parts = jnp.broadcast_to(
        head_parts.reshape(1, blk_n, 1, lo_n, rows_w, head_wide),
        (dp_n, blk_n, hi_n, lo_n, rows_w, head_wide),
    ).reshape(every, rows_w, head_wide)
    qkv_weight = lax.all_to_all(head_parts, ALL, split_axis=0, concat_axis=0, tiled=True).reshape(
        width, head_wide
    )

    ff_places = [
        (b * lo_n + l, d * hi_n + h)
        for d in range(dp_n)
        for b in range(blk_n)
        for h in range(hi_n)
        for l in range(lo_n)
    ]
    part_shape = jax.ShapeDtypeStruct((group, rows_w, ff_part), BF16)
    params = pltpu.CompilerParams(vmem_limit_bytes=VMEM_LIMIT)
    if units_w % 128 == 0:
        gate_parts, up_parts = pl.pallas_call(
            functools.partial(deal_kernel, ff_places, units_w),
            out_shape=[part_shape, part_shape],
            compiler_params=params,
            name="deal",
        )(w_gate, w_up)
    else:
        gate_parts, up_parts = unit_columns(w_gate), unit_columns(w_up)

    places = (
        (jnp.arange(blk_n)[:, None, None] * hi_n + hi) * lo_n + jnp.arange(lo_n)[None, :, None]
    ) * tok + jnp.arange(tok)[None, None, :]
    places = places.reshape(-1)
    half = HEAD_SIZE // 2
    frequency = ROPE_BASE ** (-(jnp.arange(half).astype(F32) * 2.0) / HEAD_SIZE)
    angles = places.astype(F32)[:, None] * frequency[None, :]
    cosine, sine, none = jnp.cos(angles), jnp.sin(angles), jnp.zeros_like(angles)
    tables = (
        jnp.concatenate([cosine] * 4, axis=1),
        jnp.concatenate([-sine, none] * 2, axis=1),
        jnp.concatenate([none, sine] * 2, axis=1),
    )

    inputs = hidden[0].astype(F32)
    normal_one, inverse_one = norm_parts(inputs)
    normed_one = gather_square((normal_one * gain_one).astype(BF16), 0)
    qkv = project(normed_one, qkv_weight, tables, tok)
    normed_one, w_out, w_down, gate_parts, up_parts = lax.optimization_barrier(
        (normed_one, w_out, w_down, gate_parts, up_parts)
    )
    down_weight = gather_copies(w_down)
    gate_weight = gather_copies(swap_square(gate_parts).reshape(group * rows_w, -1))
    up_weight = gather_copies(swap_square(up_parts).reshape(group * rows_w, -1))
    out_weight = gather_axis(gather_axis(w_out, "lo"), "hi").reshape(-1, width)
    out_weight = lax.all_gather(out_weight, ("dp", "blk"), axis=0, tiled=True)
    unit = lo_n * tok
    other_kv = swap_pair(qkv[:, q_cols:], "hi").reshape(blk_n, unit, 2 * k_cols)
    qkv = qkv.reshape(blk_n, unit, -1)
    scalars = jnp.stack([lengths[0], hi.astype(jnp.int32)])
    out_heads, log_heads = attend(scalars, qkv, other_kv)
    mixed = swap_square(out_heads.reshape(group, tok, q_cols))
    middle, normed_two = out_project(
        mixed, out_weight, hidden[0], gain_two, key_head, to_inner, reblock
    )

    normed_two = gather_square(inner(normed_two), 0)
    gate = dot32(normed_two, gate_weight)
    upward = dot32(normed_two, up_weight)
    sigma = jax.nn.sigmoid(gate)
    silu = gate * sigma
    units = (silu * upward).astype(BF16)
    gate_slope = (upward * sigma * (1.0 + gate * (1.0 - sigma))).astype(BF16)
    up_slope = silu.astype(BF16)
    result = middle + RESIDUAL_SCALE * scatter_square(dot32(units, down_weight), 1)

    own_places = ((blk * hi_n + hi) * lo_n + lo) * tok + jnp.arange(tok)
    valid = own_places < lengths[0]
    misfit = jnp.where(valid[:, None], result - teacher[0].astype(F32), 0.0)
    valid_count = total_of(lengths, ("dp",), dp_n).astype(F32)
    squares = total_of(jnp.sum(misfit * misfit), ALL, every)
    mse_loss = squares / (width * valid_count)
    grad_result = misfit * (dp_n * seq_len / valid_count)

    branch = gather_square((RESIDUAL_SCALE * grad_result).astype(BF16), 0)
    grad_units = dot32(branch, down_weight, ((1,), (1,)))
    grad_gate_rows = (grad_units * gate_slope.astype(F32)).astype(BF16)
    grad_up_rows = (grad_units * up_slope.astype(F32)).astype(BF16)
    grad_normal = outer(
        scatter_square(
            dot32(grad_gate_rows, gate_weight, ((1,), (1,)))
            + dot32(grad_up_rows, up_weight, ((1,), (1,))),
            1,
        )
    )
    down_sum = scatter_copies(dot32(units, branch, ((0,), (0,))))
    gate_sum = scatter_copies(dot32(normed_two, grad_gate_rows, ((0,), (0,))))
    up_sum = scatter_copies(dot32(normed_two, grad_up_rows, ((0,), (0,))))

    grad_middle, attn_rows, grad_mixed = out_back(
        grad_normal, middle, grad_result, gain_two, out_weight, q_cols, key_head, to_outer, reblock
    )
    dout = swap_square(grad_mixed).reshape(blk_n, unit, q_cols)
    dq, dkv = attend_back(scalars, qkv, other_kv, dout, out_heads, log_heads)
    dkv = dkv.reshape(2, group * tok, 2 * k_cols)
    dqkv = back_rope(
        dq.reshape(group * tok, q_cols), dkv[0], swap_pair(dkv[1], "hi"), tables, tok
    )
    grad_first = scatter_square(dot32(dqkv, qkv_weight, ((1,), (1,))), 1) * gain_one
    grad_hidden = grad_middle + inverse_one * (
        grad_first - normal_one * jnp.mean(grad_first * normal_one, axis=-1, keepdims=True)
    )
    head_grads = dot32(normed_one, dqkv, ((0,), (0,))).astype(BF16).reshape(every, rows_w, head_wide)
    head_grads = lax.all_to_all(head_grads, ALL, split_axis=0, concat_axis=0, tiled=True)
    head_grads = jnp.sum(
        head_grads.reshape(dp_n, blk_n, hi_n, lo_n, rows_w, head_wide).astype(F32), axis=(0, 2)
    ).reshape(group, rows_w, head_wide)

    square_attn = lax.all_gather(attn_rows, SQUARE, axis=0, tiled=True)
    own_out = dot32(out_heads.reshape(group * tok, q_cols), square_attn, ((0,), (0,))).astype(BF16)
    own_head = lo * blk_n + blk
    if rows_w * hi_n * lo_n == q_cols:
        spread = jnp.where((jnp.arange(dp_n) == lo)[:, None, None], own_out[None], 0)
        grad_out = lax.psum_scatter(
            spread.reshape(dp_n * q_cols, width), ("dp", "hi", "lo"), scatter_dimension=0, tiled=True
        ).astype(F32)
    else:
        spread = jnp.where((jnp.arange(group) == own_head)[:, None, None], own_out[None], 0)
        grad_out = lax.psum_scatter(
            spread.reshape(width, width), ALL, scatter_dimension=0, tiled=True
        ).astype(F32)

    own_one, own_two = attn_gain.astype(F32)[:, None], mlp_gain.astype(F32)[:, None]
    grad_query = head_columns_back(head_grads[:, :, :q_cols])
    grad_key = head_columns_back(head_grads[:, :, q_cols : q_cols + k_cols])
    grad_value = head_columns_back(head_grads[:, :, q_cols + k_cols :])

    def row_sums(*pairs):
        return sum(jnp.sum(w.astype(F32) * g, axis=1, keepdims=True) for w, g in pairs)

    grad_gain_one = (
        row_sums((w_query, grad_query), (key_projection, grad_key), (value_projection, grad_value))
        / own_one
    )
    gate_parts, up_parts = (
        swap_square(g.astype(BF16).reshape(group, rows_w, -1)) for g in (gate_sum, up_sum)
    )
    if units_w % 128 == 0:
        ff_shape = jax.ShapeDtypeStruct(w_gate.shape, F32)
        grad_gate, grad_up, grad_gain_two = pl.pallas_call(
            functools.partial(collect_kernel, ff_places, units_w),
            out_shape=[ff_shape, ff_shape, jax.ShapeDtypeStruct((rows_w, 1), F32)],
            compiler_params=params,
            name="collect",
        )(gate_parts, up_parts, w_gate, w_up, own_two)
    else:
        grad_gate = unit_columns_back(gate_parts.astype(F32))
        grad_up = unit_columns_back(up_parts.astype(F32))
        grad_gain_two = row_sums((w_gate, grad_gate), (w_up, grad_up)) / own_two
    return (
        result.astype(BF16)[None],
        mse_loss,
        grad_hidden[None],
        grad_gain_one[:, 0],
        grad_query,
        grad_key,
        grad_value,
        grad_out,
        grad_gain_two[:, 0],
        grad_gate,
        grad_up,
        down_sum,
    )


def solution(mesh):
    dp_n, blk_n, head_n = (mesh.shape[a] for a in ("dp", "blk", "head"))
    fine = Mesh(mesh.devices.reshape(dp_n, blk_n, 2, head_n // 2), ALL)
    tokens = P("dp", SEQ, None)
    rows, row = P(ALL, None), P(ALL)
    return jax.shard_map(
        shards,
        mesh=fine,
        in_specs=(tokens, tokens, P("dp"), row, rows, rows, rows, rows, row, rows, rows, rows),
        out_specs=(tokens, P(), tokens, row, rows, rows, rows, rows, row, rows, rows, rows),
        check_vma=False,
    )
```

time: 6770 us -> 1140 us (0.17)
  waiting for transfers between devices: 5580 us -> 294 us
  Pallas kernels: 0 us -> 443 us
  blocking collectives: 470 us -> 28.9 us
  matrix products: 362 us -> 166 us
  local copies, waits for them, and re-layouts: 189 us -> 38.5 us
    reduce_scatter x9 -> x1, waiting for transfers between devices: 5270 us -> 0.01 us  [shards(): lax.psum_scatter(spread.reshape(dp_n * q_cols, width), ('dp', 'hi', 'lo')...]
    pallas_call x0 -> x14, Pallas kernels: none -> 443 us  [the longest x3 181 us: scatter_square(): pl.pallas_call(scatter_kernel, in_specs=[pl.BlockSpec(memory_space=pl.ANY...]
    psum x2 -> x0, blocking collectives: 316 us -> none  [shards(): lax.psum((jnp.sum(misfit * misfit), jnp.sum(valid_rows.astype(jnp.float32...]
    ppermute x0 -> x16, waiting for transfers between devices: none -> 275 us  [swap_pair(): return lax.ppermute(block, axis, [(0, 1), (1, 0)])]
    all_gather x9 -> x2, waiting for transfers between devices: 251 us -> 0.01 us  [the longest x1 0.01 us: shards(): square_attn = lax.all_gather(attn_rows, SQUARE, axis=0, tiled=True)]
    dot_general x93 -> x12, matrix products: 362 us -> 166 us  [dot32(): return lax.dot_general(a, b, (dims, ((), ())), preferred_element_type=F32)]
    all_to_all x5 -> x2, blocking collectives: 112 us -> 28.9 us  [the longest x1 22.8 us: swap_square(): lax.all_to_all(blocks, SQUARE, split_axis=0, concat_axis=0, tiled=True)]
  transfers between devices with their start and end apart: 21 -> 28, of which waited for: 14 -> 14; matrix products, arithmetic and copies ran while one was open for 6% -> 13% of each run, Pallas kernels for 0% -> 19%
where the time goes in v1:
time: 1140 us; the launch traced here: 1130 us
  Pallas kernels  443 us (39%)
  waiting for transfers between devices  294 us (26%)
  matrix products  166 us (15%)
  starting transfers between devices  77.7 us (7%)
  other arithmetic  68.4 us (6%)
  local copies, waits for them, and re-layouts  38.5 us (3%)
  blocking collectives  28.9 us (3%)
  between operations  18 us (2%)
    ppermute x16, waiting for transfers between devices, swap_pair(): return lax.ppermute(block, axis, [(0, 1), (1, 0)])  275 us
    pallas_call x3, Pallas kernels, scatter_square(): pl.pallas_call(scatter_kernel, in_specs=[pl.BlockSpec(memory_space=pl.ANY...  181 us
    dot_general x12, matrix products, dot32(): return lax.dot_general(a, b, (dims, ((), ())), preferred_element_type=F32)  166 us
    pallas_call x3, Pallas kernels, gather_square(): pl.pallas_call(gather_kernel, in_specs=[pl.BlockSpec(memory_space=pl.ANY)...  117 us
    pallas_call x1, Pallas kernels, attend_back(): pl.pallas_call(attend_back_kernel, grid=(units,), in_specs=[pl.BlockSpec(...  56.5 us
    pallas_call x1, Pallas kernels, attend(): pl.pallas_call(attend_kernel, grid=(blocks,), in_specs=[pl.BlockSpec(memo...  38.6 us
    ppermute x16, starting transfers between devices, swap_pair(): return lax.ppermute(block, axis, [(0, 1), (1, 0)])  35.1 us
    all_to_all x1, blocking collectives, swap_square(): lax.all_to_all(blocks, SQUARE, split_axis=0, concat_axis=0, tiled=True)  22.8 us
  transfers between devices with their start and end apart: 28, of which 14 were waited for; matrix products, arithmetic and copies ran while one was open for 13% of the time, Pallas kernels for 19%

profile of v1, /device:TPU:0, one launch (start us, length us, event | category | flops | bytes accessed | tf_op | source)
XLA Modules:
  0.0 1133.8 jit_solution(6620687454014892533)
XLA Ops:
  25.8 38.8 %gather_square.3 = bf16[8,256,2048]{2,1,0:T(8,128)(2,1)} custom-call(bf16[256,2048]{1,0:T(8,128)(2,1)} %fusion.12.rows_ref), custom_call_target="tpu_custom_call" | custom-call | bytes 120000000 | tf_op jit(solution)/shard_map/gather_square/pallas_call | solution.py:411
  75.1 23.9 %collective-permute-done.2 = bf16[2,64,2048]{2,1,0:T(8,128)(2,1)S(1)} collective-permute-done((bf16[2,64,2048]{2,1,0:T(8,128)(2,1)S(1)}, bf16[2,64,2048]{2,1,0:T(8,128)(2,1)S(1)}, u32[]{:S(2)}, u32[]{:S(2)}) %collective-permute-start.2) | collective-permute-done | bytes 524320 | tf_op jit(solution)/shard_map/ppermute | solution.py:541
  106.9 22.8 %all_to_all.59 = bf16[8,64,1024]{2,1,0:T(8,128)(2,1)S(1)} all-to-all(bf16[8,64,1024]{2,1,0:T(8,128)(2,1)S(1)} %copy-done.29), channel_id=1, replica_groups=mesh['dp'=2,'blk'=4,'hi'=2,'lo'=2] {'blk','lo'}, dimensions={0} | all-to-all | bytes 2097152 | tf_op jit(solution)/shard_map/all_to_all | solution.py:537
  134.8 16.2 %all-to-all-done.3 = bf16[8,64,1024]{2,1,0:T(8,128)(2,1)} async-done(((bf16[8,64,1024]{2,1,0:T(8,128)(2,1)}), bf16[8,64,1024]{2,1,0:T(8,128)(2,1)}, u32[]{:S(2)}, u32[]{:S(2)}) %all-to-all-start.3) | async-done | bytes 1048608 | tf_op jit(solution)/shard_map/all_to_all | solution.py:537
  174.2 111.2 %collective-permute-done.7 = bf16[256,2048]{1,0:T(8,128)(2,1)} collective-permute-done((bf16[256,2048]{1,0:T(8,128)(2,1)S(1)}, bf16[256,2048]{1,0:T(8,128)(2,1)}, u32[]{:S(2)}, u32[]{:S(2)}) %collective-permute-start.7) | collective-permute-done | bytes 1048608 | tf_op jit(solution)/shard_map/ppermute | solution.py:541
  290.0 11.7 %project.1 = bf16[2048,384]{1,0:T(8,128)(2,1)} custom-call(bf16[2048,2048]{1,0:T(8,128)(2,1)} %bitcast.192, bf16[2048,384]{1,0:T(8,128)(2,1)} %bitcast.13.weight_ref, f32[2048,128]{1,0:T(8,128)} %get-tuple-element.85.cos_ref, f32[2048,128]{1,0:T(8,128)} %get-tuple-element.75.sina_ref, f32[2048,128]{1,0:T(8,128)} %get-tuple-element.74.sinb_ref), custom_call_target="tpu_custom_call" | custom-call | flops 3221225472 | bytes 16777216 | tf_op jit(solution)/shard_map/project/pallas_call | solution.py:52
  302.9 16.2 %collective-permute-done.5 = bf16[512,1024]{1,0:T(8,128)(2,1)} collective-permute-done((bf16[512,1024]{1,0:T(8,128)(2,1)S(1)}, bf16[512,1024]{1,0:T(8,128)(2,1)}, u32[]{:S(2)}, u32[]{:S(2)}) %collective-permute-start.5) | collective-permute-done | bytes 1048608 | tf_op jit(solution)/shard_map/ppermute | solution.py:541
  319.1 22.5 %collective-permute-done.3 = bf16[512,1024]{1,0:T(8,128)(2,1)} collective-permute-done((bf16[512,1024]{1,0:T(8,128)(2,1)}, bf16[512,1024]{1,0:T(8,128)(2,1)}, u32[]{:S(2)}, u32[]{:S(2)}) %collective-permute-start.3) | collective-permute-done | bytes 1048608 | tf_op jit(solution)/shard_map/ppermute | solution.py:541
  353.0 38.6 %attend.1 = (bf16[4,512,256]{2,1,0:T(8,128)(2,1)}, f32[4,8,512]{2,1,0:T(8,128)}) custom-call(s32[2]{0:T(128)} %pad_add_fusion.scalar_ref, bf16[4,512,384]{2,1,0:T(8,128)(2,1)} %bitcast.218, bf16[4,512,128]{2,1,0:T(8,128)(2,1)} %bitcast.232), custom_call_target="tpu_custom_call" | custom-call | flops 40000000000 | bytes 8000000 | tf_op jit(solution)/shard_map/attend/pallas_call | solution.py:189
  404.5 33.0 %collective-permute-done.6 = bf16[2,512,1024]{2,1,0:T(8,128)(2,1)} collective-permute-done((bf16[2,512,1024]{2,1,0:T(8,128)(2,1)}, bf16[2,512,1024]{2,1,0:T(8,128)(2,1)}, u32[]{:S(2)}, u32[]{:S(2)}) %collective-permute-start.6) | collective-permute-done | bytes 2097184 | tf_op jit(solution)/shard_map/ppermute | solution.py:541
  441.7 10.8 out_project.1
  452.6 39.3 %gather_square.4 = bf16[8,256,2048]{2,1,0:T(8,128)(2,1)} custom-call(bf16[256,2048]{1,0:T(8,128)(2,1)} %get-tuple-element.36.rows_ref), custom_call_target="tpu_custom_call" | custom-call | bytes 120000000 | tf_op jit(solution)/shard_map/gather_square/pallas_call | solution.py:411
  491.8 14.7 %fusion.35 = f32[2048,1024]{0,1:T(8,128)} fusion(bf16[2048,2048]{1,0:T(8,128)(2,1)} %bitcast.194, bf16[2048,1024]{1,0:T(8,128)(2,1)} %bitcast.213), kind=kOutput, calls=%fused_computation.115 | convolution fusion | flops 8589934592 | bytes 20971520 | tf_op jit(solution)/shard_map/dot_general | solution.py:28
  506.5 17.8 %fusion = (bf16[1024,2048]{1,0:T(8,128)(2,1)}, f32[2048,1024]{0,1:T(8,128)}) fusion(f32[2048,1024]{0,1:T(8,128)} %fusion.35, bf16[2048,2048]{1,0:T(8,128)(2,1)} %bitcast.195, bf16[2048,1024]{1,0:T(8,128)(2,1)} %bitcast.215), kind=kOutput, calls=%fused_computation.2 | convolution fusion | flops 8602517504 | bytes 33554432 | tf_op jit(solution)/shard_map/dot_general | solution.py:28
  524.3 18.0 %convolution_convert_fusion.1 = bf16[2048,2048]{1,0:T(8,128)(2,1)} fusion(bf16[1024,2048]{1,0:T(8,128)(2,1)S(1)} %bitcast.212, f32[2048,1024]{0,1:T(8,128)} %get-tuple-element.84, f32[2048,1024]{0,1:T(8,128)} %fusion.35), kind=kOutput, calls=%fused_computation.15 | convolution fusion | flops 8606711808 | bytes 29360128 | tf_op jit(solution)/shard_map/dot_general | solution.py:28
  542.3 41.1 %scatter_square.3 = f32[256,2048]{1,0:T(8,128)} custom-call(bf16[8,256,2048]{2,1,0:T(8,128)(2,1)} %bitcast.200), custom_call_target="tpu_custom_call" | custom-call | bytes 120000000 | tf_op jit(solution)/shard_map/scatter_square/pallas_call | solution.py:512
  588.4 38.9 %gather_square.5 = bf16[8,256,2048]{2,1,0:T(8,128)(2,1)} custom-call(bf16[256,2048]{1,0:T(8,128)(2,1)} %get-tuple-element.52.rows_ref), custom_call_target="tpu_custom_call" | custom-call | bytes 120000000 | tf_op jit(solution)/shard_map/gather_square/pallas_call | solution.py:411
  627.3 21.7 %multiply_convert_fusion = (bf16[2048,1024]{0,1:T(8,128)(2,1)}, bf16[2048,1024]{0,1:T(8,128)(2,1)}) fusion(f32[2048,1024]{0,1:T(8,128)} %fusion.35, f32[2048,1024]{0,1:T(8,128)} %get-tuple-element.84, bf16[2048,2048]{1,0:T(8,128)(2,1)} %bitcast.201, bf16[1024,2048]{1,0:T(8,128)(2,1)} %bitcast.211), kind=kOutput, calls=%fused_computation.8 | convolution fusion | flops 8625586176 | bytes 37748736 | tf_op jit(solution)/shard_map/dot_general | solution.py:28
  649.0 14.2 %fusion.36 = f32[2048,2048]{1,0:T(8,128)} fusion(bf16[2048,1024]{0,1:T(8,128)(2,1)} %get-tuple-element.55, bf16[2048,1024]{1,0:T(8,128)(2,1)S(1)} %bitcast.214), kind=kOutput, calls=%fused_computation.116 | convolution fusion | flops 8589934592 | bytes 25165824 | tf_op jit(solution)/shard_map/dot_general | solution.py:28
  663.3 16.1 %add_convert_fusion = bf16[2048,2048]{1,0:T(8,128)(2,1)} fusion(f32[2048,2048]{1,0:T(8,128)} %fusion.36, bf16[2048,1024]{0,1:T(8,128)(2,1)} %get-tuple-element.54, bf16[2048,1024]{1,0:T(8,128)(2,1)S(1)} %bitcast.216), kind=kOutput, calls=%fused_computation | convolution fusion | flops 8598323200 | bytes 33554432 | tf_op jit(solution)/shard_map/dot_general | solution.py:28
  679.3 41.1 %scatter_square.4.grad_ref = f32[256,2048]{1,0:T(8,128)} custom-call(bf16[8,256,2048]{2,1,0:T(8,128)(2,1)} %bitcast.198), custom_call_target="tpu_custom_call" | custom-call | bytes 120000000 | tf_op jit(solution)/shard_map/scatter_square/pallas_call | solution.py:512
  720.5 12.4 %out_back.1 = (f32[256,2048]{1,0:T(8,128)}, bf16[256,2048]{1,0:T(8,128)(2,1)}, bf16[8,256,256]{2,1,0:T(8,128)(2,1)}) custom-call(f32[256,2048]{1,0:T(8,128)} %scatter_square.4.grad_ref, f32[256,2048]{1,0:T(8,128)} %get-tuple-element.35.middle_ref, f32[256,2048]{1,0:T(8,128)} %get-tuple-element.53.result_ref, f32[1,2048]{1,0:T(1,128)} %reshape_squeeze.4.gain_ref, ...), custom_call_target="tpu_custom_call" | custom-call | flops 2147483648 | bytes 20000000 | tf_op jit(solution)/shard_map/out_back/pallas_call | solution.py:654
  732.9 11.8 %copy.76 = bf16[2048,2048]{1,0:T(8,128)(2,1)} copy(bf16[2048,2048]{0,1:T(8,128)(2,1)} %bitcast.196) | data formatting | bytes 16777216 | tf_op jit(solution)/shard_map/dot_general | solution.py:28
  744.7 12.9 %fusion.7 = f32[2,2,512,1024]{3,2,1,0:T(8,128)S(1)} fusion(bf16[2,2,512,2048]{3,2,1,0:T(8,128)(2,1)} %bitcast.203, bf16[2048,1024]{0,1:T(8,128)(2,1)} %get-tuple-element.55), kind=kOutput, calls=%fused_computation.24 | convolution fusion | flops 8589934592 | bytes 20971520 | tf_op jit(solution)/shard_map/dot_general | solution.py:28
  767.2 12.9 %fusion.5 = f32[2,2,512,1024]{3,2,1,0:T(8,128)S(1)} fusion(bf16[2,2,512,2048]{3,2,1,0:T(8,128)(2,1)} %bitcast.204, bf16[2048,1024]{0,1:T(8,128)(2,1)} %get-tuple-element.54), kind=kOutput, calls=%fused_computation.21 | convolution fusion | flops 8589934592 | bytes 20971520 | tf_op jit(solution)/shard_map/dot_general | solution.py:28
  783.6 26.3 %collective-permute-done.10 = bf16[2,512,1024]{2,1,0:T(8,128)(2,1)} collective-permute-done((bf16[2,512,1024]{2,1,0:T(8,128)(2,1)S(1)}, bf16[2,512,1024]{2,1,0:T(8,128)(2,1)}, u32[]{:S(2)}, u32[]{:S(2)}) %collective-permute-start.10) | collective-permute-done | bytes 2097184 | tf_op jit(solution)/shard_map/ppermute | solution.py:541
  820.6 14.7 %fusion.37 = f32[2,2,256,2048]{3,2,1,0:T(8,128)} fusion(bf16[2,2,256,2048]{3,2,1,0:T(8,128)(2,1)} %bitcast.235, bf16[2048,2048,1,1]{1,0,3,2:T(8,128)(2,1)} %bitcast.202), kind=kOutput, calls=%fused_computation.117 | convolution fusion | flops 8589934592 | bytes 20971520 | tf_op jit(solution)/shard_map/dot_general | solution.py:28
  835.3 19.1 %collective-permute-done.12 = bf16[2,512,1024]{2,1,0:T(8,128)(2,1)} collective-permute-done((bf16[2,512,1024]{2,1,0:T(8,128)(2,1)}, bf16[2,512,1024]{2,1,0:T(8,128)(2,1)}, u32[]{:S(2)}, u32[]{:S(2)}) %collective-permute-start.12) | collective-permute-done | bytes 2097184 | tf_op jit(solution)/shard_map/ppermute | solution.py:541
  866.8 56.5 %attend_back.1 = (bf16[4,512,256]{2,1,0:T(8,128)(2,1)}, bf16[2,4,512,128]{3,2,1,0:T(8,128)(2,1)}) custom-call(s32[2]{0:T(128)} %pad_add_fusion.scalar_ref, bf16[4,512,384]{2,1,0:T(8,128)(2,1)} %bitcast.219, bf16[4,512,128]{2,1,0:T(8,128)(2,1)} %bitcast.233, bf16[4,512,256]{2,1,0:T(8,128)(2,1)} %bitcast.46.dout_ref, ...), custom_call_target="tpu_custom_call" | custom-call | flops 60000002048 | bytes 10000000 | tf_op jit(solution)/shard_map/attend_back/pallas_call | solution.py:310
  925.6 13.2 %collective-permute-start.9 = (bf16[2048,128]{1,0:T(8,128)(2,1)S(1)}, bf16[2048,128]{1,0:T(8,128)(2,1)}, u32[]{:S(2)}, u32[]{:S(2)}) collective-permute-start(bf16[2048,128]{1,0:T(8,128)(2,1)S(1)} %bitcast.229), channel_id=1, source_target_pairs={{0,2},{2,0},{1,3},{3,1},{4,6},{6,4},{5,7},{7,5},{8,10},{10,8},{9,1... | collective-permute-start | bytes 1572872 | tf_op jit(solution)/shard_map/ppermute | solution.py:541
  952.1 10.6 collective-permute-done.9.other_ref
  1008.0 98.6 %scatter_square.5 = f32[256,2048]{1,0:T(8,128)} custom-call(bf16[8,256,2048]{2,1,0:T(8,128)(2,1)} %bitcast.199), custom_call_target="tpu_custom_call" | custom-call | bytes 120000000 | tf_op jit(solution)/shard_map/scatter_square/pallas_call | solution.py:512
  (233 shorter events, 218.4 us)
Async XLA Ops:
  8.6 14.4 %all-to-all-start = ((bf16[32,1,128]{2,1,0:T(2,128)(2,1)}), bf16[32,1,128]{2,1,0:T(2,128)(2,1)S(1)}, u32[]{:S(2)}, u32[]{:S(2)}) async-start(bf16[32,1,128]{2,1,0:T(2,128)(2,1)} %broadcast_in_dim.91), calls=%async_computation | async-start | bytes 32768 | tf_op jit(solution)/shard_map/all_to_all | solution.py:775
  15.9 425.8 %all-gather.3.cloned.1.call-start = ((), (), s32[]{:S(2)}) async-start(), calls=%async_computation.12 | async-start | bytes 9437184 | tf_op jit(solution)/shard_map/all_gather | solution.py:839
  64.6 8.6 collective-permute-start.1
  73.4 25.6 %collective-permute-start.2 = (bf16[2,64,2048]{2,1,0:T(8,128)(2,1)S(1)}, bf16[2,64,2048]{2,1,0:T(8,128)(2,1)S(1)}, u32[]{:S(2)}, u32[]{:S(2)}) collective-permute-start(bf16[2,64,2048]{2,1,0:T(8,128)(2,1)S(1)} %pad_maximum_fusion.10), channel_id=1, source_target_pairs={{0,2},{2,0},{1,3},{3,1},{4,6},{6,4},{5,7},{7,5},{8,10},{10,8},{9,1... | collective-permute-start | bytes 1572872 | tf_op jit(solution)/shard_map/ppermute | solution.py:541
  129.7 21.3 %all-to-all-start.3 = ((bf16[8,64,1024]{2,1,0:T(8,128)(2,1)}), bf16[8,64,1024]{2,1,0:T(8,128)(2,1)}, u32[]{:S(2)}, u32[]{:S(2)}) async-start(bf16[8,64,1024]{2,1,0:T(8,128)(2,1)} %get-tuple-element.37), calls=%async_computation.3 | async-start | bytes 2097152 | tf_op jit(solution)/shard_map/all_to_all | solution.py:537
  152.4 137.7 %all-to-all-start.1 = ((bf16[32,64,384]{2,1,0:T(8,128)(2,1)}), bf16[32,64,384]{2,1,0:T(8,128)(2,1)}, u32[]{:S(2)}, u32[]{:S(2)}) async-start(bf16[32,64,384]{2,1,0:T(8,128)(2,1)} %bitcast.12), calls=%async_computation.1 | async-start | bytes 3145728 | tf_op jit(solution)/shard_map/all_to_all | solution.py:791
  157.8 127.6 %collective-permute-start.7 = (bf16[256,2048]{1,0:T(8,128)(2,1)S(1)}, bf16[256,2048]{1,0:T(8,128)(2,1)}, u32[]{:S(2)}, u32[]{:S(2)}) collective-permute-start(bf16[256,2048]{1,0:T(8,128)(2,1)S(1)} %copy-done.27), channel_id=1, source_target_pairs={{0,2},{2,0},{1,3},{3,1},{4,6},{6,4},{5,7},{7,5},{8,10},{10,8},{9,1... | collective-permute-start | bytes 3145736 | tf_op jit(solution)/shard_map/ppermute | solution.py:541
  171.3 147.8 %collective-permute-start.5 = (bf16[512,1024]{1,0:T(8,128)(2,1)S(1)}, bf16[512,1024]{1,0:T(8,128)(2,1)}, u32[]{:S(2)}, u32[]{:S(2)}) collective-permute-start(bf16[512,1024]{1,0:T(8,128)(2,1)S(1)} %bitcast.210), channel_id=1, source_target_pairs={{0,2},{2,0},{1,3},{3,1},{4,6},{6,4},{5,7},{7,5},{8,10},{10,8},{9,1... | collective-permute-start | bytes 3145736 | tf_op jit(solution)/shard_map/ppermute | solution.py:541
  171.5 170.1 %collective-permute-start.3 = (bf16[512,1024]{1,0:T(8,128)(2,1)}, bf16[512,1024]{1,0:T(8,128)(2,1)}, u32[]{:S(2)}, u32[]{:S(2)}) collective-permute-start(bf16[512,1024]{1,0:T(8,128)(2,1)} %bitcast.23), channel_id=1, source_target_pairs={{0,2},{2,0},{1,3},{3,1},{4,6},{6,4},{5,7},{7,5},{8,10},{10,8},{9,1... | collective-permute-start | bytes 3145736 | tf_op jit(solution)/shard_map/ppermute | solution.py:541
  288.6 107.3 %collective-permute-start.8 = (bf16[2,256,2048]{2,1,0:T(8,128)(2,1)}, bf16[2,256,2048]{2,1,0:T(8,128)(2,1)}, u32[]{:S(2)}, u32[]{:S(2)}) collective-permute-start(bf16[2,256,2048]{2,1,0:T(8,128)(2,1)} %pad_maximum_fusion.5), channel_id=1, source_target_pairs={{0,16},{16,0},{1,17},{17,1},{2,18},{18,2},{3,19},{19,3},{4,20},{20... | collective-permute-start | bytes 6291464 | tf_op jit(solution)/shard_map/ppermute | solution.py:541
  290.0 51.5 %copy-start.19 = (bf16[8,64,1024]{2,1,0:T(8,128)(2,1)S(1)}, bf16[8,64,1024]{2,1,0:T(8,128)(2,1)}, u32[]{:S(2)}) copy-start(bf16[8,64,1024]{2,1,0:T(8,128)(2,1)} %copy-done.18) | copy-start | bytes 3145732
  302.8 49.4 %collective-permute-start = (bf16[2048,128]{1,0:T(8,128)(2,1)S(1)}, bf16[2048,128]{1,0:T(8,128)(2,1)S(1)}, u32[]{:S(2)}, u32[]{:S(2)}) collective-permute-start(bf16[2048,128]{1,0:T(8,128)(2,1)S(1)} %slice.35), channel_id=1, source_target_pairs={{0,2},{2,0},{1,3},{3,1},{4,6},{6,4},{5,7},{7,5},{8,10},{10,8},{9,1... | collective-permute-start | bytes 1572872 | tf_op jit(solution)/shard_map/ppermute | solution.py:541
  345.5 54.7 %collective-permute-start.4 = (bf16[2,512,1024]{2,1,0:T(8,128)(2,1)}, bf16[2,512,1024]{2,1,0:T(8,128)(2,1)}, u32[]{:S(2)}, u32[]{:S(2)}) collective-permute-start(bf16[2,512,1024]{2,1,0:T(8,128)(2,1)} %pad_maximum_fusion.3), channel_id=1, source_target_pairs={{0,16},{16,0},{1,17},{17,1},{2,18},{18,2},{3,19},{19,3},{4,20},{20... | collective-permute-start | bytes 6291464 | tf_op jit(solution)/shard_map/ppermute | solution.py:541
  348.5 89.0 %collective-permute-start.6 = (bf16[2,512,1024]{2,1,0:T(8,128)(2,1)}, bf16[2,512,1024]{2,1,0:T(8,128)(2,1)}, u32[]{:S(2)}, u32[]{:S(2)}) collective-permute-start(bf16[2,512,1024]{2,1,0:T(8,128)(2,1)} %pad_maximum_fusion.4), channel_id=1, source_target_pairs={{0,16},{16,0},{1,17},{17,1},{2,18},{18,2},{3,19},{19,3},{4,20},{20... | collective-permute-start | bytes 6291464 | tf_op jit(solution)/shard_map/ppermute | solution.py:541
  391.6 50.1 %all-to-all-start.2 = ((bf16[8,256,256]{2,1,0:T(8,128)(2,1)}), bf16[8,256,256]{2,1,0:T(8,128)(2,1)}, u32[]{:S(2)}, u32[]{:S(2)}) async-start(bf16[8,256,256]{2,1,0:T(8,128)(2,1)} %bitcast.205), calls=%async_computation.2 | async-start | bytes 2097152 | tf_op jit(solution)/shard_map/all_to_all | solution.py:537
  395.9 574.0 %all-gather.5.cloned.1.call-start = ((), (), s32[]{:S(2)}) async-start(), calls=%async_computation.13 | async-start | bytes 9437184 | tf_op jit(solution)/shard_map/all_gather | solution.py:902
  761.2 48.8 %collective-permute-start.10 = (bf16[2,512,1024]{2,1,0:T(8,128)(2,1)S(1)}, bf16[2,512,1024]{2,1,0:T(8,128)(2,1)}, u32[]{:S(2)}, u32[]{:S(2)}) collective-permute-start(bf16[2,512,1024]{2,1,0:T(8,128)(2,1)S(1)} %fusion.19), channel_id=1, source_target_pairs={{0,16},{16,0},{1,17},{17,1},{2,18},{18,2},{3,19},{19,3},{4,20},{20... | collective-permute-start | bytes 6291464 | tf_op jit(solution)/shard_map/ppermute | solution.py:541
  764.7 51.3 %all-to-all-start.5 = ((f32[32,1,1]{2,1,0:T(1,128)}), f32[32,1,1]{2,1,0:T(1,128)S(1)}, u32[]{:S(2)}, u32[]{:S(2)}) async-start(f32[32,1,1]{2,1,0:T(1,128)} %broadcast_in_dim.98), calls=%async_computation.5 | async-start | bytes 32768 | tf_op jit(solution)/shard_map/all_to_all | solution.py:574
  782.0 72.4 %collective-permute-start.12 = (bf16[2,512,1024]{2,1,0:T(8,128)(2,1)}, bf16[2,512,1024]{2,1,0:T(8,128)(2,1)}, u32[]{:S(2)}, u32[]{:S(2)}) collective-permute-start(bf16[2,512,1024]{2,1,0:T(8,128)(2,1)} %fusion.20), channel_id=1, source_target_pairs={{0,16},{16,0},{1,17},{17,1},{2,18},{18,2},{3,19},{19,3},{4,20},{20... | collective-permute-start | bytes 6291464 | tf_op jit(solution)/shard_map/ppermute | solution.py:541
  814.5 47.4 %collective-permute-start.11 = (bf16[512,1024]{1,0:T(8,128)(2,1)S(1)}, bf16[512,1024]{1,0:T(8,128)(2,1)S(1)}, u32[]{:S(2)}, u32[]{:S(2)}) collective-permute-start(bf16[512,1024]{1,0:T(8,128)(2,1)S(1)} %fusion.27), channel_id=1, source_target_pairs={{0,2},{2,0},{1,3},{3,1},{4,6},{6,4},{5,7},{7,5},{8,10},{10,8},{9,1... | collective-permute-start | bytes 3145736 | tf_op jit(solution)/shard_map/ppermute | solution.py:541
  816.0 47.3 %all-to-all-start.7 = ((bf16[8,256,256]{2,1,0:T(8,128)(2,1)}), bf16[8,256,256]{2,1,0:T(8,128)(2,1)}, u32[]{:S(2)}, u32[]{:S(2)}) async-start(bf16[8,256,256]{2,1,0:T(8,128)(2,1)} %get-tuple-element.41), calls=%async_computation.7 | async-start | bytes 2097152 | tf_op jit(solution)/shard_map/all_to_all | solution.py:537
  860.3 83.8 %collective-permute-start.13 = (bf16[512,1024]{1,0:T(8,128)(2,1)}, bf16[512,1024]{1,0:T(8,128)(2,1)S(1)}, u32[]{:S(2)}, u32[]{:S(2)}) collective-permute-start(bf16[512,1024]{1,0:T(8,128)(2,1)} %fusion.28), channel_id=1, source_target_pairs={{0,2},{2,0},{1,3},{3,1},{4,6},{6,4},{5,7},{7,5},{8,10},{10,8},{9,1... | collective-permute-start | bytes 3145736 | tf_op jit(solution)/shard_map/ppermute | solution.py:541
  863.3 82.1 %all-to-all-start.9 = ((bf16[8,64,1024]{2,1,0:T(8,128)(2,1)}), bf16[8,64,1024]{2,1,0:T(8,128)(2,1)S(1)}, u32[]{:S(2)}, u32[]{:S(2)}) async-start(bf16[8,64,1024]{2,1,0:T(8,128)(2,1)} %bitcast.70), calls=%async_computation.10 | async-start | bytes 2097152 | tf_op jit(solution)/shard_map/all_to_all | solution.py:537
  925.6 37.1 %collective-permute-start.9 = (bf16[2048,128]{1,0:T(8,128)(2,1)S(1)}, bf16[2048,128]{1,0:T(8,128)(2,1)}, u32[]{:S(2)}, u32[]{:S(2)}) collective-permute-start(bf16[2048,128]{1,0:T(8,128)(2,1)S(1)} %bitcast.229), channel_id=1, source_target_pairs={{0,2},{2,0},{1,3},{3,1},{4,6},{6,4},{5,7},{7,5},{8,10},{10,8},{9,1... | collective-permute-start | bytes 1572872 | tf_op jit(solution)/shard_map/ppermute | solution.py:541
  942.6 50.7 %collective-permute-start.14 = (bf16[2,256,2048]{2,1,0:T(8,128)(2,1)}, bf16[2,256,2048]{2,1,0:T(8,128)(2,1)}, u32[]{:S(2)}, u32[]{:S(2)}) collective-permute-start(bf16[2,256,2048]{2,1,0:T(8,128)(2,1)} %fusion.21), channel_id=1, source_target_pairs={{0,16},{16,0},{1,17},{17,1},{2,18},{18,2},{3,19},{19,3},{4,20},{20... | collective-permute-start | bytes 6291464 | tf_op jit(solution)/shard_map/ppermute | solution.py:541
  945.4 41.4 %all-to-all-start.10 = ((bf16[8,64,1024]{2,1,0:T(8,128)(2,1)}), bf16[8,64,1024]{2,1,0:T(8,128)(2,1)}, u32[]{:S(2)}, u32[]{:S(2)}) async-start(bf16[8,64,1024]{2,1,0:T(8,128)(2,1)} %bitcast.76), calls=%async_computation.11 | async-start | bytes 2097152 | tf_op jit(solution)/shard_map/all_to_all | solution.py:537
  950.0 174.2 %reduce-scatter.2.cloned.1.call-start = ((), (), s32[]{:S(2)}) async-start(), calls=%async_computation.14 | async-start | bytes 2359296 | tf_op jit(solution)/shard_map/reduce_scatter | solution.py:907
  986.8 134.6 %all-to-all-start.8 = ((bf16[32,64,384]{2,1,0:T(8,128)(2,1)}), bf16[32,64,384]{2,1,0:T(8,128)(2,1)S(1)}, u32[]{:S(2)}, u32[]{:S(2)}) async-start(bf16[32,64,384]{2,1,0:T(8,128)(2,1)} %bitcast.222), calls=%async_computation.8 | async-start | bytes 3145728 | tf_op jit(solution)/shard_map/all_to_all | solution.py:897
  997.3 115.1 %collective-permute-start.15 = (bf16[256,2048]{1,0:T(8,128)(2,1)S(1)}, bf16[256,2048]{1,0:T(8,128)(2,1)}, u32[]{:S(2)}, u32[]{:S(2)}) collective-permute-start(bf16[256,2048]{1,0:T(8,128)(2,1)S(1)} %fusion.29), channel_id=1, source_target_pairs={{0,2},{2,0},{1,3},{3,1},{4,6},{6,4},{5,7},{7,5},{8,10},{10,8},{9,1... | collective-permute-start | bytes 3145736 | tf_op jit(solution)/shard_map/ppermute | solution.py:541
  1008.0 98.6 %copy-start = (bf16[1,256,2048]{2,1,0:T(8,128)(2,1)S(1)}, bf16[1,256,2048]{2,1,0:T(8,128)(2,1)}, u32[]{:S(2)}) copy-start(bf16[1,256,2048]{2,1,0:T(8,128)(2,1)} %param.12) | copy-start | bytes 3145732
  1008.0 98.6 %copy-start.40 = (f32[2048]{0:T(1024)S(1)}, f32[2048]{0:T(1024)}, u32[]{:S(2)}) copy-start(f32[2048]{0:T(1024)} %copy-done.39) | copy-start | bytes 24580
  1008.0 98.6 %copy-start.42 = (f32[256]{0:T(256)S(1)}, f32[256]{0:T(256)}, u32[]{:S(2)}) copy-start(f32[256]{0:T(256)} %copy-done.41) | copy-start | bytes 3076
  (42 other events, 779.6 us)
Sparse Core Ops, SparseCore 0:
  100.3 86.1 all-gather.2
  733.0 47.1 all-gather.4
  977.4 93.7 reduce-scatter.1

commit v2 on v1

--- a/solution.py
+++ b/solution.py
@@ -1,7 +1,9 @@
 import functools
+import math
 
 import jax
 import jax.numpy as jnp
+import numpy as np
 from jax import lax
 from jax.experimental import pallas as pl
 from jax.experimental.pallas import tpu as pltpu
@@ -28,8 +30,23 @@
     return lax.dot_general(a, b, (dims, ((), ())), preferred_element_type=F32)
 
 
-def proj_kernel(rows_ref, weight_ref, cos_ref, sina_ref, sinb_ref, out_ref):
-    made = dot32(rows_ref[...], weight_ref[...])
+def rope_tables(seq_len):
+    half = HEAD_SIZE // 2
+    frequency = ROPE_BASE ** (-(np.arange(half) * 2.0) / HEAD_SIZE)
+    angles = np.arange(seq_len).astype(np.float32)[:, None] * frequency.astype(np.float32)[None, :]
+    cosine, sine = np.cos(angles.astype(np.float64)), np.sin(angles.astype(np.float64))
+    none = np.zeros_like(cosine)
+    rows = ([cosine] * 4, [-sine, none] * 2, [none, sine] * 2)
+    return tuple(np.concatenate(row, axis=1).astype(np.float32) for row in rows)
+
+
+def table_spec(tok):
+    return pl.BlockSpec((tok, 128), lambda i, hi: ((i // 2 * 2 + hi[0]) * 2 + i % 2, 0))
+
+
+def proj_kernel(hi_ref, rows_ref, gain_ref, weight_ref, cos_ref, sina_ref, sinb_ref, normed_ref, q_ref, kv_ref):
+    normed_ref[...] = (norm_parts(rows_ref[...].astype(F32))[0] * gain_ref[...]).astype(BF16)
+    made = dot32(normed_ref[...], weight_ref[...])
     cosine, sina, sinb = cos_ref[...], sina_ref[...], sinb_ref[...]
     low = lanes_low(cosine.shape)
     half = HEAD_SIZE // 2
@@ -38,38 +55,42 @@
         up, down = pltpu.roll(u, 128 - half, 1), pltpu.roll(u, half, 1)
         turned = u * cosine + up * sina + down * sinb
         if part < 2:
-            out_ref[:, 128 * part : 128 * part + 128] = (
+            q_ref[:, 128 * part : 128 * part + 128] = (
                 turned.astype(BF16).astype(F32) * ATTN_SCALE
             ).astype(BF16)
         else:
-            out_ref[:, 256:384] = jnp.where(low, turned, u).astype(BF16)
-
-
-def project(rows, weight, tables, tile):
+            kv_ref[...] = jnp.where(low, turned, u).astype(BF16)
+
+
+def project(hi, rows, gain, weight, tables, tile):
     count, depth = rows.shape
     wide = weight.shape[1]
-    table_spec = pl.BlockSpec((tile, 128), lambda i: (i, 0))
+    by_rows = lambda cols: pl.BlockSpec((tile, cols), lambda i, hi: (i, 0))
+    whole = lambda *shape: pl.BlockSpec(shape, lambda i, hi: (0, 0))
     return pl.pallas_call(
         proj_kernel,
-        grid=(count // tile,),
-        in_specs=[
-            pl.BlockSpec((tile, depth), lambda i: (i, 0)),
-            pl.BlockSpec((depth, wide), lambda i: (0, 0)),
-            table_spec,
-            table_spec,
-            table_spec,
-        ],
-        out_specs=pl.BlockSpec((tile, wide), lambda i: (i, 0)),
-        out_shape=jax.ShapeDtypeStruct((count, wide), BF16),
+        grid_spec=pltpu.PrefetchScalarGridSpec(
+            num_scalar_prefetch=1,
+            grid=(count // tile,),
+            in_specs=[by_rows(depth), whole(1, depth), whole(depth, wide)] + [table_spec(tile)] * 3,
+            out_specs=[by_rows(depth), by_rows(256), by_rows(128)],
+        ),
+        out_shape=[
+            jax.ShapeDtypeStruct((count, depth), BF16),
+            jax.ShapeDtypeStruct((count, 256), BF16),
+            jax.ShapeDtypeStruct((count, 128), BF16),
+        ],
         compiler_params=pltpu.CompilerParams(vmem_limit_bytes=VMEM_LIMIT),
         cost_estimate=pl.CostEstimate(
             flops=2 * count * depth * wide, bytes_accessed=4 * count * depth, transcendentals=0
         ),
         name="project",
-    )(rows, weight, *tables)
-
-
-def back_rope_kernel(dq_ref, own_ref, other_ref, cos_ref, sina_ref, sinb_ref, out_ref):
+    )(hi, rows, gain, weight, *tables)
+
+
+def back_rope_kernel(
+    hi_ref, dq_ref, own_ref, other_ref, cos_ref, sina_ref, sinb_ref, first_ref, out_ref
+):
     cosine, sina, sinb = cos_ref[...], sina_ref[...], sinb_ref[...]
     low = lanes_low(cosine.shape)
     half = HEAD_SIZE // 2
@@ -82,18 +103,24 @@
         out_ref[:, 128 * part : 128 * part + 128] = turned.astype(BF16)
 
 
-def back_rope(dq, own, other, tables, tile):
+def back_rope(hi, dq, own, other, tables, first, tile):
     count = dq.shape[0]
-    rows = lambda wide: pl.BlockSpec((tile, wide), lambda i: (i, 0))
+    by_rows = lambda wide: pl.BlockSpec((tile, wide), lambda i, hi: (i, 0))
     return pl.pallas_call(
         back_rope_kernel,
-        grid=(count // tile,),
-        in_specs=[rows(256)] + [rows(128)] * 5,
-        out_specs=rows(384),
+        grid_spec=pltpu.PrefetchScalarGridSpec(
+            num_scalar_prefetch=1,
+            grid=(count // tile,),
+            in_specs=[by_rows(256), by_rows(128), by_rows(128)]
+            + [table_spec(tile)] * 3
+            + [pl.BlockSpec(memory_space=pl.ANY)],
+            out_specs=by_rows(384),
+        ),
         out_shape=jax.ShapeDtypeStruct((count, 384), BF16),
         compiler_params=pltpu.CompilerParams(vmem_limit_bytes=VMEM_LIMIT),
+        cost_estimate=pl.CostEstimate(flops=0, bytes_accessed=20_000_000, transcendentals=0),
         name="back_rope",
-    )(dq, own, other, *tables)
+    )(hi, dq, own, other, *tables, first)
 
 
 def lanes_low(shape):
@@ -118,9 +145,9 @@
     )
 
 
-def attend_kernel(scalar_ref, qkv_ref, other_ref, out_ref, log_ref, keys, values, peak, sums):
+def attend_kernel(scalar_ref, q_ref, kv_ref, other_ref, out_ref, log_ref, keys, values, peak, sums):
     b = pl.program_id(0)
-    blocks, unit, _ = qkv_ref.shape
+    blocks, unit, _ = q_ref.shape
     units = 2 * blocks
     length, hi = scalar_ref[0], scalar_ref[1]
     n = 2 * b + hi
@@ -129,7 +156,7 @@
     def _():
         def spread(c, carry):
             for j, kv in (
-                (2 * c + hi, qkv_ref[c, :, 256:384]),
+                (2 * c + hi, kv_ref[c]),
                 (2 * c + 1 - hi, other_ref[c]),
             ):
                 keys[0, j], keys[1, j] = both_keys(kv)
@@ -146,7 +173,7 @@
 
     def step(j, masked):
         for h in range(4):
-            query = qkv_ref[b, :, 128 * (h // 2) : 128 * (h // 2) + 128]
+            query = q_ref[b, :, 128 * (h // 2) : 128 * (h // 2) + 128]
             scores = dot32(keys[h % 2, j], query, ((1,), (1,)))
             if masked:
                 row = j * unit + lax.broadcasted_iota(jnp.int32, scores.shape, 0)
@@ -182,14 +209,14 @@
         ).astype(BF16)
 
 
-def attend(scalars, qkv, other):
-    blocks, unit, _ = qkv.shape
+def attend(scalars, q, kv, other):
+    blocks, unit, _ = q.shape
     units = 2 * blocks
     whole = lambda a: pl.BlockSpec(a.shape, lambda i: (0,) * a.ndim)
     return pl.pallas_call(
         attend_kernel,
         grid=(blocks,),
-        in_specs=[pl.BlockSpec(memory_space=pltpu.SMEM), whole(qkv), whole(other)],
+        in_specs=[pl.BlockSpec(memory_space=pltpu.SMEM), whole(q), whole(kv), whole(other)],
         out_specs=[
             pl.BlockSpec((1, unit, 256), lambda i: (i, 0, 0)),
             pl.BlockSpec((1, 8, unit), lambda i: (i, 0, 0)),
@@ -209,14 +236,27 @@
             flops=40_000_000_000, bytes_accessed=8_000_000, transcendentals=20_000_000
         ),
         name="attend",
-    )(scalars, qkv, other)
+    )(scalars, q, kv, other)
 
 
 def attend_back_kernel(
-    scalar_ref, qkv_ref, other_ref, dout_ref, out_ref, log_ref, dq_ref, dkv_ref, delta, dq, dk, dv
+    scalar_ref,
+    q_ref,
+    kv_ref,
+    other_ref,
+    dout_ref,
+    out_ref,
+    log_ref,
+    first_ref,
+    dq_ref,
+    dkv_ref,
+    delta,
+    dq,
+    dk,
+    dv,
 ):
     j = pl.program_id(0)
-    blocks, unit, _ = qkv_ref.shape
+    blocks, unit, _ = q_ref.shape
     units = 2 * blocks
     length, hi = scalar_ref[0], scalar_ref[1]
 
@@ -244,7 +284,7 @@
         lax.fori_loop(0, blocks, dots, 0)
 
     foreign = jnp.where(j % 2 == hi, 0, 1)
-    kv = jnp.where(foreign == 0, qkv_ref[j // 2, :, 256:384], other_ref[j // 2])
+    kv = jnp.where(foreign == 0, kv_ref[j // 2], other_ref[j // 2])
     keys, values = both_keys(kv), both_values(kv)
     dk[...] = jnp.zeros_like(dk)
     dv[...] = jnp.zeros_like(dv)
@@ -253,7 +293,7 @@
         n = 2 * b + hi
         for pair in range(2):
             lanes = slice(128 * pair, 128 * pair + 128)
-            query = qkv_ref[b, :, lanes]
+            query = q_ref[b, :, lanes]
             dout = dout_ref[b, :, lanes]
             dq_part = None
             for side in range(2):
@@ -301,8 +341,8 @@
         lax.fori_loop(0, blocks, store, 0)
 
 
-def attend_back(scalars, qkv, other, dout, out, log):
-    blocks, unit, _ = qkv.shape
+def attend_back(scalars, q, kv, other, dout, out, log, first):
+    blocks, unit, _ = q.shape
     units = 2 * blocks
     whole = lambda a: pl.BlockSpec(a.shape, lambda i: (0,) * a.ndim)
     dq_shape = jax.ShapeDtypeStruct((blocks, unit, 256), BF16)
@@ -312,11 +352,13 @@
         grid=(units,),
         in_specs=[
             pl.BlockSpec(memory_space=pltpu.SMEM),
-            whole(qkv),
+            whole(q),
+            whole(kv),
             whole(other),
             whole(dout),
             whole(out),
             whole(log),
+            pl.BlockSpec(memory_space=pl.ANY),
         ],
         out_specs=[whole(dq_shape), whole(dkv_shape)],
         out_shape=[dq_shape, dkv_shape],
@@ -331,7 +373,7 @@
             flops=60_000_000_000, bytes_accessed=10_000_000, transcendentals=20_000_000
         ),
         name="attend_back",
-    )(scalars, qkv, other, dout, out, log)
+    )(scalars, q, kv, other, dout, out, log, first)
 
 
 PIECES = 4
@@ -351,31 +393,89 @@
     pl.semaphore_wait(barrier, len(ids))
 
 
-def gather_kernel(rows_ref, out_ref, send, recv, local):
+def remote(source, target, send, recv, to):
+    copy = pltpu.make_async_remote_copy(
+        src_ref=source,
+        dst_ref=target,
+        send_sem=send,
+        recv_sem=recv,
+        device_id=to,
+        device_id_type=MESH_ID,
+    )
+    copy.start()
+    return copy
+
+
+def local_copy(source, target, sem):
+    copy = pltpu.make_async_copy(source, target, sem)
+    copy.start()
+    return copy
+
+
+class Carried:
+    def __init__(self, source, target, held, sem):
+        self.held, self.target, self.sem = held, target, sem
+        self.copy = local_copy(source, held, sem)
+
+    def turn(self):
+        self.copy.wait()
+        self.copy = local_copy(self.held, self.target, self.sem)
+
+    def wait(self):
+        self.copy.wait()
+
+
+def finish(copies):
+    for copy in copies:
+        if isinstance(copy, Carried):
+            copy.turn()
+    for copy in copies:
+        copy.wait()
+
+
+def square_peers():
+    blk, lo = lax.axis_index("blk"), lax.axis_index("lo")
+    mine = blk * 2 + lo
+    others = [lax.rem(mine + d, 8) for d in range(1, 8)]
+    return mine, others, [{"blk": o // 2, "lo": lax.rem(o, 2)} for o in others]
+
+
+def other_hi():
+    return {"hi": 1 - lax.axis_index("hi")}
+
+
+def dp_peers():
+    dp, dp_n = lax.axis_index("dp"), lax.axis_size("dp")
+    return [{"dp": lax.rem(dp + d, dp_n)} for d in range(1, dp_n)]
+
+
+def every_peer():
+    sizes = [lax.axis_size(a) for a in ALL]
+    places = [lax.axis_index(a) for a in ALL]
+    found = []
+    for k in range(1, math.prod(sizes)):
+        to, rest = {}, k
+        for a, size, place in reversed(list(zip(ALL, sizes, places))):
+            to[a] = lax.rem(place + rest % size, size)
+            rest //= size
+        found.append(to)
+    return found
+
+
+def gather_begin(rows_ref, out_ref, send, recv, local, held):
     blk, lo, mate, side = square_places()
     slot = lambda b, l: b * 2 + l
     mine = slot(blk, lo)
     to_mate, to_side, to_next = {"blk": mate}, {"blk": side}, {"lo": 1 - lo}
-    greet([to_mate, to_side, to_next])
     step = rows_ref.shape[0] // PIECES
 
     def push(source, place, piece, kind, to):
-        rows = pl.ds(piece * step, step)
-        copy = pltpu.make_async_remote_copy(
-            src_ref=source,
-            dst_ref=out_ref.at[place, rows],
-            send_sem=send.at[kind, piece],
-            recv_sem=recv.at[kind, piece],
-            device_id=to,
-            device_id_type=MESH_ID,
-        )
-        copy.start()
-        return copy
-
-    own = pltpu.make_async_copy(rows_ref, out_ref.at[mine], local)
-    own.start()
+        target = out_ref.at[place, pl.ds(piece * step, step)]
+        return remote(source, target, send.at[kind, piece], recv.at[kind, piece], to)
+
+    own = Carried(rows_ref, out_ref.at[mine], held, local)
     piece_of = lambda p: rows_ref.at[pl.ds(p * step, step)]
-    held = lambda place, p: out_ref.at[place, pl.ds(p * step, step)]
+    came = lambda place, p: out_ref.at[place, pl.ds(p * step, step)]
     side_order, next_order = (2, 3, 0, 1), (0, 1, 2, 3)
     by_side, by_next, by_mate, across = {}, {}, [], {}
     for k in range(PIECES):
@@ -384,83 +484,407 @@
         by_next[q] = push(piece_of(q), mine, q, 1, to_next)
     for p in range(PIECES):
         by_mate.append(push(piece_of(p), mine, p, 3, to_mate))
-    from_side, from_next, from_across = slot(side, lo), slot(blk, 1 - lo), slot(side, 1 - lo)
-    for k in range(PIECES):
-        p, q = side_order[k], next_order[k]
-        by_side[p].wait_recv()
-        if p >= 2:
-            across[p] = push(held(from_side, p), from_side, p, 2, to_next)
-        by_mate.append(push(held(from_side, p), from_side, p, 4, to_mate))
-        by_next[q].wait_recv()
-        if q < 2:
-            across[q] = push(held(from_next, q), from_next, q, 2, to_side)
-        by_mate.append(push(held(from_next, q), from_next, q, 5, to_mate))
-    for p in (0, 2, 1, 3):
-        across[p].wait_recv()
-        by_mate.append(push(held(from_across, p), from_across, p, 6, to_mate))
-    for copy in by_mate:
-        copy.wait()
-    for copies in (by_side, by_next, across):
-        for copy in copies.values():
-            copy.wait_send()
-    own.wait()
+
+    def end(between=lambda k: None):
+        own.turn()
+        from_side, from_next, from_across = slot(side, lo), slot(blk, 1 - lo), slot(side, 1 - lo)
+        for k in range(PIECES):
+            p, q = side_order[k], next_order[k]
+            by_side[p].wait_recv()
+            if p >= 2:
+                across[p] = push(came(from_side, p), from_side, p, 2, to_next)
+            by_mate.append(push(came(from_side, p), from_side, p, 4, to_mate))
+            by_next[q].wait_recv()
+            if q < 2:
+                across[q] = push(came(from_next, q), from_next, q, 2, to_side)
+            by_mate.append(push(came(from_next, q), from_next, q, 5, to_mate))
+            between(k)
+        for p in (0, 2, 1, 3):
+            across[p].wait_recv()
+            by_mate.append(push(came(from_across, p), from_across, p, 6, to_mate))
+            between(PIECES + p)
+        for copy in by_mate:
+            copy.wait()
+        for copies in (by_side, by_next, across):
+            for copy in copies.values():
+                copy.wait_send()
+        own.wait()
+
+    return end
+
+
+def gather_scratch(tok, width):
+    return [
+        pltpu.SemaphoreType.DMA((7, PIECES)),
+        pltpu.SemaphoreType.DMA((7, PIECES)),
+        pltpu.SemaphoreType.DMA,
+        pltpu.VMEM((tok, width), BF16),
+    ]
+
+
+def sems(count):
+    return [pltpu.SemaphoreType.DMA((count,))] * 2
+
+
+def swap_scratch(part):
+    return sems(7) + [pltpu.SemaphoreType.DMA, pltpu.VMEM(part, BF16)]
+
+
+def square_greeting():
+    blk, lo, mate, side = square_places()
+    return [{"blk": mate}, {"blk": side}, {"lo": 1 - lo}]
+
+
+def gather_kernel(rows_ref, out_ref, send, recv, local, held):
+    greet(square_greeting())
+    gather_begin(rows_ref, out_ref, send, recv, local, held)()
+
+
+def comm_call(kernel, number, arrays, shapes, scratch, name):
+    anywhere = pl.BlockSpec(memory_space=pl.ANY)
+    return pl.pallas_call(
+        kernel,
+        in_specs=[anywhere] * len(arrays),
+        out_specs=[anywhere] * len(shapes),
+        out_shape=[jax.ShapeDtypeStruct(shape, dtype) for shape, dtype in shapes],
+        scratch_shapes=scratch,
+        compiler_params=pltpu.CompilerParams(
+            collective_id=number, has_side_effects=True, vmem_limit_bytes=VMEM_LIMIT
+        ),
+        cost_estimate=pl.CostEstimate(flops=0, bytes_accessed=120_000_000, transcendentals=0),
+        name=name,
+    )(*arrays)
 
 
 def gather_square(rows, number):
     tok, width = rows.shape
-    return pl.pallas_call(
+    (out,) = comm_call(
         gather_kernel,
-        in_specs=[pl.BlockSpec(memory_space=pl.ANY)],
-        out_specs=pl.BlockSpec(memory_space=pl.ANY),
-        out_shape=jax.ShapeDtypeStruct((8, tok, width), rows.dtype),
-        scratch_shapes=[
-            pltpu.SemaphoreType.DMA((7, PIECES)),
-            pltpu.SemaphoreType.DMA((7, PIECES)),
-            pltpu.SemaphoreType.DMA,
-        ],
-        compiler_params=pltpu.CompilerParams(collective_id=number, has_side_effects=True),
-        cost_estimate=pl.CostEstimate(flops=0, bytes_accessed=120_000_000, transcendentals=0),
-        name="gather_square",
-    )(rows).reshape(8 * tok, width)
-
-
-def scatter_kernel(
-    parts_ref, out_ref, mine, mates, made, got_across, got_side, got_next, send, recv, local
+        number,
+        [rows],
+        [((8, tok, width), rows.dtype)],
+        gather_scratch(tok, width),
+        "gather_square",
+    )
+    return out.reshape(8 * tok, width)
+
+
+def swap_begin(parts_ref, out_ref, send, recv, local, held):
+    mine, others, ids = square_peers()
+    own = Carried(parts_ref.at[mine], out_ref.at[mine], held, local)
+    copies = [
+        remote(parts_ref.at[o], out_ref.at[mine], send.at[d], recv.at[d], to)
+        for d, (o, to) in enumerate(zip(others, ids))
+    ]
+    return copies + [own]
+
+
+def dp_begin(pieces, out_ref, send, recv, local, held):
+    dp = lax.axis_index("dp")
+    copies = []
+    for k, (place, ref) in enumerate(pieces):
+        copies.append(Carried(ref, out_ref.at[dp, place], held.at[k], local.at[k]))
+        for d, to in enumerate(dp_peers()):
+            n = 2 * d + k
+            copies.append(remote(ref, out_ref.at[dp, place], send.at[n], recv.at[n], to))
+    return copies
+
+
+def device_place():
+    mine = 0
+    for a in ALL:
+        mine = mine * lax.axis_size(a) + lax.axis_index(a)
+    return mine
+
+
+def seq_peers():
+    sizes = [lax.axis_size(a) for a in SEQ]
+    places = [lax.axis_index(a) for a in SEQ]
+    found = []
+    for k in range(1, math.prod(sizes)):
+        to, source, digits, rest = {}, 0, [], k
+        for size in reversed(sizes):
+            digits.append(rest % size)
+            rest //= size
+        for a, size, place, digit in zip(SEQ, sizes, places, reversed(digits)):
+            to[a] = lax.rem(place + digit, size)
+            source = source * size + lax.rem(place + size - digit, size)
+        found.append((to, source))
+    return found
+
+
+def seq_place(to):
+    place = 0
+    for a in SEQ:
+        place = place * lax.axis_size(a) + to[a]
+    return place
+
+
+def open_kernel(
+    rows_ref, heads_ref, small_ref, wout_ref, out_ref, weight_ref, smalls_ref, wouts_ref, g_send, g_recv,
+    g_local, g_held, w_send, w_recv, d_send, d_recv, s_send, s_recv, o_send, o_recv, local, w_held, o_held,
 ):
-    blk, lo, mate, side = square_places()
-    slot = lambda b, l: b * 2 + l
-    to_mate, to_side, to_next = {"blk": mate}, {"blk": side}, {"lo": 1 - lo}
-    mate_side = (mate + 2) % 4
-    own_slots = (slot(side, 1 - lo), slot(side, lo), slot(blk, 1 - lo), slot(blk, lo))
-    mate_slots = (slot(mate_side, 1 - lo), slot(mate_side, lo), slot(mate, 1 - lo), slot(mate, lo))
-    step = parts_ref.shape[1] // PIECES
-    loads = []
-    for k in range(4):
-        copy = pltpu.make_async_copy(parts_ref.at[own_slots[k]], mine.at[k], local.at[k])
-        copy.start()
-        loads.append(copy)
-    greet([to_mate, to_side, to_next])
-
-    def push(source, target, kind, piece, to):
+    blk, hi, lo = (lax.axis_index(a) for a in SEQ)
+    mine = device_place()
+    peers = every_peer()
+    greet(peers)
+    copies = [
+        Carried(heads_ref.at[blk * 2 + lo], weight_ref.at[mine], w_held, local.at[0]),
+        local_copy(small_ref, smalls_ref.at[mine], local.at[1]),
+        Carried(wout_ref, wouts_ref.at[hi, lo], o_held, local.at[2]),
+    ]
+    for k, to in enumerate(peers):
+        copies.append(remote(small_ref, smalls_ref.at[mine], s_send.at[k], s_recv.at[k], to))
+    end = gather_begin(rows_ref, out_ref, g_send, g_recv, g_local, g_held)
+    wout = remote(wout_ref, wouts_ref.at[hi, lo], o_send.at[0], o_recv.at[0], other_hi())
+    next_lo = {"lo": 1 - lo}
+    copies.append(remote(wout_ref, wouts_ref.at[hi, lo], o_send.at[1], o_recv.at[1], next_lo))
+    dp, seq = lax.axis_index("dp"), seq_peers()
+    seq_n = len(seq) + 1
+    straight = []
+    for k, (to, source) in enumerate(seq):
+        part = heads_ref.at[to["blk"] * 2 + to["lo"]]
+        straight.append(remote(part, weight_ref.at[mine], w_send.at[k], w_recv.at[k], to))
+
+    def hand_on(part, place, k):
+        for d, to in enumerate(dp_peers()):
+            n = d * seq_n + k
+            copies.append(remote(part, weight_ref.at[place], d_send.at[n], d_recv.at[n], to))
+
+    hand_on(heads_ref.at[blk * 2 + lo], mine, seq_n - 1)
+
+    def pass_on(turn):
+        for k, (to, source) in enumerate(seq):
+            if k * 2 * PIECES // len(seq) == turn:
+                straight[k].wait()
+                place = dp * seq_n + source
+                hand_on(weight_ref.at[place], place, k)
+
+    end(pass_on)
+    wout.wait()
+    there = wouts_ref.at[1 - hi, lo]
+    copies.append(remote(there, there, o_send.at[2], o_recv.at[2], next_lo))
+    finish(copies)
+
+
+def keys_kernel(
+    kv_ref, gate_ref, up_ref, down_ref, other_ref, gates_ref, ups_ref, downs_ref, k_send, k_recv, g_send,
+    g_recv, g_local, g_held, u_send, u_recv, u_local, u_held, d_send, d_recv,
+):
+    greet(square_peers()[2] + [other_hi()] + dp_peers())
+    copies = [remote(kv_ref, other_ref, k_send.at[0], k_recv.at[0], other_hi())]
+    for d, to in enumerate(dp_peers()):
+        copies.append(remote(down_ref, downs_ref.at[d], d_send.at[d], d_recv.at[d], to))
+    copies += swap_begin(gate_ref, gates_ref, g_send, g_recv, g_local, g_held)
+    copies += swap_begin(up_ref, ups_ref, u_send, u_recv, u_local, u_held)
+    finish(copies)
+
+
+def heads_kernel(
+    heads_ref, gate_ref, gate_other_ref, up_ref, mixed_ref, gates_ref, up_other_ref, m_send, m_recv,
+    m_local, m_held, g_send, g_recv, u_send, u_recv, g_local, g_held,
+):
+    hi = lax.axis_index("hi")
+    greet(square_peers()[2] + [other_hi()] + dp_peers())
+    copies = swap_begin(heads_ref, mixed_ref, m_send, m_recv, m_local, m_held)
+    copies.append(remote(up_ref, up_other_ref, u_send.at[0], u_recv.at[0], other_hi()))
+    copies += dp_begin(
+        [(hi, gate_ref), (1 - hi, gate_other_ref)], gates_ref, g_send, g_recv, g_local, g_held
+    )
+    finish(copies)
+
+
+def rows_kernel(
+    rows_ref, up_ref, up_other_ref, down_ref, out_ref, ups_ref, down_other_ref, r_send, r_recv, r_local,
+    r_held, u_send, u_recv, d_send, d_recv, u_local, u_held,
+):
+    hi = lax.axis_index("hi")
+    greet(square_greeting() + [other_hi()] + dp_peers())
+    end = gather_begin(rows_ref, out_ref, r_send, r_recv, r_local, r_held)
+    copies = [remote(down_ref, down_other_ref, d_send.at[0], d_recv.at[0], other_hi())]
+    copies += dp_begin(
+        [(hi, up_ref), (1 - hi, up_other_ref)], ups_ref, u_send, u_recv, u_local, u_held
+    )
+    end()
+    finish(copies)
+
+
+def sum_begin(own_ref, got_ref, place, own, got, sem):
+    return [
+        local_copy(own_ref.at[place], own, sem.at[0]),
+        local_copy(got_ref.at[place], got, sem.at[1]),
+    ]
+
+
+def wait_all(copies):
+    for copy in copies:
+        copy.wait()
+
+
+def douts_kernel(
+    over_dp, parts_ref, gate_ref, gate_got_ref, up_ref, up_got_ref, gate_made_ref, out_ref, gate_away_ref,
+    up_away_ref, gate_kept_ref, send, recv, local, held, own, got, sem, d_send, d_recv,
+):
+    hi = lax.axis_index("hi")
+    loads = [
+        [local_copy(ref.at[1 - hi], own.at[k], sem.at[k, 0]), local_copy(got_ref, got.at[k], sem.at[k, 1])]
+        for k, (ref, got_ref) in enumerate(((gate_ref, gate_got_ref), (up_ref, up_got_ref)))
+    ]
+    loads.append([local_copy(gate_ref.at[hi], own.at[2], sem.at[2, 0])])
+    greet(square_peers()[2] + (dp_peers() if over_dp else []))
+    loads[2] += pair_begin(gate_made_ref, hi, got.at[2], d_send.at[0], d_recv.at[0], over_dp)
+    copies = swap_begin(parts_ref, out_ref, send, recv, local, held)
+    for k, target in enumerate((gate_away_ref, up_away_ref, gate_kept_ref)):
+        wait_all(loads[k])
+        target[...] = (own[k] + got[k].astype(F32)).astype(target.dtype)
+    finish(copies)
+
+
+def dkeys_kernel(
+    over_dp, dkv_ref, gate_ref, gate_got_ref, up_ref, up_made_ref, first_ref, other_ref, gates_ref, up_kept_ref,
+    k_send, k_recv, g_send, g_recv, g_local, g_held, own, got, made, sem, up_own, up_got, d_send, d_recv,
+):
+    hi = lax.axis_index("hi")
+    loads = [local_copy(gate_ref, own, sem.at[0]), local_copy(gate_got_ref, got, sem.at[1])]
+    up_loads = [local_copy(up_ref.at[hi], up_own, sem.at[2])]
+    greet(square_peers()[2] + [other_hi()] + (dp_peers() if over_dp else []))
+    copies = [remote(dkv_ref.at[1], other_ref, k_send.at[0], k_recv.at[0], other_hi())]
+    up_loads += pair_begin(up_made_ref, hi, up_got, d_send.at[0], d_recv.at[0], over_dp)
+    wait_all(loads)
+    made[...] = (own[...] + got[...].astype(F32)).astype(BF16)
+    copies += swap_begin(made, gates_ref, g_send, g_recv, g_local, g_held)
+    wait_all(up_loads)
+    up_kept_ref[...] = up_own[...] + up_got[...].astype(F32)
+    finish(copies)
+
+
+def own_out_begin(out_ref, outs_ref, send, recv, local, held):
+    dp, hi, lo = (lax.axis_index(a) for a in ("dp", "hi", "lo"))
+    away = dp != lo
+    mine = dp * 2 + hi
+
+    def push(a, b, start):
+        hi_to, lo_to = lax.rem(hi + a, 2), lax.rem(lo + b, 2)
         copy = pltpu.make_async_remote_copy(
-            src_ref=source,
-            dst_ref=target,
-            send_sem=send.at[kind, piece],
-            recv_sem=recv.at[kind, piece],
-            device_id=to,
+            src_ref=out_ref.at[hi_to, lo_to],
+            dst_ref=outs_ref.at[mine],
+            send_sem=send.at[2 * a + b],
+            recv_sem=recv.at[mine],
+            device_id={"dp": lo, "hi": hi_to, "lo": lo_to},
             device_id_type=MESH_ID,
         )
-        copy.start()
-        return copy
-
+        if start:
+            copy.start()
+        else:
+            copy.wait_send()
+
+    def own_copy():
+        copy = local_copy(out_ref.at[hi, lo], held, local)
+        copy.wait()
+        copy = local_copy(held, outs_ref.at[mine], local)
+        copy.wait()
+
+    for a, b in ((0, 1), (1, 0), (1, 1)):
+        push(a, b, True)
+    pl.when(away)(lambda: push(0, 0, True))
+
+    def arrive(slot):
+        pltpu.make_async_remote_copy(
+            src_ref=out_ref.at[0, 0],
+            dst_ref=outs_ref.at[slot],
+            send_sem=send.at[0],
+            recv_sem=recv.at[slot],
+            device_id={"dp": lo},
+            device_id_type=MESH_ID,
+        ).wait_recv()
+
+    def end():
+        pl.when(jnp.logical_not(away))(own_copy)
+        for a, b in ((0, 1), (1, 0), (1, 1)):
+            push(a, b, False)
+        pl.when(away)(lambda: push(0, 0, False))
+        for d in range(2):
+            for h in range(2):
+                itself = (d == dp) & (h == hi) & (dp == lo)
+                pl.when(jnp.logical_not(itself))(functools.partial(arrive, 2 * d + h))
+
+    return end
+
+
+def close_kernel(with_out, *refs):
+    refs = iter(refs)
+    take = lambda n: [next(refs) for _ in range(n)]
+    parts_ref, heads_ref, up_ref, up_got_ref, square_ref = take(5)
+    out_rows_ref = next(refs) if with_out else None
+    total_ref, head_ref, ups_ref, squares_ref = take(4)
+    outs_ref = next(refs) if with_out else None
+    scatter = take(9)
+    h_send, h_recv, s_send, s_recv, local, h_held = take(6)
+    swap = take(4)
+    own, got, made, sem = take(4)
+    out_scratch = take(4) if with_out else None
+    mine = device_place()
+    peers, seq = every_peer(), seq_peers()
+    place = seq_place({a: lax.axis_index(a) for a in SEQ})
+    loads = scatter_load(parts_ref, scatter)
+    up_loads = [local_copy(up_ref, own, sem.at[0]), local_copy(up_got_ref, got, sem.at[1])]
+    greet(peers)
+    copies = [
+        Carried(heads_ref.at[place], head_ref.at[place], h_held, local.at[0]),
+        local_copy(square_ref, squares_ref.at[mine], local.at[1]),
+    ]
+    mates = scatter_mates(parts_ref, scatter)
+    for k, to in enumerate(peers):
+        copies.append(remote(square_ref, squares_ref.at[mine], s_send.at[k], s_recv.at[k], to))
+    for k, (to, source) in enumerate(seq):
+        part = heads_ref.at[seq_place(to)]
+        copies.append(remote(part, head_ref.at[place], h_send.at[k], h_recv.at[k], to))
+    end = own_out_begin(out_rows_ref, outs_ref, *out_scratch) if with_out else None
+    wait_all(up_loads)
+    made[...] = (own[...] + got[...].astype(F32)).astype(BF16)
+    copies += swap_begin(made, ups_ref, *swap)
+    scatter_end_square(loads, mates, total_ref, scatter)
+    if with_out:
+        end()
+    finish(copies)
+
+
+def remote_to(source, target, sems_of, kind, piece, to):
+    send, recv = sems_of
+    return remote(source, target, send.at[kind, piece], recv.at[kind, piece], to)
+
+
+def scatter_load(parts_ref, scratch):
+    mine, local = scratch[0], scratch[8]
+    blk, lo, mate, side = square_places()
+    places = (side * 2 + 1 - lo, side * 2 + lo, blk * 2 + 1 - lo, blk * 2 + lo)
+    return [local_copy(parts_ref.at[p], mine.at[k], local.at[k]) for k, p in enumerate(places)]
+
+
+def scatter_mates(parts_ref, scratch):
+    mates, sems_of = scratch[1], scratch[6:8]
+    blk, lo, mate, side = square_places()
+    mate_side = (mate + 2) % 4
+    places = (mate_side * 2 + 1 - lo, mate_side * 2 + lo, mate * 2 + 1 - lo, mate * 2 + lo)
+    step = parts_ref.shape[1] // PIECES
     rows = lambda p: pl.ds(p * step, step)
     orders = ((0, 2, 1, 3), (0, 1, 2, 3), (2, 3, 0, 1), (0, 1, 2, 3))
-    from_mate = {}
-    for k in range(4):
-        for p in orders[k]:
-            from_mate[k, p] = push(
-                parts_ref.at[mate_slots[k], rows(p)], mates.at[k, rows(p)], k, p, to_mate
-            )
+    return {
+        (k, p): remote_to(
+            parts_ref.at[places[k], rows(p)], mates.at[k, rows(p)], sems_of, k, p, {"blk": mate}
+        )
+        for k in range(4)
+        for p in orders[k]
+    }
+
+
+def scatter_end_square(loads, from_mate, out_ref, scratch):
+    mine, mates, made, got_across, got_side, got_next = scratch[:6]
+    sems_of = scratch[6:8]
+    blk, lo, mate, side = square_places()
+    to_side, to_next = {"blk": side}, {"lo": 1 - lo}
+    step = mine.shape[1] // PIECES
+    rows = lambda p: pl.ds(p * step, step)
 
     def summed(k, p):
         from_mate[k, p].wait_recv()
@@ -468,11 +892,12 @@
 
     sent = {}
     loads[0].wait()
-    for p in orders[0]:
+    for p in (0, 2, 1, 3):
         made[0, rows(p), :] = summed(0, p).astype(BF16)
-        sent[0, p] = push(
+        sent[0, p] = remote_to(
             made.at[0, rows(p)],
             got_across.at[rows(p)],
+            sems_of,
             4,
             p,
             to_side if p < 2 else to_next,
@@ -485,9 +910,10 @@
             sent[0, p].wait_recv()
             total = total + got_across[rows(p), :].astype(F32)
         made[k, rows(p), :] = total.astype(BF16)
-        sent[k, p] = push(
+        sent[k, p] = remote_to(
             made.at[k, rows(p)],
             (got_side if k == 1 else got_next).at[rows(p)],
+            sems_of,
             4 + k,
             p,
             to_side if k == 1 else to_next,
@@ -506,31 +932,102 @@
         copy.wait_send()
 
 
-def scatter_square(parts, number):
+def scatter_scratch(tok, width):
+    return [
+        pltpu.VMEM((4, tok, width), BF16),
+        pltpu.VMEM((4, tok, width), BF16),
+        pltpu.VMEM((3, tok, width), BF16),
+        pltpu.VMEM((tok, width), BF16),
+        pltpu.VMEM((tok, width), BF16),
+        pltpu.VMEM((tok, width), BF16),
+        pltpu.SemaphoreType.DMA((7, PIECES)),
+        pltpu.SemaphoreType.DMA((7, PIECES)),
+        pltpu.SemaphoreType.DMA((4,)),
+    ]
+
+
+def scatter_kernel(firsts, parts_ref, *refs):
+    out_ref, scratch = refs[firsts], refs[firsts + 1 :]
+    loads = scatter_load(parts_ref, scratch)
+    greet(square_greeting())
+    scatter_end_square(loads, scatter_mates(parts_ref, scratch), out_ref, scratch)
+
+
+def scatter_square(parts, number, *first):
     count, width = parts.shape
     tok = count // 8
     return pl.pallas_call(
-        scatter_kernel,
-        in_specs=[pl.BlockSpec(memory_space=pl.ANY)],
+        functools.partial(scatter_kernel, len(first)),
+        in_specs=[pl.BlockSpec(memory_space=pl.ANY)] * (1 + len(first)),
         out_specs=pl.BlockSpec(memory_space=pltpu.VMEM),
         out_shape=jax.ShapeDtypeStruct((tok, width), F32),
-        scratch_shapes=[
-            pltpu.VMEM((4, tok, width), BF16),
-            pltpu.VMEM((4, tok, width), BF16),
-            pltpu.VMEM((3, tok, width), BF16),
-            pltpu.VMEM((tok, width), BF16),
-            pltpu.VMEM((tok, width), BF16),
-            pltpu.VMEM((tok, width), BF16),
-            pltpu.SemaphoreType.DMA((7, PIECES)),
-            pltpu.SemaphoreType.DMA((7, PIECES)),
-            pltpu.SemaphoreType.DMA((4,)),
-        ],
+        scratch_shapes=scatter_scratch(tok, width),
         compiler_params=pltpu.CompilerParams(
             collective_id=number, has_side_effects=True, vmem_limit_bytes=VMEM_LIMIT
         ),
         cost_estimate=pl.CostEstimate(flops=0, bytes_accessed=120_000_000, transcendentals=0),
         name="scatter_square",
-    )(parts.astype(BF16).reshape(8, tok, width))
+    )(parts.astype(BF16).reshape(8, tok, width), *first)
+
+
+def pair_begin(parts_ref, place, out_ref, send, recv, over_dp):
+    if not over_dp:
+        return [local_copy(parts_ref.at[place], out_ref, recv)]
+    return [remote(parts_ref.at[place], out_ref, send, recv, dp_peers()[0])]
+
+
+def scatter_down_kernel(
+    over_dp, parts_ref, down_ref, got_ref, gate_ref, up_ref, out_ref, sum_ref, gate_got_ref, up_got_ref, *scratch
+):
+    scratch, (own, got, away, came, sem, send, recv) = scratch[:9], scratch[9:]
+    hi = lax.axis_index("hi")
+    down = sum_begin(down_ref, got_ref, 1 - hi, own, got, sem)
+    loads = scatter_load(parts_ref, scratch)
+    greet(square_greeting() + [other_hi()] + (dp_peers() if over_dp else []))
+    mates = scatter_mates(parts_ref, scratch)
+    pairs = pair_begin(gate_ref, 1 - hi, gate_got_ref, send.at[1], recv.at[1], over_dp)
+    pairs += pair_begin(up_ref, 1 - hi, up_got_ref, send.at[2], recv.at[2], over_dp)
+    wait_all(down)
+    away[...] = (own[...] + got[...].astype(F32)).astype(BF16)
+    over = remote(away, came, send.at[0], recv.at[0], other_hi())
+    down = sum_begin(down_ref, got_ref, hi, own, got, sem)
+    scatter_end_square(loads, mates, out_ref, scratch)
+    wait_all(down)
+    over.wait()
+    sum_ref[...] = own[...] + got[...].astype(F32) + came[...].astype(F32)
+    wait_all(pairs)
+
+
+def scatter_down(parts, number, down, gate_away, up_away):
+    count, width = parts.shape
+    tok = count // 8
+    part = down[0].shape[1:]
+    anywhere = pl.BlockSpec(memory_space=pl.ANY)
+    return pl.pallas_call(
+        functools.partial(scatter_down_kernel, lax.axis_size("dp") == 2),
+        in_specs=[anywhere] * 5,
+        out_specs=[pl.BlockSpec(memory_space=pltpu.VMEM)] * 2 + [anywhere] * 2,
+        out_shape=[
+            jax.ShapeDtypeStruct((tok, width), F32),
+            jax.ShapeDtypeStruct(part, F32),
+            jax.ShapeDtypeStruct(gate_away.shape[1:], BF16),
+            jax.ShapeDtypeStruct(up_away.shape[1:], BF16),
+        ],
+        scratch_shapes=scatter_scratch(tok, width)
+        + [
+            pltpu.VMEM(part, F32),
+            pltpu.VMEM(part, BF16),
+            pltpu.VMEM(part, BF16),
+            pltpu.VMEM(part, BF16),
+            pltpu.SemaphoreType.DMA((2,)),
+        ]
+        + sems(3),
+        compiler_params=pltpu.CompilerParams(
+            collective_id=number, has_side_effects=True, vmem_limit_bytes=VMEM_LIMIT
+        ),
+        cost_estimate=pl.CostEstimate(flops=0, bytes_accessed=160_000_000, transcendentals=0),
+        name="scatter_down",
+    )(parts.reshape(8, tok, width), *down, gate_away, up_away)
 
 
 def swap_square(blocks):
@@ -541,32 +1038,38 @@
     return lax.ppermute(block, axis, [(0, 1), (1, 0)])
 
 
-def gather_axis(rows, axis):
+def gather_start(rows, axis):
     if lax.axis_size(axis) != 2:
         return lax.all_gather(rows, axis, axis=0, tiled=False)
-    other = swap_pair(rows, axis)
+    return rows, swap_pair(rows, axis)
+
+
+def gather_end(parts, axis):
+    if lax.axis_size(axis) != 2:
+        return parts
+    rows, other = parts
     first = lax.axis_index(axis) == 0
     return jnp.stack([jnp.where(first, rows, other), jnp.where(first, other, rows)])
 
 
-def gather_copies(rows):
-    both = gather_axis(gather_axis(rows, "hi"), "dp")
-    return both.reshape((-1,) + rows.shape[1:])
-
-
-def scatter_axis(parts, axis):
+def scatter_start(parts, axis):
     if lax.axis_size(axis) != 2:
-        return lax.psum_scatter(parts.astype(BF16), axis, scatter_dimension=0, tiled=False).astype(F32)
+        return lax.psum_scatter(parts.astype(BF16), axis, scatter_dimension=0, tiled=False)
     place = lax.axis_index(axis)
     away = lax.dynamic_index_in_dim(parts, 1 - place, 0, False).astype(BF16)
     own = lax.dynamic_index_in_dim(parts, place, 0, False)
-    return own + swap_pair(away, axis).astype(F32)
-
-
-def scatter_copies(rows):
+    return own, swap_pair(away, axis)
+
+
+def scatter_end(parts, axis):
+    if lax.axis_size(axis) != 2:
+        return parts.astype(F32)
+    return parts[0] + parts[1].astype(F32)
+
+
+def by_copy(rows):
     dp_n, hi_n = lax.axis_size("dp"), lax.axis_size("hi")
-    parts = rows.reshape((dp_n, hi_n, rows.shape[0] // (dp_n * hi_n)) + rows.shape[1:])
-    return scatter_axis(scatter_axis(parts, "dp"), "hi")
+    return rows.reshape((dp_n, hi_n, rows.shape[0] // (dp_n * hi_n)) + rows.shape[1:])
 
 
 def total_of(value, axes, count):
@@ -629,7 +1132,7 @@
 
 
 def out_back_kernel(
-    pairs, block, grad_ref, middle_ref, result_ref, gain_ref, weight_ref, sum_ref, rows_ref, mixed_ref, work
+    pairs, block, grad_ref, middle_ref, result_ref, gain_ref, weight_ref, first_ref, sum_ref, rows_ref, mixed_ref, work
 ):
     f = pl.program_id(0)
 
@@ -647,7 +1150,7 @@
     mixed_ref[0] = dot32(rows_ref[...], weight_ref[...], ((1,), (1,))).astype(BF16)
 
 
-def out_back(grad, middle, result, gain, weight, cols, order, pairs, block):
+def out_back(grad, middle, result, gain, weight, first, cols, order, pairs, block):
     tok, width = middle.shape
     group = width // cols
     whole = pl.BlockSpec((tok, width), lambda f: (0, 0))
@@ -660,6 +1163,7 @@
             whole,
             pl.BlockSpec((1, width), lambda f: (0, 0)),
             pl.BlockSpec((cols, width), lambda f: (order(f), 0)),
+            pl.BlockSpec(memory_space=pl.ANY),
         ],
         out_specs=[whole, whole, pl.BlockSpec((1, tok, cols), lambda f: (f, 0, 0))],
         out_shape=[
@@ -673,7 +1177,114 @@
             flops=2 * tok * width * width, bytes_accessed=20_000_000, transcendentals=0
         ),
         name="out_back",
-    )(grad, middle, result, gain, weight)
+    )(grad, middle, result, gain, weight, first)
+
+
+def weight_grad_kernel(dp_ref, left_ref, right_ref, first_ref, away_ref, own_ref):
+    i = pl.program_id(0)
+    total = dot32(left_ref[...], right_ref[...], ((0,), (0,)))
+
+    @pl.when(i < 2)
+    def _():
+        away_ref[0] = total.astype(BF16)
+
+    @pl.when(i >= 2)
+    def _():
+        own_ref[0] = total
+
+
+def weight_grad_start(left, right, first):
+    dp_n, hi_n = lax.axis_size("dp"), lax.axis_size("hi")
+    depth, rows = left.shape
+    cols = right.shape[1]
+    if dp_n != 2:
+        sums = scatter_start(by_copy(dot32(left, right, ((0,), (0,)))), "dp")
+        return sums.astype(F32), jnp.zeros(sums.shape, BF16)
+    part = rows // (dp_n * hi_n)
+    place = lax.axis_index("dp").astype(jnp.int32).reshape(1)
+    away, own = pl.pallas_call(
+        weight_grad_kernel,
+        grid_spec=pltpu.PrefetchScalarGridSpec(
+            num_scalar_prefetch=1,
+            grid=(4,),
+            in_specs=[
+                pl.BlockSpec(
+                    (depth, part),
+                    lambda i, dp: (0, jnp.where(i < 2, 2 * (1 - dp[0]) + i, 2 * dp[0] + i - 2)),
+                ),
+                pl.BlockSpec((depth, cols), lambda i, dp: (0, 0)),
+                pl.BlockSpec(memory_space=pl.ANY),
+            ],
+            out_specs=[
+                pl.BlockSpec((1, part, cols), lambda i, dp: (jnp.minimum(i, 1), 0, 0)),
+                pl.BlockSpec((1, part, cols), lambda i, dp: (jnp.maximum(i - 2, 0), 0, 0)),
+            ],
+        ),
+        out_shape=[
+            jax.ShapeDtypeStruct((2, part, cols), BF16),
+            jax.ShapeDtypeStruct((2, part, cols), F32),
+        ],
+        compiler_params=pltpu.CompilerParams(vmem_limit_bytes=VMEM_LIMIT),
+        cost_estimate=pl.CostEstimate(
+            flops=2 * depth * rows * cols, bytes_accessed=24_000_000, transcendentals=0
+        ),
+        name="weight_grad",
+    )(place, left, right, first)
+    return own, away
+
+
+def ff_back_kernel(
+    tile, grad_ref, gate_slope_ref, up_slope_ref, gate_ref, up_ref, down_ref, first_ref, dgate_ref, dup_ref,
+    out_ref, total,
+):
+    total[...] = jnp.zeros_like(total)
+
+    def step(t, carry):
+        cols = pl.ds(pl.multiple_of(t * tile, tile), tile)
+        dunits = dot32(grad_ref[...], down_ref[cols, :], ((1,), (1,)))
+        dgate = (dunits * gate_slope_ref[:, cols].astype(F32)).astype(BF16)
+        dup = (dunits * up_slope_ref[:, cols].astype(F32)).astype(BF16)
+        dgate_ref[:, cols] = dgate
+        dup_ref[:, cols] = dup
+        total[...] += dot32(dgate, gate_ref[:, cols], ((1,), (1,))) + dot32(
+            dup, up_ref[:, cols], ((1,), (1,))
+        )
+        return carry
+
+    lax.fori_loop(0, down_ref.shape[0] // tile, step, 0)
+    out_ref[...] = total[...].astype(BF16)
+
+
+def ff_back(grad, gate_slope, up_slope, gate_weight, up_weight, down_weight, first, tok):
+    count, width = grad.shape
+    ff = down_weight.shape[0]
+    rows = lambda cols: pl.BlockSpec((tok, cols), lambda i: (i, 0))
+    whole = lambda a: pl.BlockSpec(a.shape, lambda i: (0, 0), pipeline_mode=pl.Buffered(1))
+    return pl.pallas_call(
+        functools.partial(ff_back_kernel, ff),
+        grid=(count // tok,),
+        in_specs=[
+            rows(width),
+            rows(ff),
+            rows(ff),
+            whole(gate_weight),
+            whole(up_weight),
+            whole(down_weight),
+            pl.BlockSpec(memory_space=pl.ANY),
+        ],
+        out_specs=[rows(ff), rows(ff), rows(width)],
+        out_shape=[
+            jax.ShapeDtypeStruct((count, ff), BF16),
+            jax.ShapeDtypeStruct((count, ff), BF16),
+            jax.ShapeDtypeStruct((count, width), BF16),
+        ],
+        scratch_shapes=[pltpu.VMEM((tok, width), F32)],
+        compiler_params=pltpu.CompilerParams(vmem_limit_bytes=VMEM_LIMIT),
+        cost_estimate=pl.CostEstimate(
+            flops=6 * count * width * ff, bytes_accessed=40_000_000, transcendentals=0
+        ),
+        name="ff_back",
+    )(grad, gate_slope, up_slope, gate_weight, up_weight, down_weight, first)
 
 
 def deal_kernel(places, wide, gate_ref, up_ref, gates_ref, ups_ref):
@@ -771,27 +1382,12 @@
             .reshape(rows_w, group * ff_part)
         )
 
-    gains = jnp.stack([attn_gain, mlp_gain]).reshape(1, 2 * rows_w)
-    gains = lax.all_to_all(
-        jnp.broadcast_to(gains, (every, 2 * rows_w)), ALL, split_axis=0, concat_axis=0, tiled=True
-    )
-    gains = gains.astype(F32).reshape(every, 2, rows_w)
-    gain_one, gain_two = gains[:, 0].reshape(1, width), gains[:, 1].reshape(1, width)
-
     q_cols = w_query.shape[1] // group
     k_cols = key_projection.shape[1] // group
     head_parts = jnp.concatenate(
         [head_columns(w) for w in (w_query, key_projection, value_projection)], axis=2
     )
     head_wide = head_parts.shape[2]
-    head_parts = jnp.broadcast_to(
-        head_parts.reshape(1, blk_n, 1, lo_n, rows_w, head_wide),
-        (dp_n, blk_n, hi_n, lo_n, rows_w, head_wide),
-    ).reshape(every, rows_w, head_wide)
-    qkv_weight = lax.all_to_all(head_parts, ALL, split_axis=0, concat_axis=0, tiled=True).reshape(
-        width, head_wide
-    )
-
     ff_places = [
         (b * lo_n + l, d * hi_n + h)
         for d in range(dp_n)
@@ -811,43 +1407,106 @@
     else:
         gate_parts, up_parts = unit_columns(w_gate), unit_columns(w_up)
 
-    places = (
-        (jnp.arange(blk_n)[:, None, None] * hi_n + hi) * lo_n + jnp.arange(lo_n)[None, :, None]
-    ) * tok + jnp.arange(tok)[None, None, :]
-    places = places.reshape(-1)
-    half = HEAD_SIZE // 2
-    frequency = ROPE_BASE ** (-(jnp.arange(half).astype(F32) * 2.0) / HEAD_SIZE)
-    angles = places.astype(F32)[:, None] * frequency[None, :]
-    cosine, sine, none = jnp.cos(angles), jnp.sin(angles), jnp.zeros_like(angles)
-    tables = (
-        jnp.concatenate([cosine] * 4, axis=1),
-        jnp.concatenate([-sine, none] * 2, axis=1),
-        jnp.concatenate([none, sine] * 2, axis=1),
-    )
-
-    inputs = hidden[0].astype(F32)
-    normal_one, inverse_one = norm_parts(inputs)
-    normed_one = gather_square((normal_one * gain_one).astype(BF16), 0)
-    qkv = project(normed_one, qkv_weight, tables, tok)
-    normed_one, w_out, w_down, gate_parts, up_parts = lax.optimization_barrier(
-        (normed_one, w_out, w_down, gate_parts, up_parts)
-    )
-    down_weight = gather_copies(w_down)
-    gate_weight = gather_copies(swap_square(gate_parts).reshape(group * rows_w, -1))
-    up_weight = gather_copies(swap_square(up_parts).reshape(group * rows_w, -1))
-    out_weight = gather_axis(gather_axis(w_out, "lo"), "hi").reshape(-1, width)
-    out_weight = lax.all_gather(out_weight, ("dp", "blk"), axis=0, tiled=True)
+    pad = jnp.zeros((7 * 128 + 128 - 2 * rows_w - 1,), F32)
+    small = jnp.concatenate(
+        [attn_gain.astype(F32), mlp_gain.astype(F32), lengths.astype(F32), pad]
+    ).reshape(8, 128)
+    rows_all, qkv_weight, smalls, out_rows = comm_call(
+        open_kernel,
+        0,
+        [hidden[0], head_parts, small, w_out],
+        [
+            ((group, tok, width), BF16),
+            ((every, rows_w, head_wide), BF16),
+            ((every, 8, 128), F32),
+            ((hi_n, lo_n, rows_w, width), BF16),
+        ],
+        gather_scratch(tok, width)
+        + sems(every // dp_n - 1)
+        + sems((dp_n - 1) * every // dp_n)
+        + sems(every - 1)
+        + sems(3)
+        + [
+            pltpu.SemaphoreType.DMA((3,)),
+            pltpu.VMEM((rows_w, head_wide), BF16),
+            pltpu.VMEM((rows_w, width), BF16),
+        ],
+        "open",
+    )
+    qkv_weight = qkv_weight.reshape(width, head_wide)
+    gain_one = smalls[:, 0, :rows_w].reshape(1, width)
+    gain_two = smalls[:, 0, rows_w : 2 * rows_w].reshape(1, width)
+    valid_count = jnp.sum(smalls.reshape(every, -1)[:: every // dp_n, 2 * rows_w])
+    hi_index = hi.astype(jnp.int32).reshape(1)
+    tables = rope_tables(seq_len)
+    normed_one, q, kv = project(
+        hi_index, rows_all.reshape(group * tok, width), gain_one, qkv_weight, tables, tok
+    )
     unit = lo_n * tok
-    other_kv = swap_pair(qkv[:, q_cols:], "hi").reshape(blk_n, unit, 2 * k_cols)
-    qkv = qkv.reshape(blk_n, unit, -1)
+    part_rows = group * rows_w
+    other_kv, gate_parts, up_parts, downs = comm_call(
+        keys_kernel,
+        2,
+        [kv, gate_parts, up_parts, w_down],
+        [
+            (kv.shape, BF16),
+            (gate_parts.shape, BF16),
+            (up_parts.shape, BF16),
+            ((dp_n - 1,) + w_down.shape, BF16),
+        ],
+        sems(1) + swap_scratch((rows_w, ff_part)) * 2 + sems(dp_n - 1),
+        "keys",
+    )
+    gate_parts = gate_parts.reshape(part_rows, -1)
+    up_parts = up_parts.reshape(part_rows, -1)
+    gate_other = swap_pair(gate_parts, "hi")
+    out_weight = lax.all_gather(out_rows.reshape(-1, width), ("dp", "blk"), axis=0, tiled=True)
+    q = q.reshape(blk_n, unit, q_cols)
+    kv, other_kv = kv.reshape(blk_n, unit, -1), other_kv.reshape(blk_n, unit, -1)
     scalars = jnp.stack([lengths[0], hi.astype(jnp.int32)])
-    out_heads, log_heads = attend(scalars, qkv, other_kv)
-    mixed = swap_square(out_heads.reshape(group, tok, q_cols))
+    out_heads, log_heads = attend(scalars, q, kv, other_kv)
+    dp_sems = sems(2 * (dp_n - 1))
+    dp_scratch = [pltpu.SemaphoreType.DMA((2,)), pltpu.VMEM((2, part_rows, ff_part), BF16)]
+    weight_shape = ((dp_n, hi_n, part_rows, ff_part), BF16)
+    mixed, gate_weight, up_other = comm_call(
+        heads_kernel,
+        3,
+        [out_heads.reshape(group, tok, q_cols), gate_parts, gate_other, up_parts],
+        [((group, tok, q_cols), BF16), weight_shape, (up_parts.shape, BF16)],
+        swap_scratch((tok, q_cols)) + dp_sems + sems(1) + dp_scratch,
+        "heads",
+    )
+    gate_weight = gate_weight.reshape(width, ff_part)
     middle, normed_two = out_project(
         mixed, out_weight, hidden[0], gain_two, key_head, to_inner, reblock
     )
 
-    normed_two = gather_square(inner(normed_two), 0)
+    normed_two, up_weight, down_other = comm_call(
+        rows_kernel,
+        4,
+        [inner(normed_two), up_parts, up_other, w_down],
+        [((group, tok, width), BF16), weight_shape, (w_down.shape, BF16)],
+        gather_scratch(tok, width) + dp_sems + sems(1) + dp_scratch,
+        "rows",
+    )
+    normed_two = normed_two.reshape(group * tok, width)
+    up_weight = up_weight.reshape(width, ff_part)
+    dp_index = lax.axis_index("dp")
+    own_first = hi == 0
+
+    def by_hi(own, other):
+        return jnp.stack([jnp.where(own_first, own, other), jnp.where(own_first, other, own)])
+
+    down_parts = by_hi(w_down, down_other)
+    if dp_n == 2:
+        far = by_hi(downs[0], swap_pair(down_other, "dp"))
+        dp_first = dp_index == 0
+        down_parts = jnp.stack(
+            [jnp.where(dp_first, down_parts, far), jnp.where(dp_first, far, down_parts)]
+        )
+    else:
+        down_parts = lax.all_gather(down_parts, "dp", axis=0, tiled=False)
+    down_weight = down_parts.reshape(-1, width)
     gate = dot32(normed_two, gate_weight)
     upward = dot32(normed_two, up_weight)
     sigma = jax.nn.sigmoid(gate)
@@ -860,58 +1519,131 @@
     own_places = ((blk * hi_n + hi) * lo_n + lo) * tok + jnp.arange(tok)
     valid = own_places < lengths[0]
     misfit = jnp.where(valid[:, None], result - teacher[0].astype(F32), 0.0)
-    valid_count = total_of(lengths, ("dp",), dp_n).astype(F32)
-    squares = total_of(jnp.sum(misfit * misfit), ALL, every)
-    mse_loss = squares / (width * valid_count)
+    squares = jnp.broadcast_to(jnp.sum(misfit * misfit), (8, 128))
     grad_result = misfit * (dp_n * seq_len / valid_count)
 
-    branch = gather_square((RESIDUAL_SCALE * grad_result).astype(BF16), 0)
-    grad_units = dot32(branch, down_weight, ((1,), (1,)))
-    grad_gate_rows = (grad_units * gate_slope.astype(F32)).astype(BF16)
-    grad_up_rows = (grad_units * up_slope.astype(F32)).astype(BF16)
-    grad_normal = outer(
-        scatter_square(
-            dot32(grad_gate_rows, gate_weight, ((1,), (1,)))
-            + dot32(grad_up_rows, up_weight, ((1,), (1,))),
-            1,
-        )
-    )
-    down_sum = scatter_copies(dot32(units, branch, ((0,), (0,))))
-    gate_sum = scatter_copies(dot32(normed_two, grad_gate_rows, ((0,), (0,))))
-    up_sum = scatter_copies(dot32(normed_two, grad_up_rows, ((0,), (0,))))
+    branch = gather_square((RESIDUAL_SCALE * grad_result).astype(BF16), 5)
+    down_sum = weight_grad_start(units, branch, branch)
+    grad_gate_rows, grad_up_rows, grad_normal = ff_back(
+        branch, gate_slope, up_slope, gate_weight, up_weight, down_weight, down_sum[0], 2 * tok
+    )
+    gate_sum = weight_grad_start(normed_two, grad_gate_rows, down_sum[0])
+    up_sum = weight_grad_start(normed_two, grad_up_rows, gate_sum[0])
+    down_got = swap_pair(down_sum[1], "dp") if dp_n == 2 else down_sum[1]
+    grad_normal, down_sum, gate_got, up_got = scatter_down(
+        grad_normal, 9, (down_sum[0], down_got), gate_sum[1], up_sum[1]
+    )
+    grad_normal = outer(grad_normal)
 
     grad_middle, attn_rows, grad_mixed = out_back(
-        grad_normal, middle, grad_result, gain_two, out_weight, q_cols, key_head, to_outer, reblock
-    )
-    dout = swap_square(grad_mixed).reshape(blk_n, unit, q_cols)
-    dq, dkv = attend_back(scalars, qkv, other_kv, dout, out_heads, log_heads)
+        grad_normal, middle, grad_result, gain_two, out_weight, up_sum[0], q_cols, key_head, to_outer, reblock
+    )
+    square_attn = lax.all_gather(attn_rows, SQUARE, axis=0, tiled=True)
+    part_shape = (part_rows, ff_part)
+    anywhere, inside = pl.BlockSpec(memory_space=pl.ANY), pl.BlockSpec(memory_space=pltpu.VMEM)
+    over_dp = dp_n == 2
+    dout, gate_away, up_away, gate_kept = pl.pallas_call(
+        functools.partial(douts_kernel, over_dp),
+        in_specs=[anywhere] * 6,
+        out_specs=[anywhere] + [inside] * 3,
+        out_shape=[jax.ShapeDtypeStruct(grad_mixed.shape, BF16)]
+        + [jax.ShapeDtypeStruct(part_shape, dtype) for dtype in (BF16, BF16, F32)],
+        scratch_shapes=swap_scratch((tok, q_cols))
+        + [
+            pltpu.VMEM((3,) + part_shape, F32),
+            pltpu.VMEM((3,) + part_shape, BF16),
+            pltpu.SemaphoreType.DMA((3, 2)),
+        ]
+        + sems(1),
+        compiler_params=pltpu.CompilerParams(
+            collective_id=6, has_side_effects=True, vmem_limit_bytes=VMEM_LIMIT
+        ),
+        cost_estimate=pl.CostEstimate(flops=0, bytes_accessed=40_000_000, transcendentals=0),
+        name="douts",
+    )(grad_mixed, gate_sum[0], gate_got, up_sum[0], up_got, gate_sum[1])
+    gate_got, up_got = swap_pair(gate_away, "hi"), swap_pair(up_away, "hi")
+    dout = dout.reshape(blk_n, unit, q_cols)
+    dq, dkv = attend_back(scalars, q, kv, other_kv, dout, out_heads, log_heads, gate_away)
     dkv = dkv.reshape(2, group * tok, 2 * k_cols)
+    columns = (group, rows_w, ff_part)
+    sum_scratch = [
+        pltpu.VMEM(columns, F32),
+        pltpu.VMEM(columns, BF16),
+        pltpu.VMEM(columns, BF16),
+        pltpu.SemaphoreType.DMA((3,)),
+    ]
+    own_out = dot32(out_heads.reshape(group * tok, q_cols), square_attn, ((0,), (0,))).astype(BF16)
+    other_dkv, gate_parts, up_kept = pl.pallas_call(
+        functools.partial(dkeys_kernel, over_dp),
+        in_specs=[anywhere] * 6,
+        out_specs=[anywhere, anywhere, inside],
+        out_shape=[
+            jax.ShapeDtypeStruct(dkv.shape[1:], BF16),
+            jax.ShapeDtypeStruct(columns, BF16),
+            jax.ShapeDtypeStruct(part_shape, F32),
+        ],
+        scratch_shapes=sems(1)
+        + swap_scratch((rows_w, ff_part))
+        + sum_scratch
+        + [pltpu.VMEM(part_shape, F32), pltpu.VMEM(part_shape, BF16)]
+        + sems(1),
+        compiler_params=pltpu.CompilerParams(
+            collective_id=7, has_side_effects=True, vmem_limit_bytes=VMEM_LIMIT
+        ),
+        cost_estimate=pl.CostEstimate(flops=0, bytes_accessed=40_000_000, transcendentals=0),
+        name="dkeys",
+    )(dkv, gate_kept.reshape(columns), gate_got.reshape(columns), up_sum[0], up_sum[1], own_out)
     dqkv = back_rope(
-        dq.reshape(group * tok, q_cols), dkv[0], swap_pair(dkv[1], "hi"), tables, tok
-    )
-    grad_first = scatter_square(dot32(dqkv, qkv_weight, ((1,), (1,))), 1) * gain_one
-    grad_hidden = grad_middle + inverse_one * (
-        grad_first - normal_one * jnp.mean(grad_first * normal_one, axis=-1, keepdims=True)
-    )
-    head_grads = dot32(normed_one, dqkv, ((0,), (0,))).astype(BF16).reshape(every, rows_w, head_wide)
-    head_grads = lax.all_to_all(head_grads, ALL, split_axis=0, concat_axis=0, tiled=True)
-    head_grads = jnp.sum(
-        head_grads.reshape(dp_n, blk_n, hi_n, lo_n, rows_w, head_wide).astype(F32), axis=(0, 2)
-    ).reshape(group, rows_w, head_wide)
-
-    square_attn = lax.all_gather(attn_rows, SQUARE, axis=0, tiled=True)
-    own_out = dot32(out_heads.reshape(group * tok, q_cols), square_attn, ((0,), (0,))).astype(BF16)
-    own_head = lo * blk_n + blk
-    if rows_w * hi_n * lo_n == q_cols:
-        spread = jnp.where((jnp.arange(dp_n) == lo)[:, None, None], own_out[None], 0)
-        grad_out = lax.psum_scatter(
-            spread.reshape(dp_n * q_cols, width), ("dp", "hi", "lo"), scatter_dimension=0, tiled=True
-        ).astype(F32)
+        hi_index, dq.reshape(group * tok, q_cols), dkv[0], other_dkv, tables, up_got, tok
+    )
+    head_grads = dot32(normed_one, dqkv, ((0,), (0,))).reshape(dp_n, -1, rows_w, head_wide)
+    head_grads = scatter_end(scatter_start(head_grads, "dp"), "dp").astype(BF16)
+    grad_first = dot32(dqkv, qkv_weight, ((1,), (1,))).astype(BF16)
+    with_out = dp_n == 2 and rows_w * hi_n * lo_n == q_cols
+    arrays = [grad_first.reshape(group, tok, width), head_grads]
+    arrays += [up_kept.reshape(columns), up_got.reshape(columns), squares]
+    shapes = [
+        ((tok, width), F32),
+        (head_grads.shape, BF16),
+        (columns, BF16),
+        ((every, 8, 128), F32),
+    ]
+    scratch = scatter_scratch(tok, width) + sems(every // dp_n - 1) + sems(every - 1)
+    scratch += [pltpu.SemaphoreType.DMA((2,)), pltpu.VMEM((rows_w, head_wide), BF16)]
+    scratch += swap_scratch((rows_w, ff_part)) + sum_scratch
+    if with_out:
+        arrays.append(own_out.reshape(hi_n, lo_n, rows_w, width))
+        shapes.append(((dp_n * hi_n, rows_w, width), BF16))
+        scratch += sems(4) + [pltpu.SemaphoreType.DMA, pltpu.VMEM((rows_w, width), BF16)]
+    grad_first, head_grads, up_parts, squares, *outs = pl.pallas_call(
+        functools.partial(close_kernel, with_out),
+        in_specs=[anywhere] * len(arrays),
+        out_specs=[pl.BlockSpec(memory_space=pltpu.VMEM)] + [anywhere] * (len(shapes) - 1),
+        out_shape=[jax.ShapeDtypeStruct(shape, dtype) for shape, dtype in shapes],
+        scratch_shapes=scratch,
+        compiler_params=pltpu.CompilerParams(
+            collective_id=8, has_side_effects=True, vmem_limit_bytes=VMEM_LIMIT
+        ),
+        cost_estimate=pl.CostEstimate(flops=0, bytes_accessed=120_000_000, transcendentals=0),
+        name="close",
+    )(*arrays)
+    mse_loss = jnp.sum(squares[:, 0, 0]) / (width * valid_count)
+    if with_out:
+        grad_out = jnp.sum(outs[0].astype(F32), axis=0)
     else:
+        own_head = lo * blk_n + blk
         spread = jnp.where((jnp.arange(group) == own_head)[:, None, None], own_out[None], 0)
         grad_out = lax.psum_scatter(
             spread.reshape(width, width), ALL, scatter_dimension=0, tiled=True
         ).astype(F32)
+    grad_first = grad_first * gain_one
+    normal_one, inverse_one = norm_parts(hidden[0].astype(F32))
+    grad_hidden = grad_middle + inverse_one * (
+        grad_first - normal_one * jnp.mean(grad_first * normal_one, axis=-1, keepdims=True)
+    )
+    head_grads = jnp.sum(
+        head_grads.reshape(blk_n, hi_n, lo_n, rows_w, head_wide).astype(F32), axis=1
+    ).reshape(group, rows_w, head_wide)
 
     own_one, own_two = attn_gain.astype(F32)[:, None], mlp_gain.astype(F32)[:, None]
     grad_query = head_columns_back(head_grads[:, :, :q_cols])
@@ -924,9 +1656,6 @@
     grad_gain_one = (
         row_sums((w_query, grad_query), (key_projection, grad_key), (value_projection, grad_value))
         / own_one
-    )
-    gate_parts, up_parts = (
-        swap_square(g.astype(BF16).reshape(group, rows_w, -1)) for g in (gate_sum, up_sum)
     )
     if units_w % 128 == 0:
         ff_shape = jax.ShapeDtypeStruct(w_gate.shape, F32)

time: 1140 us -> 943 us (0.83)
  Pallas kernels: 443 us -> 776 us
  waiting for transfers between devices: 294 us -> 19.3 us
  matrix products: 166 us -> 65 us
  starting transfers between devices: 77.7 us -> 6.72 us
  other arithmetic: 68.4 us -> 24.3 us
  blocking collectives: 28.9 us -> 0 us
    pallas_call x8 -> x16, Pallas kernels: 317 us -> 649 us  [the longest x5 281 us: comm_call(): pl.pallas_call(kernel, in_specs=[anywhere] * len(arrays), out_specs=[anyw...]
    ppermute x16 -> x6, waiting for transfers between devices: 275 us -> 15.2 us  [swap_pair(): return lax.ppermute(block, axis, [(0, 1), (1, 0)])]
    dot_general x12 -> x6, matrix products: 166 us -> 65 us  [dot32(): return lax.dot_general(a, b, (dims, ((), ())), preferred_element_type=F32)]
    all_to_all x9 -> x0, starting transfers between devices: 42.4 us -> none  [the longest x5 21.2 us: swap_square(): lax.all_to_all(blocks, SQUARE, split_axis=0, concat_axis=0, tiled=True)]
    all_to_all x2 -> x0, blocking collectives: 28.9 us -> none  [the longest x1 22.8 us: swap_square(): lax.all_to_all(blocks, SQUARE, split_axis=0, concat_axis=0, tiled=True)]
    ppermute x16 -> x6, starting transfers between devices: 35.1 us -> 6.34 us  [swap_pair(): return lax.ppermute(block, axis, [(0, 1), (1, 0)])]
    another operation x16 -> x3, other arithmetic: 23.2 us -> 0.67 us  [the longest x1 0.39 us: shards(): jnp.stack([jnp.where(dp_first, down_parts, far), jnp.where(dp_first, far,...]
    all_to_all x9 -> x0, waiting for transfers between devices: 18.6 us -> none  [the longest x5 16.2 us: swap_square(): lax.all_to_all(blocks, SQUARE, split_axis=0, concat_axis=0, tiled=True)]
  transfers between devices with their start and end apart: 28 -> 8, of which waited for: 14 -> 3; matrix products, arithmetic and copies ran while one was open for 13% -> 6% of each run, Pallas kernels for 19% -> 37%
where the time goes in v2:
time: 943 us; the launch traced here: 939 us
  Pallas kernels  776 us (82%)
  matrix products  65 us (7%)
  local copies, waits for them, and re-layouts  29.5 us (3%)
  other arithmetic  24.3 us (3%)
  waiting for transfers between devices  19.3 us (2%)
  between operations  18.4 us (2%)
    pallas_call x5, Pallas kernels, comm_call(): pl.pallas_call(kernel, in_specs=[anywhere] * len(arrays), out_specs=[anyw...  281 us
    pallas_call x1, Pallas kernels, shards(): pl.pallas_call(functools.partial(close_kernel, with_out), in_specs=[anywh...  88.1 us
    dot_general x6, matrix products, dot32(): return lax.dot_general(a, b, (dims, ((), ())), preferred_element_type=F32)  65 us
    pallas_call x1, Pallas kernels, scatter_down(): pl.pallas_call(functools.partial(scatter_down_kernel, lax.axis_size('dp')...  64.7 us
    pallas_call x1, Pallas kernels, attend_back(): pl.pallas_call(attend_back_kernel, grid=(units,), in_specs=[pl.BlockSpec(...  57 us
    pallas_call x3, Pallas kernels, weight_grad_start(): pl.pallas_call(weight_grad_kernel, grid_spec=pltpu.PrefetchScalarGridSpec...  45 us
    pallas_call x1, Pallas kernels, shards(): pl.pallas_call(functools.partial(dkeys_kernel, over_dp), in_specs=[anywhe...  44.9 us
    pallas_call x1, Pallas kernels, scatter_square(): pl.pallas_call(functools.partial(scatter_kernel, len(first)), in_specs=[p...  41 us
  transfers between devices with their start and end apart: 8, of which 3 were waited for; matrix products, arithmetic and copies ran while one was open for 6% of the time, Pallas kernels for 37%

profile of v2, /device:TPU:0, one launch (start us, length us, event | category | flops | bytes accessed | tf_op | source)
XLA Modules:
  0.0 938.8 jit_solution(3259231002590630611)
XLA Ops:
  14.4 80.5 %open.1 = (bf16[8,256,2048]{2,1,0:T(8,128)(2,1)}, bf16[32,64,384]{2,1,0:T(8,128)(2,1)}, f32[32,8,128]{2,1,0:T(8,128)}, bf16[2,2,64,2048]{3,2,1,0:T(8,128)(2,1)}) custom-call(bf16[256,2048]{1,0:T(8,128)(2,1)} %bitcast.108, bf16[8,64,384]{2,1,0:T(8,128)(2,1)} %pad_maximum_fusion.3.heads_ref, f32[8,128]{1,0:T(8,128)} %maximum_bitcast_fusion.small_ref, ...), custom_call_target="tpu_custom_call" | custom-call | bytes 120000000 | tf_op jit(solution)/shard_map/open/pallas_call | solution.py:545
  101.0 12.9 %project.1 = (bf16[2048,2048]{1,0:T(8,128)(2,1)}, bf16[2048,256]{1,0:T(8,128)(2,1)}, bf16[2048,128]{1,0:T(8,128)(2,1)}) custom-call(s32[1]{0:T(128)} %bitcast.hi_ref, bf16[2048,2048]{1,0:T(8,128)(2,1)} %bitcast.116, f32[1,2048]{1,0:T(1,128)} %reshape_squeeze.6.gain_ref, bf16[2048,384]{1,0:T(8,128)(2,1)} %bitcast.134, f32[4096,128]{1,0:T(8,128)} %constant.54.clone.cos_ref, ...), custom_call_target="tpu_custom_call" | custom-call | flops 3221225472 | bytes 16777216 | tf_op jit(solution)/shard_map/project/pallas_call | solution.py:70
  113.8 43.9 %keys.1 = (bf16[2048,128]{1,0:T(8,128)(2,1)}, bf16[8,64,1024]{2,1,0:T(8,128)(2,1)}, bf16[8,64,1024]{2,1,0:T(8,128)(2,1)}, bf16[1,256,2048]{2,1,0:T(8,128)(2,1)}) custom-call(bf16[2048,128]{1,0:T(8,128)(2,1)} %get-tuple-element.72.kv_ref, bf16[8,64,1024]{2,1,0:T(8,128)(2,1)} %get-tuple-element.73.gate_ref, bf16[8,64,1024]{2,1,0:T(8,128)(2,1)} %get-tuple-element.74.up_ref, ...), custom_call_target="tpu_custom_call" | custom-call | bytes 120000000 | tf_op jit(solution)/shard_map/keys/pallas_call | solution.py:545
  158.9 38.1 %attend.1 = (bf16[4,512,256]{2,1,0:T(8,128)(2,1)}, f32[4,8,512]{2,1,0:T(8,128)}) custom-call(s32[2]{0:T(128)} %pad_add_fusion.scalar_ref, bf16[4,512,256]{2,1,0:T(8,128)(2,1)} %bitcast.159, bf16[4,512,128]{2,1,0:T(8,128)(2,1)} %bitcast.144, bf16[4,512,128]{2,1,0:T(8,128)(2,1)} %bitcast.162), custom_call_target="tpu_custom_call" | custom-call | flops 40000000000 | bytes 8000000 | tf_op jit(solution)/shard_map/attend/pallas_call | solution.py:216
  199.0 4.5 collective-permute-done.gate_other_ref
  204.5 53.9 %heads.1 = (bf16[8,256,256]{2,1,0:T(8,128)(2,1)}, bf16[2,2,512,1024]{3,2,1,0:T(8,128)(2,1)}, bf16[512,1024]{1,0:T(8,128)(2,1)}) custom-call(bf16[8,256,256]{2,1,0:T(8,128)(2,1)} %bitcast.118, bf16[512,1024]{1,0:T(8,128)(2,1)} %bitcast.141, bf16[512,1024]{1,0:T(8,128)(2,1)} %copy-done.15, bf16[512,1024]{1,0:T(8,128)(2,1)} %bitcast.124), custom_call_target="tpu_custom_call" | custom-call | bytes 120000000 | tf_op jit(solution)/shard_map/heads/pallas_call | solution.py:545
  258.4 10.7 %out_project.1 = (f32[256,2048]{1,0:T(8,128)}, bf16[256,2048]{1,0:T(8,128)(2,1)}) custom-call(bf16[8,256,256]{2,1,0:T(8,128)(2,1)} %get-tuple-element.79.mixed_ref, bf16[2048,2048]{1,0:T(8,128)(2,1)} %all-gather.3.cloned.1.call-done.weight_ref, bf16[256,2048]{1,0:T(8,128)(2,1)} %bitcast.109, f32[1,2048]{1,0:T(1,128)} %reshape_squeeze.7.gain_ref), custom_call_target="tpu_custom_call" | custom-call | flops 2147483648 | bytes 16000000 | tf_op jit(solution)/shard_map/out_project/pallas_call | solution.py:1111
  269.1 63.3 %rows.1 = (bf16[8,256,2048]{2,1,0:T(8,128)(2,1)}, bf16[2,2,512,1024]{3,2,1,0:T(8,128)(2,1)}, bf16[256,2048]{1,0:T(8,128)(2,1)}) custom-call(bf16[256,2048]{1,0:T(8,128)(2,1)} %get-tuple-element.82.rows_ref, bf16[512,1024]{1,0:T(8,128)(2,1)} %bitcast.125, bf16[512,1024]{1,0:T(8,128)(2,1)} %get-tuple-element.83.up_other_ref, bf16[256,2048]{1,0:T(8,128)(2,1)} %down_ref.3), custom_call_target="tpu_custom_call" | custom-call | bytes 120000000 | tf_op jit(solution)/shard_map/rows/pallas_call | solution.py:545
  333.8 14.5 %fusion.18 = f32[2048,1024]{1,0:T(8,128)} fusion(bf16[2048,2048]{1,0:T(8,128)(2,1)} %bitcast.151, bf16[2048,1024]{1,0:T(8,128)(2,1)} %bitcast.157), kind=kOutput, calls=%fused_computation.58 | convolution fusion | flops 8589934592 | bytes 20971520 | tf_op jit(solution)/shard_map/dot_general | solution.py:30
  348.4 18.2 %multiply_convert_fusion = (bf16[2048,1024]{1,0:T(8,128)(2,1)}, bf16[2048,1024]{1,0:T(8,128)(2,1)}, bf16[2048,1024]{1,0:T(8,128)(2,1)}) fusion(f32[2048,1024]{1,0:T(8,128)} %fusion.18, bf16[2048,2048]{1,0:T(8,128)(2,1)S(1)} %bitcast.154, bf16[2048,1024]{1,0:T(8,128)(2,1)} %bitcast.155), kind=kOutput, calls=%fused_computation | convolution fusion | flops 8617197568 | bytes 33554432 | tf_op jit(solution)/shard_map/dot_general | solution.py:30
  372.1 10.9 %convolution_convert_fusion.1 = bf16[2048,2048]{1,0:T(8,128)(2,1)} fusion(bf16[2048,1024]{1,0:T(8,128)(2,1)S(1)} %copy-done.28, bf16[1024,2048]{1,0:T(8,128)(2,1)S(1)} %bitcast.122), kind=kOutput, calls=%fused_computation.5 | convolution fusion | flops 8594128896 | bytes 16777216 | tf_op jit(solution)/shard_map/dot_general | solution.py:30
  383.0 41.0 %scatter_square.1 = f32[256,2048]{1,0:T(8,128)} custom-call(bf16[8,256,2048]{2,1,0:T(8,128)(2,1)} %bitcast.112), custom_call_target="tpu_custom_call" | custom-call | bytes 120000000 | tf_op jit(solution)/shard_map/scatter_square/pallas_call | solution.py:959
  424.0 4.9 multiply_convert_fusion.2
  428.9 39.2 %gather_square.1 = bf16[8,256,2048]{2,1,0:T(8,128)(2,1)} custom-call(bf16[256,2048]{1,0:T(8,128)(2,1)} %get-tuple-element.126.rows_ref), custom_call_target="tpu_custom_call" | custom-call | bytes 120000000 | tf_op jit(solution)/shard_map/gather_square/pallas_call | solution.py:545
  468.1 15.7 %weight_grad.3 = (bf16[2,256,2048]{2,1,0:T(8,128)(2,1)}, f32[2,256,2048]{2,1,0:T(8,128)}) custom-call(s32[1]{0:T(128)} %bitcast.32.dp_ref, bf16[2048,1024]{1,0:T(8,128)(2,1)} %get-tuple-element.129.left_ref, bf16[2048,2048]{1,0:T(8,128)(2,1)} %bitcast.113, bf16[2048,2048]{1,0:T(8,128)(2,1)} %bitcast.114), custom_call_target="tpu_custom_call" | custom-call | flops 8589934592 | bytes 24000000 | tf_op jit(solution)/shard_map/weight_grad/pallas_call | solution.py:1205
  484.6 35.0 %ff_back.1 = (bf16[2048,1024]{1,0:T(8,128)(2,1)}, bf16[2048,1024]{1,0:T(8,128)(2,1)}, bf16[2048,2048]{1,0:T(8,128)(2,1)}) custom-call(bf16[2048,2048]{1,0:T(8,128)(2,1)} %bitcast.115, bf16[2048,1024]{1,0:T(8,128)(2,1)} %get-tuple-element.128.gate_slope_ref, bf16[2048,1024]{1,0:T(8,128)(2,1)} %get-tuple-element.130.up_slope_ref, ...), custom_call_target="tpu_custom_call" | custom-call | flops 25769803776 | bytes 40000000 | tf_op jit(solution)/shard_map/ff_back/pallas_call | solution.py:1263
  519.6 14.6 %weight_grad.4 = (bf16[2,512,1024]{2,1,0:T(8,128)(2,1)}, f32[2,512,1024]{2,1,0:T(8,128)}) custom-call(s32[1]{0:T(128)} %bitcast.32.dp_ref, bf16[2048,2048]{1,0:T(8,128)(2,1)} %bitcast.152, bf16[2048,1024]{1,0:T(8,128)(2,1)} %get-tuple-element.92.right_ref, f32[2,256,2048]{2,1,0:T(8,128)} %get-tuple-element.89.first_ref.down_ref), custom_call_target="tpu_custom_call" | custom-call | flops 8589934592 | bytes 24000000 | tf_op jit(solution)/shard_map/weight_grad/pallas_call | solution.py:1205
  534.2 14.6 %weight_grad.5 = (bf16[2,512,1024]{2,1,0:T(8,128)(2,1)}, f32[2,512,1024]{2,1,0:T(8,128)}) custom-call(s32[1]{0:T(128)} %bitcast.32.dp_ref, bf16[2048,2048]{1,0:T(8,128)(2,1)} %bitcast.153, bf16[2048,1024]{1,0:T(8,128)(2,1)} %get-tuple-element.94.right_ref, f32[2,512,1024]{2,1,0:T(8,128)} %get-tuple-element.95.first_ref.gate_ref), custom_call_target="tpu_custom_call" | custom-call | flops 8589934592 | bytes 24000000 | tf_op jit(solution)/shard_map/weight_grad/pallas_call | solution.py:1205
  550.1 64.7 %scatter_down.1 = (f32[256,2048]{1,0:T(8,128)}, f32[256,2048]{1,0:T(8,128)}, bf16[512,1024]{1,0:T(8,128)(2,1)}, bf16[512,1024]{1,0:T(8,128)(2,1)}) custom-call(bf16[8,256,2048]{2,1,0:T(8,128)(2,1)} %bitcast.117, f32[2,256,2048]{2,1,0:T(8,128)} %get-tuple-element.89.first_ref.down_ref, bf16[2,256,2048]{2,1,0:T(8,128)(2,1)} %copy-done.7, ...), custom_call_target="tpu_custom_call" | custom-call | bytes 160000000 | tf_op jit(solution)/shard_map/scatter_down/pallas_call | solution.py:1006
  614.9 12.5 %out_back.1 = (f32[256,2048]{1,0:T(8,128)}, bf16[256,2048]{1,0:T(8,128)(2,1)}, bf16[8,256,256]{2,1,0:T(8,128)(2,1)}) custom-call(f32[256,2048]{1,0:T(8,128)} %get-tuple-element.97.grad_ref, f32[256,2048]{1,0:T(8,128)} %get-tuple-element.81.middle_ref, f32[256,2048]{1,0:T(8,128)} %get-tuple-element.127.result_ref, f32[1,2048]{1,0:T(1,128)} %reshape_squeeze.7.gain_ref, ...), custom_call_target="tpu_custom_call" | custom-call | flops 2147483648 | bytes 20000000 | tf_op jit(solution)/shard_map/out_back/pallas_call | solution.py:1157
  629.1 29.8 %douts.1 = (bf16[8,256,256]{2,1,0:T(8,128)(2,1)}, bf16[512,1024]{1,0:T(8,128)(2,1)}, bf16[512,1024]{1,0:T(8,128)(2,1)}, f32[512,1024]{1,0:T(8,128)}) custom-call(bf16[8,256,256]{2,1,0:T(8,128)(2,1)} %get-tuple-element.99.parts_ref, f32[2,512,1024]{2,1,0:T(8,128)} %get-tuple-element.95.first_ref.gate_ref, bf16[512,1024]{1,0:T(8,128)(2,1)} %get-tuple-element.100.gate_got_ref, ...), custom_call_target="tpu_custom_call" | custom-call | bytes 40000000 | tf_op jit(solution)/shard_map/douts/pallas_call | solution.py:1545
  661.9 57.0 %attend_back.1 = (bf16[4,512,256]{2,1,0:T(8,128)(2,1)}, bf16[2,4,512,128]{3,2,1,0:T(8,128)(2,1)}) custom-call(s32[2]{0:T(128)} %pad_add_fusion.scalar_ref, bf16[4,512,256]{2,1,0:T(8,128)(2,1)} %bitcast.160, bf16[4,512,128]{2,1,0:T(8,128)(2,1)} %bitcast.145, bf16[4,512,128]{2,1,0:T(8,128)(2,1)} %bitcast.163, bf16[4,512,256]{2,1,0:T(8,128)(2,1)} %bitcast.161, ...), custom_call_target="tpu_custom_call" | custom-call | flops 60000002048 | bytes 10000000 | tf_op jit(solution)/shard_map/attend_back/pallas_call | solution.py:350
  720.8 4.1 all-gather.5.cloned.1.call-done
  724.9 6.7 convolution_convert_fusion.2.first_ref
  731.6 44.9 %dkeys.1 = (bf16[2048,128]{1,0:T(8,128)(2,1)}, bf16[8,64,1024]{2,1,0:T(8,128)(2,1)}, f32[512,1024]{1,0:T(8,128)}) custom-call(bf16[2,2048,128]{2,1,0:T(8,128)(2,1)} %bitcast.127, f32[8,64,1024]{2,1,0:T(8,128)} %bitcast.131, bf16[8,64,1024]{2,1,0:T(8,128)(2,1)} %bitcast.39.gate_got_ref, f32[2,512,1024]{2,1,0:T(8,128)} %get-tuple-element.98.first_ref.up_ref, ...), custom_call_target="tpu_custom_call" | custom-call | bytes 40000000 | tf_op jit(solution)/shard_map/dkeys/pallas_call | solution.py:1576
  777.4 7.2 back_rope.1
  784.6 7.6 fusion.19
  793.1 7.1 convolution_convert_fusion
  800.2 10.7 %collective-permute-done.5 = bf16[16,64,384]{2,1,0:T(8,128)(2,1)S(1)} collective-permute-done((bf16[16,64,384]{2,1,0:T(8,128)(2,1)S(1)}, bf16[16,64,384]{2,1,0:T(8,128)(2,1)S(1)}, u32[]{:S(2)}, u32[]{:S(2)}) %collective-permute-start.5) | collective-permute-done | bytes 786464 | tf_op jit(solution)/shard_map/ppermute | solution.py:1038
  813.2 88.1 %close.1 = (f32[256,2048]{1,0:T(8,128)}, bf16[16,64,384]{2,1,0:T(8,128)(2,1)}, bf16[8,64,1024]{2,1,0:T(8,128)(2,1)}, f32[32,8,128]{2,1,0:T(8,128)}, bf16[4,64,2048]{2,1,0:T(8,128)(2,1)}) custom-call(bf16[8,256,2048]{2,1,0:T(8,128)(2,1)} %bitcast.111, bf16[16,64,384]{2,1,0:T(8,128)(2,1)} %fusion.10.refs_1_, f32[8,64,1024]{2,1,0:T(8,128)} %bitcast.130, ...), custom_call_target="tpu_custom_call" | custom-call | bytes 120000000 | tf_op jit(solution)/shard_map/close/pallas_call | solution.py:1618
  915.9 4.8 collect.1
  922.8 3.5 fusion.7
  (123 shorter events, 55.5 us)
Async XLA Ops:
  7.2 251.2 %all-gather.3.cloned.1.call-start = ((), (), s32[]{:S(2)}) async-start(), calls=%async_computation | async-start | bytes 9437184 | tf_op jit(solution)/shard_map/all_gather | solution.py:1463
  95.0 629.9 %all-gather.5.cloned.1.call-start = ((), (), s32[]{:S(2)}) async-start(), calls=%async_computation.1 | async-start | bytes 9437184 | tf_op jit(solution)/shard_map/all_gather | solution.py:1541
  157.8 45.7 %collective-permute-start = (bf16[512,1024]{1,0:T(8,128)(2,1)}, bf16[512,1024]{1,0:T(8,128)(2,1)S(1)}, u32[]{:S(2)}, u32[]{:S(2)}) collective-permute-start(bf16[512,1024]{1,0:T(8,128)(2,1)} %bitcast.140), channel_id=1, source_target_pairs={{0,2},{2,0},{1,3},{3,1},{4,6},{6,4},{5,7},{7,5},{8,10},{10,8},{9,1... | collective-permute-start | bytes 3145736 | tf_op jit(solution)/shard_map/ppermute | solution.py:1038
  158.9 38.8 %copy-start.20 = (f32[32,8,128]{2,1,0:T(8,128)S(1)}, f32[32,8,128]{2,1,0:T(8,128)}, u32[]{:S(2)}) copy-start(f32[32,8,128]{2,1,0:T(8,128)} %get-tuple-element.69) | copy-start | bytes 393220
  332.4 34.4 %collective-permute-start.1 = (bf16[256,2048]{1,0:T(8,128)(2,1)}, bf16[256,2048]{1,0:T(8,128)(2,1)S(1)}, u32[]{:S(2)}, u32[]{:S(2)}) collective-permute-start(bf16[256,2048]{1,0:T(8,128)(2,1)} %get-tuple-element.87), channel_id=1, source_target_pairs={{0,16},{16,0},{1,17},{17,1},{2,18},{18,2},{3,19},{19,3},{4,20},{20... | collective-permute-start | bytes 3145736 | tf_op jit(solution)/shard_map/ppermute | solution.py:1038
  333.8 14.6 %copy-start.27 = (bf16[8,256,2048]{2,1,0:T(8,128)(2,1)S(1)}, bf16[8,256,2048]{2,1,0:T(8,128)(2,1)}, u32[]{:S(2)}) copy-start(bf16[8,256,2048]{2,1,0:T(8,128)(2,1)} %get-tuple-element.84) | copy-start | bytes 25165828
  348.3 18.2 %copy-start.1 = (bf16[256,2048]{1,0:T(8,128)(2,1)S(1)}, bf16[256,2048]{1,0:T(8,128)(2,1)}, u32[]{:S(2)}) copy-start(bf16[256,2048]{1,0:T(8,128)(2,1)} %down_ref.3) | copy-start | bytes 3145732
  348.3 18.2 %copy-start.12 = (bf16[256,2048]{1,0:T(8,128)(2,1)S(1)}, bf16[256,2048]{1,0:T(8,128)(2,1)}, u32[]{:S(2)}) copy-start(bf16[256,2048]{1,0:T(8,128)(2,1)} %get-tuple-element.87) | copy-start | bytes 3145732
  368.4 3.7 copy-start.28
  368.8 14.2 %copy-start.5 = (bf16[2,2,256,2048]{3,2,1,0:T(8,128)(2,1)}, bf16[2,2,256,2048]{3,2,1,0:T(8,128)(2,1)S(1)}, u32[]{:S(2)}) copy-start(bf16[2,2,256,2048]{3,2,1,0:T(8,128)(2,1)S(1)} %pad_maximum_fusion) | copy-start | bytes 12582916
  383.0 41.0 %copy-start.2 = (f32[256,2048]{1,0:T(8,128)S(1)}, f32[256,2048]{1,0:T(8,128)}, u32[]{:S(2)}) copy-start(f32[256,2048]{1,0:T(8,128)} %get-tuple-element.81.middle_ref) | copy-start | bytes 6291460
  383.0 41.0 %copy-start.10 = (bf16[1,256,2048]{2,1,0:T(8,128)(2,1)S(1)}, bf16[1,256,2048]{2,1,0:T(8,128)(2,1)}, u32[]{:S(2)}) copy-start(bf16[1,256,2048]{2,1,0:T(8,128)(2,1)} %param.16) | copy-start | bytes 3145732
  483.9 64.9 %collective-permute-start.2 = (bf16[2,256,2048]{2,1,0:T(8,128)(2,1)}, bf16[2,256,2048]{2,1,0:T(8,128)(2,1)S(1)}, u32[]{:S(2)}, u32[]{:S(2)}) collective-permute-start(bf16[2,256,2048]{2,1,0:T(8,128)(2,1)} %get-tuple-element.91), channel_id=1, source_target_pairs={{0,16},{16,0},{1,17},{17,1},{2,18},{18,2},{3,19},{19,3},{4,20},{20... | collective-permute-start | bytes 6291464 | tf_op jit(solution)/shard_map/ppermute | solution.py:1038
  614.8 12.5 %copy-start.25 = (f32[64,1]{0,1:T(1,128)S(1)}, f32[64,1]{0,1:T(1,128)}, u32[]{:S(2)}) copy-start(f32[64,1]{0,1:T(1,128)} %get-tuple-element.142) | copy-start | bytes 772
  614.9 13.2 %copy-start.21 = (f32[32,1,64]{2,1,0:T(1,128)S(1)}, f32[32,1,64]{2,1,0:T(1,128)}, u32[]{:S(2)}) copy-start(f32[32,1,64]{2,1,0:T(1,128)} %get-tuple-element.141) | copy-start | bytes 24580
  614.9 13.9 %copy-start = (bf16[1,256,2048]{2,1,0:T(8,128)(2,1)S(1)}, bf16[1,256,2048]{2,1,0:T(8,128)(2,1)}, u32[]{:S(2)}) copy-start(bf16[1,256,2048]{2,1,0:T(8,128)(2,1)} %param.15) | copy-start | bytes 3145732
  658.9 72.7 %collective-permute-start.3 = (bf16[512,1024]{1,0:T(8,128)(2,1)}, bf16[512,1024]{1,0:T(8,128)(2,1)}, u32[]{:S(2)}, u32[]{:S(2)}) collective-permute-start(bf16[512,1024]{1,0:T(8,128)(2,1)} %get-tuple-element.104.first_ref), channel_id=1, source_target_pairs={{0,2},{2,0},{1,3},{3,1},{4,6},{6,4},{5,7},{7,5},{8,10},{10,8},{9,1... | collective-permute-start | bytes 3145736 | tf_op jit(solution)/shard_map/ppermute | solution.py:1038
  660.4 116.0 %collective-permute-start.4 = (bf16[512,1024]{1,0:T(8,128)(2,1)}, bf16[512,1024]{1,0:T(8,128)(2,1)S(1)}, u32[]{:S(2)}, u32[]{:S(2)}) collective-permute-start(bf16[512,1024]{1,0:T(8,128)(2,1)} %get-tuple-element.110), channel_id=1, source_target_pairs={{0,2},{2,0},{1,3},{3,1},{4,6},{6,4},{5,7},{7,5},{8,10},{10,8},{9,1... | collective-permute-start | bytes 3145736 | tf_op jit(solution)/shard_map/ppermute | solution.py:1038
  718.8 6.0 copy-start.4
  784.6 8.5 copy-start.8
  784.6 8.5 copy-start.9
  792.3 18.5 %collective-permute-start.5 = (bf16[16,64,384]{2,1,0:T(8,128)(2,1)S(1)}, bf16[16,64,384]{2,1,0:T(8,128)(2,1)S(1)}, u32[]{:S(2)}, u32[]{:S(2)}) collective-permute-start(bf16[16,64,384]{2,1,0:T(8,128)(2,1)S(1)} %fusion.15), channel_id=1, source_target_pairs={{0,16},{16,0},{1,17},{17,1},{2,18},{18,2},{3,19},{19,3},{4,20},{20... | collective-permute-start | bytes 2359304 | tf_op jit(solution)/shard_map/ppermute | solution.py:1038
  904.5 8.5 copy-start.3
  904.6 17.4 %copy-start.16 = (f32[64,512]{1,0:T(8,128)}, f32[64,512]{1,0:T(8,128)S(1)}, u32[]{:S(2)}) copy-start(f32[64,512]{1,0:T(8,128)S(1)} %reshape.344) | copy-start | bytes 393220
  906.7 4.3 copy-start.14
  915.9 6.2 copy-start.17
  915.9 6.2 copy-start.18
  915.9 6.2 copy-start.19
  922.8 4.2 copy-start.22
  922.8 4.2 copy-start.23
  922.8 4.2 copy-start.24
  922.8 4.2 copy-start.26
  (5 other events, 6.9 us)
Sparse Core Ops, SparseCore 0:
  95.1 68.9 all-gather.2
  627.5 97.3 all-gather.4

commit v3 on v2

--- a/solution.py
+++ b/solution.py
@@ -722,112 +722,118 @@
 
 
 def douts_kernel(
-    over_dp, parts_ref, gate_ref, gate_got_ref, up_ref, up_got_ref, gate_made_ref, out_ref, gate_away_ref,
-    up_away_ref, gate_kept_ref, send, recv, local, held, own, got, sem, d_send, d_recv,
+    parts_ref, gate_ref, gate_got_ref, up_ref, up_got_ref, out_ref, gate_away_ref, up_away_ref, send, recv, local,
+    held, own, got, sem,
 ):
     hi = lax.axis_index("hi")
     loads = [
         [local_copy(ref.at[1 - hi], own.at[k], sem.at[k, 0]), local_copy(got_ref, got.at[k], sem.at[k, 1])]
         for k, (ref, got_ref) in enumerate(((gate_ref, gate_got_ref), (up_ref, up_got_ref)))
     ]
-    loads.append([local_copy(gate_ref.at[hi], own.at[2], sem.at[2, 0])])
-    greet(square_peers()[2] + (dp_peers() if over_dp else []))
-    loads[2] += pair_begin(gate_made_ref, hi, got.at[2], d_send.at[0], d_recv.at[0], over_dp)
+    greet(square_peers()[2])
     copies = swap_begin(parts_ref, out_ref, send, recv, local, held)
-    for k, target in enumerate((gate_away_ref, up_away_ref, gate_kept_ref)):
+    for k, target in enumerate((gate_away_ref, up_away_ref)):
         wait_all(loads[k])
-        target[...] = (own[k] + got[k].astype(F32)).astype(target.dtype)
+        target[...] = (own[k] + got[k].astype(F32)).astype(BF16)
     finish(copies)
 
 
+def sum_three(place, own_ref, over_dp_ref, over_hi_ref, own, over_dp, over_hi, sem):
+    return [
+        local_copy(own_ref.at[place], own, sem.at[0]),
+        local_copy(over_dp_ref, over_dp, sem.at[1]),
+        local_copy(over_hi_ref, over_hi, sem.at[2]),
+    ]
+
+
 def dkeys_kernel(
-    over_dp, dkv_ref, gate_ref, gate_got_ref, up_ref, up_made_ref, first_ref, other_ref, gates_ref, up_kept_ref,
-    k_send, k_recv, g_send, g_recv, g_local, g_held, own, got, made, sem, up_own, up_got, d_send, d_recv,
+    dkv_ref, gate_ref, gate_dp_ref, gate_hi_ref, other_ref, gates_ref, k_send, k_recv, g_send, g_recv, g_local,
+    g_held, own, over_dp, over_hi, made, sem,
 ):
     hi = lax.axis_index("hi")
-    loads = [local_copy(gate_ref, own, sem.at[0]), local_copy(gate_got_ref, got, sem.at[1])]
-    up_loads = [local_copy(up_ref.at[hi], up_own, sem.at[2])]
-    greet(square_peers()[2] + [other_hi()] + (dp_peers() if over_dp else []))
+    loads = sum_three(hi, gate_ref, gate_dp_ref, gate_hi_ref, own, over_dp, over_hi, sem)
+    greet(square_peers()[2] + [other_hi()])
     copies = [remote(dkv_ref.at[1], other_ref, k_send.at[0], k_recv.at[0], other_hi())]
-    up_loads += pair_begin(up_made_ref, hi, up_got, d_send.at[0], d_recv.at[0], over_dp)
     wait_all(loads)
-    made[...] = (own[...] + got[...].astype(F32)).astype(BF16)
+    made[...] = (own[...] + over_dp[...].astype(F32) + over_hi[...].astype(F32)).astype(BF16)
     copies += swap_begin(made, gates_ref, g_send, g_recv, g_local, g_held)
-    wait_all(up_loads)
-    up_kept_ref[...] = up_own[...] + up_got[...].astype(F32)
     finish(copies)
 
 
-def own_out_begin(out_ref, outs_ref, send, recv, local, held):
-    dp, hi, lo = (lax.axis_index(a) for a in ("dp", "hi", "lo"))
-    away = dp != lo
-    mine = dp * 2 + hi
-
-    def push(a, b, start):
-        hi_to, lo_to = lax.rem(hi + a, 2), lax.rem(lo + b, 2)
-        copy = pltpu.make_async_remote_copy(
-            src_ref=out_ref.at[hi_to, lo_to],
-            dst_ref=outs_ref.at[mine],
-            send_sem=send.at[2 * a + b],
-            recv_sem=recv.at[mine],
-            device_id={"dp": lo, "hi": hi_to, "lo": lo_to},
+class OwnOut:
+    def __init__(self, out_ref, outs_ref, send, recv, local, own, got, made):
+        self.outs_ref, self.made, self.send, self.recv, self.local = outs_ref, made, send, recv, local
+        self.own, self.got = own, got
+        self.dp, self.hi, self.lo = (lax.axis_index(a) for a in ("dp", "hi", "lo"))
+        self.load = local_copy(out_ref, own, local.at[0])
+        self.over = remote(out_ref, got, send.at[0], recv.at[0], dp_peers()[0])
+
+    def push(self, a, b):
+        hi, lo = lax.rem(self.hi + a, 2), lax.rem(self.lo + b, 2)
+        return pltpu.make_async_remote_copy(
+            src_ref=self.made.at[hi, lo],
+            dst_ref=self.outs_ref.at[self.hi],
+            send_sem=self.send.at[1 + 2 * a + b],
+            recv_sem=self.recv.at[1 + self.hi],
+            device_id={"hi": hi, "lo": lo},
             device_id_type=MESH_ID,
         )
-        if start:
-            copy.start()
-        else:
-            copy.wait_send()
-
-    def own_copy():
-        copy = local_copy(out_ref.at[hi, lo], held, local)
-        copy.wait()
-        copy = local_copy(held, outs_ref.at[mine], local)
-        copy.wait()
-
-    for a, b in ((0, 1), (1, 0), (1, 1)):
-        push(a, b, True)
-    pl.when(away)(lambda: push(0, 0, True))
-
-    def arrive(slot):
-        pltpu.make_async_remote_copy(
-            src_ref=out_ref.at[0, 0],
-            dst_ref=outs_ref.at[slot],
-            send_sem=send.at[0],
-            recv_sem=recv.at[slot],
-            device_id={"dp": lo},
-            device_id_type=MESH_ID,
-        ).wait_recv()
-
-    def end():
-        pl.when(jnp.logical_not(away))(own_copy)
-        for a, b in ((0, 1), (1, 0), (1, 1)):
-            push(a, b, False)
-        pl.when(away)(lambda: push(0, 0, False))
-        for d in range(2):
-            for h in range(2):
-                itself = (d == dp) & (h == hi) & (dp == lo)
-                pl.when(jnp.logical_not(itself))(functools.partial(arrive, 2 * d + h))
-
-    return end
+
+    def own_copy(self):
+        return pltpu.make_async_copy(
+            self.made.at[self.hi, self.lo], self.outs_ref.at[self.hi], self.local.at[1]
+        )
+
+    def turn(self):
+        self.load.wait()
+        self.over.wait()
+        self.made[...] = (self.own[...].astype(F32) + self.got[...].astype(F32)).astype(BF16)
+
+        @pl.when(self.dp == self.lo)
+        def _():
+            for a, b in ((0, 1), (1, 0), (1, 1)):
+                self.push(a, b).start()
+            self.own_copy().start()
+
+    def wait(self):
+        @pl.when(self.dp == self.lo)
+        def _():
+            for a, b in ((0, 1), (1, 0), (1, 1)):
+                self.push(a, b).wait_send()
+            self.own_copy().wait()
+
+        for h in range(2):
+
+            @pl.when(jnp.logical_not((h == self.hi) & (self.dp == self.lo)))
+            def _(h=h):
+                pltpu.make_async_remote_copy(
+                    src_ref=self.made.at[0, 0],
+                    dst_ref=self.outs_ref.at[h],
+                    send_sem=self.send.at[1],
+                    recv_sem=self.recv.at[1 + h],
+                    device_id={"lo": 1 - self.lo},
+                    device_id_type=MESH_ID,
+                ).wait_recv()
 
 
 def close_kernel(with_out, *refs):
     refs = iter(refs)
     take = lambda n: [next(refs) for _ in range(n)]
-    parts_ref, heads_ref, up_ref, up_got_ref, square_ref = take(5)
+    parts_ref, heads_ref, up_ref, up_dp_ref, up_hi_ref, square_ref = take(6)
     out_rows_ref = next(refs) if with_out else None
     total_ref, head_ref, ups_ref, squares_ref = take(4)
     outs_ref = next(refs) if with_out else None
     scatter = take(9)
     h_send, h_recv, s_send, s_recv, local, h_held = take(6)
     swap = take(4)
-    own, got, made, sem = take(4)
-    out_scratch = take(4) if with_out else None
+    own, over_dp, over_hi, made, sem = take(5)
+    out_scratch = take(6) if with_out else None
     mine = device_place()
     peers, seq = every_peer(), seq_peers()
     place = seq_place({a: lax.axis_index(a) for a in SEQ})
     loads = scatter_load(parts_ref, scatter)
-    up_loads = [local_copy(up_ref, own, sem.at[0]), local_copy(up_got_ref, got, sem.at[1])]
+    hi = lax.axis_index("hi")
+    up_loads = sum_three(hi, up_ref, up_dp_ref, up_hi_ref, own, over_dp, over_hi, sem)
     greet(peers)
     copies = [
         Carried(heads_ref.at[place], head_ref.at[place], h_held, local.at[0]),
@@ -839,14 +845,14 @@
     for k, (to, source) in enumerate(seq):
         part = heads_ref.at[seq_place(to)]
         copies.append(remote(part, head_ref.at[place], h_send.at[k], h_recv.at[k], to))
-    end = own_out_begin(out_rows_ref, outs_ref, *out_scratch) if with_out else None
+    own_out = OwnOut(out_rows_ref, outs_ref, *out_scratch) if with_out else None
     wait_all(up_loads)
-    made[...] = (own[...] + got[...].astype(F32)).astype(BF16)
+    made[...] = (own[...] + over_dp[...].astype(F32) + over_hi[...].astype(F32)).astype(BF16)
     copies += swap_begin(made, ups_ref, *swap)
-    scatter_end_square(loads, mates, total_ref, scatter)
+    scatter_end_square(loads, mates, total_ref, scatter, own_out.turn if with_out else None)
+    finish(copies)
     if with_out:
-        end()
-    finish(copies)
+        own_out.wait()
 
 
 def remote_to(source, target, sems_of, kind, piece, to):
@@ -878,7 +884,8 @@
     }
 
 
-def scatter_end_square(loads, from_mate, out_ref, scratch):
+def scatter_end_square(loads, from_mate, out_ref, scratch, between=None, work=()):
+    work = list(work)
     mine, mates, made, got_across, got_side, got_next = scratch[:6]
     sems_of = scratch[6:8]
     blk, lo, mate, side = square_places()
@@ -904,7 +911,9 @@
         )
     loads[1].wait()
     loads[2].wait()
-    for k, p in ((1, 0), (2, 2), (1, 1), (2, 3), (1, 2), (2, 0), (1, 3), (2, 1)):
+    for n, (k, p) in enumerate(((1, 0), (2, 2), (1, 1), (2, 3), (1, 2), (2, 0), (1, 3), (2, 1))):
+        if work and n % 2 == 0:
+            work.pop(0)()
         total = summed(k, p)
         if (k == 1) == (p >= 2):
             sent[0, p].wait_recv()
@@ -918,6 +927,10 @@
             p,
             to_side if k == 1 else to_next,
         )
+    for one in work:
+        one()
+    if between is not None:
+        between()
     loads[3].wait()
     for p in range(PIECES):
         total = summed(3, p)
@@ -970,64 +983,97 @@
     )(parts.astype(BF16).reshape(8, tok, width), *first)
 
 
-def pair_begin(parts_ref, place, out_ref, send, recv, over_dp):
-    if not over_dp:
-        return [local_copy(parts_ref.at[place], out_ref, recv)]
-    return [remote(parts_ref.at[place], out_ref, send, recv, dp_peers()[0])]
-
-
 def scatter_down_kernel(
-    over_dp, parts_ref, down_ref, got_ref, gate_ref, up_ref, out_ref, sum_ref, gate_got_ref, up_got_ref, *scratch
+    parts_ref, down_ref, got_ref, rows_ref, dgate_ref, dup_ref, out_ref, sum_ref, gate_own_ref, up_own_ref,
+    gate_stay_ref, up_stay_ref, gate_got_ref, up_got_ref, *scratch,
 ):
-    scratch, (own, got, away, came, sem, send, recv) = scratch[:9], scratch[9:]
-    hi = lax.axis_index("hi")
+    scratch, rest = scratch[:9], scratch[9:]
+    own, got, away, came, sem, send, recv, left, gate_right, up_right, gate_away, up_away, w_sem = rest
+    dp, hi = lax.axis_index("dp"), lax.axis_index("hi")
+    part = left.shape[2]
+    blocks = ((1 - dp, 1 - hi), (dp, 1 - hi), (1 - dp, hi), (dp, hi))
+
+    def load_left(n):
+        d, h = blocks[n]
+        cols = pl.ds(pl.multiple_of((d * 2 + h) * part, part), part)
+        return local_copy(rows_ref.at[:, cols], left.at[n % 2], w_sem.at[n % 2])
+
+    rights = [local_copy(dgate_ref, gate_right, w_sem.at[2]), local_copy(dup_ref, up_right, w_sem.at[3])]
+    lefts = {0: load_left(0), 1: load_left(1)}
     down = sum_begin(down_ref, got_ref, 1 - hi, own, got, sem)
     loads = scatter_load(parts_ref, scratch)
-    greet(square_greeting() + [other_hi()] + (dp_peers() if over_dp else []))
+    greet(square_greeting() + [other_hi()] + dp_peers())
     mates = scatter_mates(parts_ref, scratch)
-    pairs = pair_begin(gate_ref, 1 - hi, gate_got_ref, send.at[1], recv.at[1], over_dp)
-    pairs += pair_begin(up_ref, 1 - hi, up_got_ref, send.at[2], recv.at[2], over_dp)
     wait_all(down)
     away[...] = (own[...] + got[...].astype(F32)).astype(BF16)
     over = remote(away, came, send.at[0], recv.at[0], other_hi())
     down = sum_begin(down_ref, got_ref, hi, own, got, sem)
-    scatter_end_square(loads, mates, out_ref, scratch)
+    pairs = []
+
+    def gradient(n, up):
+        if not up:
+            lefts[n].wait()
+        if n == 0:
+            rights[up].wait()
+        total = dot32(left[n % 2], (up_right if up else gate_right)[...], ((0,), (0,)))
+        if n == 0:
+            target, got_there = (up_away, up_got_ref) if up else (gate_away, gate_got_ref)
+            target[...] = total.astype(BF16)
+            pairs.append(remote(target, got_there, send.at[1 + up], recv.at[1 + up], dp_peers()[0]))
+        elif n == 2:
+            (up_stay_ref if up else gate_stay_ref)[...] = total.astype(BF16)
+        else:
+            (up_own_ref if up else gate_own_ref)[blocks[n][1]] = total
+        if up and n < 2:
+            lefts[n + 2] = load_left(n + 2)
+
+    work = [functools.partial(gradient, n, up) for n in range(4) for up in range(2)]
+    scatter_end_square(loads, mates, out_ref, scratch, work=work)
     wait_all(down)
     over.wait()
     sum_ref[...] = own[...] + got[...].astype(F32) + came[...].astype(F32)
     wait_all(pairs)
 
 
-def scatter_down(parts, number, down, gate_away, up_away):
+def scatter_down(parts, number, down, rows, dgate, dup):
     count, width = parts.shape
     tok = count // 8
     part = down[0].shape[1:]
-    anywhere = pl.BlockSpec(memory_space=pl.ANY)
+    depth, cols = dgate.shape
+    grad = (rows.shape[1] // 4, cols)
+    anywhere, inside = pl.BlockSpec(memory_space=pl.ANY), pl.BlockSpec(memory_space=pltpu.VMEM)
     return pl.pallas_call(
-        functools.partial(scatter_down_kernel, lax.axis_size("dp") == 2),
-        in_specs=[anywhere] * 5,
-        out_specs=[pl.BlockSpec(memory_space=pltpu.VMEM)] * 2 + [anywhere] * 2,
+        scatter_down_kernel,
+        in_specs=[anywhere] * 6,
+        out_specs=[inside] * 6 + [anywhere] * 2,
         out_shape=[
             jax.ShapeDtypeStruct((tok, width), F32),
             jax.ShapeDtypeStruct(part, F32),
-            jax.ShapeDtypeStruct(gate_away.shape[1:], BF16),
-            jax.ShapeDtypeStruct(up_away.shape[1:], BF16),
+            jax.ShapeDtypeStruct((2,) + grad, F32),
+            jax.ShapeDtypeStruct((2,) + grad, F32),
+        ]
+        + [jax.ShapeDtypeStruct(grad, BF16)] * 4,
+        scratch_shapes=scatter_scratch(tok, width)
+        + [pltpu.VMEM(part, F32)]
+        + [pltpu.VMEM(part, BF16)] * 3
+        + [pltpu.SemaphoreType.DMA((2,))]
+        + sems(3)
+        + [
+            pltpu.VMEM((2, depth, grad[0]), BF16),
+            pltpu.VMEM((depth, cols), BF16),
+            pltpu.VMEM((depth, cols), BF16),
+            pltpu.VMEM(grad, BF16),
+            pltpu.VMEM(grad, BF16),
+            pltpu.SemaphoreType.DMA((4,)),
         ],
-        scratch_shapes=scatter_scratch(tok, width)
-        + [
-            pltpu.VMEM(part, F32),
-            pltpu.VMEM(part, BF16),
-            pltpu.VMEM(part, BF16),
-            pltpu.VMEM(part, BF16),
-            pltpu.SemaphoreType.DMA((2,)),
-        ]
-        + sems(3),
         compiler_params=pltpu.CompilerParams(
             collective_id=number, has_side_effects=True, vmem_limit_bytes=VMEM_LIMIT
         ),
-        cost_estimate=pl.CostEstimate(flops=0, bytes_accessed=160_000_000, transcendentals=0),
+        cost_estimate=pl.CostEstimate(
+            flops=4 * depth * cols * rows.shape[1], bytes_accessed=160_000_000, transcendentals=0
+        ),
         name="scatter_down",
-    )(parts.reshape(8, tok, width), *down, gate_away, up_away)
+    )(parts.reshape(8, tok, width), *down, rows, dgate, dup)
 
 
 def swap_square(blocks):
@@ -1287,7 +1333,15 @@
     )(grad, gate_slope, up_slope, gate_weight, up_weight, down_weight, first)
 
 
-def deal_kernel(places, wide, gate_ref, up_ref, gates_ref, ups_ref):
+def deal_kernel(
+    key_head, places, wide, query_ref, key_ref, value_ref, gate_ref, up_ref, heads_ref, gates_ref, ups_ref
+):
+    columns, k_columns = query_ref.shape[1] // 8, key_ref.shape[1] // 8
+    for f in range(8):
+        g = key_head(f)
+        cols, k_cols = slice(g * columns, g * columns + columns), slice(g * k_columns, g * k_columns + k_columns)
+        heads_ref[f, :, :columns] = query_ref[:, cols]
+        heads_ref[f, :, columns:] = jnp.concatenate([key_ref[:, k_cols], value_ref[:, k_cols]], axis=1)
     for at, (f, to) in enumerate(places):
         here, there = slice(at * wide, at * wide + wide), slice(to * wide, to * wide + wide)
         gates_ref[f, :, there] = gate_ref[:, here]
@@ -1305,6 +1359,46 @@
         dup_ref[:, here] = dup
         total += gate_ref[:, here].astype(F32) * dgate + up_ref[:, here].astype(F32) * dup
     dgain_ref[...] = jnp.sum(total, axis=1, keepdims=True) / gain_ref[...]
+
+
+def final_kernel(
+    key_head, places, wide, first_ref, middle_ref, rows_ref, gain_ref, heads_ref, query_ref, key_ref, value_ref,
+    gates_ref, ups_ref, gate_ref, up_ref, small_ref, outs_ref, down_ref, dhidden_ref, dquery_ref, dkey_ref,
+    dvalue_ref, dgain_one_ref, dgate_ref, dup_ref, dgain_two_ref, dout_ref, ddown_ref,
+):
+    rows_w = gate_ref.shape[0]
+    normal, inverse = norm_parts(rows_ref[...].astype(F32))
+    grad = first_ref[...] * gain_ref[...]
+    dhidden_ref[...] = middle_ref[...] + inverse * (
+        grad - normal * jnp.mean(grad * normal, axis=-1, keepdims=True)
+    )
+    gains = jnp.transpose(jnp.broadcast_to(small_ref[0:1, :], (128, 128)))[:, 0:1]
+    columns = query_ref.shape[1] // 8
+    k_columns = key_ref.shape[1] // 8
+    total = jnp.zeros((rows_w, columns), F32)
+    k_total = jnp.zeros((rows_w, k_columns), F32)
+    for f in range(8):
+        b, l, g = f // 2, f % 2, key_head(f)
+        both = heads_ref[b * 4 + l].astype(F32) + heads_ref[b * 4 + 2 + l].astype(F32)
+        cols, k_cols = slice(g * columns, g * columns + columns), slice(g * k_columns, g * k_columns + k_columns)
+        dquery = both[:, :columns]
+        dkey, dvalue = both[:, columns : columns + k_columns], both[:, columns + k_columns :]
+        dquery_ref[:, cols], dkey_ref[:, k_cols], dvalue_ref[:, k_cols] = dquery, dkey, dvalue
+        total += query_ref[:, cols].astype(F32) * dquery
+        k_total += key_ref[:, k_cols].astype(F32) * dkey + value_ref[:, k_cols].astype(F32) * dvalue
+    dgain_one_ref[...] = (
+        jnp.sum(total, axis=1, keepdims=True) + jnp.sum(k_total, axis=1, keepdims=True)
+    ) / gains[:rows_w]
+    total = jnp.zeros((rows_w, wide), F32)
+    for at, (f, to) in enumerate(places):
+        here, there = slice(at * wide, at * wide + wide), slice(to * wide, to * wide + wide)
+        dgate, dup = gates_ref[f, :, there].astype(F32), ups_ref[f, :, there].astype(F32)
+        dgate_ref[:, here] = dgate
+        dup_ref[:, here] = dup
+        total += gate_ref[:, here].astype(F32) * dgate + up_ref[:, here].astype(F32) * dup
+    dgain_two_ref[...] = jnp.sum(total, axis=1, keepdims=True) / gains[rows_w : 2 * rows_w]
+    dout_ref[...] = outs_ref[0].astype(F32) + outs_ref[1].astype(F32)
+    ddown_ref[...] = down_ref[...]
 
 
 def shards(
@@ -1384,10 +1478,6 @@
 
     q_cols = w_query.shape[1] // group
     k_cols = key_projection.shape[1] // group
-    head_parts = jnp.concatenate(
-        [head_columns(w) for w in (w_query, key_projection, value_projection)], axis=2
-    )
-    head_wide = head_parts.shape[2]
     ff_places = [
         (b * lo_n + l, d * hi_n + h)
         for d in range(dp_n)
@@ -1398,14 +1488,19 @@
     part_shape = jax.ShapeDtypeStruct((group, rows_w, ff_part), BF16)
     params = pltpu.CompilerParams(vmem_limit_bytes=VMEM_LIMIT)
     if units_w % 128 == 0:
-        gate_parts, up_parts = pl.pallas_call(
-            functools.partial(deal_kernel, ff_places, units_w),
-            out_shape=[part_shape, part_shape],
+        head_shape = jax.ShapeDtypeStruct((group, rows_w, q_cols + 2 * k_cols), BF16)
+        head_parts, gate_parts, up_parts = pl.pallas_call(
+            functools.partial(deal_kernel, key_head, ff_places, units_w),
+            out_shape=[head_shape, part_shape, part_shape],
             compiler_params=params,
             name="deal",
-        )(w_gate, w_up)
+        )(w_query, key_projection, value_projection, w_gate, w_up)
     else:
+        head_parts = jnp.concatenate(
+            [head_columns(w) for w in (w_query, key_projection, value_projection)], axis=2
+        )
         gate_parts, up_parts = unit_columns(w_gate), unit_columns(w_up)
+    head_wide = head_parts.shape[2]
 
     pad = jnp.zeros((7 * 128 + 128 - 2 * rows_w - 1,), F32)
     small = jnp.concatenate(
@@ -1527,81 +1622,71 @@
     grad_gate_rows, grad_up_rows, grad_normal = ff_back(
         branch, gate_slope, up_slope, gate_weight, up_weight, down_weight, down_sum[0], 2 * tok
     )
-    gate_sum = weight_grad_start(normed_two, grad_gate_rows, down_sum[0])
-    up_sum = weight_grad_start(normed_two, grad_up_rows, gate_sum[0])
-    down_got = swap_pair(down_sum[1], "dp") if dp_n == 2 else down_sum[1]
-    grad_normal, down_sum, gate_got, up_got = scatter_down(
-        grad_normal, 9, (down_sum[0], down_got), gate_sum[1], up_sum[1]
-    )
+    if dp_n == 2:
+        down_got = swap_pair(down_sum[1], "dp")
+        grad_normal, down_sum, gate_own, up_own, gate_stay, up_stay, gate_got, up_got = scatter_down(
+            grad_normal, 9, (down_sum[0], down_got), normed_two, grad_gate_rows, grad_up_rows
+        )
+        gate_stay, up_stay = swap_pair(gate_stay, "dp"), swap_pair(up_stay, "dp")
+    else:
+        grad_normal = scatter_square(grad_normal, 9)
+        down_sum = scatter_end(scatter_start(down_sum[0], "hi"), "hi")
+        gate_own = weight_grad_start(normed_two, grad_gate_rows, grad_normal)[0]
+        up_own = weight_grad_start(normed_two, grad_up_rows, grad_normal)[0]
+        gate_stay = up_stay = gate_got = up_got = jnp.zeros(gate_own.shape[1:], BF16)
     grad_normal = outer(grad_normal)
 
     grad_middle, attn_rows, grad_mixed = out_back(
-        grad_normal, middle, grad_result, gain_two, out_weight, up_sum[0], q_cols, key_head, to_outer, reblock
-    )
-    square_attn = lax.all_gather(attn_rows, SQUARE, axis=0, tiled=True)
+        grad_normal, middle, grad_result, gain_two, out_weight, grad_normal, q_cols, key_head, to_outer, reblock
+    )
     part_shape = (part_rows, ff_part)
     anywhere, inside = pl.BlockSpec(memory_space=pl.ANY), pl.BlockSpec(memory_space=pltpu.VMEM)
-    over_dp = dp_n == 2
-    dout, gate_away, up_away, gate_kept = pl.pallas_call(
-        functools.partial(douts_kernel, over_dp),
-        in_specs=[anywhere] * 6,
-        out_specs=[anywhere] + [inside] * 3,
+    dout, gate_away, up_away = pl.pallas_call(
+        douts_kernel,
+        in_specs=[anywhere] * 5,
+        out_specs=[anywhere] + [inside] * 2,
         out_shape=[jax.ShapeDtypeStruct(grad_mixed.shape, BF16)]
-        + [jax.ShapeDtypeStruct(part_shape, dtype) for dtype in (BF16, BF16, F32)],
+        + [jax.ShapeDtypeStruct(part_shape, BF16)] * 2,
         scratch_shapes=swap_scratch((tok, q_cols))
         + [
-            pltpu.VMEM((3,) + part_shape, F32),
-            pltpu.VMEM((3,) + part_shape, BF16),
-            pltpu.SemaphoreType.DMA((3, 2)),
-        ]
-        + sems(1),
+            pltpu.VMEM((2,) + part_shape, F32),
+            pltpu.VMEM((2,) + part_shape, BF16),
+            pltpu.SemaphoreType.DMA((2, 2)),
+        ],
         compiler_params=pltpu.CompilerParams(
             collective_id=6, has_side_effects=True, vmem_limit_bytes=VMEM_LIMIT
         ),
         cost_estimate=pl.CostEstimate(flops=0, bytes_accessed=40_000_000, transcendentals=0),
         name="douts",
-    )(grad_mixed, gate_sum[0], gate_got, up_sum[0], up_got, gate_sum[1])
-    gate_got, up_got = swap_pair(gate_away, "hi"), swap_pair(up_away, "hi")
+    )(grad_mixed, gate_own, gate_got, up_own, up_got)
+    columns = (group, rows_w, ff_part)
+
+    gate_dp, up_dp = gate_stay.reshape(columns), up_stay.reshape(columns)
+    gate_hi, up_hi = (swap_pair(a, "hi").reshape(columns) for a in (gate_away, up_away))
+    square_attn = lax.all_gather(attn_rows, SQUARE, axis=0, tiled=True)
     dout = dout.reshape(blk_n, unit, q_cols)
     dq, dkv = attend_back(scalars, q, kv, other_kv, dout, out_heads, log_heads, gate_away)
     dkv = dkv.reshape(2, group * tok, 2 * k_cols)
-    columns = (group, rows_w, ff_part)
-    sum_scratch = [
-        pltpu.VMEM(columns, F32),
-        pltpu.VMEM(columns, BF16),
-        pltpu.VMEM(columns, BF16),
-        pltpu.SemaphoreType.DMA((3,)),
-    ]
+    sum_scratch = [pltpu.VMEM(columns, F32)] + [pltpu.VMEM(columns, BF16)] * 3
+    sum_scratch.append(pltpu.SemaphoreType.DMA((3,)))
     own_out = dot32(out_heads.reshape(group * tok, q_cols), square_attn, ((0,), (0,))).astype(BF16)
-    other_dkv, gate_parts, up_kept = pl.pallas_call(
-        functools.partial(dkeys_kernel, over_dp),
-        in_specs=[anywhere] * 6,
-        out_specs=[anywhere, anywhere, inside],
-        out_shape=[
-            jax.ShapeDtypeStruct(dkv.shape[1:], BF16),
-            jax.ShapeDtypeStruct(columns, BF16),
-            jax.ShapeDtypeStruct(part_shape, F32),
-        ],
-        scratch_shapes=sems(1)
-        + swap_scratch((rows_w, ff_part))
-        + sum_scratch
-        + [pltpu.VMEM(part_shape, F32), pltpu.VMEM(part_shape, BF16)]
-        + sems(1),
-        compiler_params=pltpu.CompilerParams(
-            collective_id=7, has_side_effects=True, vmem_limit_bytes=VMEM_LIMIT
-        ),
-        cost_estimate=pl.CostEstimate(flops=0, bytes_accessed=40_000_000, transcendentals=0),
-        name="dkeys",
-    )(dkv, gate_kept.reshape(columns), gate_got.reshape(columns), up_sum[0], up_sum[1], own_out)
+    other_dkv, gate_parts = comm_call(
+        dkeys_kernel,
+        7,
+        [dkv, gate_own.reshape((hi_n,) + columns), gate_dp, gate_hi],
+        [(dkv.shape[1:], BF16), (columns, BF16)],
+        sems(1) + swap_scratch((rows_w, ff_part)) + sum_scratch,
+        "dkeys",
+    )
     dqkv = back_rope(
-        hi_index, dq.reshape(group * tok, q_cols), dkv[0], other_dkv, tables, up_got, tok
+        hi_index, dq.reshape(group * tok, q_cols), dkv[0], other_dkv, tables, up_hi, tok
     )
     head_grads = dot32(normed_one, dqkv, ((0,), (0,))).reshape(dp_n, -1, rows_w, head_wide)
     head_grads = scatter_end(scatter_start(head_grads, "dp"), "dp").astype(BF16)
     grad_first = dot32(dqkv, qkv_weight, ((1,), (1,))).astype(BF16)
     with_out = dp_n == 2 and rows_w * hi_n * lo_n == q_cols
     arrays = [grad_first.reshape(group, tok, width), head_grads]
-    arrays += [up_kept.reshape(columns), up_got.reshape(columns), squares]
+    arrays += [up_own.reshape((hi_n,) + columns), up_dp, up_hi, squares]
     shapes = [
         ((tok, width), F32),
         (head_grads.shape, BF16),
@@ -1613,8 +1698,9 @@
     scratch += swap_scratch((rows_w, ff_part)) + sum_scratch
     if with_out:
         arrays.append(own_out.reshape(hi_n, lo_n, rows_w, width))
-        shapes.append(((dp_n * hi_n, rows_w, width), BF16))
-        scratch += sems(4) + [pltpu.SemaphoreType.DMA, pltpu.VMEM((rows_w, width), BF16)]
+        shapes.append(((hi_n, rows_w, width), BF16))
+        scratch += sems(5) + [pltpu.SemaphoreType.DMA((2,))]
+        scratch += [pltpu.VMEM((hi_n, lo_n, rows_w, width), BF16)] * 3
     grad_first, head_grads, up_parts, squares, *outs = pl.pallas_call(
         functools.partial(close_kernel, with_out),
         in_specs=[anywhere] * len(arrays),
@@ -1628,6 +1714,53 @@
         name="close",
     )(*arrays)
     mse_loss = jnp.sum(squares[:, 0, 0]) / (width * valid_count)
+    if with_out and units_w % 128 == 0 and 2 * rows_w == 128:
+        shape = lambda *dims: jax.ShapeDtypeStruct(dims, F32)
+        grads = pl.pallas_call(
+            functools.partial(final_kernel, key_head, ff_places, units_w),
+            out_shape=[
+                shape(tok, width),
+                shape(*w_query.shape),
+                shape(*key_projection.shape),
+                shape(*value_projection.shape),
+                shape(rows_w, 1),
+                shape(*w_gate.shape),
+                shape(*w_up.shape),
+                shape(rows_w, 1),
+                shape(*w_out.shape),
+                shape(*w_down.shape),
+            ],
+            compiler_params=params,
+            name="final",
+        )(
+            grad_first,
+            grad_middle,
+            hidden[0],
+            gain_one,
+            head_grads,
+            w_query,
+            key_projection,
+            value_projection,
+            gate_parts,
+            up_parts,
+            w_gate,
+            w_up,
+            small,
+            outs[0],
+            down_sum,
+        )
+        return (
+            result.astype(BF16)[None],
+            mse_loss,
+            grads[0][None],
+            grads[4][:, 0],
+            *grads[1:4],
+            grads[8],
+            grads[7][:, 0],
+            grads[5],
+            grads[6],
+            grads[9],
+        )
     if with_out:
         grad_out = jnp.sum(outs[0].astype(F32), axis=0)
     else:

time: 943 us -> 928 us (0.984)
  Pallas kernels: 776 us -> 736 us
  waiting for transfers between devices: 19.3 us -> 50.6 us
  local copies, waits for them, and re-layouts: 29.5 us -> 17.2 us
    pallas_call x5 -> x4, Pallas kernels: 147 us -> 105 us  [the longest x1 71.4 us: scatter_down(): pl.pallas_call(scatter_down_kernel, in_specs=[anywhere] * 6, out_specs=[i...]
    pallas_call x5 -> x6, Pallas kernels: 281 us -> 317 us  [comm_call(): pl.pallas_call(kernel, in_specs=[anywhere] * len(arrays), out_specs=[anyw...]
    ppermute x6 -> x8, waiting for transfers between devices: 15.2 us -> 50.5 us  [swap_pair(): return lax.ppermute(block, axis, [(0, 1), (1, 0)])]
    pallas_call x3 -> x1, Pallas kernels: 45 us -> 15.5 us  [weight_grad_start(): pl.pallas_call(weight_grad_kernel, grid_spec=pltpu.PrefetchScalarGridSpec...]
  transfers between devices with their start and end apart: 8 -> 10, of which waited for: 3 -> 5; matrix products, arithmetic and copies ran while one was open for 6% -> 7% of each run, Pallas kernels for 37% -> 33%
where the time goes in v3:
time: 928 us; the launch traced here: 915 us
  Pallas kernels  736 us (79%)
  matrix products  67.6 us (7%)
  waiting for transfers between devices  50.6 us (5%)
  between operations  18.4 us (2%)
  local copies, waits for them, and re-layouts  17.2 us (2%)
  other arithmetic  15.8 us (2%)
  starting transfers between devices  9.69 us (1%)
    pallas_call x6, Pallas kernels, comm_call(): pl.pallas_call(kernel, in_specs=[anywhere] * len(arrays), out_specs=[anyw...  317 us
    pallas_call x1, Pallas kernels, shards(): pl.pallas_call(functools.partial(close_kernel, with_out), in_specs=[anywh...  84.1 us
    pallas_call x1, Pallas kernels, scatter_down(): pl.pallas_call(scatter_down_kernel, in_specs=[anywhere] * 6, out_specs=[i...  71.4 us
    dot_general x6, matrix products, dot32(): return lax.dot_general(a, b, (dims, ((), ())), preferred_element_type=F32)  67.6 us
    pallas_call x1, Pallas kernels, attend_back(): pl.pallas_call(attend_back_kernel, grid=(units,), in_specs=[pl.BlockSpec(...  56.8 us
    ppermute x8, waiting for transfers between devices, swap_pair(): return lax.ppermute(block, axis, [(0, 1), (1, 0)])  50.5 us
    pallas_call x1, Pallas kernels, scatter_square(): pl.pallas_call(functools.partial(scatter_kernel, len(first)), in_specs=[p...  41.1 us
    pallas_call x1, Pallas kernels, attend(): pl.pallas_call(attend_kernel, grid=(blocks,), in_specs=[pl.BlockSpec(memo...  38.1 us
  transfers between devices with their start and end apart: 10, of which 5 were waited for; matrix products, arithmetic and copies ran while one was open for 7% of the time, Pallas kernels for 33%

profile of v3, /device:TPU:0, one launch (start us, length us, event | category | flops | bytes accessed | tf_op | source)
XLA Modules:
  0.0 915.4 jit_solution(5357542431159490882)
XLA Ops:
  13.1 80.5 %open.1 = (bf16[8,256,2048]{2,1,0:T(8,128)(2,1)}, bf16[32,64,384]{2,1,0:T(8,128)(2,1)}, f32[32,8,128]{2,1,0:T(8,128)}, bf16[2,2,64,2048]{3,2,1,0:T(8,128)(2,1)}) custom-call(bf16[256,2048]{1,0:T(8,128)(2,1)} %bitcast.84, bf16[8,64,384]{2,1,0:T(8,128)(2,1)} %get-tuple-element.74.heads_ref, f32[8,128]{1,0:T(8,128)} %maximum_bitcast_fusion.small_ref, ...), custom_call_target="tpu_custom_call" | custom-call | bytes 120000000 | tf_op jit(solution)/shard_map/open/pallas_call | solution.py:545
  95.5 13.3 %project.1 = (bf16[2048,2048]{1,0:T(8,128)(2,1)}, bf16[2048,256]{1,0:T(8,128)(2,1)}, bf16[2048,128]{1,0:T(8,128)(2,1)}) custom-call(s32[1]{0:T(128)} %bitcast.hi_ref, bf16[2048,2048]{1,0:T(8,128)(2,1)} %bitcast.92, f32[1,2048]{1,0:T(1,128)} %reshape_squeeze.6.gain_ref, bf16[2048,384]{1,0:T(8,128)(2,1)} %bitcast.106, f32[4096,128]{1,0:T(8,128)} %constant.48.clone.cos_ref, ...), custom_call_target="tpu_custom_call" | custom-call | flops 3221225472 | bytes 16777216 | tf_op jit(solution)/shard_map/project/pallas_call | solution.py:70
  108.8 37.4 %keys.1 = (bf16[2048,128]{1,0:T(8,128)(2,1)}, bf16[8,64,1024]{2,1,0:T(8,128)(2,1)}, bf16[8,64,1024]{2,1,0:T(8,128)(2,1)}, bf16[1,256,2048]{2,1,0:T(8,128)(2,1)}) custom-call(bf16[2048,128]{1,0:T(8,128)(2,1)} %get-tuple-element.79.kv_ref, bf16[8,64,1024]{2,1,0:T(8,128)(2,1)} %get-tuple-element.80.gate_ref, bf16[8,64,1024]{2,1,0:T(8,128)(2,1)} %get-tuple-element.81.up_ref, ...), custom_call_target="tpu_custom_call" | custom-call | bytes 120000000 | tf_op jit(solution)/shard_map/keys/pallas_call | solution.py:545
  147.9 38.1 %attend.1 = (bf16[4,512,256]{2,1,0:T(8,128)(2,1)}, f32[4,8,512]{2,1,0:T(8,128)}) custom-call(s32[2]{0:T(128)} %pad_add_fusion.scalar_ref, bf16[4,512,256]{2,1,0:T(8,128)(2,1)} %bitcast.126, bf16[4,512,128]{2,1,0:T(8,128)(2,1)} %bitcast.114, bf16[4,512,128]{2,1,0:T(8,128)(2,1)} %bitcast.129), custom_call_target="tpu_custom_call" | custom-call | flops 40000000000 | bytes 8000000 | tf_op jit(solution)/shard_map/attend/pallas_call | solution.py:216
  188.0 6.8 collective-permute-done.gate_other_ref
  195.8 51.3 %heads.1 = (bf16[8,256,256]{2,1,0:T(8,128)(2,1)}, bf16[2,2,512,1024]{3,2,1,0:T(8,128)(2,1)}, bf16[512,1024]{1,0:T(8,128)(2,1)}) custom-call(bf16[8,256,256]{2,1,0:T(8,128)(2,1)} %bitcast.93, bf16[512,1024]{1,0:T(8,128)(2,1)} %bitcast.112, bf16[512,1024]{1,0:T(8,128)(2,1)} %copy-done.14, bf16[512,1024]{1,0:T(8,128)(2,1)} %bitcast.100), custom_call_target="tpu_custom_call" | custom-call | bytes 120000000 | tf_op jit(solution)/shard_map/heads/pallas_call | solution.py:545
  247.2 10.7 %out_project.1 = (f32[256,2048]{1,0:T(8,128)}, bf16[256,2048]{1,0:T(8,128)(2,1)}) custom-call(bf16[8,256,256]{2,1,0:T(8,128)(2,1)} %get-tuple-element.86.mixed_ref, bf16[2048,2048]{1,0:T(8,128)(2,1)} %all-gather.3.cloned.1.call-done.weight_ref, bf16[256,2048]{1,0:T(8,128)(2,1)} %bitcast.85, f32[1,2048]{1,0:T(1,128)} %reshape_squeeze.7.gain_ref), custom_call_target="tpu_custom_call" | custom-call | flops 2147483648 | bytes 16000000 | tf_op jit(solution)/shard_map/out_project/pallas_call | solution.py:1157
  257.8 63.2 %rows.1 = (bf16[8,256,2048]{2,1,0:T(8,128)(2,1)}, bf16[2,2,512,1024]{3,2,1,0:T(8,128)(2,1)}, bf16[256,2048]{1,0:T(8,128)(2,1)}) custom-call(bf16[256,2048]{1,0:T(8,128)(2,1)} %get-tuple-element.89.rows_ref, bf16[512,1024]{1,0:T(8,128)(2,1)} %bitcast.101, bf16[512,1024]{1,0:T(8,128)(2,1)} %get-tuple-element.90.up_other_ref, bf16[256,2048]{1,0:T(8,128)(2,1)} %down_ref.3), custom_call_target="tpu_custom_call" | custom-call | bytes 120000000 | tf_op jit(solution)/shard_map/rows/pallas_call | solution.py:545
  321.4 14.6 %fusion.9 = f32[2048,1024]{1,0:T(8,128)} fusion(bf16[2048,2048]{1,0:T(8,128)(2,1)} %bitcast.118, bf16[2048,1024]{1,0:T(8,128)(2,1)} %bitcast.123), kind=kOutput, calls=%fused_computation.37 | convolution fusion | flops 8589934592 | bytes 20971520 | tf_op jit(solution)/shard_map/dot_general | solution.py:30
  335.9 20.9 %multiply_convert_fusion = (bf16[2048,1024]{1,0:T(8,128)(2,1)}, bf16[2048,1024]{1,0:T(8,128)(2,1)}, bf16[2048,1024]{1,0:T(8,128)(2,1)}) fusion(f32[2048,1024]{1,0:T(8,128)} %fusion.9, bf16[2048,2048]{1,0:T(8,128)(2,1)} %bitcast.119, bf16[2048,1024]{1,0:T(8,128)(2,1)S(1)} %bitcast.122), kind=kOutput, calls=%fused_computation | convolution fusion | flops 8617197568 | bytes 33554432 | tf_op jit(solution)/shard_map/dot_general | solution.py:30
  359.1 3.3 copy-done.19
  362.4 11.0 %convolution_convert_fusion.1 = bf16[2048,2048]{1,0:T(8,128)(2,1)} fusion(bf16[2048,1024]{1,0:T(8,128)(2,1)S(1)} %copy-done.19, bf16[1024,2048]{1,0:T(8,128)(2,1)S(1)} %bitcast.96), kind=kOutput, calls=%fused_computation.5 | convolution fusion | flops 8594128896 | bytes 16777216 | tf_op jit(solution)/shard_map/dot_general | solution.py:30
  373.5 41.1 %scatter_square.1 = f32[256,2048]{1,0:T(8,128)} custom-call(bf16[8,256,2048]{2,1,0:T(8,128)(2,1)} %bitcast.87), custom_call_target="tpu_custom_call" | custom-call | bytes 120000000 | tf_op jit(solution)/shard_map/scatter_square/pallas_call | solution.py:972
  414.6 4.9 multiply_convert_fusion.2
  419.6 39.1 %gather_square.1 = bf16[8,256,2048]{2,1,0:T(8,128)(2,1)} custom-call(bf16[256,2048]{1,0:T(8,128)(2,1)} %get-tuple-element.138.rows_ref), custom_call_target="tpu_custom_call" | custom-call | bytes 120000000 | tf_op jit(solution)/shard_map/gather_square/pallas_call | solution.py:545
  458.7 15.5 %weight_grad.1 = (bf16[2,256,2048]{2,1,0:T(8,128)(2,1)}, f32[2,256,2048]{2,1,0:T(8,128)}) custom-call(s32[1]{0:T(128)} %bitcast.26.dp_ref, bf16[2048,1024]{1,0:T(8,128)(2,1)} %get-tuple-element.141.left_ref, bf16[2048,2048]{1,0:T(8,128)(2,1)} %bitcast.88, bf16[2048,2048]{1,0:T(8,128)(2,1)} %bitcast.89), custom_call_target="tpu_custom_call" | custom-call | flops 8589934592 | bytes 24000000 | tf_op jit(solution)/shard_map/weight_grad/pallas_call | solution.py:1251
  476.0 35.2 %ff_back.1 = (bf16[2048,1024]{1,0:T(8,128)(2,1)}, bf16[2048,1024]{1,0:T(8,128)(2,1)}, bf16[2048,2048]{1,0:T(8,128)(2,1)}) custom-call(bf16[2048,2048]{1,0:T(8,128)(2,1)} %bitcast.90, bf16[2048,1024]{1,0:T(8,128)(2,1)} %get-tuple-element.140.gate_slope_ref, bf16[2048,1024]{1,0:T(8,128)(2,1)} %get-tuple-element.142.up_slope_ref, bf16[2048,1024]{1,0:T(8,128)(2,1)} %bitcast.121, ...), custom_call_target="tpu_custom_call" | custom-call | flops 25769803776 | bytes 40000000 | tf_op jit(solution)/shard_map/ff_back/pallas_call | solution.py:1309
  511.2 11.1 %collective-permute-done.2.got_ref = bf16[2,256,2048]{2,1,0:T(8,128)(2,1)S(1)} collective-permute-done((bf16[2,256,2048]{2,1,0:T(8,128)(2,1)}, bf16[2,256,2048]{2,1,0:T(8,128)(2,1)S(1)}, u32[]{:S(2)}, u32[]{:S(2)}) %collective-permute-start.2) | collective-permute-done | bytes 2097184 | tf_op jit(solution)/shard_map/ppermute | solution.py:1084
  523.7 71.4 %scatter_down.1 = (f32[256,2048]{1,0:T(8,128)}, f32[256,2048]{1,0:T(8,128)}, f32[2,512,1024]{2,1,0:T(8,128)}, f32[2,512,1024]{2,1,0:T(8,128)}, bf16[512,1024]{1,...) custom-call(bf16[8,256,2048]{2,1,0:T(8,128)(2,1)} %bitcast.131, ...), custom_call_target="tpu_custom_call" | custom-call | flops 17179869184 | bytes 160000000 | tf_op jit(solution)/shard_map/scatter_down/pallas_call | solution.py:1045
  595.1 12.4 %out_back.1 = (f32[256,2048]{1,0:T(8,128)}, bf16[256,2048]{1,0:T(8,128)(2,1)}, bf16[8,256,256]{2,1,0:T(8,128)(2,1)}) custom-call(f32[256,2048]{1,0:T(8,128)} %get-tuple-element.101.grad_ref.first_ref, f32[256,2048]{1,0:T(8,128)} %get-tuple-element.88.middle_ref, f32[256,2048]{1,0:T(8,128)} %get-tuple-element.139.result_ref, ...), custom_call_target="tpu_custom_call" | custom-call | flops 2147483648 | bytes 20000000 | tf_op jit(solution)/shard_map/out_back/pallas_call | solution.py:1203
  607.5 20.1 %douts.1 = (bf16[8,256,256]{2,1,0:T(8,128)(2,1)}, bf16[512,1024]{1,0:T(8,128)(2,1)}, bf16[512,1024]{1,0:T(8,128)(2,1)}) custom-call(bf16[8,256,256]{2,1,0:T(8,128)(2,1)} %get-tuple-element.102.parts_ref, f32[2,512,1024]{2,1,0:T(8,128)} %get-tuple-element.103.gate_ref, bf16[512,1024]{1,0:T(8,128)(2,1)} %get-tuple-element.104.gate_got_ref, ...), custom_call_target="tpu_custom_call" | custom-call | bytes 40000000 | tf_op jit(solution)/shard_map/douts/pallas_call | solution.py:1644
  631.9 56.8 %attend_back.1 = (bf16[4,512,256]{2,1,0:T(8,128)(2,1)}, bf16[2,4,512,128]{3,2,1,0:T(8,128)(2,1)}) custom-call(s32[2]{0:T(128)} %pad_add_fusion.scalar_ref, bf16[4,512,256]{2,1,0:T(8,128)(2,1)} %bitcast.127, bf16[4,512,128]{2,1,0:T(8,128)(2,1)} %bitcast.115, bf16[4,512,128]{2,1,0:T(8,128)(2,1)} %bitcast.130, bf16[4,512,256]{2,1,0:T(8,128)(2,1)} %bitcast.128, ...), custom_call_target="tpu_custom_call" | custom-call | flops 60000002048 | bytes 10000000 | tf_op jit(solution)/shard_map/attend_back/pallas_call | solution.py:350
  690.6 8.8 collective-permute-done.4
  700.6 45.4 %dkeys.1 = (bf16[2048,128]{1,0:T(8,128)(2,1)}, bf16[8,64,1024]{2,1,0:T(8,128)(2,1)}) custom-call(bf16[2,2048,128]{2,1,0:T(8,128)(2,1)} %bitcast.102, f32[2,8,64,1024]{3,2,1,0:T(8,128)} %bitcast.83, bf16[8,64,1024]{2,1,0:T(8,128)(2,1)} %bitcast.109, bf16[8,64,1024]{2,1,0:T(8,128)(2,1)} %bitcast.108), custom_call_target="tpu_custom_call" | custom-call | bytes 120000000 | tf_op jit(solution)/shard_map/dkeys/pallas_call | solution.py:545
  747.0 7.2 back_rope.1
  754.2 7.6 fusion.10
  767.2 6.8 convolution_convert_fusion
  774.0 11.1 %collective-permute-done.6 = bf16[16,64,384]{2,1,0:T(8,128)(2,1)} collective-permute-done((bf16[16,64,384]{2,1,0:T(8,128)(2,1)}, bf16[16,64,384]{2,1,0:T(8,128)(2,1)}, u32[]{:S(2)}, u32[]{:S(2)}) %collective-permute-start.6) | collective-permute-done | bytes 786464 | tf_op jit(solution)/shard_map/ppermute | solution.py:1084
  787.4 6.7 convolution_convert_fusion.2
  794.1 12.7 %collective-permute-done.7 = bf16[512,1024]{1,0:T(8,128)(2,1)} collective-permute-done((bf16[512,1024]{1,0:T(8,128)(2,1)}, bf16[512,1024]{1,0:T(8,128)(2,1)}, u32[]{:S(2)}, u32[]{:S(2)}) %collective-permute-start.7) | collective-permute-done | bytes 1048608 | tf_op jit(solution)/shard_map/ppermute | solution.py:1084
  808.0 84.1 %close.1 = (f32[256,2048]{1,0:T(8,128)}, bf16[16,64,384]{2,1,0:T(8,128)(2,1)}, bf16[8,64,1024]{2,1,0:T(8,128)(2,1)}, f32[32,8,128]{2,1,0:T(8,128)}, bf16[2,64,2048]{2,1,0:T(8,128)(2,1)}) custom-call(bf16[8,256,2048]{2,1,0:T(8,128)(2,1)} %bitcast.91, bf16[16,64,384]{2,1,0:T(8,128)(2,1)} %fusion.2.refs_1_, f32[2,8,64,1024]{3,2,1,0:T(8,128)} %bitcast.82, ...), custom_call_target="tpu_custom_call" | custom-call | bytes 120000000 | tf_op jit(solution)/shard_map/close/pallas_call | solution.py:1704
  892.2 10.1 %final.1 = (f32[256,2048]{1,0:T(8,128)}, f32[64,2048]{1,0:T(8,128)}, f32[64,512]{1,0:T(8,128)}, f32[64,512]{1,0:T(8,128)}, f32[64,1]{1,0:T(8,128)}, /*index=5*/f...) custom-call(f32[256,2048]{1,0:T(8,128)} %get-tuple-element.119.first_ref, ...), custom_call_target="tpu_custom_call" | custom-call | tf_op jit(solution)/shard_map/final/pallas_call | solution.py:1719
  (80 shorter events, 37.7 us)
Async XLA Ops:
  7.2 240.0 %all-gather.3.cloned.1.call-start = ((), (), s32[]{:S(2)}) async-start(), calls=%async_computation | async-start | bytes 9437184 | tf_op jit(solution)/shard_map/all_gather | solution.py:1558
  93.7 693.8 %all-gather.5.cloned.1.call-start = ((), (), s32[]{:S(2)}) async-start(), calls=%async_computation.1 | async-start | bytes 9437184 | tf_op jit(solution)/shard_map/all_gather | solution.py:1666
  146.2 48.6 %collective-permute-start = (bf16[512,1024]{1,0:T(8,128)(2,1)}, bf16[512,1024]{1,0:T(8,128)(2,1)S(1)}, u32[]{:S(2)}, u32[]{:S(2)}) collective-permute-start(bf16[512,1024]{1,0:T(8,128)(2,1)} %bitcast.111), channel_id=1, source_target_pairs={{0,2},{2,0},{1,3},{3,1},{4,6},{6,4},{5,7},{7,5},{8,10},{10,8},{9,1... | collective-permute-start | bytes 3145736 | tf_op jit(solution)/shard_map/ppermute | solution.py:1084
  147.9 38.8 %copy-start.15 = (f32[32,8,128]{2,1,0:T(8,128)S(1)}, f32[32,8,128]{2,1,0:T(8,128)}, u32[]{:S(2)}) copy-start(f32[32,8,128]{2,1,0:T(8,128)} %get-tuple-element.76) | copy-start | bytes 393220
  194.8 1.0 copy-start.14
  321.0 36.0 %collective-permute-start.1 = (bf16[256,2048]{1,0:T(8,128)(2,1)}, bf16[256,2048]{1,0:T(8,128)(2,1)S(1)}, u32[]{:S(2)}, u32[]{:S(2)}) collective-permute-start(bf16[256,2048]{1,0:T(8,128)(2,1)} %get-tuple-element.94), channel_id=1, source_target_pairs={{0,16},{16,0},{1,17},{17,1},{2,18},{18,2},{3,19},{19,3},{4,20},{20... | collective-permute-start | bytes 3145736 | tf_op jit(solution)/shard_map/ppermute | solution.py:1084
  321.4 14.6 %copy-start.16 = (bf16[2,2,512,1024]{3,2,1,0:T(8,128)(2,1)S(1)}, bf16[2,2,512,1024]{3,2,1,0:T(8,128)(2,1)}, u32[]{:S(2)}) copy-start(bf16[2,2,512,1024]{3,2,1,0:T(8,128)(2,1)} %get-tuple-element.92) | copy-start | bytes 12582916
  335.9 20.9 %copy-start = (bf16[256,2048]{1,0:T(8,128)(2,1)S(1)}, bf16[256,2048]{1,0:T(8,128)(2,1)}, u32[]{:S(2)}) copy-start(bf16[256,2048]{1,0:T(8,128)(2,1)} %down_ref.3) | copy-start | bytes 3145732
  335.9 20.9 %copy-start.13 = (bf16[256,2048]{1,0:T(8,128)(2,1)S(1)}, bf16[256,2048]{1,0:T(8,128)(2,1)}, u32[]{:S(2)}) copy-start(bf16[256,2048]{1,0:T(8,128)(2,1)} %get-tuple-element.94) | copy-start | bytes 3145732
  356.9 1.2 copy-start.10
  358.7 3.7 copy-start.19
  359.1 14.3 %copy-start.3 = (bf16[2,2,256,2048]{3,2,1,0:T(8,128)(2,1)}, bf16[2,2,256,2048]{3,2,1,0:T(8,128)(2,1)S(1)}, u32[]{:S(2)}) copy-start(bf16[2,2,256,2048]{3,2,1,0:T(8,128)(2,1)S(1)} %pad_maximum_fusion) | copy-start | bytes 12582916
  373.4 41.2 %copy-start.1 = (f32[256,2048]{1,0:T(8,128)S(1)}, f32[256,2048]{1,0:T(8,128)}, u32[]{:S(2)}) copy-start(f32[256,2048]{1,0:T(8,128)} %get-tuple-element.88.middle_ref) | copy-start | bytes 6291460
  373.5 41.2 %copy-start.9 = (bf16[1,256,2048]{2,1,0:T(8,128)(2,1)S(1)}, bf16[1,256,2048]{2,1,0:T(8,128)(2,1)}, u32[]{:S(2)}) copy-start(bf16[1,256,2048]{2,1,0:T(8,128)(2,1)} %param.16) | copy-start | bytes 3145732
  474.2 48.1 %collective-permute-start.2 = (bf16[2,256,2048]{2,1,0:T(8,128)(2,1)}, bf16[2,256,2048]{2,1,0:T(8,128)(2,1)S(1)}, u32[]{:S(2)}, u32[]{:S(2)}) collective-permute-start(bf16[2,256,2048]{2,1,0:T(8,128)(2,1)} %get-tuple-element.98), channel_id=1, source_target_pairs={{0,16},{16,0},{1,17},{17,1},{2,18},{18,2},{3,19},{19,3},{4,20},{20... | collective-permute-start | bytes 6291464 | tf_op jit(solution)/shard_map/ppermute | solution.py:1084
  522.4 1.3 copy-start.17
  607.5 21.0 %copy-start.18 = (bf16[512,1024]{1,0:T(8,128)(2,1)S(1)}, bf16[512,1024]{1,0:T(8,128)(2,1)}, u32[]{:S(2)}) copy-start(bf16[512,1024]{1,0:T(8,128)(2,1)} %get-tuple-element.112) | copy-start | bytes 3145732
  627.6 71.7 %collective-permute-start.4 = (bf16[512,1024]{1,0:T(8,128)(2,1)}, bf16[512,1024]{1,0:T(8,128)(2,1)S(1)}, u32[]{:S(2)}, u32[]{:S(2)}) collective-permute-start(bf16[512,1024]{1,0:T(8,128)(2,1)} %get-tuple-element.109.first_ref), channel_id=1, source_target_pairs={{0,2},{2,0},{1,3},{3,1},{4,6},{6,4},{5,7},{7,5},{8,10},{10,8},{9,1... | collective-permute-start | bytes 3145736 | tf_op jit(solution)/shard_map/ppermute | solution.py:1084
  628.5 70.8 %collective-permute-start.3 = (bf16[512,1024]{1,0:T(8,128)(2,1)S(1)}, bf16[512,1024]{1,0:T(8,128)(2,1)S(1)}, u32[]{:S(2)}, u32[]{:S(2)}) collective-permute-start(bf16[512,1024]{1,0:T(8,128)(2,1)S(1)} %copy-done.18), channel_id=1, source_target_pairs={{0,16},{16,0},{1,17},{17,1},{2,18},{18,2},{3,19},{19,3},{4,20},{20... | collective-permute-start | bytes 3145736 | tf_op jit(solution)/shard_map/ppermute | solution.py:1084
  629.8 116.2 %collective-permute-start.5 = (bf16[512,1024]{1,0:T(8,128)(2,1)}, bf16[512,1024]{1,0:T(8,128)(2,1)S(1)}, u32[]{:S(2)}, u32[]{:S(2)}) collective-permute-start(bf16[512,1024]{1,0:T(8,128)(2,1)} %get-tuple-element.114), channel_id=1, source_target_pairs={{0,2},{2,0},{1,3},{3,1},{4,6},{6,4},{5,7},{7,5},{8,10},{10,8},{9,1... | collective-permute-start | bytes 3145736 | tf_op jit(solution)/shard_map/ppermute | solution.py:1084
  699.3 1.0 copy-start.11
  699.3 1.3 copy-start.12
  746.1 1.0 copy-start.4
  754.2 13.0 %copy-start.7 = (bf16[32,64,384]{2,1,0:T(8,128)(2,1)S(1)}, bf16[32,64,384]{2,1,0:T(8,128)(2,1)}, u32[]{:S(2)}) copy-start(bf16[32,64,384]{2,1,0:T(8,128)(2,1)} %get-tuple-element.77) | copy-start | bytes 4718596
  754.2 13.0 %copy-start.8 = (bf16[2048,384]{1,0:T(8,128)(2,1)S(1)}, bf16[2048,384]{1,0:T(8,128)(2,1)}, u32[]{:S(2)}) copy-start(bf16[2048,384]{1,0:T(8,128)(2,1)} %back_rope.1) | copy-start | bytes 4718596
  761.8 1.6 copy-start.5
  764.5 20.7 %collective-permute-start.6 = (bf16[16,64,384]{2,1,0:T(8,128)(2,1)}, bf16[16,64,384]{2,1,0:T(8,128)(2,1)}, u32[]{:S(2)}, u32[]{:S(2)}) collective-permute-start(bf16[16,64,384]{2,1,0:T(8,128)(2,1)} %fusion.7), channel_id=1, source_target_pairs={{0,16},{16,0},{1,17},{17,1},{2,18},{18,2},{3,19},{19,3},{4,20},{20... | collective-permute-start | bytes 2359304 | tf_op jit(solution)/shard_map/ppermute | solution.py:1084
  766.5 18.7 %copy-start.6 = (f32[2048,384]{1,0:T(8,128)S(1)}, f32[2048,384]{1,0:T(8,128)}, u32[]{:S(2)}) copy-start(f32[2048,384]{1,0:T(8,128)} %copy-done.5) | copy-start | bytes 9437188
  766.5 40.3 %collective-permute-start.7 = (bf16[512,1024]{1,0:T(8,128)(2,1)}, bf16[512,1024]{1,0:T(8,128)(2,1)}, u32[]{:S(2)}, u32[]{:S(2)}) collective-permute-start(bf16[512,1024]{1,0:T(8,128)(2,1)} %get-tuple-element.116), channel_id=1, source_target_pairs={{0,16},{16,0},{1,17},{17,1},{2,18},{18,2},{3,19},{19,3},{4,20},{20... | collective-permute-start | bytes 3145736 | tf_op jit(solution)/shard_map/ppermute | solution.py:1084
  774.0 13.4 %copy-start.2 = (bf16[4,512,256]{2,1,0:T(8,128)(2,1)S(1)}, bf16[4,512,256]{2,1,0:T(8,128)(2,1)}, u32[]{:S(2)}) copy-start(bf16[4,512,256]{2,1,0:T(8,128)(2,1)} %get-tuple-element.83.out_ref) | copy-start | bytes 3145732
Sparse Core Ops, SparseCore 0:
  93.8 65.9 all-gather.2
  607.6 108.5 all-gather.4

commit v4 on v3

--- a/solution.py
+++ b/solution.py
@@ -88,9 +88,11 @@
     )(hi, rows, gain, weight, *tables)
 
 
-def back_rope_kernel(
-    hi_ref, dq_ref, own_ref, other_ref, cos_ref, sina_ref, sinb_ref, first_ref, out_ref
+def proj_back_kernel(
+    hi_ref, dq_ref, own_ref, other_ref, rows_ref, weight_ref, cos_ref, sina_ref, sinb_ref, first_ref, drows_ref,
+    dweight_ref, made, total,
 ):
+    i = pl.program_id(0)
     cosine, sina, sinb = cos_ref[...], sina_ref[...], sinb_ref[...]
     low = lanes_low(cosine.shape)
     half = HEAD_SIZE // 2
@@ -100,27 +102,50 @@
         turned = w * cosine + pltpu.roll(w * sinb, 128 - half, 1) + pltpu.roll(w * sina, half, 1)
         if part == 2:
             turned = jnp.where(low, turned, w)
-        out_ref[:, 128 * part : 128 * part + 128] = turned.astype(BF16)
-
-
-def back_rope(hi, dq, own, other, tables, first, tile):
-    count = dq.shape[0]
-    by_rows = lambda wide: pl.BlockSpec((tile, wide), lambda i, hi: (i, 0))
+        made[:, 128 * part : 128 * part + 128] = turned.astype(BF16)
+    drows_ref[...] = dot32(made[...], weight_ref[...], ((1,), (1,))).astype(BF16)
+    dweight = dot32(rows_ref[...], made[...], ((0,), (0,)))
+
+    @pl.when(i == 0)
+    def _():
+        total[...] = dweight
+
+    @pl.when(i > 0)
+    def _():
+        total[...] += dweight
+
+    @pl.when(i == pl.num_programs(0) - 1)
+    def _():
+        dweight_ref[...] = total[...].astype(BF16)
+
+
+def project_back(hi, dq, own, other, rows, weight, tables, first, unit):
+    count, width = rows.shape
+    wide = weight.shape[1]
+    by_rows = lambda cols: pl.BlockSpec((unit, cols), lambda i, hi: (i, 0))
+    whole = pl.BlockSpec((width, wide), lambda i, hi: (0, 0))
+    table = pl.BlockSpec((unit, 128), lambda i, hi: (2 * i + hi[0], 0))
     return pl.pallas_call(
-        back_rope_kernel,
+        proj_back_kernel,
         grid_spec=pltpu.PrefetchScalarGridSpec(
             num_scalar_prefetch=1,
-            grid=(count // tile,),
-            in_specs=[by_rows(256), by_rows(128), by_rows(128)]
-            + [table_spec(tile)] * 3
+            grid=(count // unit,),
+            in_specs=[by_rows(256), by_rows(128), by_rows(128), by_rows(width), whole]
+            + [table] * 3
             + [pl.BlockSpec(memory_space=pl.ANY)],
-            out_specs=by_rows(384),
+            out_specs=[by_rows(width), whole],
+            scratch_shapes=[pltpu.VMEM((unit, wide), BF16), pltpu.VMEM((width, wide), F32)],
         ),
-        out_shape=jax.ShapeDtypeStruct((count, 384), BF16),
+        out_shape=[
+            jax.ShapeDtypeStruct((count, width), BF16),
+            jax.ShapeDtypeStruct((width, wide), BF16),
+        ],
         compiler_params=pltpu.CompilerParams(vmem_limit_bytes=VMEM_LIMIT),
-        cost_estimate=pl.CostEstimate(flops=0, bytes_accessed=20_000_000, transcendentals=0),
-        name="back_rope",
-    )(hi, dq, own, other, *tables, first)
+        cost_estimate=pl.CostEstimate(
+            flops=4 * count * width * wide, bytes_accessed=24_000_000, transcendentals=0
+        ),
+        name="project_back",
+    )(hi, dq, own, other, rows, weight, *tables, first)
 
 
 def lanes_low(shape):
@@ -579,10 +604,10 @@
     return copies + [own]
 
 
-def dp_begin(pieces, out_ref, send, recv, local, held):
+def dp_begin(pieces, out_ref, send, recv, local, held, first=0):
     dp = lax.axis_index("dp")
     copies = []
-    for k, (place, ref) in enumerate(pieces):
+    for k, (place, ref) in enumerate(pieces, first):
         copies.append(Carried(ref, out_ref.at[dp, place], held.at[k], local.at[k]))
         for d, to in enumerate(dp_peers()):
             n = 2 * d + k
@@ -721,21 +746,44 @@
         copy.wait()
 
 
-def douts_kernel(
-    parts_ref, gate_ref, gate_got_ref, up_ref, up_got_ref, out_ref, gate_away_ref, up_away_ref, send, recv, local,
-    held, own, got, sem,
+def out_back_kernel(
+    order, pairs, block, grad_ref, middle_ref, result_ref, gain_ref, weight_ref, gate_ref, gate_got_ref, up_ref,
+    up_got_ref, sum_ref, rows_ref, out_ref, gate_away_ref, up_away_ref, weight, work, parts, send, recv, own, got, sem,
+    w_sem,
 ):
     hi = lax.axis_index("hi")
+    load = local_copy(weight_ref, weight, w_sem.at[0])
     loads = [
         [local_copy(ref.at[1 - hi], own.at[k], sem.at[k, 0]), local_copy(got_ref, got.at[k], sem.at[k, 1])]
         for k, (ref, got_ref) in enumerate(((gate_ref, gate_got_ref), (up_ref, up_got_ref)))
     ]
-    greet(square_peers()[2])
-    copies = swap_begin(parts_ref, out_ref, send, recv, local, held)
+    mine, others, ids = square_peers()
+    greet(ids)
+    reorder(pairs, block, grad_ref, work, lambda v: v)
+    normal, inverse = norm_parts(middle_ref[...])
+    grad = work[...] * gain_ref[...]
+    total = result_ref[...] + inverse * (
+        grad - normal * jnp.mean(grad * normal, axis=-1, keepdims=True)
+    )
+    sum_ref[...] = total
+    rows_ref[...] = (RESIDUAL_SCALE * total).astype(BF16)
+    load.wait()
+    cols = parts.shape[2]
+
+    def make(n, f):
+        part = weight[pl.ds(pl.multiple_of(order(f) * cols, cols), cols), :]
+        parts[n] = dot32(rows_ref[...], part, ((1,), (1,))).astype(BF16)
+
+    copies = []
+    for d, (other, to) in enumerate(zip(others, ids)):
+        make(d, other)
+        copies.append(remote(parts.at[d], out_ref.at[mine], send.at[d], recv.at[d], to))
+    make(7, mine)
+    copies.append(local_copy(parts.at[7], out_ref.at[mine], w_sem.at[0]))
     for k, target in enumerate((gate_away_ref, up_away_ref)):
         wait_all(loads[k])
         target[...] = (own[k] + got[k].astype(F32)).astype(BF16)
-    finish(copies)
+    wait_all(copies)
 
 
 def sum_three(place, own_ref, over_dp_ref, over_hi_ref, own, over_dp, over_hi, sem):
@@ -747,7 +795,7 @@
 
 
 def dkeys_kernel(
-    dkv_ref, gate_ref, gate_dp_ref, gate_hi_ref, other_ref, gates_ref, k_send, k_recv, g_send, g_recv, g_local,
+    dkv_ref, gate_ref, gate_dp_ref, gate_hi_ref, first_ref, other_ref, gates_ref, k_send, k_recv, g_send, g_recv, g_local,
     g_held, own, over_dp, over_hi, made, sem,
 ):
     hi = lax.axis_index("hi")
@@ -824,7 +872,7 @@
     total_ref, head_ref, ups_ref, squares_ref = take(4)
     outs_ref = next(refs) if with_out else None
     scatter = take(9)
-    h_send, h_recv, s_send, s_recv, local, h_held = take(6)
+    h_send, h_recv, s_send, s_recv, local, h_own, h_got, h_made, h_sem = take(9)
     swap = take(4)
     own, over_dp, over_hi, made, sem = take(5)
     out_scratch = take(6) if with_out else None
@@ -835,21 +883,36 @@
     hi = lax.axis_index("hi")
     up_loads = sum_three(hi, up_ref, up_dp_ref, up_hi_ref, own, over_dp, over_hi, sem)
     greet(peers)
-    copies = [
-        Carried(heads_ref.at[place], head_ref.at[place], h_held, local.at[0]),
-        local_copy(square_ref, squares_ref.at[mine], local.at[1]),
-    ]
+    copies = [local_copy(square_ref, squares_ref.at[mine], local.at[1])]
+    dp = lax.axis_index("dp")
+    own_heads = local_copy(heads_ref.at[dp], h_own, local.at[0])
+    over_heads = []
+    for d, to in enumerate(dp_peers()):
+        part = heads_ref.at[to["dp"]]
+        over_heads.append(remote(part, h_got.at[d], h_sem.at[0, d], h_sem.at[1, d], to))
     mates = scatter_mates(parts_ref, scatter)
     for k, to in enumerate(peers):
         copies.append(remote(square_ref, squares_ref.at[mine], s_send.at[k], s_recv.at[k], to))
-    for k, (to, source) in enumerate(seq):
-        part = heads_ref.at[seq_place(to)]
-        copies.append(remote(part, head_ref.at[place], h_send.at[k], h_recv.at[k], to))
+
+    def send_heads():
+        own_heads.wait()
+        wait_all(over_heads)
+        total = h_own[...].astype(F32)
+        for d in range(len(over_heads)):
+            total = total + h_got[d].astype(F32)
+        h_made[...] = total.astype(BF16)
+        copies.append(local_copy(h_made.at[place], head_ref.at[place], local.at[0]))
+        for k, (to, source) in enumerate(seq):
+            part = h_made.at[seq_place(to)]
+            copies.append(remote(part, head_ref.at[place], h_send.at[k], h_recv.at[k], to))
+
     own_out = OwnOut(out_rows_ref, outs_ref, *out_scratch) if with_out else None
     wait_all(up_loads)
     made[...] = (own[...] + over_dp[...].astype(F32) + over_hi[...].astype(F32)).astype(BF16)
     copies += swap_begin(made, ups_ref, *swap)
-    scatter_end_square(loads, mates, total_ref, scatter, own_out.turn if with_out else None)
+    nothing = lambda: None
+    work = [nothing, send_heads, nothing, nothing, own_out.turn if with_out else nothing]
+    scatter_end_square(loads, mates, total_ref, scatter, work)
     finish(copies)
     if with_out:
         own_out.wait()
@@ -884,7 +947,7 @@
     }
 
 
-def scatter_end_square(loads, from_mate, out_ref, scratch, between=None, work=()):
+def scatter_end_square(loads, from_mate, out_ref, scratch, work=()):
     work = list(work)
     mine, mates, made, got_across, got_side, got_next = scratch[:6]
     sems_of = scratch[6:8]
@@ -929,8 +992,6 @@
         )
     for one in work:
         one()
-    if between is not None:
-        between()
     loads[3].wait()
     for p in range(PIECES):
         total = summed(3, p)
@@ -1028,7 +1089,7 @@
             lefts[n + 2] = load_left(n + 2)
 
     work = [functools.partial(gradient, n, up) for n in range(4) for up in range(2)]
-    scatter_end_square(loads, mates, out_ref, scratch, work=work)
+    scatter_end_square(loads, mates, out_ref, scratch, work)
     wait_all(down)
     over.wait()
     sum_ref[...] = own[...] + got[...].astype(F32) + came[...].astype(F32)
@@ -1177,53 +1238,115 @@
     )(mixed, weight, rows, gain)
 
 
-def out_back_kernel(
-    pairs, block, grad_ref, middle_ref, result_ref, gain_ref, weight_ref, first_ref, sum_ref, rows_ref, mixed_ref, work
+def middle_kernel(
+    order, pairs, block, heads_ref, gate_ref, gate_other_ref, up_ref, down_ref, weight_ref, rows_ref, gain_ref,
+    out_ref, middle_ref, gates_ref, ups_ref, down_other_ref, up_other_ref, made_ref, m_send, m_recv, m_local,
+    m_held, g_send, g_recv, g_local, g_held, u_send, u_recv, u_local, u_held, o_send, o_recv, r_send, r_recv,
+    r_local, r_held, mixed, weight, rows, normed, total, gate_weight, chunks, sem,
 ):
-    f = pl.program_id(0)
-
-    @pl.when(f == 0)
-    def _():
-        reorder(pairs, block, grad_ref, work, lambda v: v)
-        normal, inverse = norm_parts(middle_ref[...])
-        grad = work[...] * gain_ref[...]
-        total = result_ref[...] + inverse * (
-            grad - normal * jnp.mean(grad * normal, axis=-1, keepdims=True)
-        )
-        sum_ref[...] = total
-        rows_ref[...] = (RESIDUAL_SCALE * total).astype(BF16)
-
-    mixed_ref[0] = dot32(rows_ref[...], weight_ref[...], ((1,), (1,))).astype(BF16)
-
-
-def out_back(grad, middle, result, gain, weight, first, cols, order, pairs, block):
-    tok, width = middle.shape
-    group = width // cols
-    whole = pl.BlockSpec((tok, width), lambda f: (0, 0))
+    hi = lax.axis_index("hi")
+    loads = [local_copy(weight_ref, weight, sem.at[0]), local_copy(rows_ref, rows, sem.at[1])]
+    mine, others, ids = square_peers()
+    greet(ids + [other_hi()] + dp_peers())
+    heads = swap_begin(heads_ref, mixed, m_send, m_recv, m_local, m_held)
+    up_over = remote(up_ref, up_other_ref, o_send.at[0], o_recv.at[0], other_hi())
+    gates = dp_begin([(hi, gate_ref), (1 - hi, gate_other_ref)], gates_ref, g_send, g_recv, g_local, g_held)
+    copies = dp_begin([(hi, up_ref)], ups_ref, u_send, u_recv, u_local, u_held)
+    wait_all(loads)
+    cols = mixed.shape[2]
+
+    def add(f):
+        g = order(f)
+        part = weight[pl.ds(pl.multiple_of(g * cols, cols), cols), :]
+        return dot32(mixed[f], part)
+
+    heads[7].turn()
+    heads[7].wait()
+    total[...] = add(mine)
+    for d in range(7):
+        heads[d].wait_recv()
+        total[...] += add(lax.rem(mine + 7 - d, 8))
+    middle = rows[...].astype(F32) + RESIDUAL_SCALE * total[...]
+    middle_ref[...] = middle
+    total[...] = norm_parts(middle)[0] * gain_ref[...]
+    reorder(pairs, block, total, normed, lambda v: v.astype(BF16))
+    end = gather_begin(normed, out_ref, r_send, r_recv, r_local, r_held)
+
+    def more(turn):
+        if turn == PIECES - 1:
+            up_over.wait()
+            copies.append(remote(down_ref, down_other_ref, o_send.at[1], o_recv.at[1], other_hi()))
+            copies.extend(
+                dp_begin([(1 - hi, up_other_ref)], ups_ref, u_send, u_recv, u_local, u_held, 1)
+            )
+
+    end(more)
+    finish(gates)
+    step = 2
+    load_gate = local_copy(gates_ref, gate_weight, sem.at[0])
+    load_rows = lambda n: local_copy(out_ref.at[pl.ds(n * step, step)], chunks.at[n % 2], sem.at[1 + n % 2])
+    loads = [load_rows(0), load_rows(1)]
+    load_gate.wait()
+    tok, width = rows.shape
+    for n in range(8 // step):
+        loads[n].wait()
+        made_ref[n * step * tok : (n + 1) * step * tok, :] = dot32(
+            chunks[n % 2].reshape(step * tok, width), gate_weight[...].reshape(width, -1)
+        )
+        if n + 2 < 8 // step:
+            loads.append(load_rows(n + 2))
+    for d in range(7):
+        heads[d].wait_send()
+    finish(copies)
+
+
+def through_middle(heads, gate, gate_other, up, down, weight, rows, gain, order, pairs, block):
+    group, tok, cols = heads.shape
+    width = weight.shape[1]
+    part_rows, ff_part = up.shape
+    dp_n = lax.axis_size("dp")
+    anywhere, inside = pl.BlockSpec(memory_space=pl.ANY), pl.BlockSpec(memory_space=pltpu.VMEM)
+    dp_part = sems(2 * (dp_n - 1)) + [
+        pltpu.SemaphoreType.DMA((2,)),
+        pltpu.VMEM((2, part_rows, ff_part), BF16),
+    ]
+    spread = (dp_n, 2, part_rows, ff_part)
     return pl.pallas_call(
-        functools.partial(out_back_kernel, pairs, block),
-        grid=(group,),
-        in_specs=[
-            whole,
-            whole,
-            whole,
-            pl.BlockSpec((1, width), lambda f: (0, 0)),
-            pl.BlockSpec((cols, width), lambda f: (order(f), 0)),
-            pl.BlockSpec(memory_space=pl.ANY),
+        functools.partial(middle_kernel, order, pairs, block),
+        in_specs=[anywhere] * 7 + [inside],
+        out_specs=[anywhere, inside, anywhere, anywhere, anywhere, anywhere, inside],
+        out_shape=[
+            jax.ShapeDtypeStruct((group, tok, width), BF16),
+            jax.ShapeDtypeStruct((tok, width), F32),
+            jax.ShapeDtypeStruct(spread, BF16),
+            jax.ShapeDtypeStruct(spread, BF16),
+            jax.ShapeDtypeStruct(down.shape, BF16),
+            jax.ShapeDtypeStruct(up.shape, BF16),
+            jax.ShapeDtypeStruct((group * tok, ff_part), F32),
         ],
-        out_specs=[whole, whole, pl.BlockSpec((1, tok, cols), lambda f: (f, 0, 0))],
-        out_shape=[
-            jax.ShapeDtypeStruct((tok, width), F32),
-            jax.ShapeDtypeStruct((tok, width), BF16),
-            jax.ShapeDtypeStruct((group, tok, cols), BF16),
+        scratch_shapes=swap_scratch((tok, cols))
+        + dp_part
+        + dp_part
+        + sems(2)
+        + gather_scratch(tok, width)
+        + [
+            pltpu.VMEM((group, tok, cols), BF16),
+            pltpu.VMEM(weight.shape, BF16),
+            pltpu.VMEM((tok, width), BF16),
+            pltpu.VMEM((tok, width), BF16),
+            pltpu.VMEM((tok, width), F32),
+            pltpu.VMEM(spread, BF16),
+            pltpu.VMEM((2, 2, tok, width), BF16),
+            pltpu.SemaphoreType.DMA((3,)),
         ],
-        scratch_shapes=[pltpu.VMEM((tok, width), F32)],
-        compiler_params=pltpu.CompilerParams(vmem_limit_bytes=VMEM_LIMIT),
+        compiler_params=pltpu.CompilerParams(
+            collective_id=10, has_side_effects=True, vmem_limit_bytes=VMEM_LIMIT
+        ),
         cost_estimate=pl.CostEstimate(
-            flops=2 * tok * width * width, bytes_accessed=20_000_000, transcendentals=0
+            flops=2 * group * tok * width * ff_part, bytes_accessed=250_000_000, transcendentals=0
         ),
-        name="out_back",
-    )(grad, middle, result, gain, weight, first)
+        name="middle",
+    )(heads, gate, gate_other, up, down, weight, rows, gain)
 
 
 def weight_grad_kernel(dp_ref, left_ref, right_ref, first_ref, away_ref, own_ref):
@@ -1560,30 +1683,47 @@
     kv, other_kv = kv.reshape(blk_n, unit, -1), other_kv.reshape(blk_n, unit, -1)
     scalars = jnp.stack([lengths[0], hi.astype(jnp.int32)])
     out_heads, log_heads = attend(scalars, q, kv, other_kv)
-    dp_sems = sems(2 * (dp_n - 1))
-    dp_scratch = [pltpu.SemaphoreType.DMA((2,)), pltpu.VMEM((2, part_rows, ff_part), BF16)]
-    weight_shape = ((dp_n, hi_n, part_rows, ff_part), BF16)
-    mixed, gate_weight, up_other = comm_call(
-        heads_kernel,
-        3,
-        [out_heads.reshape(group, tok, q_cols), gate_parts, gate_other, up_parts],
-        [((group, tok, q_cols), BF16), weight_shape, (up_parts.shape, BF16)],
-        swap_scratch((tok, q_cols)) + dp_sems + sems(1) + dp_scratch,
-        "heads",
-    )
-    gate_weight = gate_weight.reshape(width, ff_part)
-    middle, normed_two = out_project(
-        mixed, out_weight, hidden[0], gain_two, key_head, to_inner, reblock
-    )
-
-    normed_two, up_weight, down_other = comm_call(
-        rows_kernel,
-        4,
-        [inner(normed_two), up_parts, up_other, w_down],
-        [((group, tok, width), BF16), weight_shape, (w_down.shape, BF16)],
-        gather_scratch(tok, width) + dp_sems + sems(1) + dp_scratch,
-        "rows",
-    )
+    if reblock == block:
+        normed_two, middle, gate_weight, up_weight, down_other, _, gate = through_middle(
+            out_heads.reshape(group, tok, q_cols),
+            gate_parts,
+            gate_other,
+            up_parts,
+            w_down,
+            out_weight,
+            hidden[0],
+            gain_two,
+            key_head,
+            to_inner,
+            reblock,
+        )
+        gate_weight = gate_weight.reshape(width, ff_part)
+    else:
+        dp_sems = sems(2 * (dp_n - 1))
+        dp_scratch = [pltpu.SemaphoreType.DMA((2,)), pltpu.VMEM((2, part_rows, ff_part), BF16)]
+        weight_shape = ((dp_n, hi_n, part_rows, ff_part), BF16)
+        mixed, gate_weight, up_other = comm_call(
+            heads_kernel,
+            3,
+            [out_heads.reshape(group, tok, q_cols), gate_parts, gate_other, up_parts],
+            [((group, tok, q_cols), BF16), weight_shape, (up_parts.shape, BF16)],
+            swap_scratch((tok, q_cols)) + dp_sems + sems(1) + dp_scratch,
+            "heads",
+        )
+        gate_weight = gate_weight.reshape(width, ff_part)
+        middle, normed_two = out_project(
+            mixed, out_weight, hidden[0], gain_two, key_head, to_inner, reblock
+        )
+
+        normed_two, up_weight, down_other = comm_call(
+            rows_kernel,
+            4,
+            [inner(normed_two), up_parts, up_other, w_down],
+            [((group, tok, width), BF16), weight_shape, (w_down.shape, BF16)],
+            gather_scratch(tok, width) + dp_sems + sems(1) + dp_scratch,
+            "rows",
+        )
+        gate = dot32(normed_two.reshape(group * tok, width), gate_weight)
     normed_two = normed_two.reshape(group * tok, width)
     up_weight = up_weight.reshape(width, ff_part)
     dp_index = lax.axis_index("dp")
@@ -1602,7 +1742,6 @@
     else:
         down_parts = lax.all_gather(down_parts, "dp", axis=0, tiled=False)
     down_weight = down_parts.reshape(-1, width)
-    gate = dot32(normed_two, gate_weight)
     upward = dot32(normed_two, up_weight)
     sigma = jax.nn.sigmoid(gate)
     silu = gate * sigma
@@ -1636,29 +1775,39 @@
         gate_stay = up_stay = gate_got = up_got = jnp.zeros(gate_own.shape[1:], BF16)
     grad_normal = outer(grad_normal)
 
-    grad_middle, attn_rows, grad_mixed = out_back(
-        grad_normal, middle, grad_result, gain_two, out_weight, grad_normal, q_cols, key_head, to_outer, reblock
-    )
     part_shape = (part_rows, ff_part)
     anywhere, inside = pl.BlockSpec(memory_space=pl.ANY), pl.BlockSpec(memory_space=pltpu.VMEM)
-    dout, gate_away, up_away = pl.pallas_call(
-        douts_kernel,
-        in_specs=[anywhere] * 5,
-        out_specs=[anywhere] + [inside] * 2,
-        out_shape=[jax.ShapeDtypeStruct(grad_mixed.shape, BF16)]
-        + [jax.ShapeDtypeStruct(part_shape, BF16)] * 2,
-        scratch_shapes=swap_scratch((tok, q_cols))
+    grad_middle, attn_rows, dout, gate_away, up_away = pl.pallas_call(
+        functools.partial(out_back_kernel, key_head, to_outer, reblock),
+        in_specs=[inside] * 4 + [anywhere] * 5,
+        out_specs=[inside] * 2 + [anywhere] + [inside] * 2,
+        out_shape=[
+            jax.ShapeDtypeStruct((tok, width), F32),
+            jax.ShapeDtypeStruct((tok, width), BF16),
+            jax.ShapeDtypeStruct((group, tok, q_cols), BF16),
+            jax.ShapeDtypeStruct(part_shape, BF16),
+            jax.ShapeDtypeStruct(part_shape, BF16),
+        ],
+        scratch_shapes=[
+            pltpu.VMEM(out_weight.shape, BF16),
+            pltpu.VMEM((tok, width), F32),
+            pltpu.VMEM((group, tok, q_cols), BF16),
+        ]
+        + sems(7)
         + [
             pltpu.VMEM((2,) + part_shape, F32),
             pltpu.VMEM((2,) + part_shape, BF16),
             pltpu.SemaphoreType.DMA((2, 2)),
+            pltpu.SemaphoreType.DMA((1,)),
         ],
         compiler_params=pltpu.CompilerParams(
             collective_id=6, has_side_effects=True, vmem_limit_bytes=VMEM_LIMIT
         ),
-        cost_estimate=pl.CostEstimate(flops=0, bytes_accessed=40_000_000, transcendentals=0),
-        name="douts",
-    )(grad_mixed, gate_own, gate_got, up_own, up_got)
+        cost_estimate=pl.CostEstimate(
+            flops=2 * tok * width * width, bytes_accessed=60_000_000, transcendentals=0
+        ),
+        name="out_back",
+    )(grad_normal, middle, grad_result, gain_two, out_weight, gate_own, gate_got, up_own, up_got)
     columns = (group, rows_w, ff_part)
 
     gate_dp, up_dp = gate_stay.reshape(columns), up_stay.reshape(columns)
@@ -1673,28 +1822,36 @@
     other_dkv, gate_parts = comm_call(
         dkeys_kernel,
         7,
-        [dkv, gate_own.reshape((hi_n,) + columns), gate_dp, gate_hi],
+        [dkv, gate_own.reshape((hi_n,) + columns), gate_dp, gate_hi, up_dp],
         [(dkv.shape[1:], BF16), (columns, BF16)],
         sems(1) + swap_scratch((rows_w, ff_part)) + sum_scratch,
         "dkeys",
     )
-    dqkv = back_rope(
-        hi_index, dq.reshape(group * tok, q_cols), dkv[0], other_dkv, tables, up_hi, tok
+    grad_first, head_grads = project_back(
+        hi_index,
+        dq.reshape(group * tok, q_cols),
+        dkv[0],
+        other_dkv,
+        normed_one,
+        qkv_weight,
+        tables,
+        up_hi,
+        unit,
     )
-    head_grads = dot32(normed_one, dqkv, ((0,), (0,))).reshape(dp_n, -1, rows_w, head_wide)
-    head_grads = scatter_end(scatter_start(head_grads, "dp"), "dp").astype(BF16)
-    grad_first = dot32(dqkv, qkv_weight, ((1,), (1,))).astype(BF16)
+    head_grads = head_grads.reshape(dp_n, every // dp_n, rows_w, head_wide)
     with_out = dp_n == 2 and rows_w * hi_n * lo_n == q_cols
     arrays = [grad_first.reshape(group, tok, width), head_grads]
     arrays += [up_own.reshape((hi_n,) + columns), up_dp, up_hi, squares]
     shapes = [
         ((tok, width), F32),
-        (head_grads.shape, BF16),
+        (head_grads.shape[1:], BF16),
         (columns, BF16),
         ((every, 8, 128), F32),
     ]
     scratch = scatter_scratch(tok, width) + sems(every // dp_n - 1) + sems(every - 1)
-    scratch += [pltpu.SemaphoreType.DMA((2,)), pltpu.VMEM((rows_w, head_wide), BF16)]
+    scratch += [pltpu.SemaphoreType.DMA((2,)), pltpu.VMEM(head_grads.shape[1:], BF16)]
+    scratch += [pltpu.VMEM((dp_n - 1,) + head_grads.shape[1:], BF16)]
+    scratch += [pltpu.VMEM(head_grads.shape[1:], BF16), pltpu.SemaphoreType.DMA((2, dp_n - 1))]
     scratch += swap_scratch((rows_w, ff_part)) + sum_scratch
     if with_out:
         arrays.append(own_out.reshape(hi_n, lo_n, rows_w, width))

time: 928 us -> 859 us (0.926)
  matrix products: 67.6 us -> 30.6 us
  waiting for transfers between devices: 50.6 us -> 28.8 us
    pallas_call x6 -> x4, Pallas kernels: 317 us -> 207 us  [comm_call(): pl.pallas_call(kernel, in_specs=[anywhere] * len(arrays), out_specs=[anyw...]
    pallas_call x4 -> x3, Pallas kernels: 50.4 us -> 156 us  [the longest x1 115 us: through_middle(): pl.pallas_call(functools.partial(middle_kernel, order, pairs, block), in_...]
    dot_general x6 -> x3, matrix products: 67.6 us -> 30.6 us  [dot32(): return lax.dot_general(a, b, (dims, ((), ())), preferred_element_type=F32)]
    ppermute x8 -> x7, waiting for transfers between devices: 50.5 us -> 28.7 us  [swap_pair(): return lax.ppermute(block, axis, [(0, 1), (1, 0)])]
  transfers between devices with their start and end apart: 10 -> 9, of which waited for: 5 -> 4; matrix products, arithmetic and copies ran while one was open for 7% -> 3% of each run, Pallas kernels for 33% -> 29%
where the time goes in v4:
time: 859 us; the launch traced here: 851 us
  Pallas kernels  731 us (85%)
  matrix products  30.6 us (4%)
  waiting for transfers between devices  28.8 us (3%)
  other arithmetic  22.9 us (3%)
  between operations  18.3 us (2%)
  local copies, waits for them, and re-layouts  10.6 us (1%)
    pallas_call x4, Pallas kernels, comm_call(): pl.pallas_call(kernel, in_specs=[anywhere] * len(arrays), out_specs=[anyw...  207 us
    pallas_call x1, Pallas kernels, through_middle(): pl.pallas_call(functools.partial(middle_kernel, order, pairs, block), in_...  115 us
    pallas_call x1, Pallas kernels, shards(): pl.pallas_call(functools.partial(close_kernel, with_out), in_specs=[anywh...  86.3 us
    pallas_call x1, Pallas kernels, scatter_down(): pl.pallas_call(scatter_down_kernel, in_specs=[anywhere] * 6, out_specs=[i...  70.2 us
    pallas_call x1, Pallas kernels, attend_back(): pl.pallas_call(attend_back_kernel, grid=(units,), in_specs=[pl.BlockSpec(...  57.1 us
    pallas_call x1, Pallas kernels, scatter_square(): pl.pallas_call(functools.partial(scatter_kernel, len(first)), in_specs=[p...  39.7 us
    pallas_call x1, Pallas kernels, attend(): pl.pallas_call(attend_kernel, grid=(blocks,), in_specs=[pl.BlockSpec(memo...  38.1 us
    pallas_call x1, Pallas kernels, ff_back(): pl.pallas_call(functools.partial(ff_back_kernel, ff), grid=(count // tok,...  35.1 us
  transfers between devices with their start and end apart: 9, of which 4 were waited for; matrix products, arithmetic and copies ran while one was open for 3% of the time, Pallas kernels for 29%

profile of v4, /device:TPU:0, one launch (start us, length us, event | category | flops | bytes accessed | tf_op | source)
XLA Modules:
  0.0 850.8 jit_solution(7882298691278277920)
XLA Ops:
  9.9 3.2 deal.1
  13.1 80.5 %open.1 = (bf16[8,256,2048]{2,1,0:T(8,128)(2,1)}, bf16[32,64,384]{2,1,0:T(8,128)(2,1)}, f32[32,8,128]{2,1,0:T(8,128)}, bf16[2,2,64,2048]{3,2,1,0:T(8,128)(2,1)}) custom-call(bf16[256,2048]{1,0:T(8,128)(2,1)} %bitcast.83, bf16[8,64,384]{2,1,0:T(8,128)(2,1)} %get-tuple-element.73.heads_ref, f32[8,128]{1,0:T(8,128)} %maximum_bitcast_fusion.small_ref, ...), custom_call_target="tpu_custom_call" | custom-call | bytes 120000000 | tf_op jit(solution)/shard_map/open/pallas_call | solution.py:570
  95.5 13.3 %project.1 = (bf16[2048,2048]{1,0:T(8,128)(2,1)}, bf16[2048,256]{1,0:T(8,128)(2,1)}, bf16[2048,128]{1,0:T(8,128)(2,1)}) custom-call(s32[1]{0:T(128)} %bitcast.hi_ref, bf16[2048,2048]{1,0:T(8,128)(2,1)} %bitcast.77, f32[1,2048]{1,0:T(1,128)} %reshape_squeeze.6.gain_ref, bf16[2048,384]{1,0:T(8,128)(2,1)} %bitcast.89, f32[4096,128]{1,0:T(8,128)} %constant.38.clone.cos_ref, ...), custom_call_target="tpu_custom_call" | custom-call | flops 3221225472 | bytes 16777216 | tf_op jit(solution)/shard_map/project/pallas_call | solution.py:70
  108.8 37.4 %keys.1 = (bf16[2048,128]{1,0:T(8,128)(2,1)}, bf16[8,64,1024]{2,1,0:T(8,128)(2,1)}, bf16[8,64,1024]{2,1,0:T(8,128)(2,1)}, bf16[1,256,2048]{2,1,0:T(8,128)(2,1)}) custom-call(bf16[2048,128]{1,0:T(8,128)(2,1)} %get-tuple-element.78.kv_ref, bf16[8,64,1024]{2,1,0:T(8,128)(2,1)} %get-tuple-element.79.gate_ref, bf16[8,64,1024]{2,1,0:T(8,128)(2,1)} %get-tuple-element.80.up_ref, ...), custom_call_target="tpu_custom_call" | custom-call | bytes 120000000 | tf_op jit(solution)/shard_map/keys/pallas_call | solution.py:570
  147.9 38.1 %attend.1 = (bf16[4,512,256]{2,1,0:T(8,128)(2,1)}, f32[4,8,512]{2,1,0:T(8,128)}) custom-call(s32[2]{0:T(128)} %pad_add_fusion.scalar_ref, bf16[4,512,256]{2,1,0:T(8,128)(2,1)} %bitcast.103, bf16[4,512,128]{2,1,0:T(8,128)(2,1)} %bitcast.97, bf16[4,512,128]{2,1,0:T(8,128)(2,1)} %bitcast.109), custom_call_target="tpu_custom_call" | custom-call | flops 40000000000 | bytes 8000000 | tf_op jit(solution)/shard_map/attend/pallas_call | solution.py:241
  188.0 6.8 collective-permute-done.gate_other_ref
  195.8 114.7 %middle.1 = (bf16[8,256,2048]{2,1,0:T(8,128)(2,1)}, f32[256,2048]{1,0:T(8,128)}, bf16[2,2,512,1024]{3,2,1,0:T(8,128)(2,1)}, bf16[2,2,512,1024]{3,2,1,0:T(8,128)(...) custom-call(bf16[8,256,256]{2,1,0:T(8,128)(2,1)} %bitcast.86, ...), custom_call_target="tpu_custom_call" | custom-call | flops 8589934592 | bytes 250000000 | tf_op jit(solution)/shard_map/middle/pallas_call | solution.py:1314
  311.5 12.6 %fusion.7 = f32[2048,1024]{1,0:T(8,128)S(1)} fusion(bf16[2048,2048]{1,0:T(8,128)(2,1)} %bitcast.111, bf16[2048,1024]{1,0:T(8,128)(2,1)} %bitcast.115), kind=kOutput, calls=%fused_computation.32 | convolution fusion | flops 8589934592 | bytes 20971520 | tf_op jit(solution)/shard_map/dot_general | solution.py:30
  324.1 5.9 multiply_convert_fusion
  330.1 2.4 select_bitcast_fusion.1
  332.4 2.1 collective-permute-done.1
  336.8 11.3 %convolution_convert_fusion = bf16[2048,2048]{1,0:T(8,128)(2,1)} fusion(bf16[2048,1024]{1,0:T(8,128)(2,1)S(1)} %get-tuple-element.139.left_ref, bf16[1024,2048]{1,0:T(8,128)(2,1)S(1)} %bitcast.79), kind=kOutput, calls=%fused_computation.4 | convolution fusion | flops 8594128896 | bytes 16777216 | tf_op jit(solution)/shard_map/dot_general | solution.py:30
  348.1 39.7 %scatter_square.1 = f32[256,2048]{1,0:T(8,128)} custom-call(bf16[8,256,2048]{2,1,0:T(8,128)(2,1)} %bitcast.73), custom_call_target="tpu_custom_call" | custom-call | bytes 120000000 | tf_op jit(solution)/shard_map/scatter_square/pallas_call | solution.py:1033
  387.9 4.9 multiply_convert_fusion.2
  392.8 39.9 %gather_square.1 = bf16[8,256,2048]{2,1,0:T(8,128)(2,1)} custom-call(bf16[256,2048]{1,0:T(8,128)(2,1)} %get-tuple-element.136.rows_ref), custom_call_target="tpu_custom_call" | custom-call | bytes 120000000 | tf_op jit(solution)/shard_map/gather_square/pallas_call | solution.py:570
  432.7 15.6 %weight_grad.1 = (bf16[2,256,2048]{2,1,0:T(8,128)(2,1)}, f32[2,256,2048]{2,1,0:T(8,128)}) custom-call(s32[1]{0:T(128)} %bitcast.26.dp_ref, bf16[2048,1024]{1,0:T(8,128)(2,1)} %copy-done.2, bf16[2048,2048]{1,0:T(8,128)(2,1)} %bitcast.74, bf16[2048,2048]{1,0:T(8,128)(2,1)} %bitcast.75), custom_call_target="tpu_custom_call" | custom-call | flops 8589934592 | bytes 24000000 | tf_op jit(solution)/shard_map/weight_grad/pallas_call | solution.py:1374
  449.4 35.1 %ff_back.1 = (bf16[2048,1024]{1,0:T(8,128)(2,1)}, bf16[2048,1024]{1,0:T(8,128)(2,1)}, bf16[2048,2048]{1,0:T(8,128)(2,1)}) custom-call(bf16[2048,2048]{1,0:T(8,128)(2,1)} %bitcast.76, bf16[2048,1024]{1,0:T(8,128)(2,1)} %get-tuple-element.138.gate_slope_ref, bf16[2048,1024]{1,0:T(8,128)(2,1)} %get-tuple-element.140.up_slope_ref, bf16[2048,1024]{1,0:T(8,128)(2,1)} %bitcast.114, ...), custom_call_target="tpu_custom_call" | custom-call | flops 25769803776 | bytes 40000000 | tf_op jit(solution)/shard_map/ff_back/pallas_call | solution.py:1432
  484.5 11.9 %collective-permute-done.2.got_ref = bf16[2,256,2048]{2,1,0:T(8,128)(2,1)S(1)} collective-permute-done((bf16[2,256,2048]{2,1,0:T(8,128)(2,1)}, bf16[2,256,2048]{2,1,0:T(8,128)(2,1)S(1)}, u32[]{:S(2)}, u32[]{:S(2)}) %collective-permute-start.2) | collective-permute-done | bytes 2097184 | tf_op jit(solution)/shard_map/ppermute | solution.py:1145
  497.7 70.2 %scatter_down.1 = (f32[256,2048]{1,0:T(8,128)}, f32[256,2048]{1,0:T(8,128)}, f32[2,512,1024]{2,1,0:T(8,128)}, f32[2,512,1024]{2,1,0:T(8,128)}, bf16[512,1024]{1,...) custom-call(bf16[8,256,2048]{2,1,0:T(8,128)(2,1)} %bitcast.113, ...), custom_call_target="tpu_custom_call" | custom-call | flops 17179869184 | bytes 160000000 | tf_op jit(solution)/shard_map/scatter_down/pallas_call | solution.py:1106
  568.0 23.9 %out_back.1 = (f32[256,2048]{1,0:T(8,128)}, bf16[256,2048]{1,0:T(8,128)(2,1)}, bf16[8,256,256]{2,1,0:T(8,128)(2,1)}, bf16[512,1024]{1,0:T(8,128)(2,1)}, bf16[512,1024]{1,0:T(8,128)(2,1)}) custom-call(f32[256,2048]{1,0:T(8,128)} %get-tuple-element.98.grad_ref, f32[256,2048]{1,0:T(8,128)} %get-tuple-element.86.middle_ref, ...), custom_call_target="tpu_custom_call" | custom-call | flops 2147483648 | bytes 60000000 | tf_op jit(solution)/shard_map/out_back/pallas_call | solution.py:1780
  592.5 3.0 collective-permute-start.4
  597.6 57.1 %attend_back.1 = (bf16[4,512,256]{2,1,0:T(8,128)(2,1)}, bf16[2,4,512,128]{3,2,1,0:T(8,128)(2,1)}) custom-call(s32[2]{0:T(128)} %pad_add_fusion.scalar_ref, bf16[4,512,256]{2,1,0:T(8,128)(2,1)} %bitcast.104, bf16[4,512,128]{2,1,0:T(8,128)(2,1)} %bitcast.98, bf16[4,512,128]{2,1,0:T(8,128)(2,1)} %bitcast.110, bf16[4,512,256]{2,1,0:T(8,128)(2,1)} %bitcast.108, ...), custom_call_target="tpu_custom_call" | custom-call | flops 60000002048 | bytes 10000000 | tf_op jit(solution)/shard_map/attend_back/pallas_call | solution.py:375
  654.7 1.9 slice.19
  656.5 7.9 collective-permute-done.4
  666.1 48.7 %dkeys.1 = (bf16[2048,128]{1,0:T(8,128)(2,1)}, bf16[8,64,1024]{2,1,0:T(8,128)(2,1)}) custom-call(bf16[2,2048,128]{2,1,0:T(8,128)(2,1)} %bitcast.88, f32[2,8,64,1024]{3,2,1,0:T(8,128)} %bitcast.71, bf16[8,64,1024]{2,1,0:T(8,128)(2,1)} %bitcast.96, bf16[8,64,1024]{2,1,0:T(8,128)(2,1)} %bitcast.95, bf16[8,64,1024]{2,1,0:T(8,128)(2,1)} %bitcast.81), custom_call_target="tpu_custom_call" | custom-call | bytes 120000000 | tf_op jit(solution)/shard_map/dkeys/pallas_call | solution.py:570
  715.8 17.5 %project_back.1 = (bf16[2048,2048]{1,0:T(8,128)(2,1)}, bf16[2048,384]{1,0:T(8,128)(2,1)}) custom-call(s32[1]{0:T(128)} %bitcast.hi_ref, bf16[2048,256]{1,0:T(8,128)(2,1)} %bitcast.117, bf16[2048,128]{1,0:T(8,128)(2,1)} %bitcast.99, bf16[2048,128]{1,0:T(8,128)(2,1)} %get-tuple-element.110.other_ref, bf16[2048,2048]{1,0:T(8,128)(2,1)} %get-tuple-element.111.rows_ref, ...), custom_call_target="tpu_custom_call" | custom-call | flops 6442450944 | bytes 24000000 | tf_op jit(solution)/shard_map/project_back/pallas_call | solution.py:128
  733.4 6.7 convolution_convert_fusion.1
  741.3 86.3 %close.1 = (f32[256,2048]{1,0:T(8,128)}, bf16[16,64,384]{2,1,0:T(8,128)(2,1)}, bf16[8,64,1024]{2,1,0:T(8,128)(2,1)}, f32[32,8,128]{2,1,0:T(8,128)}, bf16[2,64,2048]{2,1,0:T(8,128)(2,1)}) custom-call(bf16[8,256,2048]{2,1,0:T(8,128)(2,1)} %bitcast.72, bf16[2,16,64,384]{3,2,1,0:T(8,128)(2,1)} %bitcast.91, f32[2,8,64,1024]{3,2,1,0:T(8,128)} %bitcast.70, ...), custom_call_target="tpu_custom_call" | custom-call | bytes 120000000 | tf_op jit(solution)/shard_map/close/pallas_call | solution.py:1861
  827.6 10.1 %final.1 = (f32[256,2048]{1,0:T(8,128)}, f32[64,2048]{1,0:T(8,128)}, f32[64,512]{1,0:T(8,128)}, f32[64,512]{1,0:T(8,128)}, f32[64,1]{1,0:T(8,128)}, /*index=5*/f...) custom-call(f32[256,2048]{1,0:T(8,128)} %get-tuple-element.117.first_ref, ...), custom_call_target="tpu_custom_call" | custom-call | tf_op jit(solution)/shard_map/final/pallas_call | solution.py:1876
  837.7 1.4 reduce.4
  839.1 1.4 reduce.5
  840.5 1.5 slice_reduce_fusion
  (65 shorter events, 19.4 us)
Async XLA Ops:
  7.2 187.7 %all-gather.3.cloned.1.call-start = ((), (), s32[]{:S(2)}) async-start(), calls=%async_computation | async-start | bytes 9437184 | tf_op jit(solution)/shard_map/all_gather | solution.py:1681
  93.7 639.7 %all-gather.5.cloned.1.call-start = ((), (), s32[]{:S(2)}) async-start(), calls=%async_computation.1 | async-start | bytes 9437184 | tf_op jit(solution)/shard_map/all_gather | solution.py:1815
  146.2 48.6 %collective-permute-start = (bf16[512,1024]{1,0:T(8,128)(2,1)}, bf16[512,1024]{1,0:T(8,128)(2,1)S(1)}, u32[]{:S(2)}, u32[]{:S(2)}) collective-permute-start(bf16[512,1024]{1,0:T(8,128)(2,1)} %bitcast.105), channel_id=1, source_target_pairs={{0,2},{2,0},{1,3},{3,1},{4,6},{6,4},{5,7},{7,5},{8,10},{10,8},{9,1... | collective-permute-start | bytes 3145736 | tf_op jit(solution)/shard_map/ppermute | solution.py:1145
  147.9 38.7 %copy-start.12 = (f32[32,8,128]{2,1,0:T(8,128)S(1)}, f32[32,8,128]{2,1,0:T(8,128)}, u32[]{:S(2)}) copy-start(f32[32,8,128]{2,1,0:T(8,128)} %get-tuple-element.75) | copy-start | bytes 393220
  194.9 1.0 copy-start.14
  310.5 24.0 %collective-permute-start.1 = (bf16[256,2048]{1,0:T(8,128)(2,1)}, bf16[256,2048]{1,0:T(8,128)(2,1)}, u32[]{:S(2)}, u32[]{:S(2)}) collective-permute-start(bf16[256,2048]{1,0:T(8,128)(2,1)} %get-tuple-element.90), channel_id=1, source_target_pairs={{0,16},{16,0},{1,17},{17,1},{2,18},{18,2},{3,19},{19,3},{4,20},{20... | collective-permute-start | bytes 3145736 | tf_op jit(solution)/shard_map/ppermute | solution.py:1145
  311.5 12.6 %copy-start = (f32[2048,1024]{1,0:T(8,128)S(1)}, f32[2048,1024]{1,0:T(8,128)}, u32[]{:S(2)}) copy-start(f32[2048,1024]{1,0:T(8,128)} %get-tuple-element.87) | copy-start | bytes 25165828
  324.1 6.0 copy-start.3
  330.0 6.7 copy-start.2
  330.0 4.5 copy-start.8
  336.8 11.3 %copy-start.4 = (bf16[2,2,256,2048]{3,2,1,0:T(8,128)(2,1)}, bf16[2,2,256,2048]{3,2,1,0:T(8,128)(2,1)S(1)}, u32[]{:S(2)}) copy-start(bf16[2,2,256,2048]{3,2,1,0:T(8,128)(2,1)S(1)} %pad_maximum_fusion) | copy-start | bytes 12582916
  348.1 39.8 %copy-start.1 = (f32[256,2048]{1,0:T(8,128)S(1)}, f32[256,2048]{1,0:T(8,128)}, u32[]{:S(2)}) copy-start(f32[256,2048]{1,0:T(8,128)} %get-tuple-element.86.middle_ref) | copy-start | bytes 6291460
  348.1 39.8 %copy-start.7 = (bf16[1,256,2048]{2,1,0:T(8,128)(2,1)S(1)}, bf16[1,256,2048]{2,1,0:T(8,128)(2,1)}, u32[]{:S(2)}) copy-start(bf16[1,256,2048]{2,1,0:T(8,128)(2,1)} %param.16) | copy-start | bytes 3145732
  448.3 48.1 %collective-permute-start.2 = (bf16[2,256,2048]{2,1,0:T(8,128)(2,1)}, bf16[2,256,2048]{2,1,0:T(8,128)(2,1)S(1)}, u32[]{:S(2)}, u32[]{:S(2)}) collective-permute-start(bf16[2,256,2048]{2,1,0:T(8,128)(2,1)} %get-tuple-element.95), channel_id=1, source_target_pairs={{0,16},{16,0},{1,17},{17,1},{2,18},{18,2},{3,19},{19,3},{4,20},{20... | collective-permute-start | bytes 6291464 | tf_op jit(solution)/shard_map/ppermute | solution.py:1145
  496.4 1.3 copy-start.13
  567.9 27.5 %copy-start.16 = (bf16[512,1024]{1,0:T(8,128)(2,1)S(1)}, bf16[512,1024]{1,0:T(8,128)(2,1)}, u32[]{:S(2)}) copy-start(bf16[512,1024]{1,0:T(8,128)(2,1)} %get-tuple-element.108) | copy-start | bytes 3145732
  568.0 28.3 %copy-start.15 = (bf16[512,1024]{1,0:T(8,128)(2,1)S(1)}, bf16[512,1024]{1,0:T(8,128)(2,1)}, u32[]{:S(2)}) copy-start(bf16[512,1024]{1,0:T(8,128)(2,1)} %get-tuple-element.109) | copy-start | bytes 3145732
  592.5 71.9 %collective-permute-start.4 = (bf16[512,1024]{1,0:T(8,128)(2,1)}, bf16[512,1024]{1,0:T(8,128)(2,1)S(1)}, u32[]{:S(2)}, u32[]{:S(2)}) collective-permute-start(bf16[512,1024]{1,0:T(8,128)(2,1)} %get-tuple-element.105.first_ref), channel_id=1, source_target_pairs={{0,2},{2,0},{1,3},{3,1},{4,6},{6,4},{5,7},{7,5},{8,10},{10,8},{9,1... | collective-permute-start | bytes 3145736 | tf_op jit(solution)/shard_map/ppermute | solution.py:1145
  595.5 68.9 %collective-permute-start.3 = (bf16[512,1024]{1,0:T(8,128)(2,1)S(1)}, bf16[512,1024]{1,0:T(8,128)(2,1)S(1)}, u32[]{:S(2)}, u32[]{:S(2)}) collective-permute-start(bf16[512,1024]{1,0:T(8,128)(2,1)S(1)} %copy-done.16), channel_id=1, source_target_pairs={{0,16},{16,0},{1,17},{17,1},{2,18},{18,2},{3,19},{19,3},{4,20},{20... | collective-permute-start | bytes 3145736 | tf_op jit(solution)/shard_map/ppermute | solution.py:1145
  596.3 68.1 %collective-permute-start.5 = (bf16[512,1024]{1,0:T(8,128)(2,1)S(1)}, bf16[512,1024]{1,0:T(8,128)(2,1)S(1)}, u32[]{:S(2)}, u32[]{:S(2)}) collective-permute-start(bf16[512,1024]{1,0:T(8,128)(2,1)S(1)} %copy-done.15), channel_id=1, source_target_pairs={{0,16},{16,0},{1,17},{17,1},{2,18},{18,2},{3,19},{19,3},{4,20},{20... | collective-permute-start | bytes 3145736 | tf_op jit(solution)/shard_map/ppermute | solution.py:1145
  597.5 117.3 %collective-permute-start.6 = (bf16[512,1024]{1,0:T(8,128)(2,1)}, bf16[512,1024]{1,0:T(8,128)(2,1)S(1)}, u32[]{:S(2)}, u32[]{:S(2)}) collective-permute-start(bf16[512,1024]{1,0:T(8,128)(2,1)} %get-tuple-element.112), channel_id=1, source_target_pairs={{0,2},{2,0},{1,3},{3,1},{4,6},{6,4},{5,7},{7,5},{8,10},{10,8},{9,1... | collective-permute-start | bytes 3145736 | tf_op jit(solution)/shard_map/ppermute | solution.py:1145
  664.4 1.0 copy-start.10
  664.4 1.3 copy-start.11
  664.4 1.7 copy-start.5
  714.8 1.0 copy-start.9
  715.8 17.5 %copy-start.6 = (bf16[4,512,256]{2,1,0:T(8,128)(2,1)S(1)}, bf16[4,512,256]{2,1,0:T(8,128)(2,1)}, u32[]{:S(2)}) copy-start(bf16[4,512,256]{2,1,0:T(8,128)(2,1)} %get-tuple-element.82.out_ref) | copy-start | bytes 3145732
Sparse Core Ops, SparseCore 0:
  93.8 65.9 all-gather.2
  592.0 131.2 all-gather.4

commit v5 on v4

--- a/solution.py
+++ b/solution.py
@@ -1236,6 +1236,174 @@
         ),
         name="out_project",
     )(mixed, weight, rows, gain)
+
+
+def start_kernel(
+    key_head, places, wide, query_ref, key_ref, value_ref, w_gate_ref, w_up_ref, rows_ref, small_ref, wout_ref,
+    down_ref, cos_ref, sina_ref, sinb_ref, all_ref, weight_ref, smalls_ref, wouts_ref, gates_ref, ups_ref, downs_ref, other_ref, normed_ref, q_ref, kv_ref, g_send,
+    g_recv, g_local, g_held, w_send, w_recv, d_send, d_recv, s_send, s_recv, o_send, o_recv, local, w_held, o_held,
+    ga_send, ga_recv, ga_local, ga_held, up_send, up_recv, up_local, up_held, x_send, x_recv, k_send, k_recv, heads_ref,
+    gate_ref, up_ref, weight, smalls, gain, chunks, cosines, sinas, sinbs, sem, t_sem,
+):
+    blk, hi, lo = (lax.axis_index(a) for a in SEQ)
+    mine = device_place()
+    peers = every_peer()
+    unit = chunks.shape[1]
+    tables = []
+    for b in range(4):
+        rows_of = pl.ds(pl.multiple_of((2 * b + hi) * unit, unit), unit)
+        for t, (ref, table) in enumerate(((cos_ref, cosines), (sina_ref, sinas), (sinb_ref, sinbs))):
+            tables.append(local_copy(ref.at[rows_of], table.at[b], t_sem.at[b, t]))
+    deal_heads(key_head, query_ref, key_ref, value_ref, heads_ref)
+    greet(peers)
+    own_head = Carried(heads_ref.at[blk * 2 + lo], weight_ref.at[mine], w_held, local.at[0])
+    small_copies = [local_copy(small_ref, smalls_ref.at[mine], local.at[1])]
+    for k, to in enumerate(peers):
+        small_copies.append(remote(small_ref, smalls_ref.at[mine], s_send.at[k], s_recv.at[k], to))
+    end = gather_begin(rows_ref, all_ref, g_send, g_recv, g_local, g_held)
+    dp, seq = lax.axis_index("dp"), seq_peers()
+    seq_n = len(seq) + 1
+    straight, handed = [], []
+    for k, (to, source) in enumerate(seq):
+        part = heads_ref.at[to["blk"] * 2 + to["lo"]]
+        straight.append(remote(part, weight_ref.at[mine], w_send.at[k], w_recv.at[k], to))
+
+    def hand_on(part, place, k):
+        for d, to in enumerate(dp_peers()):
+            n = d * seq_n + k
+            handed.append(remote(part, weight_ref.at[place], d_send.at[n], d_recv.at[n], to))
+
+    hand_on(heads_ref.at[blk * 2 + lo], mine, seq_n - 1)
+    deal_units(places, wide, w_gate_ref, w_up_ref, gate_ref, up_ref)
+
+    def pass_on(turn):
+        for k, (to, source) in enumerate(seq):
+            if k * 2 * PIECES // len(seq) == turn:
+                straight[k].wait()
+                place = dp * seq_n + source
+                hand_on(weight_ref.at[place], place, k)
+
+    end(pass_on)
+    copies = [Carried(wout_ref, wouts_ref.at[hi, lo], o_held, local.at[2])]
+    next_lo = {"lo": 1 - lo}
+    wout = remote(wout_ref, wouts_ref.at[hi, lo], o_send.at[0], o_recv.at[0], other_hi())
+    copies.append(remote(wout_ref, wouts_ref.at[hi, lo], o_send.at[1], o_recv.at[1], next_lo))
+    copies += swap_begin(gate_ref, gates_ref, ga_send, ga_recv, ga_local, ga_held)
+    copies += swap_begin(up_ref, ups_ref, up_send, up_recv, up_local, up_held)
+    own_head.turn()
+    wait_all(small_copies)
+    load_smalls = local_copy(smalls_ref, smalls, sem.at[2])
+    load_rows = lambda b: local_copy(all_ref.at[pl.ds(2 * b, 2)], chunks_of(chunks, b), sem.at[b % 2])
+    loads = [load_rows(0), load_rows(1)]
+    own_head.wait()
+    wait_all(handed)
+    load_weight = local_copy(weight_ref, weight, sem.at[3])
+    for d, to in enumerate(dp_peers()):
+        copies.append(remote(down_ref, downs_ref.at[d], x_send.at[d], x_recv.at[d], to))
+    load_smalls.wait()
+    low = lanes_low((1, 128))
+    for j in range(smalls.shape[0] // 2):
+        gain[:, 128 * j : 128 * j + 128] = jnp.where(
+            low, smalls[2 * j, 0:1, :], pltpu.roll(smalls[2 * j + 1, 0:1, :], HEAD_SIZE, 1)
+        )
+    load_weight.wait()
+    wait_all(tables)
+    width = gain.shape[1]
+    half = HEAD_SIZE // 2
+    low = lanes_low((unit, 128))
+    for b in range(4):
+        here = slice(b * unit, b * unit + unit)
+        loads[b].wait()
+        rows = chunks[b % 2].astype(F32)
+        normed_ref[here, :] = (norm_parts(rows)[0] * gain[...]).astype(BF16)
+        if b + 2 < 4:
+            loads.append(load_rows(b + 2))
+        made = dot32(normed_ref[here, :], weight[...].reshape(width, -1))
+        cosine, sina, sinb = cosines[b], sinas[b], sinbs[b]
+        for part in range(3):
+            u = made[:, 128 * part : 128 * part + 128]
+            up, down = pltpu.roll(u, 128 - half, 1), pltpu.roll(u, half, 1)
+            turned = u * cosine + up * sina + down * sinb
+            if part < 2:
+                q_ref[here, 128 * part : 128 * part + 128] = (
+                    turned.astype(BF16).astype(F32) * ATTN_SCALE
+                ).astype(BF16)
+            else:
+                kv_ref[here, :] = jnp.where(low, turned, u).astype(BF16)
+        piece = pl.ds(b * unit, unit)
+        copies.append(
+            remote(kv_ref.at[piece], other_ref.at[piece], k_send.at[b], k_recv.at[b], other_hi())
+        )
+        if b == 2:
+            wout.wait()
+            there = wouts_ref.at[1 - hi, lo]
+            copies.append(remote(there, there, o_send.at[2], o_recv.at[2], next_lo))
+    finish(copies)
+
+
+def chunks_of(chunks, b):
+    return chunks.at[b % 2].reshape(2, chunks.shape[1] // 2, chunks.shape[2])
+
+
+def through_start(key_head, places, wide_w, heads_shape, part_shape, weights, rows, small, wout, down, tables):
+    tok, width = rows.shape
+    rows_w = wout.shape[0]
+    part = part_shape[1:]
+    dp_n, hi_n, lo_n = (lax.axis_size(a) for a in ("dp", "hi", "lo"))
+    every = dp_n * hi_n * lo_n * lax.axis_size("blk")
+    wide = heads_shape[2]
+    anywhere, inside = pl.BlockSpec(memory_space=pl.ANY), pl.BlockSpec(memory_space=pltpu.VMEM)
+    shapes = [
+        ((8, tok, width), BF16),
+        ((every, rows_w, wide), BF16),
+        ((every, 8, 128), F32),
+        ((hi_n, lo_n, rows_w, width), BF16),
+        (part_shape, BF16),
+        (part_shape, BF16),
+        ((dp_n - 1,) + down.shape, BF16),
+        ((8 * tok, 128), BF16),
+        ((8 * tok, width), BF16),
+        ((8 * tok, 256), BF16),
+        ((8 * tok, 128), BF16),
+    ]
+    return pl.pallas_call(
+        functools.partial(start_kernel, key_head, places, wide_w),
+        in_specs=[inside] * 5 + [anywhere] * 7,
+        out_specs=[anywhere] * 8 + [inside] * 3,
+        out_shape=[jax.ShapeDtypeStruct(shape, dtype) for shape, dtype in shapes],
+        scratch_shapes=gather_scratch(tok, width)
+        + sems(every // dp_n - 1)
+        + sems((dp_n - 1) * every // dp_n)
+        + sems(every - 1)
+        + sems(3)
+        + [
+            pltpu.SemaphoreType.DMA((3,)),
+            pltpu.VMEM((rows_w, wide), BF16),
+            pltpu.VMEM((rows_w, width), BF16),
+        ]
+        + swap_scratch(part)
+        + swap_scratch(part)
+        + sems(dp_n - 1)
+        + sems(4)
+        + [
+            pltpu.VMEM(heads_shape, BF16),
+            pltpu.VMEM(part_shape, BF16),
+            pltpu.VMEM(part_shape, BF16),
+            pltpu.VMEM((every, rows_w, wide), BF16),
+            pltpu.VMEM((every, 8, 128), F32),
+            pltpu.VMEM((1, width), F32),
+            pltpu.VMEM((2, 2 * tok, width), BF16),
+        ]
+        + [pltpu.VMEM((4, 2 * tok, 128), F32)] * 3
+        + [pltpu.SemaphoreType.DMA((4,)), pltpu.SemaphoreType.DMA((4, 3))],
+        compiler_params=pltpu.CompilerParams(
+            collective_id=11, has_side_effects=True, vmem_limit_bytes=VMEM_LIMIT
+        ),
+        cost_estimate=pl.CostEstimate(
+            flops=16 * tok * width * wide, bytes_accessed=250_000_000, transcendentals=0
+        ),
+        name="start",
+    )(*weights, rows, small, wout, down, *tables)
 
 
 def middle_kernel(
@@ -1459,12 +1627,20 @@
 def deal_kernel(
     key_head, places, wide, query_ref, key_ref, value_ref, gate_ref, up_ref, heads_ref, gates_ref, ups_ref
 ):
+    deal_heads(key_head, query_ref, key_ref, value_ref, heads_ref)
+    deal_units(places, wide, gate_ref, up_ref, gates_ref, ups_ref)
+
+
+def deal_heads(key_head, query_ref, key_ref, value_ref, heads_ref):
     columns, k_columns = query_ref.shape[1] // 8, key_ref.shape[1] // 8
     for f in range(8):
         g = key_head(f)
         cols, k_cols = slice(g * columns, g * columns + columns), slice(g * k_columns, g * k_columns + k_columns)
         heads_ref[f, :, :columns] = query_ref[:, cols]
         heads_ref[f, :, columns:] = jnp.concatenate([key_ref[:, k_cols], value_ref[:, k_cols]], axis=1)
+
+
+def deal_units(places, wide, gate_ref, up_ref, gates_ref, ups_ref):
     for at, (f, to) in enumerate(places):
         here, there = slice(at * wide, at * wide + wide), slice(to * wide, to * wide + wide)
         gates_ref[f, :, there] = gate_ref[:, here]
@@ -1610,7 +1786,11 @@
     ]
     part_shape = jax.ShapeDtypeStruct((group, rows_w, ff_part), BF16)
     params = pltpu.CompilerParams(vmem_limit_bytes=VMEM_LIMIT)
-    if units_w % 128 == 0:
+    one_start = reblock == block and rows_w == HEAD_SIZE and blk_n == 4 and units_w % 128 == 0
+    head_wide = q_cols + 2 * k_cols
+    if one_start:
+        pass
+    elif units_w % 128 == 0:
         head_shape = jax.ShapeDtypeStruct((group, rows_w, q_cols + 2 * k_cols), BF16)
         head_parts, gate_parts, up_parts = pl.pallas_call(
             functools.partial(deal_kernel, key_head, ff_places, units_w),
@@ -1623,58 +1803,76 @@
             [head_columns(w) for w in (w_query, key_projection, value_projection)], axis=2
         )
         gate_parts, up_parts = unit_columns(w_gate), unit_columns(w_up)
-    head_wide = head_parts.shape[2]
 
     pad = jnp.zeros((7 * 128 + 128 - 2 * rows_w - 1,), F32)
     small = jnp.concatenate(
         [attn_gain.astype(F32), mlp_gain.astype(F32), lengths.astype(F32), pad]
     ).reshape(8, 128)
-    rows_all, qkv_weight, smalls, out_rows = comm_call(
-        open_kernel,
-        0,
-        [hidden[0], head_parts, small, w_out],
-        [
-            ((group, tok, width), BF16),
-            ((every, rows_w, head_wide), BF16),
-            ((every, 8, 128), F32),
-            ((hi_n, lo_n, rows_w, width), BF16),
-        ],
-        gather_scratch(tok, width)
-        + sems(every // dp_n - 1)
-        + sems((dp_n - 1) * every // dp_n)
-        + sems(every - 1)
-        + sems(3)
-        + [
-            pltpu.SemaphoreType.DMA((3,)),
-            pltpu.VMEM((rows_w, head_wide), BF16),
-            pltpu.VMEM((rows_w, width), BF16),
-        ],
-        "open",
-    )
+    hi_index = hi.astype(jnp.int32).reshape(1)
+    tables = rope_tables(seq_len)
+    unit = lo_n * tok
+    part_rows = group * rows_w
+    if one_start:
+        _, qkv_weight, smalls, out_rows, gate_parts, up_parts, downs, other_kv, normed_one, q, kv = (
+            through_start(
+                key_head,
+                ff_places,
+                units_w,
+                (group, rows_w, head_wide),
+                (group, rows_w, ff_part),
+                (w_query, key_projection, value_projection, w_gate, w_up),
+                hidden[0],
+                small,
+                w_out,
+                w_down,
+                tables,
+            )
+        )
+    else:
+        rows_all, qkv_weight, smalls, out_rows = comm_call(
+            open_kernel,
+            0,
+            [hidden[0], head_parts, small, w_out],
+            [
+                ((group, tok, width), BF16),
+                ((every, rows_w, head_wide), BF16),
+                ((every, 8, 128), F32),
+                ((hi_n, lo_n, rows_w, width), BF16),
+            ],
+            gather_scratch(tok, width)
+            + sems(every // dp_n - 1)
+            + sems((dp_n - 1) * every // dp_n)
+            + sems(every - 1)
+            + sems(3)
+            + [
+                pltpu.SemaphoreType.DMA((3,)),
+                pltpu.VMEM((rows_w, head_wide), BF16),
+                pltpu.VMEM((rows_w, width), BF16),
+            ],
+            "open",
+        )
+        qkv_weight = qkv_weight.reshape(width, head_wide)
+        gain_one = smalls[:, 0, :rows_w].reshape(1, width)
+        normed_one, q, kv = project(
+            hi_index, rows_all.reshape(group * tok, width), gain_one, qkv_weight, tables, tok
+        )
+        other_kv, gate_parts, up_parts, downs = comm_call(
+            keys_kernel,
+            2,
+            [kv, gate_parts, up_parts, w_down],
+            [
+                (kv.shape, BF16),
+                (gate_parts.shape, BF16),
+                (up_parts.shape, BF16),
+                ((dp_n - 1,) + w_down.shape, BF16),
+            ],
+            sems(1) + swap_scratch((rows_w, ff_part)) * 2 + sems(dp_n - 1),
+            "keys",
+        )
     qkv_weight = qkv_weight.reshape(width, head_wide)
     gain_one = smalls[:, 0, :rows_w].reshape(1, width)
     gain_two = smalls[:, 0, rows_w : 2 * rows_w].reshape(1, width)
     valid_count = jnp.sum(smalls.reshape(every, -1)[:: every // dp_n, 2 * rows_w])
-    hi_index = hi.astype(jnp.int32).reshape(1)
-    tables = rope_tables(seq_len)
-    normed_one, q, kv = project(
-        hi_index, rows_all.reshape(group * tok, width), gain_one, qkv_weight, tables, tok
-    )
-    unit = lo_n * tok
-    part_rows = group * rows_w
-    other_kv, gate_parts, up_parts, downs = comm_call(
-        keys_kernel,
-        2,
-        [kv, gate_parts, up_parts, w_down],
-        [
-            (kv.shape, BF16),
-            (gate_parts.shape, BF16),
-            (up_parts.shape, BF16),
-            ((dp_n - 1,) + w_down.shape, BF16),
-        ],
-        sems(1) + swap_scratch((rows_w, ff_part)) * 2 + sems(dp_n - 1),
-        "keys",
-    )
     gate_parts = gate_parts.reshape(part_rows, -1)
     up_parts = up_parts.reshape(part_rows, -1)
     gate_other = swap_pair(gate_parts, "hi")

time: 859 us -> 849 us (0.988)
  Pallas kernels: 731 us -> 699 us
  waiting for transfers between devices: 28.8 us -> 51.5 us
    pallas_call x4 -> x2, Pallas kernels: 207 us -> 73.1 us  [comm_call(): pl.pallas_call(kernel, in_specs=[anywhere] * len(arrays), out_specs=[anyw...]
    pallas_call x2 -> x1, Pallas kernels: 16.5 us -> 120 us  [through_start(): pl.pallas_call(functools.partial(start_kernel, key_head, places, wide_w),...]
    ppermute x7, waiting for transfers between devices: 28.7 us -> 47.4 us  [swap_pair(): return lax.ppermute(block, axis, [(0, 1), (1, 0)])]
  transfers between devices with their start and end apart: 9 -> 9, of which waited for: 4 -> 5; matrix products, arithmetic and copies ran while one was open for 3% -> 3% of each run, Pallas kernels for 29% -> 22%
where the time goes in v5:
time: 849 us; the launch traced here: 842 us
  Pallas kernels  699 us (82%)
  waiting for transfers between devices  51.5 us (6%)
  matrix products  30.6 us (4%)
  other arithmetic  22.9 us (3%)
  between operations  18.4 us (2%)
  starting transfers between devices  10.2 us (1%)
  local copies, waits for them, and re-layouts  8.65 us (1%)
    pallas_call x1, Pallas kernels, through_start(): pl.pallas_call(functools.partial(start_kernel, key_head, places, wide_w),...  120 us
    pallas_call x1, Pallas kernels, through_middle(): pl.pallas_call(functools.partial(middle_kernel, order, pairs, block), in_...  114 us
    pallas_call x1, Pallas kernels, shards(): pl.pallas_call(functools.partial(close_kernel, with_out), in_specs=[anywh...  84.5 us
    pallas_call x2, Pallas kernels, comm_call(): pl.pallas_call(kernel, in_specs=[anywhere] * len(arrays), out_specs=[anyw...  73.1 us
    pallas_call x1, Pallas kernels, scatter_down(): pl.pallas_call(scatter_down_kernel, in_specs=[anywhere] * 6, out_specs=[i...  70.3 us
    pallas_call x1, Pallas kernels, attend_back(): pl.pallas_call(attend_back_kernel, grid=(units,), in_specs=[pl.BlockSpec(...  56.8 us
    ppermute x7, waiting for transfers between devices, swap_pair(): return lax.ppermute(block, axis, [(0, 1), (1, 0)])  47.4 us
    pallas_call x1, Pallas kernels, scatter_square(): pl.pallas_call(functools.partial(scatter_kernel, len(first)), in_specs=[p...  40.3 us
  transfers between devices with their start and end apart: 9, of which 5 were waited for; matrix products, arithmetic and copies ran while one was open for 3% of the time, Pallas kernels for 22%

profile of v5, /device:TPU:0, one launch (start us, length us, event | category | flops | bytes accessed | tf_op | source)
XLA Modules:
  0.0 841.6 jit_solution(3029803637454003558)
XLA Ops:
  9.8 119.6 %start.1 = (bf16[8,256,2048]{2,1,0:T(8,128)(2,1)}, bf16[32,64,384]{2,1,0:T(8,128)(2,1)}, f32[32,8,128]{2,1,0:T(8,128)}, bf16[2,2,64,2048]{3,2,1,0:T(8,128)(2,1)}...) custom-call(bf16[64,2048]{1,0:T(8,128)(2,1)} %query_ref.3, ...), custom_call_target="tpu_custom_call" | custom-call | flops 3221225472 | bytes 250000000 | tf_op jit(solution)/shard_map/start/pallas_call | solution.py:1369
  129.5 2.6 collective-permute-start
  132.7 38.7 %attend.1 = (bf16[4,512,256]{2,1,0:T(8,128)(2,1)}, f32[4,8,512]{2,1,0:T(8,128)}) custom-call(s32[2]{0:T(128)} %pad_add_fusion.scalar_ref, bf16[4,512,256]{2,1,0:T(8,128)(2,1)} %bitcast.107, bf16[4,512,128]{2,1,0:T(8,128)(2,1)} %bitcast.113, bf16[4,512,128]{2,1,0:T(8,128)(2,1)} %bitcast.111), custom_call_target="tpu_custom_call" | custom-call | flops 40000000000 | bytes 8000000 | tf_op jit(solution)/shard_map/attend/pallas_call | solution.py:241
  173.5 4.8 collective-permute-done.gate_other_ref
  178.3 4.0 all-gather.3.cloned.1.call-done.weight_ref
  182.4 113.7 %middle.1 = (bf16[8,256,2048]{2,1,0:T(8,128)(2,1)}, f32[256,2048]{1,0:T(8,128)}, bf16[2,2,512,1024]{3,2,1,0:T(8,128)(2,1)}, bf16[2,2,512,1024]{3,2,1,0:T(8,128)(...) custom-call(bf16[8,256,256]{2,1,0:T(8,128)(2,1)} %bitcast.81, ...), custom_call_target="tpu_custom_call" | custom-call | flops 8589934592 | bytes 250000000 | tf_op jit(solution)/shard_map/middle/pallas_call | solution.py:1482
  297.2 12.7 %fusion.7 = f32[2048,1024]{1,0:T(8,128)S(1)} fusion(bf16[2048,2048]{1,0:T(8,128)(2,1)} %bitcast.100, bf16[2048,1024]{1,0:T(8,128)(2,1)} %bitcast.104), kind=kOutput, calls=%fused_computation.32 | convolution fusion | flops 8589934592 | bytes 20971520 | tf_op jit(solution)/shard_map/dot_general | solution.py:30
  310.0 5.9 multiply_convert_fusion
  315.9 2.4 select_bitcast_fusion.1
  318.3 1.4 collective-permute-done.1
  321.9 11.1 %convolution_convert_fusion = bf16[2048,2048]{1,0:T(8,128)(2,1)} fusion(bf16[2048,1024]{1,0:T(8,128)(2,1)S(1)} %get-tuple-element.131.left_ref, bf16[1024,2048]{1,0:T(8,128)(2,1)S(1)} %bitcast.77), kind=kOutput, calls=%fused_computation.4 | convolution fusion | flops 8594128896 | bytes 16777216 | tf_op jit(solution)/shard_map/dot_general | solution.py:30
  333.1 40.3 %scatter_square.1 = f32[256,2048]{1,0:T(8,128)} custom-call(bf16[8,256,2048]{2,1,0:T(8,128)(2,1)} %bitcast.72), custom_call_target="tpu_custom_call" | custom-call | bytes 120000000 | tf_op jit(solution)/shard_map/scatter_square/pallas_call | solution.py:1033
  373.4 4.9 multiply_convert_fusion.2
  378.3 39.9 %gather_square.1 = bf16[8,256,2048]{2,1,0:T(8,128)(2,1)} custom-call(bf16[256,2048]{1,0:T(8,128)(2,1)} %get-tuple-element.128.rows_ref), custom_call_target="tpu_custom_call" | custom-call | bytes 120000000 | tf_op jit(solution)/shard_map/gather_square/pallas_call | solution.py:570
  418.2 15.6 %weight_grad.1 = (bf16[2,256,2048]{2,1,0:T(8,128)(2,1)}, f32[2,256,2048]{2,1,0:T(8,128)}) custom-call(s32[1]{0:T(128)} %bitcast.24.dp_ref, bf16[2048,1024]{1,0:T(8,128)(2,1)} %copy-done.2, bf16[2048,2048]{1,0:T(8,128)(2,1)} %bitcast.73, bf16[2048,2048]{1,0:T(8,128)(2,1)} %bitcast.74), custom_call_target="tpu_custom_call" | custom-call | flops 8589934592 | bytes 24000000 | tf_op jit(solution)/shard_map/weight_grad/pallas_call | solution.py:1542
  433.8 1.4 collective-permute-start.2
  435.2 35.4 %ff_back.1 = (bf16[2048,1024]{1,0:T(8,128)(2,1)}, bf16[2048,1024]{1,0:T(8,128)(2,1)}, bf16[2048,2048]{1,0:T(8,128)(2,1)}) custom-call(bf16[2048,2048]{1,0:T(8,128)(2,1)} %bitcast.75, bf16[2048,1024]{1,0:T(8,128)(2,1)} %get-tuple-element.130.gate_slope_ref, bf16[2048,1024]{1,0:T(8,128)(2,1)} %get-tuple-element.132.up_slope_ref, bf16[2048,1024]{1,0:T(8,128)(2,1)} %bitcast.103, ...), custom_call_target="tpu_custom_call" | custom-call | flops 25769803776 | bytes 40000000 | tf_op jit(solution)/shard_map/ff_back/pallas_call | solution.py:1600
  470.6 11.3 %collective-permute-done.2.got_ref = bf16[2,256,2048]{2,1,0:T(8,128)(2,1)S(1)} collective-permute-done((bf16[2,256,2048]{2,1,0:T(8,128)(2,1)}, bf16[2,256,2048]{2,1,0:T(8,128)(2,1)S(1)}, u32[]{:S(2)}, u32[]{:S(2)}) %collective-permute-start.2) | collective-permute-done | bytes 2097184 | tf_op jit(solution)/shard_map/ppermute | solution.py:1145
  483.2 70.3 %scatter_down.1 = (f32[256,2048]{1,0:T(8,128)}, f32[256,2048]{1,0:T(8,128)}, f32[2,512,1024]{2,1,0:T(8,128)}, f32[2,512,1024]{2,1,0:T(8,128)}, bf16[512,1024]{1,...) custom-call(bf16[8,256,2048]{2,1,0:T(8,128)(2,1)} %bitcast.102, ...), custom_call_target="tpu_custom_call" | custom-call | flops 17179869184 | bytes 160000000 | tf_op jit(solution)/shard_map/scatter_down/pallas_call | solution.py:1106
  553.6 24.0 %out_back.1 = (f32[256,2048]{1,0:T(8,128)}, bf16[256,2048]{1,0:T(8,128)(2,1)}, bf16[8,256,256]{2,1,0:T(8,128)(2,1)}, bf16[512,1024]{1,0:T(8,128)(2,1)}, bf16[512,1024]{1,0:T(8,128)(2,1)}) custom-call(f32[256,2048]{1,0:T(8,128)} %get-tuple-element.89.grad_ref, f32[256,2048]{1,0:T(8,128)} %get-tuple-element.77.middle_ref, ...), custom_call_target="tpu_custom_call" | custom-call | flops 2147483648 | bytes 60000000 | tf_op jit(solution)/shard_map/out_back/pallas_call | solution.py:1978
  578.9 2.6 collective-permute-start.6
  581.9 1.4 collective-permute-start.3
  583.9 56.8 %attend_back.1 = (bf16[4,512,256]{2,1,0:T(8,128)(2,1)}, bf16[2,4,512,128]{3,2,1,0:T(8,128)(2,1)}) custom-call(s32[2]{0:T(128)} %pad_add_fusion.scalar_ref, bf16[4,512,256]{2,1,0:T(8,128)(2,1)} %bitcast.108, bf16[4,512,128]{2,1,0:T(8,128)(2,1)} %bitcast.114, bf16[4,512,128]{2,1,0:T(8,128)(2,1)} %bitcast.112, bf16[4,512,256]{2,1,0:T(8,128)(2,1)} %bitcast.99, ...), custom_call_target="tpu_custom_call" | custom-call | flops 60000002048 | bytes 10000000 | tf_op jit(solution)/shard_map/attend_back/pallas_call | solution.py:375
  640.8 1.9 slice.18
  642.6 29.9 %collective-permute-done.4 = bf16[512,1024]{1,0:T(8,128)(2,1)S(1)} collective-permute-done((bf16[512,1024]{1,0:T(8,128)(2,1)}, bf16[512,1024]{1,0:T(8,128)(2,1)S(1)}, u32[]{:S(2)}, u32[]{:S(2)}) %collective-permute-start.4) | collective-permute-done | bytes 1048608 | tf_op jit(solution)/shard_map/ppermute | solution.py:1145
  674.3 33.2 %dkeys.1 = (bf16[2048,128]{1,0:T(8,128)(2,1)}, bf16[8,64,1024]{2,1,0:T(8,128)(2,1)}) custom-call(bf16[2,2048,128]{2,1,0:T(8,128)(2,1)} %bitcast.83, f32[2,8,64,1024]{3,2,1,0:T(8,128)} %bitcast.70, bf16[8,64,1024]{2,1,0:T(8,128)(2,1)} %bitcast.92, bf16[8,64,1024]{2,1,0:T(8,128)(2,1)} %bitcast.91, bf16[8,64,1024]{2,1,0:T(8,128)(2,1)} %bitcast.79), custom_call_target="tpu_custom_call" | custom-call | bytes 120000000 | tf_op jit(solution)/shard_map/dkeys/pallas_call | solution.py:570
  708.5 17.4 %project_back.1 = (bf16[2048,2048]{1,0:T(8,128)(2,1)}, bf16[2048,384]{1,0:T(8,128)(2,1)}) custom-call(s32[1]{0:T(128)} %bitcast.hi_ref, bf16[2048,256]{1,0:T(8,128)(2,1)} %bitcast.110, bf16[2048,128]{1,0:T(8,128)(2,1)} %bitcast.93, bf16[2048,128]{1,0:T(8,128)(2,1)} %get-tuple-element.101.other_ref, bf16[2048,2048]{1,0:T(8,128)(2,1)} %get-tuple-element.102.rows_ref, ...), custom_call_target="tpu_custom_call" | custom-call | flops 6442450944 | bytes 24000000 | tf_op jit(solution)/shard_map/project_back/pallas_call | solution.py:128
  725.9 6.7 convolution_convert_fusion.1
  733.9 84.5 %close.1 = (f32[256,2048]{1,0:T(8,128)}, bf16[16,64,384]{2,1,0:T(8,128)(2,1)}, bf16[8,64,1024]{2,1,0:T(8,128)(2,1)}, f32[32,8,128]{2,1,0:T(8,128)}, bf16[2,64,2048]{2,1,0:T(8,128)(2,1)}) custom-call(bf16[8,256,2048]{2,1,0:T(8,128)(2,1)} %bitcast.71, bf16[2,16,64,384]{3,2,1,0:T(8,128)(2,1)} %bitcast.84, f32[2,8,64,1024]{3,2,1,0:T(8,128)} %bitcast.69, ...), custom_call_target="tpu_custom_call" | custom-call | bytes 120000000 | tf_op jit(solution)/shard_map/close/pallas_call | solution.py:2059
  818.4 1.5 slice_reduce_fusion.1
  819.9 10.0 %final.1 = (f32[256,2048]{1,0:T(8,128)}, f32[64,2048]{1,0:T(8,128)}, f32[64,512]{1,0:T(8,128)}, f32[64,512]{1,0:T(8,128)}, f32[64,1]{1,0:T(8,128)}, /*index=5*/f...) custom-call(f32[256,2048]{1,0:T(8,128)} %get-tuple-element.109.first_ref, ...), custom_call_target="tpu_custom_call" | custom-call | tf_op jit(solution)/shard_map/final/pallas_call | solution.py:2074
  830.0 1.4 reduce.4
  (62 shorter events, 15.8 us)
Async XLA Ops:
  7.2 175.2 %all-gather.3.cloned.1.call-start = ((), (), s32[]{:S(2)}) async-start(), calls=%async_computation | async-start | bytes 9437184 | tf_op jit(solution)/shard_map/all_gather | solution.py:1879
  129.5 596.5 %all-gather.5.cloned.1.call-start = ((), (), s32[]{:S(2)}) async-start(), calls=%async_computation.1 | async-start | bytes 9437184 | tf_op jit(solution)/shard_map/all_gather | solution.py:2013
  129.5 48.8 %collective-permute-start = (bf16[512,1024]{1,0:T(8,128)(2,1)}, bf16[512,1024]{1,0:T(8,128)(2,1)S(1)}, u32[]{:S(2)}, u32[]{:S(2)}) collective-permute-start(bf16[512,1024]{1,0:T(8,128)(2,1)} %bitcast.97), channel_id=1, source_target_pairs={{0,2},{2,0},{1,3},{3,1},{4,6},{6,4},{5,7},{7,5},{8,10},{10,8},{9,1... | collective-permute-start | bytes 3145736 | tf_op jit(solution)/shard_map/ppermute | solution.py:1145
  132.7 38.7 %copy-start.12 = (f32[32,8,128]{2,1,0:T(8,128)S(1)}, f32[32,8,128]{2,1,0:T(8,128)}, u32[]{:S(2)}) copy-start(f32[32,8,128]{2,1,0:T(8,128)} %get-tuple-element.76) | copy-start | bytes 393220
  178.3 4.0 copy-start.14
  296.1 23.6 %collective-permute-start.1 = (bf16[256,2048]{1,0:T(8,128)(2,1)}, bf16[256,2048]{1,0:T(8,128)(2,1)}, u32[]{:S(2)}, u32[]{:S(2)}) collective-permute-start(bf16[256,2048]{1,0:T(8,128)(2,1)} %get-tuple-element.81), channel_id=1, source_target_pairs={{0,16},{16,0},{1,17},{17,1},{2,18},{18,2},{3,19},{19,3},{4,20},{20... | collective-permute-start | bytes 3145736 | tf_op jit(solution)/shard_map/ppermute | solution.py:1145
  297.2 12.8 %copy-start = (f32[2048,1024]{1,0:T(8,128)S(1)}, f32[2048,1024]{1,0:T(8,128)}, u32[]{:S(2)}) copy-start(f32[2048,1024]{1,0:T(8,128)} %get-tuple-element.78) | copy-start | bytes 25165828
  309.9 5.9 copy-start.6
  315.9 6.0 copy-start.2
  315.9 3.8 copy-start.8
  321.9 11.1 %copy-start.3 = (bf16[2,2,256,2048]{3,2,1,0:T(8,128)(2,1)}, bf16[2,2,256,2048]{3,2,1,0:T(8,128)(2,1)S(1)}, u32[]{:S(2)}) copy-start(bf16[2,2,256,2048]{3,2,1,0:T(8,128)(2,1)S(1)} %pad_maximum_fusion) | copy-start | bytes 12582916
  333.1 40.3 %copy-start.1 = (f32[256,2048]{1,0:T(8,128)S(1)}, f32[256,2048]{1,0:T(8,128)}, u32[]{:S(2)}) copy-start(f32[256,2048]{1,0:T(8,128)} %get-tuple-element.77.middle_ref) | copy-start | bytes 6291460
  333.1 40.3 %copy-start.7 = (bf16[1,256,2048]{2,1,0:T(8,128)(2,1)S(1)}, bf16[1,256,2048]{2,1,0:T(8,128)(2,1)}, u32[]{:S(2)}) copy-start(bf16[1,256,2048]{2,1,0:T(8,128)(2,1)} %param.16) | copy-start | bytes 3145732
  433.8 48.1 %collective-permute-start.2 = (bf16[2,256,2048]{2,1,0:T(8,128)(2,1)}, bf16[2,256,2048]{2,1,0:T(8,128)(2,1)S(1)}, u32[]{:S(2)}, u32[]{:S(2)}) collective-permute-start(bf16[2,256,2048]{2,1,0:T(8,128)(2,1)} %get-tuple-element.86), channel_id=1, source_target_pairs={{0,16},{16,0},{1,17},{17,1},{2,18},{18,2},{3,19},{19,3},{4,20},{20... | collective-permute-start | bytes 6291464 | tf_op jit(solution)/shard_map/ppermute | solution.py:1145
  481.9 1.3 copy-start.13
  553.6 28.3 %copy-start.16 = (bf16[512,1024]{1,0:T(8,128)(2,1)S(1)}, bf16[512,1024]{1,0:T(8,128)(2,1)}, u32[]{:S(2)}) copy-start(bf16[512,1024]{1,0:T(8,128)(2,1)} %get-tuple-element.99) | copy-start | bytes 3145732
  553.6 29.7 %copy-start.15 = (bf16[512,1024]{1,0:T(8,128)(2,1)S(1)}, bf16[512,1024]{1,0:T(8,128)(2,1)}, u32[]{:S(2)}) copy-start(bf16[512,1024]{1,0:T(8,128)(2,1)} %get-tuple-element.100) | copy-start | bytes 3145732
  578.9 128.6 %collective-permute-start.6 = (bf16[512,1024]{1,0:T(8,128)(2,1)}, bf16[512,1024]{1,0:T(8,128)(2,1)S(1)}, u32[]{:S(2)}, u32[]{:S(2)}) collective-permute-start(bf16[512,1024]{1,0:T(8,128)(2,1)} %get-tuple-element.104), channel_id=1, source_target_pairs={{0,2},{2,0},{1,3},{3,1},{4,6},{6,4},{5,7},{7,5},{8,10},{10,8},{9,1... | collective-permute-start | bytes 3145736 | tf_op jit(solution)/shard_map/ppermute | solution.py:1145
  581.5 91.0 %collective-permute-start.4 = (bf16[512,1024]{1,0:T(8,128)(2,1)}, bf16[512,1024]{1,0:T(8,128)(2,1)S(1)}, u32[]{:S(2)}, u32[]{:S(2)}) collective-permute-start(bf16[512,1024]{1,0:T(8,128)(2,1)} %get-tuple-element.96.first_ref), channel_id=1, source_target_pairs={{0,2},{2,0},{1,3},{3,1},{4,6},{6,4},{5,7},{7,5},{8,10},{10,8},{9,1... | collective-permute-start | bytes 3145736 | tf_op jit(solution)/shard_map/ppermute | solution.py:1145
  581.9 90.6 %collective-permute-start.3 = (bf16[512,1024]{1,0:T(8,128)(2,1)S(1)}, bf16[512,1024]{1,0:T(8,128)(2,1)S(1)}, u32[]{:S(2)}, u32[]{:S(2)}) collective-permute-start(bf16[512,1024]{1,0:T(8,128)(2,1)S(1)} %copy-done.16), channel_id=1, source_target_pairs={{0,16},{16,0},{1,17},{17,1},{2,18},{18,2},{3,19},{19,3},{4,20},{20... | collective-permute-start | bytes 3145736 | tf_op jit(solution)/shard_map/ppermute | solution.py:1145
  583.3 89.2 %collective-permute-start.5 = (bf16[512,1024]{1,0:T(8,128)(2,1)S(1)}, bf16[512,1024]{1,0:T(8,128)(2,1)S(1)}, u32[]{:S(2)}, u32[]{:S(2)}) collective-permute-start(bf16[512,1024]{1,0:T(8,128)(2,1)S(1)} %copy-done.15), channel_id=1, source_target_pairs={{0,16},{16,0},{1,17},{17,1},{2,18},{18,2},{3,19},{19,3},{4,20},{20... | collective-permute-start | bytes 3145736 | tf_op jit(solution)/shard_map/ppermute | solution.py:1145
  672.5 1.0 copy-start.10
  672.5 1.3 copy-start.11
  672.6 1.7 copy-start.4
  707.5 1.0 copy-start.9
  708.5 17.5 %copy-start.5 = (bf16[4,512,256]{2,1,0:T(8,128)(2,1)S(1)}, bf16[4,512,256]{2,1,0:T(8,128)(2,1)}, u32[]{:S(2)}) copy-start(bf16[4,512,256]{2,1,0:T(8,128)(2,1)} %get-tuple-element.72.out_ref) | copy-start | bytes 3145732
Sparse Core Ops, SparseCore 0:
  129.6 52.7 all-gather.2
  577.7 130.3 all-gather.4

commit v6 on v5

--- a/solution.py
+++ b/solution.py
@@ -1042,6 +1042,73 @@
         cost_estimate=pl.CostEstimate(flops=0, bytes_accessed=120_000_000, transcendentals=0),
         name="scatter_square",
     )(parts.astype(BF16).reshape(8, tok, width), *first)
+
+
+class Then:
+    def __init__(self, step):
+        self.wait = step
+
+
+def ff_end_kernel(units_ref, down_ref, out_ref, *scratch):
+    scratch, (units, down, for_mate, sem) = scratch[:9], scratch[9:]
+    mine, mates, sems_of = scratch[0], scratch[1], scratch[6:8]
+    loads = [local_copy(down_ref, down, sem.at[0]), local_copy(units_ref, units, sem.at[1])]
+    blk, lo, mate, side = square_places()
+    mate_side = (mate + 2) % 4
+    own_places = (side * 2 + 1 - lo, side * 2 + lo, blk * 2 + 1 - lo, blk * 2 + lo)
+    mate_places = (mate_side * 2 + 1 - lo, mate_side * 2 + lo, mate * 2 + 1 - lo, mate * 2 + lo)
+    step = units.shape[1] // PIECES
+    rows = lambda p: pl.ds(p * step, step)
+    orders = ((0, 2, 1, 3), (0, 1, 2, 3), (2, 3, 0, 1), (0, 1, 2, 3))
+    from_mate = {}
+
+    def made(place):
+        return dot32(units[place], down[...]).astype(BF16)
+
+    def own(k):
+        mine[k] = made(own_places[k])
+
+    def other(k):
+        for_mate[k] = made(mate_places[k])
+        for p in orders[k]:
+            from_mate[k, p] = remote_to(
+                for_mate.at[k, rows(p)], mates.at[k, rows(p)], sems_of, k, p, {"blk": mate}
+            )
+
+    greet(square_greeting())
+    wait_all(loads)
+    other(0)
+    own(0)
+    other(1)
+    other(2)
+    steps = [Then(lambda: None)] + [Then(functools.partial(own, k)) for k in (1, 2, 3)]
+    scatter_end_square(steps, from_mate, out_ref, scratch, [functools.partial(other, 3)])
+
+
+def ff_end(units, down, number):
+    count, ff = units.shape
+    width = down.shape[1]
+    tok = count // 8
+    return pl.pallas_call(
+        ff_end_kernel,
+        in_specs=[pl.BlockSpec(memory_space=pl.ANY)] * 2,
+        out_specs=pl.BlockSpec(memory_space=pltpu.VMEM),
+        out_shape=jax.ShapeDtypeStruct((tok, width), F32),
+        scratch_shapes=scatter_scratch(tok, width)
+        + [
+            pltpu.VMEM((8, tok, ff), BF16),
+            pltpu.VMEM(down.shape, BF16),
+            pltpu.VMEM((4, tok, width), BF16),
+            pltpu.SemaphoreType.DMA((2,)),
+        ],
+        compiler_params=pltpu.CompilerParams(
+            collective_id=number, has_side_effects=True, vmem_limit_bytes=VMEM_LIMIT
+        ),
+        cost_estimate=pl.CostEstimate(
+            flops=2 * count * ff * width, bytes_accessed=120_000_000, transcendentals=0
+        ),
+        name="ff_end",
+    )(units.reshape(8, tok, ff), down)
 
 
 def scatter_down_kernel(
@@ -1946,7 +2013,7 @@
     units = (silu * upward).astype(BF16)
     gate_slope = (upward * sigma * (1.0 + gate * (1.0 - sigma))).astype(BF16)
     up_slope = silu.astype(BF16)
-    result = middle + RESIDUAL_SCALE * scatter_square(dot32(units, down_weight), 1)
+    result = middle + RESIDUAL_SCALE * ff_end(units, down_weight, 1)
 
     own_places = ((blk * hi_n + hi) * lo_n + lo) * tok + jnp.arange(tok)
     valid = own_places < lengths[0]

time: 849 us -> 842 us (level)
  matrix products: 30.6 us -> 19.5 us
    dot_general x3 -> x2, matrix products: 30.6 us -> 19.5 us  [dot32(): return lax.dot_general(a, b, (dims, ((), ())), preferred_element_type=F32)]
where the time goes in v6:
time: 842 us; the launch traced here: 835 us
  Pallas kernels  702 us (83%)
  waiting for transfers between devices  51.8 us (6%)
  other arithmetic  23.9 us (3%)
  matrix products  19.5 us (2%)
  between operations  18.3 us (2%)
  starting transfers between devices  10.3 us (1%)
  local copies, waits for them, and re-layouts  8.62 us (1%)
    pallas_call x1, Pallas kernels, through_start(): pl.pallas_call(functools.partial(start_kernel, key_head, places, wide_w),...  120 us
    pallas_call x1, Pallas kernels, through_middle(): pl.pallas_call(functools.partial(middle_kernel, order, pairs, block), in_...  114 us
    pallas_call x1, Pallas kernels, shards(): pl.pallas_call(functools.partial(close_kernel, with_out), in_specs=[anywh...  84.5 us
    pallas_call x1, Pallas kernels, scatter_down(): pl.pallas_call(scatter_down_kernel, in_specs=[anywhere] * 6, out_specs=[i...  71.5 us
    pallas_call x2, Pallas kernels, comm_call(): pl.pallas_call(kernel, in_specs=[anywhere] * len(arrays), out_specs=[anyw...  71.2 us
    pallas_call x1, Pallas kernels, attend_back(): pl.pallas_call(attend_back_kernel, grid=(units,), in_specs=[pl.BlockSpec(...  57 us
    ppermute x7, waiting for transfers between devices, swap_pair(): return lax.ppermute(block, axis, [(0, 1), (1, 0)])  47.7 us
    pallas_call x1, Pallas kernels, ff_end(): pl.pallas_call(ff_end_kernel, in_specs=[pl.BlockSpec(memory_space=pl.ANY)...  44.8 us
  transfers between devices with their start and end apart: 9, of which 5 were waited for; matrix products, arithmetic and copies ran while one was open for 3% of the time, Pallas kernels for 22%

profile of v6, /device:TPU:0, one launch (start us, length us, event | category | flops | bytes accessed | tf_op | source)
XLA Modules:
  0.0 834.7 jit_solution(15936517813662420319)
XLA Ops:
  9.9 119.6 %start.1 = (bf16[8,256,2048]{2,1,0:T(8,128)(2,1)}, bf16[32,64,384]{2,1,0:T(8,128)(2,1)}, f32[32,8,128]{2,1,0:T(8,128)}, bf16[2,2,64,2048]{3,2,1,0:T(8,128)(2,1)}...) custom-call(bf16[64,2048]{1,0:T(8,128)(2,1)} %query_ref.3, ...), custom_call_target="tpu_custom_call" | custom-call | flops 3221225472 | bytes 250000000 | tf_op jit(solution)/shard_map/start/pallas_call | solution.py:1436
  129.5 2.6 collective-permute-start
  132.7 38.7 %attend.1 = (bf16[4,512,256]{2,1,0:T(8,128)(2,1)}, f32[4,8,512]{2,1,0:T(8,128)}) custom-call(s32[2]{0:T(128)} %pad_add_fusion.scalar_ref, bf16[4,512,256]{2,1,0:T(8,128)(2,1)} %bitcast.105, bf16[4,512,128]{2,1,0:T(8,128)(2,1)} %bitcast.111, bf16[4,512,128]{2,1,0:T(8,128)(2,1)} %bitcast.109), custom_call_target="tpu_custom_call" | custom-call | flops 40000000000 | bytes 8000000 | tf_op jit(solution)/shard_map/attend/pallas_call | solution.py:241
  173.5 4.8 collective-permute-done.gate_other_ref
  178.3 4.0 all-gather.3.cloned.1.call-done.weight_ref
  182.4 113.7 %middle.1 = (bf16[8,256,2048]{2,1,0:T(8,128)(2,1)}, f32[256,2048]{1,0:T(8,128)}, bf16[2,2,512,1024]{3,2,1,0:T(8,128)(2,1)}, bf16[2,2,512,1024]{3,2,1,0:T(8,128)(...) custom-call(bf16[8,256,256]{2,1,0:T(8,128)(2,1)} %bitcast.79, ...), custom_call_target="tpu_custom_call" | custom-call | flops 8589934592 | bytes 250000000 | tf_op jit(solution)/shard_map/middle/pallas_call | solution.py:1549
  297.2 12.8 %fusion.7 = f32[2048,1024]{1,0:T(8,128)S(1)} fusion(bf16[2048,2048]{1,0:T(8,128)(2,1)} %bitcast.98, bf16[2048,1024]{1,0:T(8,128)(2,1)} %bitcast.102), kind=kOutput, calls=%fused_computation.31 | convolution fusion | flops 8589934592 | bytes 20971520 | tf_op jit(solution)/shard_map/dot_general | solution.py:30
  310.0 8.4 %multiply_convert_fusion = (bf16[2048,1024]{1,0:T(8,128)(2,1)}, bf16[2048,1024]{1,0:T(8,128)(2,1)}, bf16[2048,1024]{1,0:T(8,128)(2,1)}) fusion(f32[2048,1024]{1,0:T(8,128)S(1)} %copy-done, f32[2048,1024]{1,0:T(8,128)S(1)} %fusion.7), kind=kLoop, calls=%fused_computation | loop fusion | flops 27262976 | bytes 29360128 | tf_op jit(solution)/shard_map/convert_element_type | solution.py:2014
  320.2 2.4 pad_maximum_fusion
  322.6 44.8 %ff_end.1 = f32[256,2048]{1,0:T(8,128)} custom-call(bf16[8,256,1024]{2,1,0:T(8,128)(2,1)} %bitcast.73, bf16[1024,2048]{1,0:T(8,128)(2,1)} %bitcast.75), custom_call_target="tpu_custom_call" | custom-call | flops 8589934592 | bytes 120000000 | tf_op jit(solution)/shard_map/ff_end/pallas_call | solution.py:1092
  367.5 4.9 multiply_convert_fusion.2
  372.4 38.4 %gather_square.1 = bf16[8,256,2048]{2,1,0:T(8,128)(2,1)} custom-call(bf16[256,2048]{1,0:T(8,128)(2,1)} %get-tuple-element.128.rows_ref), custom_call_target="tpu_custom_call" | custom-call | bytes 120000000 | tf_op jit(solution)/shard_map/gather_square/pallas_call | solution.py:570
  410.8 16.0 %weight_grad.1 = (bf16[2,256,2048]{2,1,0:T(8,128)(2,1)}, f32[2,256,2048]{2,1,0:T(8,128)}) custom-call(s32[1]{0:T(128)} %bitcast.24.dp_ref, bf16[2048,1024]{1,0:T(8,128)(2,1)} %get-tuple-element.131.left_ref, bf16[2048,2048]{1,0:T(8,128)(2,1)} %bitcast.70, bf16[2048,2048]{1,0:T(8,128)(2,1)} %bitcast.71), custom_call_target="tpu_custom_call" | custom-call | flops 8589934592 | bytes 24000000 | tf_op jit(solution)/shard_map/weight_grad/pallas_call | solution.py:1609
  426.8 1.3 collective-permute-start.2
  428.1 35.2 %ff_back.1 = (bf16[2048,1024]{1,0:T(8,128)(2,1)}, bf16[2048,1024]{1,0:T(8,128)(2,1)}, bf16[2048,2048]{1,0:T(8,128)(2,1)}) custom-call(bf16[2048,2048]{1,0:T(8,128)(2,1)} %bitcast.72, bf16[2048,1024]{1,0:T(8,128)(2,1)} %get-tuple-element.130.gate_slope_ref, bf16[2048,1024]{1,0:T(8,128)(2,1)} %get-tuple-element.132.up_slope_ref, bf16[2048,1024]{1,0:T(8,128)(2,1)} %bitcast.101, ...), custom_call_target="tpu_custom_call" | custom-call | flops 25769803776 | bytes 40000000 | tf_op jit(solution)/shard_map/ff_back/pallas_call | solution.py:1667
  463.3 11.6 %collective-permute-done.2.got_ref = bf16[2,256,2048]{2,1,0:T(8,128)(2,1)S(1)} collective-permute-done((bf16[2,256,2048]{2,1,0:T(8,128)(2,1)}, bf16[2,256,2048]{2,1,0:T(8,128)(2,1)S(1)}, u32[]{:S(2)}, u32[]{:S(2)}) %collective-permute-start.2) | collective-permute-done | bytes 2097184 | tf_op jit(solution)/shard_map/ppermute | solution.py:1212
  474.9 1.3 copy-done.12
  476.2 71.5 %scatter_down.1 = (f32[256,2048]{1,0:T(8,128)}, f32[256,2048]{1,0:T(8,128)}, f32[2,512,1024]{2,1,0:T(8,128)}, f32[2,512,1024]{2,1,0:T(8,128)}, bf16[512,1024]{1,...) custom-call(bf16[8,256,2048]{2,1,0:T(8,128)(2,1)} %bitcast.100, ...), custom_call_target="tpu_custom_call" | custom-call | flops 17179869184 | bytes 160000000 | tf_op jit(solution)/shard_map/scatter_down/pallas_call | solution.py:1173
  547.7 22.9 %out_back.1 = (f32[256,2048]{1,0:T(8,128)}, bf16[256,2048]{1,0:T(8,128)(2,1)}, bf16[8,256,256]{2,1,0:T(8,128)(2,1)}, bf16[512,1024]{1,0:T(8,128)(2,1)}, bf16[512,1024]{1,0:T(8,128)(2,1)}) custom-call(f32[256,2048]{1,0:T(8,128)} %get-tuple-element.89.grad_ref, f32[256,2048]{1,0:T(8,128)} %get-tuple-element.77.middle_ref, ...), custom_call_target="tpu_custom_call" | custom-call | flops 2147483648 | bytes 60000000 | tf_op jit(solution)/shard_map/out_back/pallas_call | solution.py:2045
  571.9 3.1 collective-permute-start.6
  575.2 1.3 collective-permute-start.3
  577.2 57.0 %attend_back.1 = (bf16[4,512,256]{2,1,0:T(8,128)(2,1)}, bf16[2,4,512,128]{3,2,1,0:T(8,128)(2,1)}) custom-call(s32[2]{0:T(128)} %pad_add_fusion.scalar_ref, bf16[4,512,256]{2,1,0:T(8,128)(2,1)} %bitcast.106, bf16[4,512,128]{2,1,0:T(8,128)(2,1)} %bitcast.112, bf16[4,512,128]{2,1,0:T(8,128)(2,1)} %bitcast.110, bf16[4,512,256]{2,1,0:T(8,128)(2,1)} %bitcast.97, ...), custom_call_target="tpu_custom_call" | custom-call | flops 60000002048 | bytes 10000000 | tf_op jit(solution)/shard_map/attend_back/pallas_call | solution.py:375
  634.2 1.9 slice.18
  636.1 30.2 %collective-permute-done.4 = bf16[512,1024]{1,0:T(8,128)(2,1)S(1)} collective-permute-done((bf16[512,1024]{1,0:T(8,128)(2,1)}, bf16[512,1024]{1,0:T(8,128)(2,1)S(1)}, u32[]{:S(2)}, u32[]{:S(2)}) %collective-permute-start.4) | collective-permute-done | bytes 1048608 | tf_op jit(solution)/shard_map/ppermute | solution.py:1212
  668.0 32.8 %dkeys.1 = (bf16[2048,128]{1,0:T(8,128)(2,1)}, bf16[8,64,1024]{2,1,0:T(8,128)(2,1)}) custom-call(bf16[2,2048,128]{2,1,0:T(8,128)(2,1)} %bitcast.81, f32[2,8,64,1024]{3,2,1,0:T(8,128)} %bitcast.68, bf16[8,64,1024]{2,1,0:T(8,128)(2,1)} %bitcast.90, bf16[8,64,1024]{2,1,0:T(8,128)(2,1)} %bitcast.89, bf16[8,64,1024]{2,1,0:T(8,128)(2,1)} %bitcast.77), custom_call_target="tpu_custom_call" | custom-call | bytes 120000000 | tf_op jit(solution)/shard_map/dkeys/pallas_call | solution.py:570
  701.7 17.3 %project_back.1 = (bf16[2048,2048]{1,0:T(8,128)(2,1)}, bf16[2048,384]{1,0:T(8,128)(2,1)}) custom-call(s32[1]{0:T(128)} %bitcast.hi_ref, bf16[2048,256]{1,0:T(8,128)(2,1)} %bitcast.108, bf16[2048,128]{1,0:T(8,128)(2,1)} %bitcast.91, bf16[2048,128]{1,0:T(8,128)(2,1)} %get-tuple-element.101.other_ref, bf16[2048,2048]{1,0:T(8,128)(2,1)} %get-tuple-element.102.rows_ref, ...), custom_call_target="tpu_custom_call" | custom-call | flops 6442450944 | bytes 24000000 | tf_op jit(solution)/shard_map/project_back/pallas_call | solution.py:128
  719.1 6.7 convolution_convert_fusion
  727.1 84.5 %close.1 = (f32[256,2048]{1,0:T(8,128)}, bf16[16,64,384]{2,1,0:T(8,128)(2,1)}, bf16[8,64,1024]{2,1,0:T(8,128)(2,1)}, f32[32,8,128]{2,1,0:T(8,128)}, bf16[2,64,2048]{2,1,0:T(8,128)(2,1)}) custom-call(bf16[8,256,2048]{2,1,0:T(8,128)(2,1)} %bitcast.69, bf16[2,16,64,384]{3,2,1,0:T(8,128)(2,1)} %bitcast.82, f32[2,8,64,1024]{3,2,1,0:T(8,128)} %bitcast.67, ...), custom_call_target="tpu_custom_call" | custom-call | bytes 120000000 | tf_op jit(solution)/shard_map/close/pallas_call | solution.py:2126
  811.5 1.5 slice_reduce_fusion.1
  813.1 10.0 %final.1 = (f32[256,2048]{1,0:T(8,128)}, f32[64,2048]{1,0:T(8,128)}, f32[64,512]{1,0:T(8,128)}, f32[64,512]{1,0:T(8,128)}, f32[64,1]{1,0:T(8,128)}, /*index=5*/f...) custom-call(f32[256,2048]{1,0:T(8,128)} %get-tuple-element.109.first_ref, ...), custom_call_target="tpu_custom_call" | custom-call | tf_op jit(solution)/shard_map/final/pallas_call | solution.py:2141
  823.1 1.4 reduce.4
  824.5 1.4 reduce.5
  (59 shorter events, 12.4 us)
Async XLA Ops:
  7.2 175.2 %all-gather.3.cloned.1.call-start = ((), (), s32[]{:S(2)}) async-start(), calls=%async_computation | async-start | bytes 9437184 | tf_op jit(solution)/shard_map/all_gather | solution.py:1946
  129.5 589.6 %all-gather.5.cloned.1.call-start = ((), (), s32[]{:S(2)}) async-start(), calls=%async_computation.1 | async-start | bytes 9437184 | tf_op jit(solution)/shard_map/all_gather | solution.py:2080
  129.5 48.8 %collective-permute-start = (bf16[512,1024]{1,0:T(8,128)(2,1)}, bf16[512,1024]{1,0:T(8,128)(2,1)S(1)}, u32[]{:S(2)}, u32[]{:S(2)}) collective-permute-start(bf16[512,1024]{1,0:T(8,128)(2,1)} %bitcast.95), channel_id=1, source_target_pairs={{0,2},{2,0},{1,3},{3,1},{4,6},{6,4},{5,7},{7,5},{8,10},{10,8},{9,1... | collective-permute-start | bytes 3145736 | tf_op jit(solution)/shard_map/ppermute | solution.py:1212
  132.7 38.7 %copy-start.11 = (f32[32,8,128]{2,1,0:T(8,128)S(1)}, f32[32,8,128]{2,1,0:T(8,128)}, u32[]{:S(2)}) copy-start(f32[32,8,128]{2,1,0:T(8,128)} %get-tuple-element.76) | copy-start | bytes 393220
  178.3 4.0 copy-start.13
  296.1 23.5 %collective-permute-start.1 = (bf16[256,2048]{1,0:T(8,128)(2,1)}, bf16[256,2048]{1,0:T(8,128)(2,1)S(1)}, u32[]{:S(2)}, u32[]{:S(2)}) collective-permute-start(bf16[256,2048]{1,0:T(8,128)(2,1)} %get-tuple-element.81), channel_id=1, source_target_pairs={{0,16},{16,0},{1,17},{17,1},{2,18},{18,2},{3,19},{19,3},{4,20},{20... | collective-permute-start | bytes 3145736 | tf_op jit(solution)/shard_map/ppermute | solution.py:1212
  297.2 12.8 %copy-start = (f32[2048,1024]{1,0:T(8,128)S(1)}, f32[2048,1024]{1,0:T(8,128)}, u32[]{:S(2)}) copy-start(f32[2048,1024]{1,0:T(8,128)} %get-tuple-element.78) | copy-start | bytes 25165828
  310.0 8.4 %copy-start.4 = (bf16[256,2048]{1,0:T(8,128)(2,1)S(1)}, bf16[256,2048]{1,0:T(8,128)(2,1)}, u32[]{:S(2)}) copy-start(bf16[256,2048]{1,0:T(8,128)(2,1)} %down_ref.3) | copy-start | bytes 3145732
  310.0 8.4 %copy-start.8 = (bf16[256,2048]{1,0:T(8,128)(2,1)S(1)}, bf16[256,2048]{1,0:T(8,128)(2,1)}, u32[]{:S(2)}) copy-start(bf16[256,2048]{1,0:T(8,128)(2,1)} %get-tuple-element.81) | copy-start | bytes 3145732
  318.4 1.2 copy-start.6
  322.6 44.8 %copy-start.1 = (f32[256,2048]{1,0:T(8,128)S(1)}, f32[256,2048]{1,0:T(8,128)}, u32[]{:S(2)}) copy-start(f32[256,2048]{1,0:T(8,128)} %get-tuple-element.77.middle_ref) | copy-start | bytes 6291460
  322.6 44.9 %copy-start.5 = (bf16[1,256,2048]{2,1,0:T(8,128)(2,1)S(1)}, bf16[1,256,2048]{2,1,0:T(8,128)(2,1)}, u32[]{:S(2)}) copy-start(bf16[1,256,2048]{2,1,0:T(8,128)(2,1)} %param.16) | copy-start | bytes 3145732
  426.8 48.1 %collective-permute-start.2 = (bf16[2,256,2048]{2,1,0:T(8,128)(2,1)}, bf16[2,256,2048]{2,1,0:T(8,128)(2,1)S(1)}, u32[]{:S(2)}, u32[]{:S(2)}) collective-permute-start(bf16[2,256,2048]{2,1,0:T(8,128)(2,1)} %get-tuple-element.86), channel_id=1, source_target_pairs={{0,16},{16,0},{1,17},{17,1},{2,18},{18,2},{3,19},{19,3},{4,20},{20... | collective-permute-start | bytes 6291464 | tf_op jit(solution)/shard_map/ppermute | solution.py:1212
  474.9 1.3 copy-start.12
  547.7 27.5 %copy-start.15 = (bf16[512,1024]{1,0:T(8,128)(2,1)S(1)}, bf16[512,1024]{1,0:T(8,128)(2,1)}, u32[]{:S(2)}) copy-start(bf16[512,1024]{1,0:T(8,128)(2,1)} %get-tuple-element.99) | copy-start | bytes 3145732
  547.7 28.8 %copy-start.14 = (bf16[512,1024]{1,0:T(8,128)(2,1)S(1)}, bf16[512,1024]{1,0:T(8,128)(2,1)}, u32[]{:S(2)}) copy-start(bf16[512,1024]{1,0:T(8,128)(2,1)} %get-tuple-element.100) | copy-start | bytes 3145732
  571.9 128.8 %collective-permute-start.6 = (bf16[512,1024]{1,0:T(8,128)(2,1)}, bf16[512,1024]{1,0:T(8,128)(2,1)S(1)}, u32[]{:S(2)}, u32[]{:S(2)}) collective-permute-start(bf16[512,1024]{1,0:T(8,128)(2,1)} %get-tuple-element.104), channel_id=1, source_target_pairs={{0,2},{2,0},{1,3},{3,1},{4,6},{6,4},{5,7},{7,5},{8,10},{10,8},{9,1... | collective-permute-start | bytes 3145736 | tf_op jit(solution)/shard_map/ppermute | solution.py:1212
  575.1 91.2 %collective-permute-start.4 = (bf16[512,1024]{1,0:T(8,128)(2,1)}, bf16[512,1024]{1,0:T(8,128)(2,1)S(1)}, u32[]{:S(2)}, u32[]{:S(2)}) collective-permute-start(bf16[512,1024]{1,0:T(8,128)(2,1)} %get-tuple-element.96.first_ref), channel_id=1, source_target_pairs={{0,2},{2,0},{1,3},{3,1},{4,6},{6,4},{5,7},{7,5},{8,10},{10,8},{9,1... | collective-permute-start | bytes 3145736 | tf_op jit(solution)/shard_map/ppermute | solution.py:1212
  575.2 91.1 %collective-permute-start.3 = (bf16[512,1024]{1,0:T(8,128)(2,1)S(1)}, bf16[512,1024]{1,0:T(8,128)(2,1)S(1)}, u32[]{:S(2)}, u32[]{:S(2)}) collective-permute-start(bf16[512,1024]{1,0:T(8,128)(2,1)S(1)} %copy-done.15), channel_id=1, source_target_pairs={{0,16},{16,0},{1,17},{17,1},{2,18},{18,2},{3,19},{19,3},{4,20},{20... | collective-permute-start | bytes 3145736 | tf_op jit(solution)/shard_map/ppermute | solution.py:1212
  576.5 89.8 %collective-permute-start.5 = (bf16[512,1024]{1,0:T(8,128)(2,1)S(1)}, bf16[512,1024]{1,0:T(8,128)(2,1)S(1)}, u32[]{:S(2)}, u32[]{:S(2)}) collective-permute-start(bf16[512,1024]{1,0:T(8,128)(2,1)S(1)} %copy-done.14), channel_id=1, source_target_pairs={{0,16},{16,0},{1,17},{17,1},{2,18},{18,2},{3,19},{19,3},{4,20},{20... | collective-permute-start | bytes 3145736 | tf_op jit(solution)/shard_map/ppermute | solution.py:1212
  666.3 1.0 copy-start.9
  666.3 1.3 copy-start.10
  666.3 1.7 copy-start.2
  700.8 1.0 copy-start.7
  701.7 17.4 %copy-start.3 = (bf16[4,512,256]{2,1,0:T(8,128)(2,1)S(1)}, bf16[4,512,256]{2,1,0:T(8,128)(2,1)}, u32[]{:S(2)}) copy-start(bf16[4,512,256]{2,1,0:T(8,128)(2,1)} %get-tuple-element.72.out_ref) | copy-start | bytes 3145732
Sparse Core Ops, SparseCore 0:
  129.6 52.7 all-gather.2
  570.7 131.0 all-gather.4

commit v7 on v6

--- a/solution.py
+++ b/solution.py
@@ -1342,6 +1342,8 @@
 
     hand_on(heads_ref.at[blk * 2 + lo], mine, seq_n - 1)
     deal_units(places, wide, w_gate_ref, w_up_ref, gate_ref, up_ref)
+    copies, wouts = [], []
+    next_lo = {"lo": 1 - lo}
 
     def pass_on(turn):
         for k, (to, source) in enumerate(seq):
@@ -1349,14 +1351,18 @@
                 straight[k].wait()
                 place = dp * seq_n + source
                 hand_on(weight_ref.at[place], place, k)
+        if turn == PIECES - 1:
+            copies.append(Carried(wout_ref, wouts_ref.at[hi, lo], o_held, local.at[2]))
+            wouts.append(
+                remote(wout_ref, wouts_ref.at[hi, lo], o_send.at[0], o_recv.at[0], other_hi())
+            )
+            copies.append(
+                remote(wout_ref, wouts_ref.at[hi, lo], o_send.at[1], o_recv.at[1], next_lo)
+            )
+            copies.extend(swap_begin(gate_ref, gates_ref, ga_send, ga_recv, ga_local, ga_held))
+            copies.extend(swap_begin(up_ref, ups_ref, up_send, up_recv, up_local, up_held))
 
     end(pass_on)
-    copies = [Carried(wout_ref, wouts_ref.at[hi, lo], o_held, local.at[2])]
-    next_lo = {"lo": 1 - lo}
-    wout = remote(wout_ref, wouts_ref.at[hi, lo], o_send.at[0], o_recv.at[0], other_hi())
-    copies.append(remote(wout_ref, wouts_ref.at[hi, lo], o_send.at[1], o_recv.at[1], next_lo))
-    copies += swap_begin(gate_ref, gates_ref, ga_send, ga_recv, ga_local, ga_held)
-    copies += swap_begin(up_ref, ups_ref, up_send, up_recv, up_local, up_held)
     own_head.turn()
     wait_all(small_copies)
     load_smalls = local_copy(smalls_ref, smalls, sem.at[2])
@@ -1402,7 +1408,7 @@
             remote(kv_ref.at[piece], other_ref.at[piece], k_send.at[b], k_recv.at[b], other_hi())
         )
         if b == 2:
-            wout.wait()
+            wouts[0].wait()
             there = wouts_ref.at[1 - hi, lo]
             copies.append(remote(there, there, o_send.at[2], o_recv.at[2], next_lo))
     finish(copies)

time: 842 us -> 838 us (level)
  no operation moved by 1% of the time
where the time goes in v7:
time: 838 us; the launch traced here: 831 us
  Pallas kernels  699 us (83%)
  waiting for transfers between devices  51.9 us (6%)
  other arithmetic  23.9 us (3%)
  matrix products  19.5 us (2%)
  between operations  18.3 us (2%)
  starting transfers between devices  9.82 us (1%)
  local copies, waits for them, and re-layouts  8.6 us (1%)
    pallas_call x1, Pallas kernels, through_start(): pl.pallas_call(functools.partial(start_kernel, key_head, places, wide_w),...  116 us
    pallas_call x1, Pallas kernels, through_middle(): pl.pallas_call(functools.partial(middle_kernel, order, pairs, block), in_...  114 us
    pallas_call x1, Pallas kernels, shards(): pl.pallas_call(functools.partial(close_kernel, with_out), in_specs=[anywh...  84.5 us
    pallas_call x1, Pallas kernels, scatter_down(): pl.pallas_call(scatter_down_kernel, in_specs=[anywhere] * 6, out_specs=[i...  71.6 us
    pallas_call x2, Pallas kernels, comm_call(): pl.pallas_call(kernel, in_specs=[anywhere] * len(arrays), out_specs=[anyw...  71.1 us
    pallas_call x1, Pallas kernels, attend_back(): pl.pallas_call(attend_back_kernel, grid=(units,), in_specs=[pl.BlockSpec(...  57 us
    ppermute x7, waiting for transfers between devices, swap_pair(): return lax.ppermute(block, axis, [(0, 1), (1, 0)])  47.6 us
    pallas_call x1, Pallas kernels, ff_end(): pl.pallas_call(ff_end_kernel, in_specs=[pl.BlockSpec(memory_space=pl.ANY)...  44.7 us
  transfers between devices with their start and end apart: 9, of which 5 were waited for; matrix products, arithmetic and copies ran while one was open for 3% of the time, Pallas kernels for 22%

profile of v7, /device:TPU:0, one launch (start us, length us, event | category | flops | bytes accessed | tf_op | source)
XLA Modules:
  0.0 830.7 jit_solution(15950537155585770539)
XLA Ops:
  9.9 116.0 %start.1 = (bf16[8,256,2048]{2,1,0:T(8,128)(2,1)}, bf16[32,64,384]{2,1,0:T(8,128)(2,1)}, f32[32,8,128]{2,1,0:T(8,128)}, bf16[2,2,64,2048]{3,2,1,0:T(8,128)(2,1)}...) custom-call(bf16[64,2048]{1,0:T(8,128)(2,1)} %query_ref.3, ...), custom_call_target="tpu_custom_call" | custom-call | flops 3221225472 | bytes 250000000 | tf_op jit(solution)/shard_map/start/pallas_call | solution.py:1442
  125.9 2.3 collective-permute-start
  128.9 38.7 %attend.1 = (bf16[4,512,256]{2,1,0:T(8,128)(2,1)}, f32[4,8,512]{2,1,0:T(8,128)}) custom-call(s32[2]{0:T(128)} %pad_add_fusion.scalar_ref, bf16[4,512,256]{2,1,0:T(8,128)(2,1)} %bitcast.105, bf16[4,512,128]{2,1,0:T(8,128)(2,1)} %bitcast.111, bf16[4,512,128]{2,1,0:T(8,128)(2,1)} %bitcast.109), custom_call_target="tpu_custom_call" | custom-call | flops 40000000000 | bytes 8000000 | tf_op jit(solution)/shard_map/attend/pallas_call | solution.py:241
  169.7 4.5 collective-permute-done.gate_other_ref
  174.2 4.3 all-gather.3.cloned.1.call-done.weight_ref
  178.5 113.7 %middle.1 = (bf16[8,256,2048]{2,1,0:T(8,128)(2,1)}, f32[256,2048]{1,0:T(8,128)}, bf16[2,2,512,1024]{3,2,1,0:T(8,128)(2,1)}, bf16[2,2,512,1024]{3,2,1,0:T(8,128)(...) custom-call(bf16[8,256,256]{2,1,0:T(8,128)(2,1)} %bitcast.79, ...), custom_call_target="tpu_custom_call" | custom-call | flops 8589934592 | bytes 250000000 | tf_op jit(solution)/shard_map/middle/pallas_call | solution.py:1555
  293.2 12.8 %fusion.7 = f32[2048,1024]{1,0:T(8,128)S(1)} fusion(bf16[2048,2048]{1,0:T(8,128)(2,1)} %bitcast.98, bf16[2048,1024]{1,0:T(8,128)(2,1)} %bitcast.102), kind=kOutput, calls=%fused_computation.31 | convolution fusion | flops 8589934592 | bytes 20971520 | tf_op jit(solution)/shard_map/dot_general | solution.py:30
  306.0 8.4 %multiply_convert_fusion = (bf16[2048,1024]{1,0:T(8,128)(2,1)}, bf16[2048,1024]{1,0:T(8,128)(2,1)}, bf16[2048,1024]{1,0:T(8,128)(2,1)}) fusion(f32[2048,1024]{1,0:T(8,128)S(1)} %copy-done, f32[2048,1024]{1,0:T(8,128)S(1)} %fusion.7), kind=kLoop, calls=%fused_computation | loop fusion | flops 27262976 | bytes 29360128 | tf_op jit(solution)/shard_map/convert_element_type | solution.py:2020
  316.3 2.4 pad_maximum_fusion
  318.7 44.7 %ff_end.1 = f32[256,2048]{1,0:T(8,128)} custom-call(bf16[8,256,1024]{2,1,0:T(8,128)(2,1)} %bitcast.73, bf16[1024,2048]{1,0:T(8,128)(2,1)} %bitcast.75), custom_call_target="tpu_custom_call" | custom-call | flops 8589934592 | bytes 120000000 | tf_op jit(solution)/shard_map/ff_end/pallas_call | solution.py:1092
  363.4 4.9 multiply_convert_fusion.2
  368.4 38.4 %gather_square.1 = bf16[8,256,2048]{2,1,0:T(8,128)(2,1)} custom-call(bf16[256,2048]{1,0:T(8,128)(2,1)} %get-tuple-element.128.rows_ref), custom_call_target="tpu_custom_call" | custom-call | bytes 120000000 | tf_op jit(solution)/shard_map/gather_square/pallas_call | solution.py:570
  406.8 16.0 %weight_grad.1 = (bf16[2,256,2048]{2,1,0:T(8,128)(2,1)}, f32[2,256,2048]{2,1,0:T(8,128)}) custom-call(s32[1]{0:T(128)} %bitcast.24.dp_ref, bf16[2048,1024]{1,0:T(8,128)(2,1)} %get-tuple-element.131.left_ref, bf16[2048,2048]{1,0:T(8,128)(2,1)} %bitcast.70, bf16[2048,2048]{1,0:T(8,128)(2,1)} %bitcast.71), custom_call_target="tpu_custom_call" | custom-call | flops 8589934592 | bytes 24000000 | tf_op jit(solution)/shard_map/weight_grad/pallas_call | solution.py:1615
  422.8 1.3 collective-permute-start.2
  424.0 35.2 %ff_back.1 = (bf16[2048,1024]{1,0:T(8,128)(2,1)}, bf16[2048,1024]{1,0:T(8,128)(2,1)}, bf16[2048,2048]{1,0:T(8,128)(2,1)}) custom-call(bf16[2048,2048]{1,0:T(8,128)(2,1)} %bitcast.72, bf16[2048,1024]{1,0:T(8,128)(2,1)} %get-tuple-element.130.gate_slope_ref, bf16[2048,1024]{1,0:T(8,128)(2,1)} %get-tuple-element.132.up_slope_ref, bf16[2048,1024]{1,0:T(8,128)(2,1)} %bitcast.101, ...), custom_call_target="tpu_custom_call" | custom-call | flops 25769803776 | bytes 40000000 | tf_op jit(solution)/shard_map/ff_back/pallas_call | solution.py:1673
  459.2 11.7 %collective-permute-done.2.got_ref = bf16[2,256,2048]{2,1,0:T(8,128)(2,1)S(1)} collective-permute-done((bf16[2,256,2048]{2,1,0:T(8,128)(2,1)}, bf16[2,256,2048]{2,1,0:T(8,128)(2,1)S(1)}, u32[]{:S(2)}, u32[]{:S(2)}) %collective-permute-start.2) | collective-permute-done | bytes 2097184 | tf_op jit(solution)/shard_map/ppermute | solution.py:1212
  470.9 1.3 copy-done.12
  472.2 71.6 %scatter_down.1 = (f32[256,2048]{1,0:T(8,128)}, f32[256,2048]{1,0:T(8,128)}, f32[2,512,1024]{2,1,0:T(8,128)}, f32[2,512,1024]{2,1,0:T(8,128)}, bf16[512,1024]{1,...) custom-call(bf16[8,256,2048]{2,1,0:T(8,128)(2,1)} %bitcast.100, ...), custom_call_target="tpu_custom_call" | custom-call | flops 17179869184 | bytes 160000000 | tf_op jit(solution)/shard_map/scatter_down/pallas_call | solution.py:1173
  543.8 22.9 %out_back.1 = (f32[256,2048]{1,0:T(8,128)}, bf16[256,2048]{1,0:T(8,128)(2,1)}, bf16[8,256,256]{2,1,0:T(8,128)(2,1)}, bf16[512,1024]{1,0:T(8,128)(2,1)}, bf16[512,1024]{1,0:T(8,128)(2,1)}) custom-call(f32[256,2048]{1,0:T(8,128)} %get-tuple-element.89.grad_ref, f32[256,2048]{1,0:T(8,128)} %get-tuple-element.77.middle_ref, ...), custom_call_target="tpu_custom_call" | custom-call | flops 2147483648 | bytes 60000000 | tf_op jit(solution)/shard_map/out_back/pallas_call | solution.py:2051
  568.0 3.1 collective-permute-start.6
  571.2 1.3 collective-permute-start.3
  573.2 57.0 %attend_back.1 = (bf16[4,512,256]{2,1,0:T(8,128)(2,1)}, bf16[2,4,512,128]{3,2,1,0:T(8,128)(2,1)}) custom-call(s32[2]{0:T(128)} %pad_add_fusion.scalar_ref, bf16[4,512,256]{2,1,0:T(8,128)(2,1)} %bitcast.106, bf16[4,512,128]{2,1,0:T(8,128)(2,1)} %bitcast.112, bf16[4,512,128]{2,1,0:T(8,128)(2,1)} %bitcast.110, bf16[4,512,256]{2,1,0:T(8,128)(2,1)} %bitcast.97, ...), custom_call_target="tpu_custom_call" | custom-call | flops 60000002048 | bytes 10000000 | tf_op jit(solution)/shard_map/attend_back/pallas_call | solution.py:375
  630.2 1.9 slice.18
  632.1 30.2 %collective-permute-done.4 = bf16[512,1024]{1,0:T(8,128)(2,1)S(1)} collective-permute-done((bf16[512,1024]{1,0:T(8,128)(2,1)}, bf16[512,1024]{1,0:T(8,128)(2,1)S(1)}, u32[]{:S(2)}, u32[]{:S(2)}) %collective-permute-start.4) | collective-permute-done | bytes 1048608 | tf_op jit(solution)/shard_map/ppermute | solution.py:1212
  664.0 32.7 %dkeys.1 = (bf16[2048,128]{1,0:T(8,128)(2,1)}, bf16[8,64,1024]{2,1,0:T(8,128)(2,1)}) custom-call(bf16[2,2048,128]{2,1,0:T(8,128)(2,1)} %bitcast.81, f32[2,8,64,1024]{3,2,1,0:T(8,128)} %bitcast.68, bf16[8,64,1024]{2,1,0:T(8,128)(2,1)} %bitcast.90, bf16[8,64,1024]{2,1,0:T(8,128)(2,1)} %bitcast.89, bf16[8,64,1024]{2,1,0:T(8,128)(2,1)} %bitcast.77), custom_call_target="tpu_custom_call" | custom-call | bytes 120000000 | tf_op jit(solution)/shard_map/dkeys/pallas_call | solution.py:570
  697.7 17.3 %project_back.1 = (bf16[2048,2048]{1,0:T(8,128)(2,1)}, bf16[2048,384]{1,0:T(8,128)(2,1)}) custom-call(s32[1]{0:T(128)} %bitcast.hi_ref, bf16[2048,256]{1,0:T(8,128)(2,1)} %bitcast.108, bf16[2048,128]{1,0:T(8,128)(2,1)} %bitcast.91, bf16[2048,128]{1,0:T(8,128)(2,1)} %get-tuple-element.101.other_ref, bf16[2048,2048]{1,0:T(8,128)(2,1)} %get-tuple-element.102.rows_ref, ...), custom_call_target="tpu_custom_call" | custom-call | flops 6442450944 | bytes 24000000 | tf_op jit(solution)/shard_map/project_back/pallas_call | solution.py:128
  715.1 6.7 convolution_convert_fusion
  723.0 84.5 %close.1 = (f32[256,2048]{1,0:T(8,128)}, bf16[16,64,384]{2,1,0:T(8,128)(2,1)}, bf16[8,64,1024]{2,1,0:T(8,128)(2,1)}, f32[32,8,128]{2,1,0:T(8,128)}, bf16[2,64,2048]{2,1,0:T(8,128)(2,1)}) custom-call(bf16[8,256,2048]{2,1,0:T(8,128)(2,1)} %bitcast.69, bf16[2,16,64,384]{3,2,1,0:T(8,128)(2,1)} %bitcast.82, f32[2,8,64,1024]{3,2,1,0:T(8,128)} %bitcast.67, ...), custom_call_target="tpu_custom_call" | custom-call | bytes 120000000 | tf_op jit(solution)/shard_map/close/pallas_call | solution.py:2132
  807.5 1.5 slice_reduce_fusion.1
  809.1 10.0 %final.1 = (f32[256,2048]{1,0:T(8,128)}, f32[64,2048]{1,0:T(8,128)}, f32[64,512]{1,0:T(8,128)}, f32[64,512]{1,0:T(8,128)}, f32[64,1]{1,0:T(8,128)}, /*index=5*/f...) custom-call(f32[256,2048]{1,0:T(8,128)} %get-tuple-element.109.first_ref, ...), custom_call_target="tpu_custom_call" | custom-call | tf_op jit(solution)/shard_map/final/pallas_call | solution.py:2147
  819.1 1.4 reduce.4
  820.5 1.4 reduce.5
  (59 shorter events, 12.4 us)
Async XLA Ops:
  7.2 171.3 %all-gather.3.cloned.1.call-start = ((), (), s32[]{:S(2)}) async-start(), calls=%async_computation | async-start | bytes 9437184 | tf_op jit(solution)/shard_map/all_gather | solution.py:1952
  125.9 589.2 %all-gather.5.cloned.1.call-start = ((), (), s32[]{:S(2)}) async-start(), calls=%async_computation.1 | async-start | bytes 9437184 | tf_op jit(solution)/shard_map/all_gather | solution.py:2086
  125.9 48.3 %collective-permute-start = (bf16[512,1024]{1,0:T(8,128)(2,1)}, bf16[512,1024]{1,0:T(8,128)(2,1)S(1)}, u32[]{:S(2)}, u32[]{:S(2)}) collective-permute-start(bf16[512,1024]{1,0:T(8,128)(2,1)} %bitcast.95), channel_id=1, source_target_pairs={{0,2},{2,0},{1,3},{3,1},{4,6},{6,4},{5,7},{7,5},{8,10},{10,8},{9,1... | collective-permute-start | bytes 3145736 | tf_op jit(solution)/shard_map/ppermute | solution.py:1212
  128.9 38.7 %copy-start.11 = (f32[32,8,128]{2,1,0:T(8,128)S(1)}, f32[32,8,128]{2,1,0:T(8,128)}, u32[]{:S(2)}) copy-start(f32[32,8,128]{2,1,0:T(8,128)} %get-tuple-element.76) | copy-start | bytes 393220
  174.2 4.3 copy-start.13
  292.2 23.5 %collective-permute-start.1 = (bf16[256,2048]{1,0:T(8,128)(2,1)}, bf16[256,2048]{1,0:T(8,128)(2,1)S(1)}, u32[]{:S(2)}, u32[]{:S(2)}) collective-permute-start(bf16[256,2048]{1,0:T(8,128)(2,1)} %get-tuple-element.81), channel_id=1, source_target_pairs={{0,16},{16,0},{1,17},{17,1},{2,18},{18,2},{3,19},{19,3},{4,20},{20... | collective-permute-start | bytes 3145736 | tf_op jit(solution)/shard_map/ppermute | solution.py:1212
  293.2 12.8 %copy-start = (f32[2048,1024]{1,0:T(8,128)S(1)}, f32[2048,1024]{1,0:T(8,128)}, u32[]{:S(2)}) copy-start(f32[2048,1024]{1,0:T(8,128)} %get-tuple-element.78) | copy-start | bytes 25165828
  305.9 8.4 %copy-start.4 = (bf16[256,2048]{1,0:T(8,128)(2,1)S(1)}, bf16[256,2048]{1,0:T(8,128)(2,1)}, u32[]{:S(2)}) copy-start(bf16[256,2048]{1,0:T(8,128)(2,1)} %down_ref.3) | copy-start | bytes 3145732
  306.0 8.4 %copy-start.8 = (bf16[256,2048]{1,0:T(8,128)(2,1)S(1)}, bf16[256,2048]{1,0:T(8,128)(2,1)}, u32[]{:S(2)}) copy-start(bf16[256,2048]{1,0:T(8,128)(2,1)} %get-tuple-element.81) | copy-start | bytes 3145732
  314.4 1.3 copy-start.6
  318.7 44.7 %copy-start.1 = (f32[256,2048]{1,0:T(8,128)S(1)}, f32[256,2048]{1,0:T(8,128)}, u32[]{:S(2)}) copy-start(f32[256,2048]{1,0:T(8,128)} %get-tuple-element.77.middle_ref) | copy-start | bytes 6291460
  318.7 44.8 %copy-start.5 = (bf16[1,256,2048]{2,1,0:T(8,128)(2,1)S(1)}, bf16[1,256,2048]{2,1,0:T(8,128)(2,1)}, u32[]{:S(2)}) copy-start(bf16[1,256,2048]{2,1,0:T(8,128)(2,1)} %param.16) | copy-start | bytes 3145732
  422.8 48.1 %collective-permute-start.2 = (bf16[2,256,2048]{2,1,0:T(8,128)(2,1)}, bf16[2,256,2048]{2,1,0:T(8,128)(2,1)S(1)}, u32[]{:S(2)}, u32[]{:S(2)}) collective-permute-start(bf16[2,256,2048]{2,1,0:T(8,128)(2,1)} %get-tuple-element.86), channel_id=1, source_target_pairs={{0,16},{16,0},{1,17},{17,1},{2,18},{18,2},{3,19},{19,3},{4,20},{20... | collective-permute-start | bytes 6291464 | tf_op jit(solution)/shard_map/ppermute | solution.py:1212
  470.9 1.3 copy-start.12
  543.8 27.4 %copy-start.15 = (bf16[512,1024]{1,0:T(8,128)(2,1)S(1)}, bf16[512,1024]{1,0:T(8,128)(2,1)}, u32[]{:S(2)}) copy-start(bf16[512,1024]{1,0:T(8,128)(2,1)} %get-tuple-element.99) | copy-start | bytes 3145732
  543.8 28.7 %copy-start.14 = (bf16[512,1024]{1,0:T(8,128)(2,1)S(1)}, bf16[512,1024]{1,0:T(8,128)(2,1)}, u32[]{:S(2)}) copy-start(bf16[512,1024]{1,0:T(8,128)(2,1)} %get-tuple-element.100) | copy-start | bytes 3145732
  568.0 128.7 %collective-permute-start.6 = (bf16[512,1024]{1,0:T(8,128)(2,1)}, bf16[512,1024]{1,0:T(8,128)(2,1)S(1)}, u32[]{:S(2)}, u32[]{:S(2)}) collective-permute-start(bf16[512,1024]{1,0:T(8,128)(2,1)} %get-tuple-element.104), channel_id=1, source_target_pairs={{0,2},{2,0},{1,3},{3,1},{4,6},{6,4},{5,7},{7,5},{8,10},{10,8},{9,1... | collective-permute-start | bytes 3145736 | tf_op jit(solution)/shard_map/ppermute | solution.py:1212
  571.1 91.2 %collective-permute-start.4 = (bf16[512,1024]{1,0:T(8,128)(2,1)}, bf16[512,1024]{1,0:T(8,128)(2,1)S(1)}, u32[]{:S(2)}, u32[]{:S(2)}) collective-permute-start(bf16[512,1024]{1,0:T(8,128)(2,1)} %get-tuple-element.96.first_ref), channel_id=1, source_target_pairs={{0,2},{2,0},{1,3},{3,1},{4,6},{6,4},{5,7},{7,5},{8,10},{10,8},{9,1... | collective-permute-start | bytes 3145736 | tf_op jit(solution)/shard_map/ppermute | solution.py:1212
  571.2 91.1 %collective-permute-start.3 = (bf16[512,1024]{1,0:T(8,128)(2,1)S(1)}, bf16[512,1024]{1,0:T(8,128)(2,1)S(1)}, u32[]{:S(2)}, u32[]{:S(2)}) collective-permute-start(bf16[512,1024]{1,0:T(8,128)(2,1)S(1)} %copy-done.15), channel_id=1, source_target_pairs={{0,16},{16,0},{1,17},{17,1},{2,18},{18,2},{3,19},{19,3},{4,20},{20... | collective-permute-start | bytes 3145736 | tf_op jit(solution)/shard_map/ppermute | solution.py:1212
  572.4 89.9 %collective-permute-start.5 = (bf16[512,1024]{1,0:T(8,128)(2,1)S(1)}, bf16[512,1024]{1,0:T(8,128)(2,1)S(1)}, u32[]{:S(2)}, u32[]{:S(2)}) collective-permute-start(bf16[512,1024]{1,0:T(8,128)(2,1)S(1)} %copy-done.14), channel_id=1, source_target_pairs={{0,16},{16,0},{1,17},{17,1},{2,18},{18,2},{3,19},{19,3},{4,20},{20... | collective-permute-start | bytes 3145736 | tf_op jit(solution)/shard_map/ppermute | solution.py:1212
  662.3 1.0 copy-start.9
  662.3 1.3 copy-start.10
  662.3 1.7 copy-start.2
  696.7 1.0 copy-start.7
  697.7 17.4 %copy-start.3 = (bf16[4,512,256]{2,1,0:T(8,128)(2,1)S(1)}, bf16[4,512,256]{2,1,0:T(8,128)(2,1)}, u32[]{:S(2)}) copy-start(bf16[4,512,256]{2,1,0:T(8,128)(2,1)} %get-tuple-element.72.out_ref) | copy-start | bytes 3145732
Sparse Core Ops, SparseCore 0:
  126.0 52.4 all-gather.2
  566.8 130.9 all-gather.4
